TPU v7x, 256 devices: a whole 4x4x8 slice. The times are simulated.
256 devices in a mesh: seq: 64 (over x, z, core), head: 4 (over y).
Axes of the slice: x: 4, y: 4, z: 8, core: 2. Of those that a mesh axis runs over, the one named last changes fastest.
Arguments:
- queries: bfloat16 [8192, 8192], P('seq', 'head'), may hold values from -6 to 6
- key_vectors: bfloat16 [8192, 8192], P('seq', 'head'), may hold values from -6 to 6
- value_vectors: bfloat16 [8192, 8192], P('seq', 'head'), may hold values from -6 to 6
- cotangent: bfloat16 [8192, 8192], P('seq', 'head'), may hold values from -6 to 6
- member_ids: int32 [512], P('seq'), may hold values from 0 to 3
- in_scale: float32 [4, 8192], P(None, 'head'), may hold values from 0.3 to 3
- out_scale: float32 [4, 8192], P(None, 'head'), may hold values from 0.4 to 2.5
Outputs:
- query_grad: bfloat16 [8192, 8192], P('seq', 'head')
- key_grad: bfloat16 [8192, 8192], P('seq', 'head')
- value_grad: bfloat16 [8192, 8192], P('seq', 'head')
- in_scale_grad: float32 [4, 8192], P(None, 'head')
- out_scale_grad: float32 [4, 8192], P(None, 'head')
All inputs are finite; a program needn't handle non-finite values.
Results may differ from a plain program's by a relative error of at most 0.015.
Values may be sent and summed in bfloat16 or wider, within the bound.
No kernel may reach another device: no remote copies, remote signals or barrier semaphores. Data moves between devices by JAX's collectives and lax.ppermute only.
A program may use at most 192 MiB of HBM per device.

v0:
```python
import jax
import jax.numpy as jnp
from jax import lax
from jax.sharding import PartitionSpec as P

DH = 128
SPAN = 16
MEMBERS = 4


EPS = 1e-06
HIGH = lax.Precision.HIGHEST


def carried_in(x, axis, join, neutral, backward):
    count = lax.axis_size(axis)
    place = lax.axis_index(axis)
    ahead = count - 1 - place if backward else place
    gathered = lax.all_gather(x.astype(jnp.bfloat16), axis)
    state = jnp.zeros_like(x) + jnp.asarray(neutral, x.dtype)

    def one(step, state):
        source = count - 1 - step if backward else step
        return join(state, lax.dynamic_index_in_dim(gathered, source, 0, False).astype(x.dtype))

    return lax.fori_loop(0, ahead, one, state)


def add_states(earlier, later):
    return earlier + later


def shards(queries, key_vectors, value_vectors, cotangent, member_ids, in_scale, out_scale):
    tok_rows = queries.shape[0]
    local_width = queries.shape[1]
    head_count = local_width // DH
    full_width = local_width * lax.axis_size("head")
    per_token = jnp.repeat(member_ids, SPAN)
    onehot = (per_token[:, None] == jnp.arange(MEMBERS, dtype=jnp.int32)[None, :]).astype(
        jnp.float32
    )
    in_tok = jnp.dot(onehot, in_scale, precision=HIGH)
    out_tok = jnp.dot(onehot, out_scale, precision=HIGH)
    query_heads = queries.reshape(tok_rows, head_count, DH)
    key_heads = key_vectors.reshape(tok_rows, head_count, DH)
    scaled = (in_tok * value_vectors.astype(jnp.float32)).astype(jnp.bfloat16)
    scaled_heads = scaled.reshape(tok_rows, head_count, DH)
    delta_state = jnp.einsum(
        "jhd,jhe->hde", key_heads, scaled_heads, preferred_element_type=jnp.float32
    )
    state_low = carried_in(
        delta_state, "seq", add_states, jnp.zeros_like(delta_state), False
    ).astype(jnp.bfloat16)
    causal = jnp.arange(tok_rows)[:, None] >= jnp.arange(tok_rows)[None, :]
    scores = jnp.einsum("thd,jhd->htj", query_heads, key_heads, preferred_element_type=jnp.float32)
    weights = jnp.where(causal[None], scores, 0.0).astype(jnp.bfloat16)
    mixed = jnp.einsum(
        "htj,jhe->the", weights, scaled_heads, preferred_element_type=jnp.float32
    ) + jnp.einsum("thd,hde->the", query_heads, state_low, preferred_element_type=jnp.float32)
    mixed = mixed.reshape(tok_rows, local_width)
    cot_float = cotangent.astype(jnp.float32)
    scaled_cot = out_tok * cot_float
    square_sum, cross_sum = lax.psum(
        (jnp.sum(mixed * mixed, axis=1), jnp.sum(scaled_cot * mixed, axis=1)), "head"
    )
    rms_row = jnp.sqrt(square_sum / full_width + EPS)
    out_part = jnp.dot(onehot.T, cot_float * (mixed / rms_row[:, None]), precision=HIGH)
    grad_mixed = (
        scaled_cot / rms_row[:, None] - mixed * (cross_sum / (full_width * rms_row**3))[:, None]
    ).astype(jnp.bfloat16)
    grad_heads = grad_mixed.reshape(tok_rows, head_count, DH)
    grad_scores = jnp.einsum(
        "the,jhe->htj", grad_heads, scaled_heads, preferred_element_type=jnp.float32
    )
    grad_weights = jnp.where(causal[None], grad_scores, 0.0).astype(jnp.bfloat16)
    query_grad = jnp.einsum(
        "htj,jhd->thd", grad_weights, key_heads, preferred_element_type=jnp.float32
    ) + jnp.einsum("the,hde->thd", grad_heads, state_low, preferred_element_type=jnp.float32)
    delta_suffix = jnp.einsum(
        "thd,the->hde", query_heads, grad_heads, preferred_element_type=jnp.float32
    )
    suffix_low = carried_in(
        delta_suffix, "seq", add_states, jnp.zeros_like(delta_suffix), True
    ).astype(jnp.bfloat16)
    key_grad = jnp.einsum(
        "htj,thd->jhd", grad_weights, query_heads, preferred_element_type=jnp.float32
    ) + jnp.einsum("jhe,hde->jhd", scaled_heads, suffix_low, preferred_element_type=jnp.float32)
    scaled_grad = jnp.einsum(
        "htj,the->jhe", weights, grad_heads, preferred_element_type=jnp.float32
    ) + jnp.einsum("jhd,hde->jhe", key_heads, suffix_low, preferred_element_type=jnp.float32)
    scaled_grad = scaled_grad.reshape(tok_rows, local_width)
    value_grad = (in_tok * scaled_grad).astype(jnp.bfloat16)
    in_part = jnp.dot(onehot.T, value_vectors.astype(jnp.float32) * scaled_grad, precision=HIGH)
    in_total, out_total = lax.psum((in_part, out_part), "seq")
    return (
        query_grad.reshape(tok_rows, local_width).astype(jnp.bfloat16),
        key_grad.reshape(tok_rows, local_width).astype(jnp.bfloat16),
        value_grad,
        in_total,
        out_total,
    )


def solution(mesh):
    placed = (
        P("seq", "head"),
        P("seq", "head"),
        P("seq", "head"),
        P("seq", "head"),
        P("seq"),
        P(None, "head"),
        P(None, "head"),
    )
    return jax.shard_map(
        shards,
        mesh=mesh,
        in_specs=placed,
        out_specs=(
            P("seq", "head"),
            P("seq", "head"),
            P("seq", "head"),
            P(None, "head"),
            P(None, "head"),
        ),
        check_vma=False,
    )
```

profile of v0, /device:TPU:1, one launch (start us, length us, event | category | flops | bytes accessed | tf_op | source)
XLA Modules:
  0.0 665.2 jit_solution(460446443001263236)
XLA Ops:
  8.1 1.4 fusion.44
  11.6 1.4 fusion.6
  14.1 1.5 fusion.2
  17.0 143.9 %all-gather.5.cloned.1.call-done = bf16[1024,128,128]{2,1,0:T(8,128)(2,1)} async-done(((bf16[16,128,128]{2,1,0:T(8,128)(2,1)}), bf16[1024,128,128]{2,1,0:T(8,128)(2,1)}) %all-gather.5.cloned.1.call-update) | async-done | bytes 33554448 | tf_op jit(solution)/shard_map/all_gather | solution.py:19
  161.0 1.3 while.22
  161.0 1.3 convert_add_fusion.4
  162.3 1.4 fusion.11
  163.7 1.6 copy.62
  165.3 2.7 multiply_reduce_fusion
  168.0 8.4 %all-reduce.1 = (f32[128]{0:T(128)S(1)}, f32[128]{0:T(128)S(1)}) all-reduce(f32[128]{0:T(128)S(1)} %get-tuple-element.126, f32[128]{0:T(128)S(1)} %get-tuple-element.128), channel_id=1, replica_groups=mesh['seq'=64,'head'=4] {'head'}, use_global_device_ids=true, to_apply=%region_5.6 | all-reduce | flops 256 | bytes 2048 | tf_op jit(solution)/shard_map/psum | solution.py:63
  176.5 2.2 subtract_convert_fusion
  178.7 2.0 copy.64
  180.8 2.1 fusion.7
  182.9 2.1 copy.52
  185.0 1.6 fusion.3
  186.6 1.7 convolution_bitcast_fusion.3
  188.3 2.1 fusion.4
  190.5 2.0 copy.58
  192.5 2.3 fusion.8
  194.8 1.5 fusion.51
  196.3 205.5 %all-gather.7.cloned.1.call-done = bf16[1024,128,128]{2,1,0:T(8,128)(2,1)} async-done(((bf16[16,128,128]{2,1,0:T(8,128)(2,1)}), bf16[1024,128,128]{2,1,0:T(8,128)(2,1)}) %all-gather.7.cloned.1.call-update) | async-done | bytes 33554448 | tf_op jit(solution)/shard_map/all_gather | solution.py:19
  401.9 80.9 %while.23 = (s32[]{:T(128)}, f32[16,128,128]{2,1,0:T(8,128)S(1)}, s32[]{:T(128)}, bf16[64,16,128,128]{3,2,1,0:T(8,128)(2,1)}, s32[]{:T(128)}, /*index=5*/s32[]{:T(128)}, s32[]{:T(128)}, s32[]{:T(128)}) while((s32[]{:T(128)}, f32[16,128,128]{2,1,0:T(8,128)S(1)}, s32[]{:T(128)}, bf16[64,16,128,128]{3,2,1,0:T(8,128)(2,1)}, s32[]{:T(128)}, ...), condition=%wide.region_7.8_spmd, body=%wide.region_6.7_spmd.sunk | while | flops 524294 | bytes 2621583 | solution.py:26
  404.6 1.3 convert_add_fusion.5
  405.9 1.3 convert_add_fusion.5
  407.2 1.3 convert_add_fusion.5
  412.4 1.3 convert_add_fusion.5
  413.7 1.3 convert_add_fusion.5
  415.0 1.3 convert_add_fusion.5
  416.3 1.3 convert_add_fusion.5
  420.2 1.3 convert_add_fusion.5
  421.5 1.3 convert_add_fusion.5
  422.8 1.3 convert_add_fusion.5
  424.1 1.3 convert_add_fusion.5
  429.4 1.3 convert_add_fusion.5
  430.7 1.3 convert_add_fusion.5
  432.0 1.3 convert_add_fusion.5
  437.2 1.3 convert_add_fusion.5
  438.5 1.3 convert_add_fusion.5
  439.8 1.3 convert_add_fusion.5
  441.1 1.3 convert_add_fusion.5
  445.0 1.3 convert_add_fusion.5
  446.3 1.3 convert_add_fusion.5
  447.6 1.3 convert_add_fusion.5
  448.9 1.3 convert_add_fusion.5
  454.2 1.3 convert_add_fusion.5
  455.5 1.3 convert_add_fusion.5
  456.8 1.3 convert_add_fusion.5
  462.0 1.3 convert_add_fusion.5
  463.3 1.3 convert_add_fusion.5
  464.6 1.3 convert_add_fusion.5
  465.9 1.3 convert_add_fusion.5
  469.8 1.3 convert_add_fusion.5
  471.1 1.3 convert_add_fusion.5
  472.4 1.3 convert_add_fusion.5
  473.7 1.3 convert_add_fusion.5
  482.9 1.5 convolution_bitcast_fusion.1
  484.3 2.6 convolution_add_fusion
  486.9 1.6 copy.63
  488.5 2.1 multiply_convert_fusion
  490.6 2.2 fusion.10
  492.8 1.7 fusion.5
  495.6 160.3 %all-reduce.4.cloned.1.call-done = (f32[4,2048]{1,0:T(4,128)}, f32[4,2048]{1,0:T(4,128)}) async-done(((f32[4,2048]{1,0:T(4,128)}, f32[4,2048]{1,0:T(4,128)}), (f32[4,2048]{1,0:T(4,128)}, f32[4,2048]{1,0:T(4,128)})) %all-reduce.4.cloned.1.call-update) | async-done | bytes 65552 | tf_op jit(solution)/shard_map/psum | solution.py:94
  655.9 1.4 copy.132
  657.3 1.4 copy.133
  (53 shorter events, 43.9 us)
Async XLA Ops:
  7.2 7.0 %copy-start = (bf16[128,2048]{1,0:T(8,128)(2,1)S(1)}, bf16[128,2048]{1,0:T(8,128)(2,1)}, u32[]{:S(2)}) copy-start(bf16[128,2048]{1,0:T(8,128)(2,1)} %param.11) | copy-start | bytes 1572868
  7.2 153.7 %all-gather.5.cloned.1.call-start = ((), (), s32[]{:S(2)}) async-start(), calls=%async_computation | async-start | bytes 34078720 | tf_op jit(solution)/shard_map/all_gather | solution.py:19
  9.5 1.0 copy-start.1
  14.1 387.8 %all-gather.7.cloned.1.call-start = ((), (), s32[]{:S(2)}) async-start(), calls=%async_computation.1 | async-start | bytes 34078720 | tf_op jit(solution)/shard_map/all_gather | solution.py:19
  15.7 0.8 copy-start.3
  185.0 470.9 %all-reduce.4.cloned.1.call-start = ((), (), s32[]{:S(2)}) async-start(), calls=%async_computation.2 | async-start | bytes 131072 | tf_op jit(solution)/shard_map/psum | solution.py:94
  186.6 3.9 copy-start.2
Sparse Core Ops, SparseCore 0:
  14.2 146.6 all-gather.4
  185.1 216.6 all-gather.6
  493.0 162.8 all-reduce.3
where the time goes:
time: 669 us; the launch traced here: 665 us
  waiting for transfers between devices  510 us (76%)
  other arithmetic  86.4 us (13%)
  matrix products  28.3 us (4%)
  local copies, waits for them, and re-layouts  16.8 us (3%)
  between operations  13.9 us (2%)
  blocking collectives  8.43 us (1%)
    all_gather x2, waiting for transfers between devices, carried_in(): gathered = lax.all_gather(x.astype(jnp.bfloat16), axis)  349 us
    psum x1, waiting for transfers between devices, shards(): in_total, out_total = lax.psum((in_part, out_part), 'seq')  160 us
    add x63, other arithmetic, add_states(): return earlier + later  80.8 us
  transfers between devices with their start and end apart: 3, of which 3 were waited for; matrix products, arithmetic and copies ran while one was open for 2% of the time, Pallas kernels for 0%

commit v1 on v0

v1 whole, which is shorter than its diff:
```python
import functools

import jax
import jax.numpy as jnp
from jax import lax
from jax.experimental import pallas as pl
from jax.experimental.pallas import tpu as pltpu
from jax.sharding import PartitionSpec as P

DH = 128
SPAN = 16
MEMBERS = 4
EPS = 1e-06
CORES = 2
STEP_HEADS = 4
F32 = jnp.float32
BF16 = jnp.bfloat16

NN = (((1,), (0,)), ((), ()))
NT = (((1,), (1,)), ((), ()))
TN = (((0,), (0,)), ((), ()))


def dot(a, b, dims):
    return lax.dot_general(a, b, dims, preferred_element_type=F32)


def pair(own, other, lanes):
    return jnp.concatenate([own[:, lanes], other[:, lanes]], axis=0)


def rows_of_members(meta, scale, lanes, spans):
    choices = [scale[m : m + 1, lanes] for m in range(MEMBERS)]
    rows = []
    for s in range(spans):
        row = choices[0]
        for m in range(1, MEMBERS):
            row = jnp.where(meta[1 + s] == m, choices[m], row)
        rows.append(jnp.broadcast_to(row, (SPAN, DH)))
    return jnp.concatenate(rows, axis=0)


def member_sums(meta, x, spans):
    totals = [jnp.zeros((8, DH), F32) for _ in range(MEMBERS)]
    for s in range(spans):
        part = x[s * SPAN : s * SPAN + 8] + x[s * SPAN + 8 : (s + 1) * SPAN]
        for m in range(MEMBERS):
            keep = jnp.where(meta[1 + s] == m, 1.0, 0.0).astype(F32)
            totals[m] = totals[m] + keep * part
    return jnp.concatenate([jnp.sum(t, axis=0, keepdims=True) for t in totals], axis=0)


def causal_mask(meta, tok):
    size = 2 * tok
    core = meta[0]
    base_own = core * tok
    base_other = (1 - core) * tok - tok

    def place(axis):
        at = lax.broadcasted_iota(jnp.int32, (size, size), axis)
        return at + jnp.where(at < tok, base_own, base_other)

    return place(0) >= place(1)


def lanes_of(h):
    return pl.ds(h * DH, DH)


def states_kernel(meta, scale, k_own, k_other, v_own, v_other, scaled, delta):
    tok = k_own.shape[0]
    spans = 2 * tok // SPAN
    for h in range(delta.shape[0]):
        lanes = lanes_of(h)
        value = pair(v_own, v_other, lanes).astype(F32)
        low = (rows_of_members(meta, scale, lanes, spans) * value).astype(BF16)
        scaled[:, lanes] = low
        delta[h] = dot(pair(k_own, k_other, lanes), low, TN).astype(BF16)


def inside_kernel(meta, q_own, q_other, k_own, k_other, scaled, inside):
    tok = q_own.shape[0]
    causal = causal_mask(meta, tok)
    for h in range(scaled.shape[1] // DH):
        lanes = lanes_of(h)
        scores = dot(pair(q_own, q_other, lanes), pair(k_own, k_other, lanes), NT)
        weights = jnp.where(causal, scores, 0.0).astype(BF16)
        inside[:, lanes] = dot(weights, scaled[:, lanes], NN)


def mixed_kernel(
    meta, scale, q_own, q_other, c_own, c_other, state, inside, mixed, sums, squares, crosses
):
    tok = q_own.shape[0]
    spans = 2 * tok // SPAN
    step = pl.program_id(0)

    @pl.when(step == 0)
    def _():
        squares[...] = jnp.zeros_like(squares)
        crosses[...] = jnp.zeros_like(crosses)

    square, cross = squares[...], crosses[...]
    for h in range(state.shape[0]):
        lanes = lanes_of(h)
        mix = inside[:, lanes] + dot(pair(q_own, q_other, lanes), state[h], NN)
        mixed[:, lanes] = mix
        cot = pair(c_own, c_other, lanes).astype(F32)
        square = square + mix * mix
        cross = cross + rows_of_members(meta, scale, lanes, spans) * cot * mix
    squares[...] = square
    crosses[...] = cross

    @pl.when(step == pl.num_programs(0) - 1)
    def _():
        sums[0:1] = jnp.sum(jnp.transpose(square), axis=0, keepdims=True)
        sums[1:2] = jnp.sum(jnp.transpose(cross), axis=0, keepdims=True)


def grads_kernel(
    full_width, meta, scale, q_own, q_other, c_own, c_other, mixed, sums, grad, delta, out_part
):
    tok = q_own.shape[0]
    spans = 2 * tok // SPAN
    rms = jnp.sqrt(sums[0:1] / full_width + EPS)
    inverse = 1.0 / rms
    factor = sums[1:2] / (full_width * rms * rms * rms)
    inverse = jnp.transpose(jnp.broadcast_to(inverse, (DH, 2 * tok)))
    factor = jnp.transpose(jnp.broadcast_to(factor, (DH, 2 * tok)))
    for h in range(delta.shape[0]):
        lanes = lanes_of(h)
        cot = pair(c_own, c_other, lanes).astype(F32) * inverse
        mix = mixed[:, lanes]
        low = (rows_of_members(meta, scale, lanes, spans) * cot - mix * factor).astype(BF16)
        grad[:, lanes] = low
        delta[h] = dot(pair(q_own, q_other, lanes), low, TN).astype(BF16)
        out_part[:, lanes] = member_sums(meta, cot * mix, spans)


def back_kernel(
    meta, q_own, q_other, k_own, k_other, scaled, grad, state, query_own, query_other, key_in, value_in
):
    tok = q_own.shape[0]
    causal = causal_mask(meta, tok)
    for h in range(state.shape[0]):
        lanes = lanes_of(h)
        query = pair(q_own, q_other, lanes)
        key = pair(k_own, k_other, lanes)
        low = scaled[:, lanes]
        g = grad[:, lanes]
        weights = jnp.where(causal, dot(query, key, NT), 0.0).astype(BF16)
        grad_weights = jnp.where(causal, dot(g, low, NT), 0.0).astype(BF16)
        query_grad = (dot(grad_weights, key, NN) + dot(g, state[h], NT)).astype(BF16)
        query_own[:, lanes] = query_grad[:tok]
        query_other[:, lanes] = query_grad[tok:]
        key_in[:, lanes] = dot(grad_weights, query, TN)
        value_in[:, lanes] = dot(weights, g, TN)


def last_kernel(
    meta, scale, k_own, k_other, v_own, v_other, scaled, state, key_in, value_in,
    key_grad_own, key_grad_other, value_grad_own, value_grad_other, in_part,
):
    tok = k_own.shape[0]
    spans = 2 * tok // SPAN
    for h in range(state.shape[0]):
        lanes = lanes_of(h)
        key_grad = (key_in[:, lanes] + dot(scaled[:, lanes], state[h], NT)).astype(BF16)
        key_grad_own[:, lanes] = key_grad[:tok]
        key_grad_other[:, lanes] = key_grad[tok:]
        scaled_grad = value_in[:, lanes] + dot(pair(k_own, k_other, lanes), state[h], NN)
        value_grad = (rows_of_members(meta, scale, lanes, spans) * scaled_grad).astype(BF16)
        value_grad_own[:, lanes] = value_grad[:tok]
        value_grad_other[:, lanes] = value_grad[tok:]
        value = pair(v_own, v_other, lanes).astype(F32)
        in_part[:, lanes] = member_sums(meta, value * scaled_grad, spans)


def running_kernel(backward, pieces, sums):
    count = pieces.shape[0]
    total = jnp.zeros(pieces.shape[1:], F32)
    order = range(count - 1, -1, -1) if backward else range(count)
    for at in order:
        sums[at] = total.astype(BF16)
        total = total + pieces[at].astype(F32)


class Local:
    def __init__(self, meta, tok, width):
        self.meta = meta
        self.tok = tok
        self.width = width
        self.block = STEP_HEADS * DH
        self.steps = width // self.block

    def shared(self, rows):
        steps = self.steps
        return pl.BlockSpec((rows, self.block), lambda i, meta: (0, meta[0] * steps + i))

    def cols(self, rows):
        return pl.BlockSpec((rows, self.block), lambda i, meta: (0, i))

    def state(self):
        return pl.BlockSpec((STEP_HEADS, DH, DH), lambda i, meta: (i, 0, 0))

    def whole(self, shape):
        return pl.BlockSpec(shape, lambda i, meta: (0,) * len(shape))

    def call(self, body, ins, outs, args, shapes, name, scratch=(), flops=0):
        moved = sum(a.size * a.dtype.itemsize for a in args)
        return pl.pallas_call(
            body,
            grid_spec=pltpu.PrefetchScalarGridSpec(
                num_scalar_prefetch=1,
                grid=(self.steps,),
                in_specs=ins,
                out_specs=outs,
                scratch_shapes=scratch,
            ),
            out_shape=shapes,
            name=name,
            compiler_params=pltpu.CompilerParams(vmem_limit_bytes=32 * 2**20),
            cost_estimate=pl.CostEstimate(flops=flops, bytes_accessed=2 * moved, transcendentals=0),
        )(self.meta, *args)


def running_sums(pieces, backward):
    return pl.pallas_call(
        functools.partial(running_kernel, backward),
        out_shape=jax.ShapeDtypeStruct(pieces.shape, BF16),
        name="running_sums",
        compiler_params=pltpu.CompilerParams(vmem_limit_bytes=32 * 2**20),
    )(pieces)


def make_shards(n_seq, n_head):
    chips = n_seq // CORES
    core_swap = [(i, i ^ 1) for i in range(n_seq)]
    same_core = [[CORES * i + c for i in range(chips)] for c in range(CORES)]

    def swap(x):
        return lax.ppermute(x, "seq", core_swap)

    def scanned(delta, backward):
        heads = delta.shape[0]
        pieces = delta.reshape(chips, heads * DH // chips, DH)
        pieces = lax.all_to_all(
            pieces, "seq", 0, 0, axis_index_groups=same_core, tiled=True
        )
        sums = running_sums(pieces, backward)
        sums = lax.all_to_all(sums, "seq", 0, 0, axis_index_groups=same_core, tiled=True)
        return sums.reshape(heads, DH, DH)

    def side_by_side(core, own, other):
        return jnp.where(
            core == 0,
            jnp.concatenate([own, other], axis=1),
            jnp.concatenate([other, own], axis=1),
        )

    def shards(queries, key_vectors, value_vectors, cotangent, member_ids, in_scale, out_scale):
        tok, both = queries.shape
        width = both // CORES
        heads = width // DH
        full_width = both * n_head
        rows = 2 * tok
        core = lax.axis_index("seq") % CORES

        other_ids = swap(member_ids)
        v_other = swap(value_vectors)
        k_other = swap(key_vectors)
        meta = jnp.concatenate([core[None].astype(jnp.int32), member_ids, other_ids])
        local = Local(meta, tok, width)
        shared, cols, state = local.shared, local.cols, local.state
        sds = jax.ShapeDtypeStruct
        half = sds((tok, width), BF16)
        states = sds((heads, DH, DH), BF16)
        part = sds((MEMBERS, width), F32)
        wide = sds((rows, width), F32)
        pairs = [shared(tok), shared(tok)]
        unit = 2 * heads * rows * DH * DH

        scaled, delta = local.call(
            states_kernel,
            [shared(MEMBERS)] + pairs * 2,
            [cols(rows), state()],
            (in_scale, key_vectors, k_other, value_vectors, v_other),
            [sds((rows, width), BF16), states],
            "states",
            flops=unit,
        )
        queries_late, cotangent_late, delta = lax.optimization_barrier((queries, cotangent, delta))
        q_other = swap(queries_late)
        c_other = swap(cotangent_late)
        state_in = scanned(delta, False)
        inside = local.call(
            inside_kernel,
            pairs * 2 + [cols(rows)],
            cols(rows),
            (queries, q_other, key_vectors, k_other, scaled),
            wide,
            "inside",
            flops=4 * unit,
        )
        mixed, sums = local.call(
            mixed_kernel,
            [shared(MEMBERS)] + pairs * 2 + [state(), cols(rows)],
            [cols(rows), local.whole((2, rows))],
            (out_scale, queries, q_other, cotangent, c_other, state_in, inside),
            [wide, sds((2, rows), F32)],
            "mixed",
            scratch=[pltpu.VMEM((rows, DH), F32)] * 2,
            flops=unit,
        )
        across = swap(sums)
        sums = sums + jnp.concatenate([across[:, tok:], across[:, :tok]], axis=1)
        step = 1
        while step < n_head:
            sums = sums + lax.ppermute(sums, "head", [(i, i ^ step) for i in range(n_head)])
            step *= 2
        grad, delta_after, out_part = local.call(
            functools.partial(grads_kernel, full_width),
            [shared(MEMBERS)] + pairs * 2 + [cols(rows), local.whole((2, rows))],
            [cols(rows), state(), cols(MEMBERS)],
            (out_scale, queries, q_other, cotangent, c_other, mixed, sums),
            [sds((rows, width), BF16), states, part],
            "grads",
            flops=unit,
        )
        state_after = scanned(delta_after, True)
        query_own, query_send, key_in, value_in = local.call(
            back_kernel,
            pairs * 2 + [cols(rows), cols(rows), state()],
            [cols(tok), cols(tok), cols(rows), cols(rows)],
            (queries, q_other, key_vectors, k_other, scaled, grad, state_in),
            [half, half, wide, wide],
            "back",
            flops=11 * unit,
        )
        query_grad = side_by_side(core, query_own, swap(query_send))
        key_own, key_send, value_own, value_send, in_part = local.call(
            last_kernel,
            [shared(MEMBERS)] + pairs * 2 + [cols(rows), state(), cols(rows), cols(rows)],
            [cols(tok)] * 4 + [cols(MEMBERS)],
            (in_scale, key_vectors, k_other, value_vectors, v_other, scaled, state_after, key_in, value_in),
            [half] * 4 + [part],
            "last",
            flops=2 * unit,
        )
        parts = jnp.concatenate([in_part, out_part], axis=0)
        step = CORES
        while step < n_seq:
            parts = parts + lax.ppermute(parts, "seq", [(i, i ^ step) for i in range(n_seq)])
            step *= 2
        parts = side_by_side(core, parts, swap(parts))
        key_grad = side_by_side(core, key_own, swap(key_send))
        value_grad = side_by_side(core, value_own, swap(value_send))
        return query_grad, key_grad, value_grad, parts[:MEMBERS], parts[MEMBERS:]

    return shards


def solution(mesh):
    n_seq, n_head = mesh.shape["seq"], mesh.shape["head"]
    shards = make_shards(n_seq, n_head)
    placed = (
        P("seq", "head"),
        P("seq", "head"),
        P("seq", "head"),
        P("seq", "head"),
        P("seq"),
        P(None, "head"),
        P(None, "head"),
    )
    return jax.shard_map(
        shards,
        mesh=mesh,
        in_specs=placed,
        out_specs=(
            P("seq", "head"),
            P("seq", "head"),
            P("seq", "head"),
            P(None, "head"),
            P(None, "head"),
        ),
        check_vma=False,
    )
```

time: 669 us -> 139 us (0.21)
  waiting for transfers between devices: 510 us -> 36.5 us
  other arithmetic: 86.4 us -> 3.56 us
  starting transfers between devices: 0.12 us -> 51 us
  matrix products: 28.3 us -> 0 us
  Pallas kernels: 0 us -> 16.8 us
  between operations: 13.9 us -> 0.89 us
    all_gather x2 -> x0, waiting for transfers between devices: 349 us -> none  [carried_in(): gathered = lax.all_gather(x.astype(jnp.bfloat16), axis)]
    psum x1 -> x0, waiting for transfers between devices: 160 us -> none  [shards(): in_total, out_total = lax.psum((in_part, out_part), 'seq')]
    add x63 -> x8, other arithmetic: 80.8 us -> 0.05 us  [the longest x5 0.03 us: shards(): parts + lax.ppermute(parts, 'seq', [(i, i ^ step) for i in range(n_seq)])]
    ppermute x0 -> x17, starting transfers between devices: none -> 30 us  [the longest x10 20.6 us: swap(): return lax.ppermute(x, 'seq', core_swap)]
    dot_general x16 -> x0, matrix products: 28.3 us -> none  [the longest x1 2.74 us: shards(): out_tok = jnp.dot(onehot, out_scale, precision=HIGH)]
    all_to_all x0 -> x3, starting transfers between devices: none -> 20.9 us  [the longest x2 11.5 us: scanned(): lax.all_to_all(sums, 'seq', 0, 0, axis_index_groups=same_core, tiled=True)]
    ppermute x0 -> x17, waiting for transfers between devices: none -> 19.7 us  [the longest x5 14.4 us: shards(): lax.ppermute(parts, 'seq', [(i, i ^ step) for i in range(n_seq)])]
    pallas_call x0 -> x8, Pallas kernels: none -> 16.8 us  [the longest x6 16 us: call(): pl.pallas_call(body, grid_spec=pltpu.PrefetchScalarGridSpec(num_scalar_pr...]
  transfers between devices with their start and end apart: 3 -> 20, of which waited for: 3 -> 12; matrix products, arithmetic and copies ran while one was open for 2% -> 2% of each run, Pallas kernels for 0% -> 5%
where the time goes in v1:
time: 139 us; the launch traced here: 138 us
  starting transfers between devices  51 us (37%)
  waiting for transfers between devices  36.5 us (26%)
  Pallas kernels  16.8 us (12%)
  local copies, waits for them, and re-layouts  16 us (12%)
  blocking collectives  13.7 us (10%)
  other arithmetic  3.56 us (3%)
    ppermute x10, starting transfers between devices, swap(): return lax.ppermute(x, 'seq', core_swap)  20.6 us
    pallas_call x6, Pallas kernels, call(): pl.pallas_call(body, grid_spec=pltpu.PrefetchScalarGridSpec(num_scalar_pr...  16 us
    unnamed x52, local copies, waits for them, and re-layouts  15.4 us
    ppermute x5, waiting for transfers between devices, shards(): lax.ppermute(parts, 'seq', [(i, i ^ step) for i in range(n_seq)])  14.4 us
    all_to_all x1, blocking collectives, scanned(): lax.all_to_all(pieces, 'seq', 0, 0, axis_index_groups=same_core, tiled=True)  13.7 us
    all_to_all x2, starting transfers between devices, scanned(): lax.all_to_all(sums, 'seq', 0, 0, axis_index_groups=same_core, tiled=True)  11.5 us
    all_to_all x1, starting transfers between devices, scanned(): lax.all_to_all(pieces, 'seq', 0, 0, axis_index_groups=same_core, tiled=True)  9.43 us
    all_to_all x1, waiting for transfers between devices, scanned(): lax.all_to_all(pieces, 'seq', 0, 0, axis_index_groups=same_core, tiled=True)  8.8 us
  transfers between devices with their start and end apart: 20, of which 12 were waited for; matrix products, arithmetic and copies ran while one was open for 2% of the time, Pallas kernels for 5%

profile of v1, /device:TPU:1, one launch (start us, length us, event | category | flops | bytes accessed | tf_op | source)
XLA Modules:
  0.0 138.5 jit_solution(14837886035360498888)
XLA Ops:
  0.6 3.3 %collective-permute-start.2 = (bf16[128,2048]{1,0:T(8,128)(2,1)}, bf16[128,2048]{1,0:T(8,128)(2,1)S(1)}, u32[]{:S(2)}, u32[]{:S(2)}) collective-permute-start(bf16[128,2048]{1,0:T(8,128)(2,1)} %v_own.3), channel_id=1, source_target_pairs={{0,4},{4,0},{8,12},{12,8},{16,20},{20,16},{24,28},{28,24},{32,36},... | collective-permute-start | bytes 1572872 | tf_op jit(solution)/shard_map/ppermute | solution.py:242
  4.0 0.1 collective-permute-start.1
  4.1 0.4 collective-permute-start
  4.5 2.0 %collective-permute-done = s32[8]{0:T(128)S(1)} collective-permute-done((s32[8]{0:T(128)}, s32[8]{0:T(128)S(1)}, u32[]{:S(2)}, u32[]{:S(2)}) %collective-permute-start) | collective-permute-done | bytes 64 | tf_op jit(solution)/shard_map/ppermute | solution.py:242
  6.5 0.7 pad_add_fusion.meta
  7.2 0.0 copy-start.1
  7.2 1.2 copy-done.1
  8.5 1.0 copy-done.6
  9.5 1.4 %states.1 = (bf16[256,1024]{1,0:T(8,128)(2,1)S(1)}, bf16[8,128,128]{2,1,0:T(8,128)(2,1)S(1)}) custom-call(s32[17]{0:T(128)S(1)} %pad_add_fusion.meta, f32[4,2048]{1,0:T(4,128)S(1)} %copy-done.21, bf16[128,2048]{1,0:T(8,128)(2,1)S(1)} %copy-done.1, bf16[128,2048]{1,0:T(8,128)(2,1)S(1)} %collective-permute-done.1.k_other, bf16[128,2048]{1,0:T(8,128)(2,1)S(1)} %copy-done.6, ...), custom_call_target="tpu_custom_call" | custom-call | flops 67108864 | bytes 4259840 | tf_op jit(solution)/shard_map/states/pallas_call | solution.py:211
  10.9 0.7 copy-done.17
  11.6 9.4 %all-to-all-start = ((bf16[32,32,128]{2,1,0:T(8,128)(2,1)}), bf16[32,32,128]{2,1,0:T(8,128)(2,1)S(1)}, u32[]{:S(2)}, u32[]{:S(2)}) async-start(bf16[32,32,128]{2,1,0:T(8,128)(2,1)} %bitcast.7), calls=%async_computation | async-start | bytes 524288 | tf_op jit(solution)/shard_map/all_to_all | solution.py:247
  21.1 0.7 collective-permute-start.3
  21.8 0.1 collective-permute-start.4
  21.9 8.8 %all-to-all-done.pieces = bf16[32,32,128]{2,1,0:T(8,128)(2,1)S(1)} async-done(((bf16[32,32,128]{2,1,0:T(8,128)(2,1)}), bf16[32,32,128]{2,1,0:T(8,128)(2,1)S(1)}, u32[]{:S(2)}, u32[]{:S(2)}) %all-to-all-start) | async-done | bytes 262176 | tf_op jit(solution)/shard_map/all_to_all | solution.py:247
  30.8 0.7 copy-done.10
  31.5 6.7 %all-to-all-start.1 = ((bf16[32,32,128]{2,1,0:T(8,128)(2,1)}), bf16[32,32,128]{2,1,0:T(8,128)(2,1)S(1)}, u32[]{:S(2)}, u32[]{:S(2)}) async-start(bf16[32,32,128]{2,1,0:T(8,128)(2,1)} %copy-done.10), calls=%async_computation.1 | async-start | bytes 524288 | tf_op jit(solution)/shard_map/all_to_all | solution.py:251
  38.3 2.1 %inside.1 = f32[256,1024]{1,0:T(8,128)S(1)} custom-call(s32[17]{0:T(128)S(1)} %pad_add_fusion.meta, bf16[128,2048]{1,0:T(8,128)(2,1)S(1)} %copy-done, bf16[128,2048]{1,0:T(8,128)(2,1)S(1)} %collective-permute-done.3.q_other, bf16[128,2048]{1,0:T(8,128)(2,1)S(1)} %copy-done.2, bf16[128,2048]{1,0:T(8,128)(2,1)S(1)} %collective-permute-done.1.k_other, ...), custom_call_target="tpu_custom_call" | custom-call | flops 268435456 | bytes 5242880 | tf_op jit(solution)/shard_map/inside/pallas_call | solution.py:211
  40.4 1.0 copy-done.3
  41.4 6.5 %all-to-all-done.1 = bf16[32,32,128]{2,1,0:T(8,128)(2,1)S(1)} async-done(((bf16[32,32,128]{2,1,0:T(8,128)(2,1)}), bf16[32,32,128]{2,1,0:T(8,128)(2,1)S(1)}, u32[]{:S(2)}, u32[]{:S(2)}) %all-to-all-start.1) | async-done | bytes 262176 | tf_op jit(solution)/shard_map/all_to_all | solution.py:251
  47.9 1.2 copy-done.4
  49.1 2.4 %mixed.1 = (f32[256,1024]{1,0:T(8,128)S(1)}, f32[2,256]{1,0:T(2,128)S(1)}) custom-call(s32[17]{0:T(128)S(1)} %pad_add_fusion.meta, f32[4,2048]{1,0:T(4,128)S(1)} %copy-done.20, bf16[128,2048]{1,0:T(8,128)(2,1)S(1)} %copy-done, bf16[128,2048]{1,0:T(8,128)(2,1)S(1)} %collective-permute-done.3.q_other, bf16[128,2048]{1,0:T(8,128)(2,1)S(1)} %copy-done.5, ...), custom_call_target="tpu_custom_call" | custom-call | flops 67108864 | bytes 6881280 | tf_op jit(solution)/shard_map/mixed/pallas_call | solution.py:211
  51.5 3.7 %collective-permute-start.5 = (f32[2,256]{1,0:T(2,128)S(1)}, f32[2,256]{1,0:T(2,128)S(1)}, u32[]{:S(2)}, u32[]{:S(2)}) collective-permute-start(f32[2,256]{1,0:T(2,128)S(1)} %get-tuple-element.30), channel_id=1, source_target_pairs={{0,4},{4,0},{8,12},{12,8},{16,20},{20,16},{24,28},{28,24},{32,36},... | collective-permute-start | bytes 6152 | tf_op jit(solution)/shard_map/ppermute | solution.py:242
  55.2 0.8 collective-permute-done.5
  56.0 1.3 collective-permute-start.6
  57.3 1.1 collective-permute-done.6
  58.4 2.9 %collective-permute-start.7 = (f32[2,256]{1,0:T(2,128)S(1)}, f32[2,256]{1,0:T(2,128)S(1)}, u32[]{:S(2)}, u32[]{:S(2)}) collective-permute-start(f32[2,256]{1,0:T(2,128)S(1)} %add.30), channel_id=1, source_target_pairs={{0,2},{1,3},{2,0},{3,1},{4,6},{5,7},{6,4},{7,5},{8,10},{9,11},{10,... | collective-permute-start | bytes 6152 | tf_op jit(solution)/shard_map/ppermute | solution.py:319
  61.4 1.0 collective-permute-done.7
  62.4 2.7 %grads.1 = (bf16[256,1024]{1,0:T(8,128)(2,1)S(1)}, bf16[8,128,128]{2,1,0:T(8,128)(2,1)S(1)}, f32[4,1024]{1,0:T(4,128)S(1)}) custom-call(s32[17]{0:T(128)S(1)} %pad_add_fusion.meta, f32[4,2048]{1,0:T(4,128)S(1)} %copy-done.20, bf16[128,2048]{1,0:T(8,128)(2,1)S(1)} %copy-done, bf16[128,2048]{1,0:T(8,128)(2,1)S(1)} %collective-permute-done.3.q_other, ...), custom_call_target="tpu_custom_call" | custom-call | flops 67108864 | bytes 6361088 | tf_op jit(solution)/shard_map/grads/pallas_call | solution.py:211
  65.1 0.8 copy-done.15
  65.9 13.7 %all_to_all.20.pieces = bf16[32,32,128]{2,1,0:T(8,128)(2,1)S(1)} all-to-all(bf16[32,32,128]{2,1,0:T(8,128)(2,1)S(1)} %bitcast.8), channel_id=1, replica_groups={{0,8,16,24,32,40,48,56,64,72,80,88,96,104,112,120,128,136,144,152,160,1..., dimensions={0} | all-to-all | bytes 524288 | tf_op jit(solution)/shard_map/all_to_all | solution.py:247
  79.6 0.7 running_sums.3
  80.3 4.8 %all-to-all-start.3 = ((bf16[32,32,128]{2,1,0:T(8,128)(2,1)}), bf16[32,32,128]{2,1,0:T(8,128)(2,1)}, u32[]{:S(2)}, u32[]{:S(2)}) async-start(bf16[32,32,128]{2,1,0:T(8,128)(2,1)} %running_sums.3), calls=%async_computation.3 | async-start | bytes 524288 | tf_op jit(solution)/shard_map/all_to_all | solution.py:251
  85.2 1.0 copy-done.16
  86.2 4.4 %back.1 = (bf16[128,1024]{1,0:T(8,128)(2,1)S(1)}, bf16[128,1024]{1,0:T(8,128)(2,1)}, f32[256,1024]{1,0:T(8,128)S(1)}, f32[256,1024]{1,0:T(8,128)S(1)}) custom-call(s32[17]{0:T(128)S(1)} %pad_add_fusion.meta, bf16[128,2048]{1,0:T(8,128)(2,1)S(1)} %copy-done, bf16[128,2048]{1,0:T(8,128)(2,1)S(1)} %collective-permute-done.3.q_other, ...), custom_call_target="tpu_custom_call" | custom-call | flops 738197504 | bytes 6815744 | tf_op jit(solution)/shard_map/back/pallas_call | solution.py:211
  90.6 1.0 copy-done.11
  91.6 1.0 copy-done.13
  92.6 0.7 copy-done.18
  93.3 1.5 %all-to-all-done.3 = bf16[32,32,128]{2,1,0:T(8,128)(2,1)} async-done(((bf16[32,32,128]{2,1,0:T(8,128)(2,1)}), bf16[32,32,128]{2,1,0:T(8,128)(2,1)}, u32[]{:S(2)}, u32[]{:S(2)}) %all-to-all-start.3) | async-done | bytes 262176 | tf_op jit(solution)/shard_map/all_to_all | solution.py:251
  94.8 1.0 copy-done.9
  95.8 1.2 copy-done.12
  97.1 1.2 copy-done.14
  98.3 3.0 %last.1 = (bf16[128,1024]{1,0:T(8,128)(2,1)S(1)}, bf16[128,1024]{1,0:T(8,128)(2,1)S(1)}, bf16[128,1024]{1,0:T(8,128)(2,1)S(1)}, bf16[128,1024]{1,0:T(8,128)(2,1)S(1)}, f32[4,1024]{1,0:T(4,128)S(1)}) custom-call(s32[17]{0:T(128)S(1)} %pad_add_fusion.meta, f32[4,2048]{1,0:T(4,128)S(1)} %copy-done.21, bf16[128,2048]{1,0:T(8,128)(2,1)S(1)} %copy-done.2, ...), custom_call_target="tpu_custom_call" | custom-call | flops 134217728 | bytes 10027008 | tf_op jit(solution)/shard_map/last/pallas_call | solution.py:211
  101.2 0.7 copy-done.22
  101.9 0.7 copy-done.24
  102.7 1.8 %collective-permute-start.11 = (f32[8,1024]{1,0:T(8,128)S(1)}, f32[8,1024]{1,0:T(8,128)S(1)}, u32[]{:S(2)}, u32[]{:S(2)}) collective-permute-start(f32[8,1024]{1,0:T(8,128)S(1)} %pad_maximum_fusion), channel_id=1, source_target_pairs={{0,8},{4,12},{8,0},{12,4},{16,24},{20,28},{24,16},{28,20},{32,40},... | collective-permute-start | bytes 98312 | tf_op jit(solution)/shard_map/ppermute | solution.py:353
  104.4 5.6 %collective-permute-start.8 = (bf16[128,1024]{1,0:T(8,128)(2,1)}, bf16[128,1024]{1,0:T(8,128)(2,1)S(1)}, u32[]{:S(2)}, u32[]{:S(2)}) collective-permute-start(bf16[128,1024]{1,0:T(8,128)(2,1)} %get-tuple-element.33), channel_id=1, source_target_pairs={{0,4},{4,0},{8,12},{12,8},{16,20},{20,16},{24,28},{28,24},{32,36},... | collective-permute-start | bytes 786440 | tf_op jit(solution)/shard_map/ppermute | solution.py:242
  110.1 0.5 collective-permute-start.12
  110.6 3.3 %collective-permute-done.12 = f32[8,1024]{1,0:T(8,128)S(1)} collective-permute-done((f32[8,1024]{1,0:T(8,128)S(1)}, f32[8,1024]{1,0:T(8,128)S(1)}, u32[]{:S(2)}, u32[]{:S(2)}) %collective-permute-start.12) | collective-permute-done | bytes 32800 | tf_op jit(solution)/shard_map/ppermute | solution.py:353
  113.9 1.2 collective-permute-start.13
  115.1 5.5 %collective-permute-done.13 = f32[8,1024]{1,0:T(8,128)S(1)} collective-permute-done((f32[8,1024]{1,0:T(8,128)S(1)}, f32[8,1024]{1,0:T(8,128)S(1)}, u32[]{:S(2)}, u32[]{:S(2)}) %collective-permute-start.13) | collective-permute-done | bytes 32800 | tf_op jit(solution)/shard_map/ppermute | solution.py:353
  120.6 0.6 collective-permute-start.14
  121.3 2.4 %collective-permute-done.14 = f32[8,1024]{1,0:T(8,128)S(1)} collective-permute-done((f32[8,1024]{1,0:T(8,128)S(1)}, f32[8,1024]{1,0:T(8,128)S(1)}, u32[]{:S(2)}, u32[]{:S(2)}) %collective-permute-start.14) | collective-permute-done | bytes 32800 | tf_op jit(solution)/shard_map/ppermute | solution.py:353
  123.7 1.2 collective-permute-start.15
  124.8 3.1 %collective-permute-done.15 = f32[8,1024]{1,0:T(8,128)S(1)} collective-permute-done((f32[8,1024]{1,0:T(8,128)S(1)}, f32[8,1024]{1,0:T(8,128)S(1)}, u32[]{:S(2)}, u32[]{:S(2)}) %collective-permute-start.15) | collective-permute-done | bytes 32800 | tf_op jit(solution)/shard_map/ppermute | solution.py:353
  128.0 6.2 %collective-permute-start.16 = (f32[8,1024]{1,0:T(8,128)S(1)}, f32[8,1024]{1,0:T(8,128)S(1)}, u32[]{:S(2)}, u32[]{:S(2)}) collective-permute-start(f32[8,1024]{1,0:T(8,128)S(1)} %add.36), channel_id=1, source_target_pairs={{0,4},{4,0},{8,12},{12,8},{16,20},{20,16},{24,28},{28,24},{32,36},... | collective-permute-start | bytes 98312 | tf_op jit(solution)/shard_map/ppermute | solution.py:242
  134.1 0.9 maximum_select_fusion
  135.1 0.0 copy-done.25
  135.1 0.0 collective-permute-start.9
  135.1 0.1 copy-done.23
  135.2 0.4 collective-permute-start.10
  135.6 0.6 fusion.1
  136.2 0.4 collective-permute-done.9
  136.6 0.9 maximum_select_fusion.1
  137.5 0.9 maximum_select_fusion.2
  (53 shorter events, 0.2 us)
Async XLA Ops:
  0.6 6.6 %copy-start.21 = (f32[4,2048]{1,0:T(4,128)S(1)}, f32[4,2048]{1,0:T(4,128)}, u32[]{:S(2)}) copy-start(f32[4,2048]{1,0:T(4,128)} %scale.7) | copy-start | bytes 98308
  0.6 6.6 %collective-permute-start.2 = (bf16[128,2048]{1,0:T(8,128)(2,1)}, bf16[128,2048]{1,0:T(8,128)(2,1)S(1)}, u32[]{:S(2)}, u32[]{:S(2)}) collective-permute-start(bf16[128,2048]{1,0:T(8,128)(2,1)} %v_own.3), channel_id=1, source_target_pairs={{0,4},{4,0},{8,12},{12,8},{16,20},{20,16},{24,28},{28,24},{32,36},... | collective-permute-start | bytes 1572872 | tf_op jit(solution)/shard_map/ppermute | solution.py:242
  4.0 3.2 %collective-permute-start.1 = (bf16[128,2048]{1,0:T(8,128)(2,1)}, bf16[128,2048]{1,0:T(8,128)(2,1)S(1)}, u32[]{:S(2)}, u32[]{:S(2)}) collective-permute-start(bf16[128,2048]{1,0:T(8,128)(2,1)} %k_own.7), channel_id=1, source_target_pairs={{0,4},{4,0},{8,12},{12,8},{16,20},{20,16},{24,28},{28,24},{32,36},... | collective-permute-start | bytes 1572872 | tf_op jit(solution)/shard_map/ppermute | solution.py:242
  4.1 2.4 %collective-permute-start = (s32[8]{0:T(128)}, s32[8]{0:T(128)S(1)}, u32[]{:S(2)}, u32[]{:S(2)}) collective-permute-start(s32[8]{0:T(128)} %param.11), channel_id=1, source_target_pairs={{0,4},{4,0},{8,12},{12,8},{16,20},{20,16},{24,28},{28,24},{32,36},... | collective-permute-start | bytes 104 | tf_op jit(solution)/shard_map/ppermute | solution.py:242
  7.2 3.7 %copy-start.8 = (bf16[128,2048]{1,0:T(8,128)(2,1)}, bf16[128,2048]{1,0:T(8,128)(2,1)S(1)}, u32[]{:S(2)}) copy-start(bf16[128,2048]{1,0:T(8,128)(2,1)S(1)} %collective-permute-done.2.v_other) | copy-start | bytes 1572868
  7.2 1.2 copy-start.1
  8.5 1.0 copy-start.6
  9.5 12.3 %copy-start.5 = (bf16[128,2048]{1,0:T(8,128)(2,1)S(1)}, bf16[128,2048]{1,0:T(8,128)(2,1)}, u32[]{:S(2)}) copy-start(bf16[128,2048]{1,0:T(8,128)(2,1)} %c_own.3) | copy-start | bytes 1572868
  10.9 0.7 copy-start.17
  11.6 9.4 %copy-start = (bf16[128,2048]{1,0:T(8,128)(2,1)S(1)}, bf16[128,2048]{1,0:T(8,128)(2,1)}, u32[]{:S(2)}) copy-start(bf16[128,2048]{1,0:T(8,128)(2,1)} %q_own.7) | copy-start | bytes 1572868
  11.6 19.1 %all-to-all-start = ((bf16[32,32,128]{2,1,0:T(8,128)(2,1)}), bf16[32,32,128]{2,1,0:T(8,128)(2,1)S(1)}, u32[]{:S(2)}, u32[]{:S(2)}) async-start(bf16[32,32,128]{2,1,0:T(8,128)(2,1)} %bitcast.7), calls=%async_computation | async-start | bytes 524288 | tf_op jit(solution)/shard_map/all_to_all | solution.py:247
  21.1 17.2 %copy-start.2 = (bf16[128,2048]{1,0:T(8,128)(2,1)S(1)}, bf16[128,2048]{1,0:T(8,128)(2,1)}, u32[]{:S(2)}) copy-start(bf16[128,2048]{1,0:T(8,128)(2,1)} %k_own.7) | copy-start | bytes 1572868
  21.1 17.1 %collective-permute-start.3 = (bf16[128,2048]{1,0:T(8,128)(2,1)S(1)}, bf16[128,2048]{1,0:T(8,128)(2,1)S(1)}, u32[]{:S(2)}, u32[]{:S(2)}) collective-permute-start(bf16[128,2048]{1,0:T(8,128)(2,1)S(1)} %copy-done), channel_id=1, source_target_pairs={{0,4},{4,0},{8,12},{12,8},{16,20},{20,16},{24,28},{28,24},{32,36},... | collective-permute-start | bytes 1572872 | tf_op jit(solution)/shard_map/ppermute | solution.py:242
  21.8 19.6 %collective-permute-start.4 = (bf16[128,2048]{1,0:T(8,128)(2,1)S(1)}, bf16[128,2048]{1,0:T(8,128)(2,1)}, u32[]{:S(2)}, u32[]{:S(2)}) collective-permute-start(bf16[128,2048]{1,0:T(8,128)(2,1)S(1)} %copy-done.5), channel_id=1, source_target_pairs={{0,4},{4,0},{8,12},{12,8},{16,20},{20,16},{24,28},{28,24},{32,36},... | collective-permute-start | bytes 1572872 | tf_op jit(solution)/shard_map/ppermute | solution.py:242
  30.8 0.7 copy-start.10
  31.5 16.4 %all-to-all-start.1 = ((bf16[32,32,128]{2,1,0:T(8,128)(2,1)}), bf16[32,32,128]{2,1,0:T(8,128)(2,1)S(1)}, u32[]{:S(2)}, u32[]{:S(2)}) async-start(bf16[32,32,128]{2,1,0:T(8,128)(2,1)} %copy-done.10), calls=%async_computation.1 | async-start | bytes 524288 | tf_op jit(solution)/shard_map/all_to_all | solution.py:251
  38.2 9.6 %copy-start.20 = (f32[4,2048]{1,0:T(4,128)S(1)}, f32[4,2048]{1,0:T(4,128)}, u32[]{:S(2)}) copy-start(f32[4,2048]{1,0:T(4,128)} %scale.6) | copy-start | bytes 98308
  40.4 1.0 copy-start.3
  47.9 1.2 copy-start.4
  51.5 4.5 %collective-permute-start.5 = (f32[2,256]{1,0:T(2,128)S(1)}, f32[2,256]{1,0:T(2,128)S(1)}, u32[]{:S(2)}, u32[]{:S(2)}) collective-permute-start(f32[2,256]{1,0:T(2,128)S(1)} %get-tuple-element.30), channel_id=1, source_target_pairs={{0,4},{4,0},{8,12},{12,8},{16,20},{20,16},{24,28},{28,24},{32,36},... | collective-permute-start | bytes 6152 | tf_op jit(solution)/shard_map/ppermute | solution.py:242
  56.0 2.4 %collective-permute-start.6 = (f32[2,256]{1,0:T(2,128)S(1)}, f32[2,256]{1,0:T(2,128)S(1)}, u32[]{:S(2)}, u32[]{:S(2)}) collective-permute-start(f32[2,256]{1,0:T(2,128)S(1)} %maximum_add_fusion), channel_id=1, source_target_pairs={{0,1},{1,0},{2,3},{3,2},{4,5},{5,4},{6,7},{7,6},{8,9},{9,8},{10,11... | collective-permute-start | bytes 6152 | tf_op jit(solution)/shard_map/ppermute | solution.py:319
  58.4 3.9 %collective-permute-start.7 = (f32[2,256]{1,0:T(2,128)S(1)}, f32[2,256]{1,0:T(2,128)S(1)}, u32[]{:S(2)}, u32[]{:S(2)}) collective-permute-start(f32[2,256]{1,0:T(2,128)S(1)} %add.30), channel_id=1, source_target_pairs={{0,2},{1,3},{2,0},{3,1},{4,6},{5,7},{6,4},{7,5},{8,10},{9,11},{10,... | collective-permute-start | bytes 6152 | tf_op jit(solution)/shard_map/ppermute | solution.py:319
  65.1 0.8 copy-start.15
  80.3 14.4 %all-to-all-start.3 = ((bf16[32,32,128]{2,1,0:T(8,128)(2,1)}), bf16[32,32,128]{2,1,0:T(8,128)(2,1)}, u32[]{:S(2)}, u32[]{:S(2)}) async-start(bf16[32,32,128]{2,1,0:T(8,128)(2,1)} %running_sums.3), calls=%async_computation.3 | async-start | bytes 524288 | tf_op jit(solution)/shard_map/all_to_all | solution.py:251
  85.1 1.0 copy-start.16
  86.2 8.6 %copy-start.7 = (bf16[128,2048]{1,0:T(8,128)(2,1)S(1)}, bf16[128,2048]{1,0:T(8,128)(2,1)}, u32[]{:S(2)}) copy-start(bf16[128,2048]{1,0:T(8,128)(2,1)} %v_own.3) | copy-start | bytes 1572868
  90.6 1.0 copy-start.11
  91.6 1.0 copy-start.13
  92.6 0.7 copy-start.18
  94.8 1.0 copy-start.9
  95.8 1.2 copy-start.12
  97.1 1.2 copy-start.14
  101.2 0.7 copy-start.22
  101.9 0.7 copy-start.24
  102.6 31.5 %copy-start.19 = (bf16[128,1024]{1,0:T(8,128)(2,1)S(1)}, bf16[128,1024]{1,0:T(8,128)(2,1)}, u32[]{:S(2)}) copy-start(bf16[128,1024]{1,0:T(8,128)(2,1)} %copy-done.18) | copy-start | bytes 786436
  102.7 7.4 %collective-permute-start.11 = (f32[8,1024]{1,0:T(8,128)S(1)}, f32[8,1024]{1,0:T(8,128)S(1)}, u32[]{:S(2)}, u32[]{:S(2)}) collective-permute-start(f32[8,1024]{1,0:T(8,128)S(1)} %pad_maximum_fusion), channel_id=1, source_target_pairs={{0,8},{4,12},{8,0},{12,4},{16,24},{20,28},{24,16},{28,20},{32,40},... | collective-permute-start | bytes 98312 | tf_op jit(solution)/shard_map/ppermute | solution.py:353
  104.4 29.7 %collective-permute-start.8 = (bf16[128,1024]{1,0:T(8,128)(2,1)}, bf16[128,1024]{1,0:T(8,128)(2,1)S(1)}, u32[]{:S(2)}, u32[]{:S(2)}) collective-permute-start(bf16[128,1024]{1,0:T(8,128)(2,1)} %get-tuple-element.33), channel_id=1, source_target_pairs={{0,4},{4,0},{8,12},{12,8},{16,20},{20,16},{24,28},{28,24},{32,36},... | collective-permute-start | bytes 786440 | tf_op jit(solution)/shard_map/ppermute | solution.py:242
  110.1 3.8 %collective-permute-start.12 = (f32[8,1024]{1,0:T(8,128)S(1)}, f32[8,1024]{1,0:T(8,128)S(1)}, u32[]{:S(2)}, u32[]{:S(2)}) collective-permute-start(f32[8,1024]{1,0:T(8,128)S(1)} %fusion), channel_id=1, source_target_pairs={{0,16},{4,20},{8,24},{12,28},{16,0},{20,4},{24,8},{28,12},{32,48},... | collective-permute-start | bytes 98312 | tf_op jit(solution)/shard_map/ppermute | solution.py:353
  113.9 6.7 %collective-permute-start.13 = (f32[8,1024]{1,0:T(8,128)S(1)}, f32[8,1024]{1,0:T(8,128)S(1)}, u32[]{:S(2)}, u32[]{:S(2)}) collective-permute-start(f32[8,1024]{1,0:T(8,128)S(1)} %add.33), channel_id=1, source_target_pairs={{0,32},{4,36},{8,40},{12,44},{16,48},{20,52},{24,56},{28,60},{32,0... | collective-permute-start | bytes 98312 | tf_op jit(solution)/shard_map/ppermute | solution.py:353
  120.6 3.1 %collective-permute-start.14 = (f32[8,1024]{1,0:T(8,128)S(1)}, f32[8,1024]{1,0:T(8,128)S(1)}, u32[]{:S(2)}, u32[]{:S(2)}) collective-permute-start(f32[8,1024]{1,0:T(8,128)S(1)} %add.34), channel_id=1, source_target_pairs={{0,64},{4,68},{8,72},{12,76},{16,80},{20,84},{24,88},{28,92},{32,9... | collective-permute-start | bytes 98312 | tf_op jit(solution)/shard_map/ppermute | solution.py:353
  123.7 4.3 %collective-permute-start.15 = (f32[8,1024]{1,0:T(8,128)S(1)}, f32[8,1024]{1,0:T(8,128)S(1)}, u32[]{:S(2)}, u32[]{:S(2)}) collective-permute-start(f32[8,1024]{1,0:T(8,128)S(1)} %add.35), channel_id=1, source_target_pairs={{0,128},{4,132},{8,136},{12,140},{16,144},{20,148},{24,152},{28,15... | collective-permute-start | bytes 98312 | tf_op jit(solution)/shard_map/ppermute | solution.py:353
  128.0 7.6 %collective-permute-start.16 = (f32[8,1024]{1,0:T(8,128)S(1)}, f32[8,1024]{1,0:T(8,128)S(1)}, u32[]{:S(2)}, u32[]{:S(2)}) collective-permute-start(f32[8,1024]{1,0:T(8,128)S(1)} %add.36), channel_id=1, source_target_pairs={{0,4},{4,0},{8,12},{12,8},{16,20},{20,16},{24,28},{28,24},{32,36},... | collective-permute-start | bytes 98312 | tf_op jit(solution)/shard_map/ppermute | solution.py:242
  134.1 1.0 copy-start.25
  134.1 1.1 copy-start.23
  135.1 1.5 %collective-permute-start.9 = (bf16[128,1024]{1,0:T(8,128)(2,1)S(1)}, bf16[128,1024]{1,0:T(8,128)(2,1)S(1)}, u32[]{:S(2)}, u32[]{:S(2)}) collective-permute-start(bf16[128,1024]{1,0:T(8,128)(2,1)S(1)} %copy-done.25), channel_id=1, source_target_pairs={{0,4},{4,0},{8,12},{12,8},{16,20},{20,16},{24,28},{28,24},{32,36},... | collective-permute-start | bytes 786440 | tf_op jit(solution)/shard_map/ppermute | solution.py:242
  135.2 2.4 %collective-permute-start.10 = (bf16[128,1024]{1,0:T(8,128)(2,1)S(1)}, bf16[128,1024]{1,0:T(8,128)(2,1)S(1)}, u32[]{:S(2)}, u32[]{:S(2)}) collective-permute-start(bf16[128,1024]{1,0:T(8,128)(2,1)S(1)} %copy-done.23), channel_id=1, source_target_pairs={{0,4},{4,0},{8,12},{12,8},{16,20},{20,16},{24,28},{28,24},{32,36},... | collective-permute-start | bytes 786440 | tf_op jit(solution)/shard_map/ppermute | solution.py:242

commit v2 on v1

--- a/solution.py
+++ b/solution.py
@@ -13,6 +13,7 @@
 EPS = 1e-06
 CORES = 2
 STEP_HEADS = 4
+VMEM_BYTES = 56 * 2**20
 F32 = jnp.float32
 BF16 = jnp.bfloat16
 
@@ -118,7 +119,7 @@
 
 
 def grads_kernel(
-    full_width, meta, scale, q_own, q_other, c_own, c_other, mixed, sums, grad, delta, out_part
+    full_width, meta, scale, q_own, q_other, c_own, c_other, mixed, sums, grad, delta
 ):
     tok = q_own.shape[0]
     spans = 2 * tok // SPAN
@@ -134,14 +135,17 @@
         low = (rows_of_members(meta, scale, lanes, spans) * cot - mix * factor).astype(BF16)
         grad[:, lanes] = low
         delta[h] = dot(pair(q_own, q_other, lanes), low, TN).astype(BF16)
-        out_part[:, lanes] = member_sums(meta, cot * mix, spans)
 
 
 def back_kernel(
-    meta, q_own, q_other, k_own, k_other, scaled, grad, state, query_own, query_other, key_in, value_in
+    full_width, meta, q_own, q_other, k_own, k_other, c_own, c_other, scaled, grad, state, mixed, sums,
+    query_own, query_other, key_in, value_in, out_part,
 ):
     tok = q_own.shape[0]
+    spans = 2 * tok // SPAN
     causal = causal_mask(meta, tok)
+    inverse = 1.0 / jnp.sqrt(sums[0:1] / full_width + EPS)
+    inverse = jnp.transpose(jnp.broadcast_to(inverse, (DH, 2 * tok)))
     for h in range(state.shape[0]):
         lanes = lanes_of(h)
         query = pair(q_own, q_other, lanes)
@@ -155,25 +159,33 @@
         query_other[:, lanes] = query_grad[tok:]
         key_in[:, lanes] = dot(grad_weights, query, TN)
         value_in[:, lanes] = dot(weights, g, TN)
-
-
-def last_kernel(
-    meta, scale, k_own, k_other, v_own, v_other, scaled, state, key_in, value_in,
-    key_grad_own, key_grad_other, value_grad_own, value_grad_other, in_part,
+        normed = pair(c_own, c_other, lanes).astype(F32) * (mixed[:, lanes] * inverse)
+        out_part[:, lanes] = member_sums(meta, normed, spans)
+
+
+def value_kernel(
+    meta, scale, k_own, k_other, v_own, v_other, state, value_in,
+    value_grad_own, value_grad_other, in_part,
 ):
     tok = k_own.shape[0]
     spans = 2 * tok // SPAN
     for h in range(state.shape[0]):
         lanes = lanes_of(h)
-        key_grad = (key_in[:, lanes] + dot(scaled[:, lanes], state[h], NT)).astype(BF16)
-        key_grad_own[:, lanes] = key_grad[:tok]
-        key_grad_other[:, lanes] = key_grad[tok:]
         scaled_grad = value_in[:, lanes] + dot(pair(k_own, k_other, lanes), state[h], NN)
         value_grad = (rows_of_members(meta, scale, lanes, spans) * scaled_grad).astype(BF16)
         value_grad_own[:, lanes] = value_grad[:tok]
         value_grad_other[:, lanes] = value_grad[tok:]
         value = pair(v_own, v_other, lanes).astype(F32)
         in_part[:, lanes] = member_sums(meta, value * scaled_grad, spans)
+
+
+def key_kernel(meta, scaled, state, key_in, key_grad_own, key_grad_other):
+    tok = key_grad_own.shape[0]
+    for h in range(state.shape[0]):
+        lanes = lanes_of(h)
+        key_grad = (key_in[:, lanes] + dot(scaled[:, lanes], state[h], NT)).astype(BF16)
+        key_grad_own[:, lanes] = key_grad[:tok]
+        key_grad_other[:, lanes] = key_grad[tok:]
 
 
 def running_kernel(backward, pieces, sums):
@@ -219,7 +231,7 @@
             ),
             out_shape=shapes,
             name=name,
-            compiler_params=pltpu.CompilerParams(vmem_limit_bytes=32 * 2**20),
+            compiler_params=pltpu.CompilerParams(vmem_limit_bytes=VMEM_BYTES),
             cost_estimate=pl.CostEstimate(flops=flops, bytes_accessed=2 * moved, transcendentals=0),
         )(self.meta, *args)
 
@@ -229,7 +241,7 @@
         functools.partial(running_kernel, backward),
         out_shape=jax.ShapeDtypeStruct(pieces.shape, BF16),
         name="running_sums",
-        compiler_params=pltpu.CompilerParams(vmem_limit_bytes=32 * 2**20),
+        compiler_params=pltpu.CompilerParams(vmem_limit_bytes=VMEM_BYTES),
     )(pieces)
 
 
@@ -318,43 +330,54 @@
         while step < n_head:
             sums = sums + lax.ppermute(sums, "head", [(i, i ^ step) for i in range(n_head)])
             step *= 2
-        grad, delta_after, out_part = local.call(
+        grad, delta_after = local.call(
             functools.partial(grads_kernel, full_width),
             [shared(MEMBERS)] + pairs * 2 + [cols(rows), local.whole((2, rows))],
-            [cols(rows), state(), cols(MEMBERS)],
+            [cols(rows), state()],
             (out_scale, queries, q_other, cotangent, c_other, mixed, sums),
-            [sds((rows, width), BF16), states, part],
+            [sds((rows, width), BF16), states],
             "grads",
             flops=unit,
         )
         state_after = scanned(delta_after, True)
-        query_own, query_send, key_in, value_in = local.call(
-            back_kernel,
-            pairs * 2 + [cols(rows), cols(rows), state()],
-            [cols(tok), cols(tok), cols(rows), cols(rows)],
-            (queries, q_other, key_vectors, k_other, scaled, grad, state_in),
-            [half, half, wide, wide],
+        query_own, query_send, key_in, value_in, out_part = local.call(
+            functools.partial(back_kernel, full_width),
+            pairs * 3 + [cols(rows), cols(rows), state(), cols(rows), local.whole((2, rows))],
+            [cols(tok), cols(tok), cols(rows), cols(rows), cols(MEMBERS)],
+            (queries, q_other, key_vectors, k_other, cotangent, c_other, scaled, grad, state_in, mixed, sums),
+            [half, half, wide, wide, part],
             "back",
             flops=11 * unit,
         )
         query_grad = side_by_side(core, query_own, swap(query_send))
-        key_own, key_send, value_own, value_send, in_part = local.call(
-            last_kernel,
-            [shared(MEMBERS)] + pairs * 2 + [cols(rows), state(), cols(rows), cols(rows)],
-            [cols(tok)] * 4 + [cols(MEMBERS)],
-            (in_scale, key_vectors, k_other, value_vectors, v_other, scaled, state_after, key_in, value_in),
-            [half] * 4 + [part],
-            "last",
-            flops=2 * unit,
-        )
-        parts = jnp.concatenate([in_part, out_part], axis=0)
-        step = CORES
-        while step < n_seq:
-            parts = parts + lax.ppermute(parts, "seq", [(i, i ^ step) for i in range(n_seq)])
-            step *= 2
-        parts = side_by_side(core, parts, swap(parts))
+        value_own, value_send, in_part = local.call(
+            value_kernel,
+            [shared(MEMBERS)] + pairs * 2 + [state(), cols(rows)],
+            [cols(tok)] * 2 + [cols(MEMBERS)],
+            (in_scale, key_vectors, k_other, value_vectors, v_other, state_after, value_in),
+            [half] * 2 + [part],
+            "value",
+            flops=unit,
+        )
+        parts = jnp.concatenate([in_part, out_part], axis=0).astype(BF16)
+        copies = jnp.broadcast_to(parts[None], (chips,) + parts.shape)
+        copies = lax.all_to_all(copies, "seq", 0, 0, axis_index_groups=same_core, tiled=True)
+        key_own, key_send = local.call(
+            key_kernel,
+            [cols(rows), state(), cols(rows)],
+            [cols(tok)] * 2,
+            (scaled, state_after, key_in),
+            [half] * 2,
+            "key",
+            flops=unit,
+        )
         key_grad = side_by_side(core, key_own, swap(key_send))
         value_grad = side_by_side(core, value_own, swap(value_send))
+        copies, key_grad, value_grad, query_grad = lax.optimization_barrier(
+            (copies, key_grad, value_grad, query_grad)
+        )
+        parts = jnp.sum(copies.astype(F32), axis=0)
+        parts = side_by_side(core, parts, swap(parts))
         return query_grad, key_grad, value_grad, parts[:MEMBERS], parts[MEMBERS:]
 
     return shards

time: 139 us -> 134 us (0.964)
  Pallas kernels: 16.8 us -> 31.3 us
  waiting for transfers between devices: 36.5 us -> 22.5 us
  local copies, waits for them, and re-layouts: 16 us -> 6.73 us
  other arithmetic: 3.56 us -> 5.51 us
    ppermute x5 -> x0, waiting for transfers between devices: 14.4 us -> none  [shards(): lax.ppermute(parts, 'seq', [(i, i ^ step) for i in range(n_seq)])]
    pallas_call x6 -> x7, Pallas kernels: 16 us -> 27.9 us  [call(): pl.pallas_call(body, grid_spec=pltpu.PrefetchScalarGridSpec(num_scalar_pr...]
    unnamed x52 -> x32, local copies, waits for them, and re-layouts: 15.4 us -> 5.25 us
    all_to_all x0 -> x1, starting transfers between devices: none -> 6.87 us  [shards(): lax.all_to_all(copies, 'seq', 0, 0, axis_index_groups=same_core, tiled=True)]
    ppermute x5 -> x0, starting transfers between devices: 5.25 us -> none  [shards(): lax.ppermute(parts, 'seq', [(i, i ^ step) for i in range(n_seq)])]
    pallas_call x2, Pallas kernels: 0.79 us -> 3.38 us  [running_sums(): pl.pallas_call(functools.partial(running_kernel, backward), out_shape=jax...]
    another operation x0 -> x2, other arithmetic: none -> 1.45 us
  transfers between devices with their start and end apart: 20 -> 16, of which waited for: 12 -> 9; matrix products, arithmetic and copies ran while one was open for 2% -> 3% of each run, Pallas kernels for 5% -> 12%
where the time goes in v2:
time: 134 us; the launch traced here: 133 us
  starting transfers between devices  52.1 us (39%)
  Pallas kernels  31.3 us (23%)
  waiting for transfers between devices  22.5 us (17%)
  blocking collectives  14.2 us (11%)
  local copies, waits for them, and re-layouts  6.73 us (5%)
  other arithmetic  5.51 us (4%)
    pallas_call x7, Pallas kernels, call(): pl.pallas_call(body, grid_spec=pltpu.PrefetchScalarGridSpec(num_scalar_pr...  27.9 us
    ppermute x10, starting transfers between devices, swap(): return lax.ppermute(x, 'seq', core_swap)  20.2 us
    all_to_all x1, blocking collectives, scanned(): lax.all_to_all(pieces, 'seq', 0, 0, axis_index_groups=same_core, tiled=True)  14.2 us
    all_to_all x2, starting transfers between devices, scanned(): lax.all_to_all(sums, 'seq', 0, 0, axis_index_groups=same_core, tiled=True)  11.4 us
    all_to_all x1, starting transfers between devices, scanned(): lax.all_to_all(pieces, 'seq', 0, 0, axis_index_groups=same_core, tiled=True)  9.43 us
    all_to_all x1, waiting for transfers between devices, scanned(): lax.all_to_all(pieces, 'seq', 0, 0, axis_index_groups=same_core, tiled=True)  8.82 us
    all_to_all x2, waiting for transfers between devices, scanned(): lax.all_to_all(sums, 'seq', 0, 0, axis_index_groups=same_core, tiled=True)  7.24 us
    all_to_all x1, starting transfers between devices, shards(): lax.all_to_all(copies, 'seq', 0, 0, axis_index_groups=same_core, tiled=True)  6.87 us
  transfers between devices with their start and end apart: 16, of which 9 were waited for; matrix products, arithmetic and copies ran while one was open for 3% of the time, Pallas kernels for 12%

profile of v2, /device:TPU:1, one launch (start us, length us, event | category | flops | bytes accessed | tf_op | source)
XLA Modules:
  0.0 133.1 jit_solution(8894436225819161290)
XLA Ops:
  0.6 3.3 %collective-permute-start.2 = (bf16[128,2048]{1,0:T(8,128)(2,1)}, bf16[128,2048]{1,0:T(8,128)(2,1)S(1)}, u32[]{:S(2)}, u32[]{:S(2)}) collective-permute-start(bf16[128,2048]{1,0:T(8,128)(2,1)} %v_own.3), channel_id=1, source_target_pairs={{0,4},{4,0},{8,12},{12,8},{16,20},{20,16},{24,28},{28,24},{32,36},... | collective-permute-start | bytes 1572872 | tf_op jit(solution)/shard_map/ppermute | solution.py:254
  4.0 0.1 collective-permute-start.1
  4.1 0.4 collective-permute-start
  4.5 2.0 %collective-permute-done = s32[8]{0:T(128)S(1)} collective-permute-done((s32[8]{0:T(128)}, s32[8]{0:T(128)S(1)}, u32[]{:S(2)}, u32[]{:S(2)}) %collective-permute-start) | collective-permute-done | bytes 64 | tf_op jit(solution)/shard_map/ppermute | solution.py:254
  6.5 0.0 copy-done.13
  6.5 0.6 pad_add_fusion.meta
  7.1 0.0 collective-permute-done.2.v_other
  7.1 0.0 collective-permute-done.1.k_other
  7.1 0.8 copy-done.7
  7.9 0.8 copy-done
  8.7 3.3 %states.1 = (bf16[256,1024]{1,0:T(8,128)(2,1)}, bf16[8,128,128]{2,1,0:T(8,128)(2,1)}) custom-call(s32[17]{0:T(128)} %pad_add_fusion.meta, f32[4,2048]{1,0:T(4,128)} %scale.7, bf16[128,2048]{1,0:T(8,128)(2,1)} %k_own.7, bf16[128,2048]{1,0:T(8,128)(2,1)} %copy-done, bf16[128,2048]{1,0:T(8,128)(2,1)} %v_own.3, bf16[128,2048]{1,0:T(8,128)(2,1)} %copy-done.7), custom_call_target="tpu_custom_call" | custom-call | flops 67108864 | bytes 4259840 | tf_op jit(solution)/shard_map/states/pallas_call | solution.py:223
  12.0 9.4 %all-to-all-start = ((bf16[32,32,128]{2,1,0:T(8,128)(2,1)}), bf16[32,32,128]{2,1,0:T(8,128)(2,1)S(1)}, u32[]{:S(2)}, u32[]{:S(2)}) async-start(bf16[32,32,128]{2,1,0:T(8,128)(2,1)} %bitcast.9), calls=%async_computation | async-start | bytes 524288 | tf_op jit(solution)/shard_map/all_to_all | solution.py:259
  21.4 0.7 collective-permute-start.3
  22.2 0.1 collective-permute-start.4
  22.3 8.8 %all-to-all-done.pieces = bf16[32,32,128]{2,1,0:T(8,128)(2,1)S(1)} async-done(((bf16[32,32,128]{2,1,0:T(8,128)(2,1)}), bf16[32,32,128]{2,1,0:T(8,128)(2,1)S(1)}, u32[]{:S(2)}, u32[]{:S(2)}) %all-to-all-start) | async-done | bytes 262176 | tf_op jit(solution)/shard_map/all_to_all | solution.py:259
  31.1 0.7 copy-done.8
  31.8 1.7 %running_sums.2 = bf16[32,32,128]{2,1,0:T(8,128)(2,1)} custom-call(bf16[32,32,128]{2,1,0:T(8,128)(2,1)} %copy-done.8), custom_call_target="tpu_custom_call" | custom-call | tf_op jit(solution)/shard_map/running_sums/pallas_call | solution.py:240
  33.5 6.7 %all-to-all-start.1 = ((bf16[32,32,128]{2,1,0:T(8,128)(2,1)}), bf16[32,32,128]{2,1,0:T(8,128)(2,1)S(1)}, u32[]{:S(2)}, u32[]{:S(2)}) async-start(bf16[32,32,128]{2,1,0:T(8,128)(2,1)} %running_sums.2), calls=%async_computation.1 | async-start | bytes 524288 | tf_op jit(solution)/shard_map/all_to_all | solution.py:263
  40.2 0.0 collective-permute-done.3.q_other
  40.2 0.0 copy-start.2
  40.2 0.8 copy-done.2
  41.0 4.1 %inside.1 = f32[256,1024]{1,0:T(8,128)} custom-call(s32[17]{0:T(128)} %pad_add_fusion.meta, bf16[128,2048]{1,0:T(8,128)(2,1)} %q_own.7, bf16[128,2048]{1,0:T(8,128)(2,1)} %copy-done.2, bf16[128,2048]{1,0:T(8,128)(2,1)} %k_own.7, bf16[128,2048]{1,0:T(8,128)(2,1)} %copy-done, bf16[256,1024]{1,0:T(8,128)(2,1)} %get-tuple-element.32.scaled), custom_call_target="tpu_custom_call" | custom-call | flops 268435456 | bytes 5242880 | tf_op jit(solution)/shard_map/inside/pallas_call | solution.py:223
  45.1 0.0 collective-permute-done.4.c_other
  45.1 4.8 %all-to-all-done.1 = bf16[32,32,128]{2,1,0:T(8,128)(2,1)S(1)} async-done(((bf16[32,32,128]{2,1,0:T(8,128)(2,1)}), bf16[32,32,128]{2,1,0:T(8,128)(2,1)S(1)}, u32[]{:S(2)}, u32[]{:S(2)}) %all-to-all-start.1) | async-done | bytes 262176 | tf_op jit(solution)/shard_map/all_to_all | solution.py:263
  49.9 0.0 copy-done.4
  49.9 0.7 copy-done.6
  50.6 3.7 %mixed.1 = (f32[256,1024]{1,0:T(8,128)}, f32[2,256]{1,0:T(2,128)}) custom-call(s32[17]{0:T(128)} %pad_add_fusion.meta, f32[4,2048]{1,0:T(4,128)} %scale.6, bf16[128,2048]{1,0:T(8,128)(2,1)} %q_own.7, bf16[128,2048]{1,0:T(8,128)(2,1)} %copy-done.2, bf16[128,2048]{1,0:T(8,128)(2,1)} %c_own.5, bf16[128,2048]{1,0:T(8,128)(2,1)} %copy-done.4, ...), custom_call_target="tpu_custom_call" | custom-call | flops 67108864 | bytes 6881280 | tf_op jit(solution)/shard_map/mixed/pallas_call | solution.py:223
  54.3 3.6 %collective-permute-start.5 = (f32[2,256]{1,0:T(2,128)}, f32[2,256]{1,0:T(2,128)S(1)}, u32[]{:S(2)}, u32[]{:S(2)}) collective-permute-start(f32[2,256]{1,0:T(2,128)} %get-tuple-element.34), channel_id=1, source_target_pairs={{0,4},{4,0},{8,12},{12,8},{16,20},{20,16},{24,28},{28,24},{32,36},... | collective-permute-start | bytes 6152 | tf_op jit(solution)/shard_map/ppermute | solution.py:254
  57.9 1.0 collective-permute-done.5
  58.9 0.7 copy-done.12
  59.6 1.3 collective-permute-start.6
  60.9 1.1 collective-permute-done.6
  62.0 2.9 %collective-permute-start.7 = (f32[2,256]{1,0:T(2,128)S(1)}, f32[2,256]{1,0:T(2,128)S(1)}, u32[]{:S(2)}, u32[]{:S(2)}) collective-permute-start(f32[2,256]{1,0:T(2,128)S(1)} %add.15), channel_id=1, source_target_pairs={{0,2},{1,3},{2,0},{3,1},{4,6},{5,7},{6,4},{7,5},{8,10},{9,11},{10,... | collective-permute-start | bytes 6152 | tf_op jit(solution)/shard_map/ppermute | solution.py:331
  64.9 1.0 collective-permute-done.7
  66.0 0.6 add.16.sums
  66.5 3.6 %grads.1 = (bf16[256,1024]{1,0:T(8,128)(2,1)}, bf16[8,128,128]{2,1,0:T(8,128)(2,1)}) custom-call(s32[17]{0:T(128)} %pad_add_fusion.meta, f32[4,2048]{1,0:T(4,128)} %scale.6, bf16[128,2048]{1,0:T(8,128)(2,1)} %q_own.7, bf16[128,2048]{1,0:T(8,128)(2,1)} %copy-done.2, bf16[128,2048]{1,0:T(8,128)(2,1)} %c_own.5, bf16[128,2048]{1,0:T(8,128)(2,1)} %copy-done.4, ...), custom_call_target="tpu_custom_call" | custom-call | flops 67108864 | bytes 6361088 | tf_op jit(solution)/shard_map/grads/pallas_call | solution.py:223
  70.2 14.2 %all_to_all.25.pieces = bf16[32,32,128]{2,1,0:T(8,128)(2,1)} all-to-all(bf16[32,32,128]{2,1,0:T(8,128)(2,1)} %bitcast.10), channel_id=1, replica_groups={{0,8,16,24,32,40,48,56,64,72,80,88,96,104,112,120,128,136,144,152,160,1..., dimensions={0} | all-to-all | bytes 524288 | tf_op jit(solution)/shard_map/all_to_all | solution.py:259
  84.4 1.7 %running_sums.3 = bf16[32,32,128]{2,1,0:T(8,128)(2,1)} custom-call(bf16[32,32,128]{2,1,0:T(8,128)(2,1)} %all_to_all.25.pieces), custom_call_target="tpu_custom_call" | custom-call | tf_op jit(solution)/shard_map/running_sums/pallas_call | solution.py:240
  86.1 4.7 %all-to-all-start.3 = ((bf16[32,32,128]{2,1,0:T(8,128)(2,1)}), bf16[32,32,128]{2,1,0:T(8,128)(2,1)S(1)}, u32[]{:S(2)}, u32[]{:S(2)}) async-start(bf16[32,32,128]{2,1,0:T(8,128)(2,1)} %running_sums.3), calls=%async_computation.3 | async-start | bytes 524288 | tf_op jit(solution)/shard_map/all_to_all | solution.py:263
  90.7 6.5 %back.1 = (bf16[128,1024]{1,0:T(8,128)(2,1)}, bf16[128,1024]{1,0:T(8,128)(2,1)}, f32[256,1024]{1,0:T(8,128)}, f32[256,1024]{1,0:T(8,128)}, f32[4,1024]{1,0:T(4,128)}) custom-call(s32[17]{0:T(128)} %pad_add_fusion.meta, bf16[128,2048]{1,0:T(8,128)(2,1)} %q_own.7, bf16[128,2048]{1,0:T(8,128)(2,1)} %copy-done.2, bf16[128,2048]{1,0:T(8,128)(2,1)} %k_own.7, ...), custom_call_target="tpu_custom_call" | custom-call | flops 738197504 | bytes 11014144 | tf_op jit(solution)/shard_map/back/pallas_call | solution.py:223
  97.2 0.7 convert.7
  97.9 2.5 %all-to-all-done.3 = bf16[32,32,128]{2,1,0:T(8,128)(2,1)S(1)} async-done(((bf16[32,32,128]{2,1,0:T(8,128)(2,1)}), bf16[32,32,128]{2,1,0:T(8,128)(2,1)S(1)}, u32[]{:S(2)}, u32[]{:S(2)}) %all-to-all-start.3) | async-done | bytes 262176 | tf_op jit(solution)/shard_map/all_to_all | solution.py:263
  100.4 0.7 copy-done.5
  101.1 3.6 %value.1 = (bf16[128,1024]{1,0:T(8,128)(2,1)}, bf16[128,1024]{1,0:T(8,128)(2,1)}, f32[4,1024]{1,0:T(4,128)}) custom-call(s32[17]{0:T(128)} %pad_add_fusion.meta, f32[4,2048]{1,0:T(4,128)} %scale.7, bf16[128,2048]{1,0:T(8,128)(2,1)} %k_own.7, bf16[128,2048]{1,0:T(8,128)(2,1)} %copy-done, bf16[128,2048]{1,0:T(8,128)(2,1)} %v_own.3, ...), custom_call_target="tpu_custom_call" | custom-call | flops 67108864 | bytes 6881280 | tf_op jit(solution)/shard_map/value/pallas_call | solution.py:223
  104.7 0.7 convert.6
  105.4 0.8 broadcast_in_dim.10
  106.3 6.9 %all-to-all-start.4 = ((bf16[32,8,1024]{2,1,0:T(8,128)(2,1)}), bf16[32,8,1024]{2,1,0:T(8,128)(2,1)S(1)}, u32[]{:S(2)}, u32[]{:S(2)}) async-start(bf16[32,8,1024]{2,1,0:T(8,128)(2,1)} %broadcast_in_dim.10), calls=%async_computation.4 | async-start | bytes 1048576 | tf_op jit(solution)/shard_map/all_to_all | solution.py:364
  113.2 4.5 %collective-permute-start.10 = (bf16[128,1024]{1,0:T(8,128)(2,1)S(1)}, bf16[128,1024]{1,0:T(8,128)(2,1)S(1)}, u32[]{:S(2)}, u32[]{:S(2)}) collective-permute-start(bf16[128,1024]{1,0:T(8,128)(2,1)S(1)} %copy-done.14), channel_id=1, source_target_pairs={{0,4},{4,0},{8,12},{12,8},{16,20},{20,16},{24,28},{28,24},{32,36},... | collective-permute-start | bytes 786440 | tf_op jit(solution)/shard_map/ppermute | solution.py:254
  117.7 0.1 collective-permute-start.9
  117.8 3.2 %key.1 = (bf16[128,1024]{1,0:T(8,128)(2,1)}, bf16[128,1024]{1,0:T(8,128)(2,1)}) custom-call(s32[17]{0:T(128)} %pad_add_fusion.meta, bf16[256,1024]{1,0:T(8,128)(2,1)} %get-tuple-element.32.scaled, bf16[8,128,128]{2,1,0:T(8,128)(2,1)} %bitcast.6, f32[256,1024]{1,0:T(8,128)} %get-tuple-element.40.key_in), custom_call_target="tpu_custom_call" | custom-call | flops 67108864 | bytes 3670016 | tf_op jit(solution)/shard_map/key/pallas_call | solution.py:223
  121.0 0.4 collective-permute-start.8
  121.4 0.0 collective-permute-done.10
  121.4 0.9 maximum_select_fusion.2
  122.3 0.0 collective-permute-done.9
  122.3 0.0 copy-done.10
  122.4 0.9 maximum_select_fusion.1
  123.3 0.0 collective-permute-done.8
  123.3 0.0 copy-done.11
  123.3 0.9 maximum_select_fusion
  124.2 0.4 all-to-all-done.4
  124.6 0.1 convert_reduce_fusion
  124.7 6.9 %collective-permute-start.11 = (f32[8,1024]{1,0:T(8,128)S(1)}, f32[8,1024]{1,0:T(8,128)S(1)}, u32[]{:S(2)}, u32[]{:S(2)}) collective-permute-start(f32[8,1024]{1,0:T(8,128)S(1)} %convert_reduce_fusion), channel_id=1, source_target_pairs={{0,4},{4,0},{8,12},{12,8},{16,20},{20,16},{24,28},{28,24},{32,36},... | collective-permute-start | bytes 98312 | tf_op jit(solution)/shard_map/ppermute | solution.py:254
  131.6 0.9 collective-permute-done.11
  132.4 0.6 fusion
  (25 shorter events, 0.1 us)
Async XLA Ops:
  0.6 6.4 %collective-permute-start.2 = (bf16[128,2048]{1,0:T(8,128)(2,1)}, bf16[128,2048]{1,0:T(8,128)(2,1)S(1)}, u32[]{:S(2)}, u32[]{:S(2)}) collective-permute-start(bf16[128,2048]{1,0:T(8,128)(2,1)} %v_own.3), channel_id=1, source_target_pairs={{0,4},{4,0},{8,12},{12,8},{16,20},{20,16},{24,28},{28,24},{32,36},... | collective-permute-start | bytes 1572872 | tf_op jit(solution)/shard_map/ppermute | solution.py:254
  4.0 3.1 %collective-permute-start.1 = (bf16[128,2048]{1,0:T(8,128)(2,1)}, bf16[128,2048]{1,0:T(8,128)(2,1)S(1)}, u32[]{:S(2)}, u32[]{:S(2)}) collective-permute-start(bf16[128,2048]{1,0:T(8,128)(2,1)} %k_own.7), channel_id=1, source_target_pairs={{0,4},{4,0},{8,12},{12,8},{16,20},{20,16},{24,28},{28,24},{32,36},... | collective-permute-start | bytes 1572872 | tf_op jit(solution)/shard_map/ppermute | solution.py:254
  4.1 2.4 %collective-permute-start = (s32[8]{0:T(128)}, s32[8]{0:T(128)S(1)}, u32[]{:S(2)}, u32[]{:S(2)}) collective-permute-start(s32[8]{0:T(128)} %param.11), channel_id=1, source_target_pairs={{0,4},{4,0},{8,12},{12,8},{16,20},{20,16},{24,28},{28,24},{32,36},... | collective-permute-start | bytes 104 | tf_op jit(solution)/shard_map/ppermute | solution.py:254
  4.5 2.0 %copy-start.13 = (s32[8]{0:T(128)S(1)}, s32[8]{0:T(128)}, u32[]{:S(2)}) copy-start(s32[8]{0:T(128)} %param.11) | copy-start | bytes 100
  7.1 0.8 copy-start.7
  7.9 0.8 copy-start
  8.7 13.5 %copy-start.3 = (bf16[128,2048]{1,0:T(8,128)(2,1)S(1)}, bf16[128,2048]{1,0:T(8,128)(2,1)}, u32[]{:S(2)}) copy-start(bf16[128,2048]{1,0:T(8,128)(2,1)} %c_own.5) | copy-start | bytes 1572868
  12.0 9.4 %copy-start.1 = (bf16[128,2048]{1,0:T(8,128)(2,1)S(1)}, bf16[128,2048]{1,0:T(8,128)(2,1)}, u32[]{:S(2)}) copy-start(bf16[128,2048]{1,0:T(8,128)(2,1)} %q_own.7) | copy-start | bytes 1572868
  12.0 19.1 %all-to-all-start = ((bf16[32,32,128]{2,1,0:T(8,128)(2,1)}), bf16[32,32,128]{2,1,0:T(8,128)(2,1)S(1)}, u32[]{:S(2)}, u32[]{:S(2)}) async-start(bf16[32,32,128]{2,1,0:T(8,128)(2,1)} %bitcast.9), calls=%async_computation | async-start | bytes 524288 | tf_op jit(solution)/shard_map/all_to_all | solution.py:259
  21.4 18.8 %collective-permute-start.3 = (bf16[128,2048]{1,0:T(8,128)(2,1)S(1)}, bf16[128,2048]{1,0:T(8,128)(2,1)S(1)}, u32[]{:S(2)}, u32[]{:S(2)}) collective-permute-start(bf16[128,2048]{1,0:T(8,128)(2,1)S(1)} %copy-done.1), channel_id=1, source_target_pairs={{0,4},{4,0},{8,12},{12,8},{16,20},{20,16},{24,28},{28,24},{32,36},... | collective-permute-start | bytes 1572872 | tf_op jit(solution)/shard_map/ppermute | solution.py:254
  22.2 22.9 %collective-permute-start.4 = (bf16[128,2048]{1,0:T(8,128)(2,1)S(1)}, bf16[128,2048]{1,0:T(8,128)(2,1)S(1)}, u32[]{:S(2)}, u32[]{:S(2)}) collective-permute-start(bf16[128,2048]{1,0:T(8,128)(2,1)S(1)} %copy-done.3), channel_id=1, source_target_pairs={{0,4},{4,0},{8,12},{12,8},{16,20},{20,16},{24,28},{28,24},{32,36},... | collective-permute-start | bytes 1572872 | tf_op jit(solution)/shard_map/ppermute | solution.py:254
  31.1 0.7 copy-start.8
  33.5 16.4 %all-to-all-start.1 = ((bf16[32,32,128]{2,1,0:T(8,128)(2,1)}), bf16[32,32,128]{2,1,0:T(8,128)(2,1)S(1)}, u32[]{:S(2)}, u32[]{:S(2)}) async-start(bf16[32,32,128]{2,1,0:T(8,128)(2,1)} %running_sums.2), calls=%async_computation.1 | async-start | bytes 524288 | tf_op jit(solution)/shard_map/all_to_all | solution.py:263
  40.2 0.8 copy-start.2
  45.1 4.8 %copy-start.4 = (bf16[128,2048]{1,0:T(8,128)(2,1)}, bf16[128,2048]{1,0:T(8,128)(2,1)S(1)}, u32[]{:S(2)}) copy-start(bf16[128,2048]{1,0:T(8,128)(2,1)S(1)} %collective-permute-done.4.c_other) | copy-start | bytes 1572868
  49.9 0.7 copy-start.6
  54.3 4.6 %collective-permute-start.5 = (f32[2,256]{1,0:T(2,128)}, f32[2,256]{1,0:T(2,128)S(1)}, u32[]{:S(2)}, u32[]{:S(2)}) collective-permute-start(f32[2,256]{1,0:T(2,128)} %get-tuple-element.34), channel_id=1, source_target_pairs={{0,4},{4,0},{8,12},{12,8},{16,20},{20,16},{24,28},{28,24},{32,36},... | collective-permute-start | bytes 6152 | tf_op jit(solution)/shard_map/ppermute | solution.py:254
  58.9 0.7 copy-start.12
  59.6 2.4 %collective-permute-start.6 = (f32[2,256]{1,0:T(2,128)S(1)}, f32[2,256]{1,0:T(2,128)S(1)}, u32[]{:S(2)}, u32[]{:S(2)}) collective-permute-start(f32[2,256]{1,0:T(2,128)S(1)} %maximum_add_fusion), channel_id=1, source_target_pairs={{0,1},{1,0},{2,3},{3,2},{4,5},{5,4},{6,7},{7,6},{8,9},{9,8},{10,11... | collective-permute-start | bytes 6152 | tf_op jit(solution)/shard_map/ppermute | solution.py:331
  62.0 3.9 %collective-permute-start.7 = (f32[2,256]{1,0:T(2,128)S(1)}, f32[2,256]{1,0:T(2,128)S(1)}, u32[]{:S(2)}, u32[]{:S(2)}) collective-permute-start(f32[2,256]{1,0:T(2,128)S(1)} %add.15), channel_id=1, source_target_pairs={{0,2},{1,3},{2,0},{3,1},{4,6},{5,7},{6,4},{7,5},{8,10},{9,11},{10,... | collective-permute-start | bytes 6152 | tf_op jit(solution)/shard_map/ppermute | solution.py:331
  86.1 14.4 %all-to-all-start.3 = ((bf16[32,32,128]{2,1,0:T(8,128)(2,1)}), bf16[32,32,128]{2,1,0:T(8,128)(2,1)S(1)}, u32[]{:S(2)}, u32[]{:S(2)}) async-start(bf16[32,32,128]{2,1,0:T(8,128)(2,1)} %running_sums.3), calls=%async_computation.3 | async-start | bytes 524288 | tf_op jit(solution)/shard_map/all_to_all | solution.py:263
  100.4 0.7 copy-start.5
  106.3 6.9 %copy-start.14 = (bf16[128,1024]{1,0:T(8,128)(2,1)S(1)}, bf16[128,1024]{1,0:T(8,128)(2,1)}, u32[]{:S(2)}) copy-start(bf16[128,1024]{1,0:T(8,128)(2,1)} %get-tuple-element.46) | copy-start | bytes 786436
  106.3 11.4 %copy-start.15 = (bf16[128,1024]{1,0:T(8,128)(2,1)S(1)}, bf16[128,1024]{1,0:T(8,128)(2,1)}, u32[]{:S(2)}) copy-start(bf16[128,1024]{1,0:T(8,128)(2,1)} %get-tuple-element.44) | copy-start | bytes 786436
  106.3 18.3 %all-to-all-start.4 = ((bf16[32,8,1024]{2,1,0:T(8,128)(2,1)}), bf16[32,8,1024]{2,1,0:T(8,128)(2,1)S(1)}, u32[]{:S(2)}, u32[]{:S(2)}) async-start(bf16[32,8,1024]{2,1,0:T(8,128)(2,1)} %broadcast_in_dim.10), calls=%async_computation.4 | async-start | bytes 1048576 | tf_op jit(solution)/shard_map/all_to_all | solution.py:364
  113.2 8.3 %collective-permute-start.10 = (bf16[128,1024]{1,0:T(8,128)(2,1)S(1)}, bf16[128,1024]{1,0:T(8,128)(2,1)S(1)}, u32[]{:S(2)}, u32[]{:S(2)}) collective-permute-start(bf16[128,1024]{1,0:T(8,128)(2,1)S(1)} %copy-done.14), channel_id=1, source_target_pairs={{0,4},{4,0},{8,12},{12,8},{16,20},{20,16},{24,28},{28,24},{32,36},... | collective-permute-start | bytes 786440 | tf_op jit(solution)/shard_map/ppermute | solution.py:254
  117.7 4.7 %collective-permute-start.9 = (bf16[128,1024]{1,0:T(8,128)(2,1)S(1)}, bf16[128,1024]{1,0:T(8,128)(2,1)S(1)}, u32[]{:S(2)}, u32[]{:S(2)}) collective-permute-start(bf16[128,1024]{1,0:T(8,128)(2,1)S(1)} %copy-done.15), channel_id=1, source_target_pairs={{0,4},{4,0},{8,12},{12,8},{16,20},{20,16},{24,28},{28,24},{32,36},... | collective-permute-start | bytes 786440 | tf_op jit(solution)/shard_map/ppermute | solution.py:254
  117.8 3.6 %copy-start.9 = (bf16[128,1024]{1,0:T(8,128)(2,1)S(1)}, bf16[128,1024]{1,0:T(8,128)(2,1)}, u32[]{:S(2)}) copy-start(bf16[128,1024]{1,0:T(8,128)(2,1)} %get-tuple-element.45) | copy-start | bytes 786436
  121.0 2.3 %collective-permute-start.8 = (bf16[128,1024]{1,0:T(8,128)(2,1)}, bf16[128,1024]{1,0:T(8,128)(2,1)S(1)}, u32[]{:S(2)}, u32[]{:S(2)}) collective-permute-start(bf16[128,1024]{1,0:T(8,128)(2,1)} %get-tuple-element.42), channel_id=1, source_target_pairs={{0,4},{4,0},{8,12},{12,8},{16,20},{20,16},{24,28},{28,24},{32,36},... | collective-permute-start | bytes 786440 | tf_op jit(solution)/shard_map/ppermute | solution.py:254
  121.4 1.0 copy-start.10
  122.4 0.9 copy-start.11
  124.7 7.7 %collective-permute-start.11 = (f32[8,1024]{1,0:T(8,128)S(1)}, f32[8,1024]{1,0:T(8,128)S(1)}, u32[]{:S(2)}, u32[]{:S(2)}) collective-permute-start(f32[8,1024]{1,0:T(8,128)S(1)} %convert_reduce_fusion), channel_id=1, source_target_pairs={{0,4},{4,0},{8,12},{12,8},{16,20},{20,16},{24,28},{28,24},{32,36},... | collective-permute-start | bytes 98312 | tf_op jit(solution)/shard_map/ppermute | solution.py:254

commit v3 on v2

--- a/solution.py
+++ b/solution.py
@@ -13,7 +13,7 @@
 EPS = 1e-06
 CORES = 2
 STEP_HEADS = 4
-VMEM_BYTES = 56 * 2**20
+VMEM_BYTES = 24 * 2**20
 F32 = jnp.float32
 BF16 = jnp.bfloat16
 
@@ -164,8 +164,8 @@
 
 
 def value_kernel(
-    meta, scale, k_own, k_other, v_own, v_other, state, value_in,
-    value_grad_own, value_grad_other, in_part,
+    meta, scale, k_own, k_other, v_own, v_other, state, value_in, out_part,
+    value_grad_own, value_grad_other, parts,
 ):
     tok = k_own.shape[0]
     spans = 2 * tok // SPAN
@@ -176,7 +176,8 @@
         value_grad_own[:, lanes] = value_grad[:tok]
         value_grad_other[:, lanes] = value_grad[tok:]
         value = pair(v_own, v_other, lanes).astype(F32)
-        in_part[:, lanes] = member_sums(meta, value * scaled_grad, spans)
+        in_part = member_sums(meta, value * scaled_grad, spans)
+        parts[:, lanes] = jnp.concatenate([in_part, out_part[:, lanes]], axis=0)
 
 
 def key_kernel(meta, scaled, state, key_in, key_grad_own, key_grad_other):
@@ -198,8 +199,7 @@
 
 
 class Local:
-    def __init__(self, meta, tok, width):
-        self.meta = meta
+    def __init__(self, tok, width):
         self.tok = tok
         self.width = width
         self.block = STEP_HEADS * DH
@@ -218,7 +218,7 @@
     def whole(self, shape):
         return pl.BlockSpec(shape, lambda i, meta: (0,) * len(shape))
 
-    def call(self, body, ins, outs, args, shapes, name, scratch=(), flops=0):
+    def call(self, body, meta, ins, outs, args, shapes, name, scratch=(), flops=0):
         moved = sum(a.size * a.dtype.itemsize for a in args)
         return pl.pallas_call(
             body,
@@ -233,16 +233,24 @@
             name=name,
             compiler_params=pltpu.CompilerParams(vmem_limit_bytes=VMEM_BYTES),
             cost_estimate=pl.CostEstimate(flops=flops, bytes_accessed=2 * moved, transcendentals=0),
-        )(self.meta, *args)
+        )(meta, *args)
+
+
+def fast(x):
+    return pltpu.with_memory_space_constraint(x, pltpu.VMEM)
+
+
+def slow(x):
+    return pltpu.with_memory_space_constraint(x, pltpu.HBM)
 
 
 def running_sums(pieces, backward):
     return pl.pallas_call(
         functools.partial(running_kernel, backward),
-        out_shape=jax.ShapeDtypeStruct(pieces.shape, BF16),
+        out_shape=pltpu.HBM(pieces.shape, BF16),
         name="running_sums",
         compiler_params=pltpu.CompilerParams(vmem_limit_bytes=VMEM_BYTES),
-    )(pieces)
+    )(fast(pieces))
 
 
 def make_shards(n_seq, n_head):
@@ -269,6 +277,23 @@
             jnp.concatenate([own, other], axis=1),
             jnp.concatenate([other, own], axis=1),
         )
+
+    def turned(x, tok):
+        return jnp.concatenate([x[:, tok:], x[:, :tok]], axis=1)
+
+    def over_heads(x, tok):
+        got = None
+        for shift in range(1, n_head // 2 + 1):
+            moves = []
+            for s in range(n_seq):
+                for h in range(n_head):
+                    if s % CORES == 0:
+                        moves.append((s * n_head + h, s * n_head + (h + shift) % n_head))
+                    elif 2 * shift != n_head:
+                        moves.append((s * n_head + h, s * n_head + (h - shift) % n_head))
+            came = lax.ppermute(x, ("seq", "head"), moves)
+            got = came if got is None else got + came
+        return x + got + turned(swap(got), tok)
 
     def shards(queries, key_vectors, value_vectors, cotangent, member_ids, in_scale, out_scale):
         tok, both = queries.shape
@@ -281,23 +306,25 @@
         other_ids = swap(member_ids)
         v_other = swap(value_vectors)
         k_other = swap(key_vectors)
-        meta = jnp.concatenate([core[None].astype(jnp.int32), member_ids, other_ids])
-        local = Local(meta, tok, width)
+        place = core[None].astype(jnp.int32)
+        local = Local(tok, width)
         shared, cols, state = local.shared, local.cols, local.state
-        sds = jax.ShapeDtypeStruct
-        half = sds((tok, width), BF16)
-        states = sds((heads, DH, DH), BF16)
-        part = sds((MEMBERS, width), F32)
-        wide = sds((rows, width), F32)
+        half = pltpu.HBM((tok, width), BF16)
+        low = pltpu.HBM((rows, width), BF16)
+        wide = pltpu.HBM((rows, width), F32)
+        part = pltpu.HBM((MEMBERS, width), F32)
+        sent = pltpu.HBM((heads, DH, DH), BF16)
         pairs = [shared(tok), shared(tok)]
         unit = 2 * heads * rows * DH * DH
 
+        meta = jnp.concatenate([place, member_ids, other_ids])
         scaled, delta = local.call(
             states_kernel,
+            meta,
             [shared(MEMBERS)] + pairs * 2,
             [cols(rows), state()],
-            (in_scale, key_vectors, k_other, value_vectors, v_other),
-            [sds((rows, width), BF16), states],
+            (in_scale, slow(key_vectors), fast(k_other), slow(value_vectors), fast(v_other)),
+            [low, sent],
             "states",
             flops=unit,
         )
@@ -307,66 +334,72 @@
         state_in = scanned(delta, False)
         inside = local.call(
             inside_kernel,
+            meta,
             pairs * 2 + [cols(rows)],
             cols(rows),
-            (queries, q_other, key_vectors, k_other, scaled),
+            (slow(queries), slow(q_other), slow(key_vectors), slow(k_other), slow(scaled)),
             wide,
             "inside",
             flops=4 * unit,
         )
         mixed, sums = local.call(
             mixed_kernel,
+            meta,
             [shared(MEMBERS)] + pairs * 2 + [state(), cols(rows)],
             [cols(rows), local.whole((2, rows))],
-            (out_scale, queries, q_other, cotangent, c_other, state_in, inside),
-            [wide, sds((2, rows), F32)],
+            (out_scale, slow(queries), slow(q_other), slow(cotangent), slow(c_other), fast(state_in), slow(inside)),
+            [wide, pltpu.VMEM((2, rows), F32)],
             "mixed",
             scratch=[pltpu.VMEM((rows, DH), F32)] * 2,
             flops=unit,
         )
-        across = swap(sums)
-        sums = sums + jnp.concatenate([across[:, tok:], across[:, :tok]], axis=1)
-        step = 1
-        while step < n_head:
-            sums = sums + lax.ppermute(sums, "head", [(i, i ^ step) for i in range(n_head)])
-            step *= 2
+        sums = over_heads(sums + turned(swap(sums), tok), tok)
         grad, delta_after = local.call(
             functools.partial(grads_kernel, full_width),
+            meta,
             [shared(MEMBERS)] + pairs * 2 + [cols(rows), local.whole((2, rows))],
             [cols(rows), state()],
-            (out_scale, queries, q_other, cotangent, c_other, mixed, sums),
-            [sds((rows, width), BF16), states],
+            (out_scale, slow(queries), slow(q_other), slow(cotangent), slow(c_other), slow(mixed), sums),
+            [low, sent],
             "grads",
             flops=unit,
         )
         state_after = scanned(delta_after, True)
         query_own, query_send, key_in, value_in, out_part = local.call(
             functools.partial(back_kernel, full_width),
+            meta,
             pairs * 3 + [cols(rows), cols(rows), state(), cols(rows), local.whole((2, rows))],
             [cols(tok), cols(tok), cols(rows), cols(rows), cols(MEMBERS)],
-            (queries, q_other, key_vectors, k_other, cotangent, c_other, scaled, grad, state_in, mixed, sums),
+            (
+                slow(queries), slow(q_other), slow(key_vectors), slow(k_other), slow(cotangent), slow(c_other),
+                slow(scaled), slow(grad), slow(state_in), slow(mixed), sums,
+            ),
             [half, half, wide, wide, part],
             "back",
             flops=11 * unit,
         )
         query_grad = side_by_side(core, query_own, swap(query_send))
-        value_own, value_send, in_part = local.call(
+        value_own, value_send, parts = local.call(
             value_kernel,
-            [shared(MEMBERS)] + pairs * 2 + [state(), cols(rows)],
-            [cols(tok)] * 2 + [cols(MEMBERS)],
-            (in_scale, key_vectors, k_other, value_vectors, v_other, state_after, value_in),
-            [half] * 2 + [part],
+            meta,
+            [shared(MEMBERS)] + pairs * 2 + [state(), cols(rows), cols(MEMBERS)],
+            [cols(tok)] * 2 + [cols(2 * MEMBERS)],
+            (
+                in_scale, slow(key_vectors), slow(k_other), slow(value_vectors), slow(v_other),
+                fast(state_after), slow(value_in), slow(out_part),
+            ),
+            [half] * 2 + [pltpu.HBM((2 * MEMBERS, width), F32)],
             "value",
             flops=unit,
         )
-        parts = jnp.concatenate([in_part, out_part], axis=0).astype(BF16)
-        copies = jnp.broadcast_to(parts[None], (chips,) + parts.shape)
+        copies = jnp.broadcast_to(parts.astype(BF16)[None], (chips,) + parts.shape)
         copies = lax.all_to_all(copies, "seq", 0, 0, axis_index_groups=same_core, tiled=True)
         key_own, key_send = local.call(
             key_kernel,
+            meta,
             [cols(rows), state(), cols(rows)],
             [cols(tok)] * 2,
-            (scaled, state_after, key_in),
+            (slow(scaled), slow(state_after), slow(key_in)),
             [half] * 2,
             "key",
             flops=unit,

time: 134 us -> 132 us (0.985)
  local copies, waits for them, and re-layouts: 6.73 us -> 2.4 us
  waiting for transfers between devices: 22.5 us -> 26.7 us
  Pallas kernels: 31.3 us -> 28 us
  starting transfers between devices: 52.1 us -> 54.9 us
    unnamed x32 -> x30, local copies, waits for them, and re-layouts: 5.25 us -> 0.9 us
    all_to_all x1, waiting for transfers between devices: 0.37 us -> 4.51 us  [shards(): lax.all_to_all(copies, 'seq', 0, 0, axis_index_groups=same_core, tiled=True)]
    ppermute x10 -> x11, starting transfers between devices: 20.2 us -> 22.3 us  [swap(): return lax.ppermute(x, 'seq', core_swap)]
    all_to_all x2, starting transfers between devices: 11.4 us -> 13.5 us  [scanned(): lax.all_to_all(sums, 'seq', 0, 0, axis_index_groups=same_core, tiled=True)]
    pallas_call x2, Pallas kernels: 3.38 us -> 1.49 us  [running_sums(): pl.pallas_call(functools.partial(running_kernel, backward), out_shape=plt...]
    another operation x2 -> x0, other arithmetic: 1.45 us -> none
    ppermute x2, waiting for transfers between devices: 2.17 us -> 0.73 us  [over_heads(): came = lax.ppermute(x, ('seq', 'head'), moves)]
    pallas_call x7, Pallas kernels: 27.9 us -> 26.5 us  [call(): pl.pallas_call(body, grid_spec=pltpu.PrefetchScalarGridSpec(num_scalar_pr...]
  transfers between devices with their start and end apart: 16 -> 17, of which waited for: 9 -> 9; matrix products, arithmetic and copies ran while one was open for 3% -> 3% of each run, Pallas kernels for 12% -> 11%
where the time goes in v3:
time: 132 us; the launch traced here: 131 us
  starting transfers between devices  54.9 us (42%)
  Pallas kernels  28 us (21%)
  waiting for transfers between devices  26.7 us (20%)
  blocking collectives  14 us (11%)
  other arithmetic  4.36 us (3%)
  local copies, waits for them, and re-layouts  2.4 us (2%)
    pallas_call x7, Pallas kernels, call(): pl.pallas_call(body, grid_spec=pltpu.PrefetchScalarGridSpec(num_scalar_pr...  26.5 us
    ppermute x11, starting transfers between devices, swap(): return lax.ppermute(x, 'seq', core_swap)  22.3 us
    all_to_all x1, blocking collectives, scanned(): lax.all_to_all(pieces, 'seq', 0, 0, axis_index_groups=same_core, tiled=True)  14 us
    all_to_all x2, starting transfers between devices, scanned(): lax.all_to_all(sums, 'seq', 0, 0, axis_index_groups=same_core, tiled=True)  13.5 us
    all_to_all x1, starting transfers between devices, scanned(): lax.all_to_all(pieces, 'seq', 0, 0, axis_index_groups=same_core, tiled=True)  9.44 us
    all_to_all x1, waiting for transfers between devices, scanned(): lax.all_to_all(pieces, 'seq', 0, 0, axis_index_groups=same_core, tiled=True)  8.82 us
    all_to_all x2, waiting for transfers between devices, scanned(): lax.all_to_all(sums, 'seq', 0, 0, axis_index_groups=same_core, tiled=True)  8.17 us
    all_to_all x1, starting transfers between devices, shards(): lax.all_to_all(copies, 'seq', 0, 0, axis_index_groups=same_core, tiled=True)  6.2 us
  transfers between devices with their start and end apart: 17, of which 9 were waited for; matrix products, arithmetic and copies ran while one was open for 3% of the time, Pallas kernels for 11%

profile of v3, /device:TPU:1, one launch (start us, length us, event | category | flops | bytes accessed | tf_op | source)
XLA Modules:
  0.0 131.1 jit_solution(3483957763202830228)
XLA Ops:
  0.6 0.0 copy-start.5
  0.6 3.3 %collective-permute-start.2 = (bf16[128,2048]{1,0:T(8,128)(2,1)}, bf16[128,2048]{1,0:T(8,128)(2,1)S(1)}, u32[]{:S(2)}, u32[]{:S(2)}) collective-permute-start(bf16[128,2048]{1,0:T(8,128)(2,1)} %v_own.3), channel_id=1, source_target_pairs={{0,4},{4,0},{8,12},{12,8},{16,20},{20,16},{24,28},{28,24},{32,36},... | collective-permute-start | bytes 1572872 | tf_op jit(solution)/shard_map/ppermute | solution.py:262
  4.0 0.1 collective-permute-start.1
  4.1 0.4 collective-permute-start
  4.5 2.0 %collective-permute-done = s32[8]{0:T(128)S(1)} collective-permute-done((s32[8]{0:T(128)}, s32[8]{0:T(128)S(1)}, u32[]{:S(2)}, u32[]{:S(2)}) %collective-permute-start) | collective-permute-done | bytes 64 | tf_op jit(solution)/shard_map/ppermute | solution.py:262
  6.5 0.7 pad_add_fusion.meta
  7.2 0.0 collective-permute-done.2.v_other
  7.2 0.0 collective-permute-done.1.k_other
  7.2 0.0 copy-start
  7.2 0.0 copy-start.8
  7.2 2.9 %states.1 = (bf16[256,1024]{1,0:T(8,128)(2,1)}, bf16[8,128,128]{2,1,0:T(8,128)(2,1)}) custom-call(s32[17]{0:T(128)S(1)} %pad_add_fusion.meta, f32[4,2048]{1,0:T(4,128)S(1)} %copy-done.5, bf16[128,2048]{1,0:T(8,128)(2,1)} %k_own.7, bf16[128,2048]{1,0:T(8,128)(2,1)S(1)} %collective-permute-done.1.k_other, bf16[128,2048]{1,0:T(8,128)(2,1)} %v_own.3, ...), custom_call_target="tpu_custom_call" | custom-call | flops 67108864 | bytes 4259840 | tf_op jit(solution)/shard_map/states/pallas_call | solution.py:223
  10.1 0.0 copy-done.3
  10.1 0.0 copy-start.6
  10.2 9.4 %all-to-all-start = ((bf16[32,32,128]{2,1,0:T(8,128)(2,1)}), bf16[32,32,128]{2,1,0:T(8,128)(2,1)S(1)}, u32[]{:S(2)}, u32[]{:S(2)}) async-start(bf16[32,32,128]{2,1,0:T(8,128)(2,1)} %bitcast.9), calls=%async_computation | async-start | bytes 524288 | tf_op jit(solution)/shard_map/all_to_all | solution.py:267
  19.6 0.7 collective-permute-start.3
  20.4 0.0 copy-done.8
  20.4 0.1 collective-permute-start.4
  20.5 8.8 %all-to-all-done.pieces = bf16[32,32,128]{2,1,0:T(8,128)(2,1)S(1)} async-done(((bf16[32,32,128]{2,1,0:T(8,128)(2,1)}), bf16[32,32,128]{2,1,0:T(8,128)(2,1)S(1)}, u32[]{:S(2)}, u32[]{:S(2)}) %all-to-all-start) | async-done | bytes 262176 | tf_op jit(solution)/shard_map/all_to_all | solution.py:267
  29.3 0.8 running_sums.2
  30.0 6.7 %all-to-all-start.1 = ((bf16[32,32,128]{2,1,0:T(8,128)(2,1)}), bf16[32,32,128]{2,1,0:T(8,128)(2,1)S(1)}, u32[]{:S(2)}, u32[]{:S(2)}) async-start(bf16[32,32,128]{2,1,0:T(8,128)(2,1)} %running_sums.2), calls=%async_computation.1 | async-start | bytes 524288 | tf_op jit(solution)/shard_map/all_to_all | solution.py:271
  36.8 0.0 collective-permute-done.3.q_other
  36.8 0.0 copy-start.7
  36.8 0.8 copy-done.7
  37.6 4.0 %inside.1 = f32[256,1024]{1,0:T(8,128)} custom-call(s32[17]{0:T(128)S(1)} %pad_add_fusion.meta, bf16[128,2048]{1,0:T(8,128)(2,1)} %q_own.7, bf16[128,2048]{1,0:T(8,128)(2,1)} %copy-done.7, bf16[128,2048]{1,0:T(8,128)(2,1)} %k_own.7, bf16[128,2048]{1,0:T(8,128)(2,1)} %copy-done, bf16[256,1024]{1,0:T(8,128)(2,1)} %get-tuple-element.32.scaled), custom_call_target="tpu_custom_call" | custom-call | flops 268435456 | bytes 5242880 | tf_op jit(solution)/shard_map/inside/pallas_call | solution.py:223
  41.6 0.0 collective-permute-done.4.c_other
  41.6 4.9 %all-to-all-done.1 = bf16[32,32,128]{2,1,0:T(8,128)(2,1)S(1)} async-done(((bf16[32,32,128]{2,1,0:T(8,128)(2,1)}), bf16[32,32,128]{2,1,0:T(8,128)(2,1)S(1)}, u32[]{:S(2)}, u32[]{:S(2)}) %all-to-all-start.1) | async-done | bytes 262176 | tf_op jit(solution)/shard_map/all_to_all | solution.py:271
  46.4 0.0 copy-done.9
  46.4 3.5 %mixed.1 = (f32[256,1024]{1,0:T(8,128)}, f32[2,256]{1,0:T(2,128)S(1)}) custom-call(s32[17]{0:T(128)S(1)} %pad_add_fusion.meta, f32[4,2048]{1,0:T(4,128)S(1)} %copy-done.4, bf16[128,2048]{1,0:T(8,128)(2,1)} %q_own.7, bf16[128,2048]{1,0:T(8,128)(2,1)} %copy-done.7, bf16[128,2048]{1,0:T(8,128)(2,1)} %c_own.5, bf16[128,2048]{1,0:T(8,128)(2,1)} %copy-done.9, ...), custom_call_target="tpu_custom_call" | custom-call | flops 67108864 | bytes 6881280 | tf_op jit(solution)/shard_map/mixed/pallas_call | solution.py:223
  49.9 3.6 %collective-permute-start.5 = (f32[2,256]{1,0:T(2,128)S(1)}, f32[2,256]{1,0:T(2,128)S(1)}, u32[]{:S(2)}, u32[]{:S(2)}) collective-permute-start(f32[2,256]{1,0:T(2,128)S(1)} %get-tuple-element.34), channel_id=1, source_target_pairs={{0,4},{4,0},{8,12},{12,8},{16,20},{20,16},{24,28},{28,24},{32,36},... | collective-permute-start | bytes 6152 | tf_op jit(solution)/shard_map/ppermute | solution.py:262
  53.5 0.8 collective-permute-done.5
  54.4 0.6 collective-permute-start.7
  55.0 2.8 %collective-permute-start.6 = (f32[2,256]{1,0:T(2,128)S(1)}, f32[2,256]{1,0:T(2,128)S(1)}, u32[]{:S(2)}, u32[]{:S(2)}) collective-permute-start(f32[2,256]{1,0:T(2,128)S(1)} %maximum_add_fusion), channel_id=1, source_target_pairs={{0,1},{1,2},{2,3},{3,0},{4,7},{5,4},{6,5},{7,6},{8,9},{9,10},{10,1... | collective-permute-start | bytes 6152 | tf_op jit(solution)/shard_map/ppermute | solution.py:294
  57.8 0.0 collective-permute-done.7
  57.8 0.7 collective-permute-done.6
  58.6 6.1 %collective-permute-start.8 = (f32[2,256]{1,0:T(2,128)S(1)}, f32[2,256]{1,0:T(2,128)S(1)}, u32[]{:S(2)}, u32[]{:S(2)}) collective-permute-start(f32[2,256]{1,0:T(2,128)S(1)} %add.18), channel_id=1, source_target_pairs={{0,4},{4,0},{8,12},{12,8},{16,20},{20,16},{24,28},{28,24},{32,36},... | collective-permute-start | bytes 6152 | tf_op jit(solution)/shard_map/ppermute | solution.py:262
  64.7 0.8 collective-permute-done.8
  65.5 3.5 %grads.1 = (bf16[256,1024]{1,0:T(8,128)(2,1)}, bf16[8,128,128]{2,1,0:T(8,128)(2,1)}) custom-call(s32[17]{0:T(128)S(1)} %pad_add_fusion.meta, f32[4,2048]{1,0:T(4,128)S(1)} %copy-done.4, bf16[128,2048]{1,0:T(8,128)(2,1)} %q_own.7, bf16[128,2048]{1,0:T(8,128)(2,1)} %copy-done.7, bf16[128,2048]{1,0:T(8,128)(2,1)} %c_own.5, bf16[128,2048]{1,0:T(8,128)(2,1)} %copy-done.9, ...), custom_call_target="tpu_custom_call" | custom-call | flops 67108864 | bytes 6361088 | tf_op jit(solution)/shard_map/grads/pallas_call | solution.py:223
  69.0 14.0 %all_to_all.25.pieces = bf16[32,32,128]{2,1,0:T(8,128)(2,1)S(1)} all-to-all(bf16[32,32,128]{2,1,0:T(8,128)(2,1)} %bitcast.10), channel_id=1, replica_groups={{0,8,16,24,32,40,48,56,64,72,80,88,96,104,112,120,128,136,144,152,160,1..., dimensions={0} | all-to-all | bytes 524288 | tf_op jit(solution)/shard_map/all_to_all | solution.py:267
  82.9 0.7 running_sums.3
  83.7 6.7 %all-to-all-start.3 = ((bf16[32,32,128]{2,1,0:T(8,128)(2,1)}), bf16[32,32,128]{2,1,0:T(8,128)(2,1)S(1)}, u32[]{:S(2)}, u32[]{:S(2)}) async-start(bf16[32,32,128]{2,1,0:T(8,128)(2,1)} %running_sums.3), calls=%async_computation.3 | async-start | bytes 524288 | tf_op jit(solution)/shard_map/all_to_all | solution.py:271
  90.4 6.3 %back.1 = (bf16[128,1024]{1,0:T(8,128)(2,1)}, bf16[128,1024]{1,0:T(8,128)(2,1)}, f32[256,1024]{1,0:T(8,128)}, f32[256,1024]{1,0:T(8,128)}, f32[4,1024]{1,0:T(4,128)}) custom-call(s32[17]{0:T(128)S(1)} %pad_add_fusion.meta, bf16[128,2048]{1,0:T(8,128)(2,1)} %q_own.7, bf16[128,2048]{1,0:T(8,128)(2,1)} %copy-done.7, bf16[128,2048]{1,0:T(8,128)(2,1)} %k_own.7, ...), custom_call_target="tpu_custom_call" | custom-call | flops 738197504 | bytes 11014144 | tf_op jit(solution)/shard_map/back/pallas_call | solution.py:223
  96.8 3.3 %all-to-all-done.3 = bf16[32,32,128]{2,1,0:T(8,128)(2,1)S(1)} async-done(((bf16[32,32,128]{2,1,0:T(8,128)(2,1)}), bf16[32,32,128]{2,1,0:T(8,128)(2,1)S(1)}, u32[]{:S(2)}, u32[]{:S(2)}) %all-to-all-start.3) | async-done | bytes 262176 | tf_op jit(solution)/shard_map/all_to_all | solution.py:271
  100.1 3.4 %value.1 = (bf16[128,1024]{1,0:T(8,128)(2,1)}, bf16[128,1024]{1,0:T(8,128)(2,1)}, f32[8,1024]{1,0:T(8,128)}) custom-call(s32[17]{0:T(128)S(1)} %pad_add_fusion.meta, f32[4,2048]{1,0:T(4,128)S(1)} %copy-done.5, bf16[128,2048]{1,0:T(8,128)(2,1)} %k_own.7, bf16[128,2048]{1,0:T(8,128)(2,1)} %copy-done, bf16[128,2048]{1,0:T(8,128)(2,1)} %v_own.3, ...), custom_call_target="tpu_custom_call" | custom-call | flops 67108864 | bytes 6914048 | tf_op jit(solution)/shard_map/value/pallas_call | solution.py:223
  103.5 0.8 convert_element_type.6
  104.2 0.9 broadcast_in_dim.10
  105.1 6.2 %all-to-all-start.4 = ((bf16[32,8,1024]{2,1,0:T(8,128)(2,1)}), bf16[32,8,1024]{2,1,0:T(8,128)(2,1)S(1)}, u32[]{:S(2)}, u32[]{:S(2)}) async-start(bf16[32,8,1024]{2,1,0:T(8,128)(2,1)} %broadcast_in_dim.10), calls=%async_computation.4 | async-start | bytes 1048576 | tf_op jit(solution)/shard_map/all_to_all | solution.py:396
  111.3 2.2 %collective-permute-start.11 = (bf16[128,1024]{1,0:T(8,128)(2,1)S(1)}, bf16[128,1024]{1,0:T(8,128)(2,1)S(1)}, u32[]{:S(2)}, u32[]{:S(2)}) collective-permute-start(bf16[128,1024]{1,0:T(8,128)(2,1)S(1)} %copy-done.13), channel_id=1, source_target_pairs={{0,4},{4,0},{8,12},{12,8},{16,20},{20,16},{24,28},{28,24},{32,36},... | collective-permute-start | bytes 786440 | tf_op jit(solution)/shard_map/ppermute | solution.py:262
  113.5 0.0 copy-done.14
  113.5 0.1 collective-permute-start.10
  113.6 3.0 %key.1 = (bf16[128,1024]{1,0:T(8,128)(2,1)}, bf16[128,1024]{1,0:T(8,128)(2,1)}) custom-call(s32[17]{0:T(128)S(1)} %pad_add_fusion.meta, bf16[256,1024]{1,0:T(8,128)(2,1)} %get-tuple-element.32.scaled, bf16[8,128,128]{2,1,0:T(8,128)(2,1)} %bitcast.6, f32[256,1024]{1,0:T(8,128)} %get-tuple-element.40.key_in), custom_call_target="tpu_custom_call" | custom-call | flops 67108864 | bytes 3670016 | tf_op jit(solution)/shard_map/key/pallas_call | solution.py:223
  116.6 0.4 collective-permute-start.9
  117.0 0.0 collective-permute-done.11
  117.0 0.9 maximum_select_fusion.2
  117.9 0.0 collective-permute-done.10
  117.9 0.0 copy-done.11
  117.9 0.9 maximum_select_fusion.1
  118.8 0.0 collective-permute-done.9
  118.8 0.0 copy-done.12
  118.9 0.9 maximum_select_fusion
  119.8 4.5 %all-to-all-done.4 = bf16[32,8,1024]{2,1,0:T(8,128)(2,1)S(1)} async-done(((bf16[32,8,1024]{2,1,0:T(8,128)(2,1)}), bf16[32,8,1024]{2,1,0:T(8,128)(2,1)S(1)}, u32[]{:S(2)}, u32[]{:S(2)}) %all-to-all-start.4) | async-done | bytes 524320 | tf_op jit(solution)/shard_map/all_to_all | solution.py:396
  124.3 0.1 convert_reduce_fusion
  124.4 5.2 %collective-permute-start.12 = (f32[8,1024]{1,0:T(8,128)S(1)}, f32[8,1024]{1,0:T(8,128)S(1)}, u32[]{:S(2)}, u32[]{:S(2)}) collective-permute-start(f32[8,1024]{1,0:T(8,128)S(1)} %convert_reduce_fusion), channel_id=1, source_target_pairs={{0,4},{4,0},{8,12},{12,8},{16,20},{20,16},{24,28},{28,24},{32,36},... | collective-permute-start | bytes 98312 | tf_op jit(solution)/shard_map/ppermute | solution.py:262
  129.6 0.9 collective-permute-done.12
  130.5 0.6 fusion
  (24 shorter events, 0.1 us)
Async XLA Ops:
  0.6 6.6 %copy-start.5 = (f32[4,2048]{1,0:T(4,128)S(1)}, f32[4,2048]{1,0:T(4,128)}, u32[]{:S(2)}) copy-start(f32[4,2048]{1,0:T(4,128)} %scale.7) | copy-start | bytes 98308
  0.6 6.6 %collective-permute-start.2 = (bf16[128,2048]{1,0:T(8,128)(2,1)}, bf16[128,2048]{1,0:T(8,128)(2,1)S(1)}, u32[]{:S(2)}, u32[]{:S(2)}) collective-permute-start(bf16[128,2048]{1,0:T(8,128)(2,1)} %v_own.3), channel_id=1, source_target_pairs={{0,4},{4,0},{8,12},{12,8},{16,20},{20,16},{24,28},{28,24},{32,36},... | collective-permute-start | bytes 1572872 | tf_op jit(solution)/shard_map/ppermute | solution.py:262
  4.0 3.2 %collective-permute-start.1 = (bf16[128,2048]{1,0:T(8,128)(2,1)}, bf16[128,2048]{1,0:T(8,128)(2,1)S(1)}, u32[]{:S(2)}, u32[]{:S(2)}) collective-permute-start(bf16[128,2048]{1,0:T(8,128)(2,1)} %k_own.7), channel_id=1, source_target_pairs={{0,4},{4,0},{8,12},{12,8},{16,20},{20,16},{24,28},{28,24},{32,36},... | collective-permute-start | bytes 1572872 | tf_op jit(solution)/shard_map/ppermute | solution.py:262
  4.1 2.4 %collective-permute-start = (s32[8]{0:T(128)}, s32[8]{0:T(128)S(1)}, u32[]{:S(2)}, u32[]{:S(2)}) collective-permute-start(s32[8]{0:T(128)} %param.11), channel_id=1, source_target_pairs={{0,4},{4,0},{8,12},{12,8},{16,20},{20,16},{24,28},{28,24},{32,36},... | collective-permute-start | bytes 104 | tf_op jit(solution)/shard_map/ppermute | solution.py:262
  7.2 2.9 %copy-start.3 = (bf16[128,2048]{1,0:T(8,128)(2,1)}, bf16[128,2048]{1,0:T(8,128)(2,1)S(1)}, u32[]{:S(2)}) copy-start(bf16[128,2048]{1,0:T(8,128)(2,1)S(1)} %collective-permute-done.2.v_other) | copy-start | bytes 1572868
  7.2 2.9 %copy-start = (bf16[128,2048]{1,0:T(8,128)(2,1)}, bf16[128,2048]{1,0:T(8,128)(2,1)S(1)}, u32[]{:S(2)}) copy-start(bf16[128,2048]{1,0:T(8,128)(2,1)S(1)} %collective-permute-done.1.k_other) | copy-start | bytes 1572868
  7.2 13.1 %copy-start.8 = (bf16[128,2048]{1,0:T(8,128)(2,1)S(1)}, bf16[128,2048]{1,0:T(8,128)(2,1)}, u32[]{:S(2)}) copy-start(bf16[128,2048]{1,0:T(8,128)(2,1)} %c_own.5) | copy-start | bytes 1572868
  10.1 9.5 %copy-start.6 = (bf16[128,2048]{1,0:T(8,128)(2,1)S(1)}, bf16[128,2048]{1,0:T(8,128)(2,1)}, u32[]{:S(2)}) copy-start(bf16[128,2048]{1,0:T(8,128)(2,1)} %q_own.7) | copy-start | bytes 1572868
  10.2 19.1 %all-to-all-start = ((bf16[32,32,128]{2,1,0:T(8,128)(2,1)}), bf16[32,32,128]{2,1,0:T(8,128)(2,1)S(1)}, u32[]{:S(2)}, u32[]{:S(2)}) async-start(bf16[32,32,128]{2,1,0:T(8,128)(2,1)} %bitcast.9), calls=%async_computation | async-start | bytes 524288 | tf_op jit(solution)/shard_map/all_to_all | solution.py:267
  19.6 17.1 %collective-permute-start.3 = (bf16[128,2048]{1,0:T(8,128)(2,1)S(1)}, bf16[128,2048]{1,0:T(8,128)(2,1)S(1)}, u32[]{:S(2)}, u32[]{:S(2)}) collective-permute-start(bf16[128,2048]{1,0:T(8,128)(2,1)S(1)} %copy-done.6), channel_id=1, source_target_pairs={{0,4},{4,0},{8,12},{12,8},{16,20},{20,16},{24,28},{28,24},{32,36},... | collective-permute-start | bytes 1572872 | tf_op jit(solution)/shard_map/ppermute | solution.py:262
  20.4 21.2 %collective-permute-start.4 = (bf16[128,2048]{1,0:T(8,128)(2,1)S(1)}, bf16[128,2048]{1,0:T(8,128)(2,1)S(1)}, u32[]{:S(2)}, u32[]{:S(2)}) collective-permute-start(bf16[128,2048]{1,0:T(8,128)(2,1)S(1)} %copy-done.8), channel_id=1, source_target_pairs={{0,4},{4,0},{8,12},{12,8},{16,20},{20,16},{24,28},{28,24},{32,36},... | collective-permute-start | bytes 1572872 | tf_op jit(solution)/shard_map/ppermute | solution.py:262
  30.0 16.4 %all-to-all-start.1 = ((bf16[32,32,128]{2,1,0:T(8,128)(2,1)}), bf16[32,32,128]{2,1,0:T(8,128)(2,1)S(1)}, u32[]{:S(2)}, u32[]{:S(2)}) async-start(bf16[32,32,128]{2,1,0:T(8,128)(2,1)} %running_sums.2), calls=%async_computation.1 | async-start | bytes 524288 | tf_op jit(solution)/shard_map/all_to_all | solution.py:271
  36.8 0.8 copy-start.7
  37.6 8.9 %copy-start.4 = (f32[4,2048]{1,0:T(4,128)S(1)}, f32[4,2048]{1,0:T(4,128)}, u32[]{:S(2)}) copy-start(f32[4,2048]{1,0:T(4,128)} %scale.6) | copy-start | bytes 98308
  41.6 4.9 %copy-start.9 = (bf16[128,2048]{1,0:T(8,128)(2,1)}, bf16[128,2048]{1,0:T(8,128)(2,1)S(1)}, u32[]{:S(2)}) copy-start(bf16[128,2048]{1,0:T(8,128)(2,1)S(1)} %collective-permute-done.4.c_other) | copy-start | bytes 1572868
  46.4 3.5 %copy-start.2 = (bf16[32,32,128]{2,1,0:T(8,128)(2,1)}, bf16[32,32,128]{2,1,0:T(8,128)(2,1)S(1)}, u32[]{:S(2)}) copy-start(bf16[32,32,128]{2,1,0:T(8,128)(2,1)S(1)} %all-to-all-done.1) | copy-start | bytes 786436
  49.9 4.4 %collective-permute-start.5 = (f32[2,256]{1,0:T(2,128)S(1)}, f32[2,256]{1,0:T(2,128)S(1)}, u32[]{:S(2)}, u32[]{:S(2)}) collective-permute-start(f32[2,256]{1,0:T(2,128)S(1)} %get-tuple-element.34), channel_id=1, source_target_pairs={{0,4},{4,0},{8,12},{12,8},{16,20},{20,16},{24,28},{28,24},{32,36},... | collective-permute-start | bytes 6152 | tf_op jit(solution)/shard_map/ppermute | solution.py:262
  54.4 3.5 %collective-permute-start.7 = (f32[2,256]{1,0:T(2,128)S(1)}, f32[2,256]{1,0:T(2,128)S(1)}, u32[]{:S(2)}, u32[]{:S(2)}) collective-permute-start(f32[2,256]{1,0:T(2,128)S(1)} %maximum_add_fusion), channel_id=1, source_target_pairs={{0,2},{1,3},{2,0},{3,1},{8,10},{9,11},{10,8},{11,9},{16,18},{17,19... | collective-permute-start | bytes 6152 | tf_op jit(solution)/shard_map/ppermute | solution.py:294
  55.0 3.5 %collective-permute-start.6 = (f32[2,256]{1,0:T(2,128)S(1)}, f32[2,256]{1,0:T(2,128)S(1)}, u32[]{:S(2)}, u32[]{:S(2)}) collective-permute-start(f32[2,256]{1,0:T(2,128)S(1)} %maximum_add_fusion), channel_id=1, source_target_pairs={{0,1},{1,2},{2,3},{3,0},{4,7},{5,4},{6,5},{7,6},{8,9},{9,10},{10,1... | collective-permute-start | bytes 6152 | tf_op jit(solution)/shard_map/ppermute | solution.py:294
  58.6 6.9 %collective-permute-start.8 = (f32[2,256]{1,0:T(2,128)S(1)}, f32[2,256]{1,0:T(2,128)S(1)}, u32[]{:S(2)}, u32[]{:S(2)}) collective-permute-start(f32[2,256]{1,0:T(2,128)S(1)} %add.18), channel_id=1, source_target_pairs={{0,4},{4,0},{8,12},{12,8},{16,20},{20,16},{24,28},{28,24},{32,36},... | collective-permute-start | bytes 6152 | tf_op jit(solution)/shard_map/ppermute | solution.py:262
  83.7 16.4 %all-to-all-start.3 = ((bf16[32,32,128]{2,1,0:T(8,128)(2,1)}), bf16[32,32,128]{2,1,0:T(8,128)(2,1)S(1)}, u32[]{:S(2)}, u32[]{:S(2)}) async-start(bf16[32,32,128]{2,1,0:T(8,128)(2,1)} %running_sums.3), calls=%async_computation.3 | async-start | bytes 524288 | tf_op jit(solution)/shard_map/all_to_all | solution.py:271
  100.1 3.4 %copy-start.1 = (bf16[32,32,128]{2,1,0:T(8,128)(2,1)}, bf16[32,32,128]{2,1,0:T(8,128)(2,1)S(1)}, u32[]{:S(2)}) copy-start(bf16[32,32,128]{2,1,0:T(8,128)(2,1)S(1)} %all-to-all-done.3) | copy-start | bytes 786436
  105.1 6.2 %copy-start.13 = (bf16[128,1024]{1,0:T(8,128)(2,1)S(1)}, bf16[128,1024]{1,0:T(8,128)(2,1)}, u32[]{:S(2)}) copy-start(bf16[128,1024]{1,0:T(8,128)(2,1)} %get-tuple-element.46) | copy-start | bytes 786436
  105.1 8.4 %copy-start.14 = (bf16[128,1024]{1,0:T(8,128)(2,1)S(1)}, bf16[128,1024]{1,0:T(8,128)(2,1)}, u32[]{:S(2)}) copy-start(bf16[128,1024]{1,0:T(8,128)(2,1)} %get-tuple-element.44) | copy-start | bytes 786436
  105.1 19.2 %all-to-all-start.4 = ((bf16[32,8,1024]{2,1,0:T(8,128)(2,1)}), bf16[32,8,1024]{2,1,0:T(8,128)(2,1)S(1)}, u32[]{:S(2)}, u32[]{:S(2)}) async-start(bf16[32,8,1024]{2,1,0:T(8,128)(2,1)} %broadcast_in_dim.10), calls=%async_computation.4 | async-start | bytes 1048576 | tf_op jit(solution)/shard_map/all_to_all | solution.py:396
  111.3 5.7 %collective-permute-start.11 = (bf16[128,1024]{1,0:T(8,128)(2,1)S(1)}, bf16[128,1024]{1,0:T(8,128)(2,1)S(1)}, u32[]{:S(2)}, u32[]{:S(2)}) collective-permute-start(bf16[128,1024]{1,0:T(8,128)(2,1)S(1)} %copy-done.13), channel_id=1, source_target_pairs={{0,4},{4,0},{8,12},{12,8},{16,20},{20,16},{24,28},{28,24},{32,36},... | collective-permute-start | bytes 786440 | tf_op jit(solution)/shard_map/ppermute | solution.py:262
  113.5 4.4 %collective-permute-start.10 = (bf16[128,1024]{1,0:T(8,128)(2,1)S(1)}, bf16[128,1024]{1,0:T(8,128)(2,1)S(1)}, u32[]{:S(2)}, u32[]{:S(2)}) collective-permute-start(bf16[128,1024]{1,0:T(8,128)(2,1)S(1)} %copy-done.14), channel_id=1, source_target_pairs={{0,4},{4,0},{8,12},{12,8},{16,20},{20,16},{24,28},{28,24},{32,36},... | collective-permute-start | bytes 786440 | tf_op jit(solution)/shard_map/ppermute | solution.py:262
  113.6 3.4 %copy-start.10 = (bf16[128,1024]{1,0:T(8,128)(2,1)S(1)}, bf16[128,1024]{1,0:T(8,128)(2,1)}, u32[]{:S(2)}) copy-start(bf16[128,1024]{1,0:T(8,128)(2,1)} %get-tuple-element.45) | copy-start | bytes 786436
  116.6 2.3 %collective-permute-start.9 = (bf16[128,1024]{1,0:T(8,128)(2,1)}, bf16[128,1024]{1,0:T(8,128)(2,1)S(1)}, u32[]{:S(2)}, u32[]{:S(2)}) collective-permute-start(bf16[128,1024]{1,0:T(8,128)(2,1)} %get-tuple-element.42), channel_id=1, source_target_pairs={{0,4},{4,0},{8,12},{12,8},{16,20},{20,16},{24,28},{28,24},{32,36},... | collective-permute-start | bytes 786440 | tf_op jit(solution)/shard_map/ppermute | solution.py:262
  117.0 1.0 copy-start.11
  117.9 0.9 copy-start.12
  124.4 6.1 %collective-permute-start.12 = (f32[8,1024]{1,0:T(8,128)S(1)}, f32[8,1024]{1,0:T(8,128)S(1)}, u32[]{:S(2)}, u32[]{:S(2)}) collective-permute-start(f32[8,1024]{1,0:T(8,128)S(1)} %convert_reduce_fusion), channel_id=1, source_target_pairs={{0,4},{4,0},{8,12},{12,8},{16,20},{20,16},{24,28},{28,24},{32,36},... | collective-permute-start | bytes 98312 | tf_op jit(solution)/shard_map/ppermute | solution.py:262

commit v4 on v3

--- a/solution.py
+++ b/solution.py
@@ -5,7 +5,7 @@
 from jax import lax
 from jax.experimental import pallas as pl
 from jax.experimental.pallas import tpu as pltpu
-from jax.sharding import PartitionSpec as P
+from jax.sharding import Mesh, PartitionSpec as P
 
 DH = 128
 SPAN = 16
@@ -22,6 +22,20 @@
 TN = (((0,), (0,)), ((), ()))
 
 
+class Meta:
+    def __init__(self, place, own_ids, other_ids):
+        self.core = place[0]
+        self.ids = [own_ids[s] for s in range(own_ids.shape[0])]
+        self.ids += [other_ids[s] for s in range(other_ids.shape[0])]
+
+
+def with_meta(body):
+    def kernel(place, own_ids, other_ids, *refs):
+        body(Meta(place, own_ids, other_ids), *refs)
+
+    return kernel
+
+
 def dot(a, b, dims):
     return lax.dot_general(a, b, dims, preferred_element_type=F32)
 
@@ -36,7 +50,7 @@
     for s in range(spans):
         row = choices[0]
         for m in range(1, MEMBERS):
-            row = jnp.where(meta[1 + s] == m, choices[m], row)
+            row = jnp.where(meta.ids[s] == m, choices[m], row)
         rows.append(jnp.broadcast_to(row, (SPAN, DH)))
     return jnp.concatenate(rows, axis=0)
 
@@ -46,14 +60,14 @@
     for s in range(spans):
         part = x[s * SPAN : s * SPAN + 8] + x[s * SPAN + 8 : (s + 1) * SPAN]
         for m in range(MEMBERS):
-            keep = jnp.where(meta[1 + s] == m, 1.0, 0.0).astype(F32)
+            keep = jnp.where(meta.ids[s] == m, 1.0, 0.0).astype(F32)
             totals[m] = totals[m] + keep * part
     return jnp.concatenate([jnp.sum(t, axis=0, keepdims=True) for t in totals], axis=0)
 
 
 def causal_mask(meta, tok):
     size = 2 * tok
-    core = meta[0]
+    core = meta.core
     base_own = core * tok
     base_other = (1 - core) * tok - tok
 
@@ -62,6 +76,18 @@
         return at + jnp.where(at < tok, base_own, base_other)
 
     return place(0) >= place(1)
+
+
+def in_order(meta, x, tok):
+    turned = jnp.concatenate([x[:, tok:], x[:, :tok]], axis=1)
+    return jnp.where(meta.core == 0, x, turned)
+
+
+def head_sums(meta, sums, tok):
+    total = sums[0]
+    for at in range(1, sums.shape[0]):
+        total = total + sums[at]
+    return in_order(meta, total, tok)
 
 
 def lanes_of(h):
@@ -114,8 +140,9 @@
 
     @pl.when(step == pl.num_programs(0) - 1)
     def _():
-        sums[0:1] = jnp.sum(jnp.transpose(square), axis=0, keepdims=True)
-        sums[1:2] = jnp.sum(jnp.transpose(cross), axis=0, keepdims=True)
+        totals = [jnp.sum(jnp.transpose(t), axis=0, keepdims=True) for t in (square, cross)]
+        totals = in_order(meta, jnp.concatenate(totals, axis=0), tok)
+        sums[...] = jnp.broadcast_to(totals[None], sums.shape)
 
 
 def grads_kernel(
@@ -123,9 +150,10 @@
 ):
     tok = q_own.shape[0]
     spans = 2 * tok // SPAN
-    rms = jnp.sqrt(sums[0:1] / full_width + EPS)
+    totals = head_sums(meta, sums, tok)
+    rms = jnp.sqrt(totals[0:1] / full_width + EPS)
     inverse = 1.0 / rms
-    factor = sums[1:2] / (full_width * rms * rms * rms)
+    factor = totals[1:2] / (full_width * rms * rms * rms)
     inverse = jnp.transpose(jnp.broadcast_to(inverse, (DH, 2 * tok)))
     factor = jnp.transpose(jnp.broadcast_to(factor, (DH, 2 * tok)))
     for h in range(delta.shape[0]):
@@ -144,7 +172,8 @@
     tok = q_own.shape[0]
     spans = 2 * tok // SPAN
     causal = causal_mask(meta, tok)
-    inverse = 1.0 / jnp.sqrt(sums[0:1] / full_width + EPS)
+    totals = head_sums(meta, sums, tok)
+    inverse = 1.0 / jnp.sqrt(totals[0:1] / full_width + EPS)
     inverse = jnp.transpose(jnp.broadcast_to(inverse, (DH, 2 * tok)))
     for h in range(state.shape[0]):
         lanes = lanes_of(h)
@@ -165,7 +194,7 @@
 
 def value_kernel(
     meta, scale, k_own, k_other, v_own, v_other, state, value_in, out_part,
-    value_grad_own, value_grad_other, parts,
+    value_grad_own, value_grad_other, copies, parts,
 ):
     tok = k_own.shape[0]
     spans = 2 * tok // SPAN
@@ -177,7 +206,12 @@
         value_grad_other[:, lanes] = value_grad[tok:]
         value = pair(v_own, v_other, lanes).astype(F32)
         in_part = member_sums(meta, value * scaled_grad, spans)
-        parts[:, lanes] = jnp.concatenate([in_part, out_part[:, lanes]], axis=0)
+        here = pl.ds(pl.multiple_of(pl.program_id(0) * 2 * MEMBERS, 2 * MEMBERS), 2 * MEMBERS)
+        parts[here, lanes] = jnp.concatenate([in_part, out_part[:, lanes]], axis=0)
+
+    @pl.when(pl.program_id(0) == pl.num_programs(0) - 1)
+    def _():
+        copies[...] = jnp.broadcast_to(parts[...].astype(BF16)[None], copies.shape)
 
 
 def key_kernel(meta, scaled, state, key_in, key_grad_own, key_grad_other):
@@ -207,23 +241,23 @@
 
     def shared(self, rows):
         steps = self.steps
-        return pl.BlockSpec((rows, self.block), lambda i, meta: (0, meta[0] * steps + i))
+        return pl.BlockSpec((rows, self.block), lambda i, place, *_: (0, place[0] * steps + i))
 
     def cols(self, rows):
-        return pl.BlockSpec((rows, self.block), lambda i, meta: (0, i))
+        return pl.BlockSpec((rows, self.block), lambda i, *_: (0, i))
 
     def state(self):
-        return pl.BlockSpec((STEP_HEADS, DH, DH), lambda i, meta: (i, 0, 0))
+        return pl.BlockSpec((STEP_HEADS, DH, DH), lambda i, *_: (i, 0, 0))
 
     def whole(self, shape):
-        return pl.BlockSpec(shape, lambda i, meta: (0,) * len(shape))
+        return pl.BlockSpec(shape, lambda i, *_: (0,) * len(shape))
 
     def call(self, body, meta, ins, outs, args, shapes, name, scratch=(), flops=0):
         moved = sum(a.size * a.dtype.itemsize for a in args)
         return pl.pallas_call(
-            body,
+            with_meta(body),
             grid_spec=pltpu.PrefetchScalarGridSpec(
-                num_scalar_prefetch=1,
+                num_scalar_prefetch=len(meta),
                 grid=(self.steps,),
                 in_specs=ins,
                 out_specs=outs,
@@ -233,7 +267,7 @@
             name=name,
             compiler_params=pltpu.CompilerParams(vmem_limit_bytes=VMEM_BYTES),
             cost_estimate=pl.CostEstimate(flops=flops, bytes_accessed=2 * moved, transcendentals=0),
-        )(meta, *args)
+        )(*meta, *args)
 
 
 def fast(x):
@@ -255,20 +289,18 @@
 
 def make_shards(n_seq, n_head):
     chips = n_seq // CORES
-    core_swap = [(i, i ^ 1) for i in range(n_seq)]
-    same_core = [[CORES * i + c for i in range(chips)] for c in range(CORES)]
+    group = CORES * n_head
 
     def swap(x):
-        return lax.ppermute(x, "seq", core_swap)
+        return lax.ppermute(x, "core", [(0, 1), (1, 0)])
+
+    def scattered(pieces):
+        return lax.all_to_all(pieces, "chip", 0, 0, tiled=True)
 
     def scanned(delta, backward):
         heads = delta.shape[0]
         pieces = delta.reshape(chips, heads * DH // chips, DH)
-        pieces = lax.all_to_all(
-            pieces, "seq", 0, 0, axis_index_groups=same_core, tiled=True
-        )
-        sums = running_sums(pieces, backward)
-        sums = lax.all_to_all(sums, "seq", 0, 0, axis_index_groups=same_core, tiled=True)
+        sums = scattered(running_sums(scattered(pieces), backward))
         return sums.reshape(heads, DH, DH)
 
     def side_by_side(core, own, other):
@@ -277,23 +309,6 @@
             jnp.concatenate([own, other], axis=1),
             jnp.concatenate([other, own], axis=1),
         )
-
-    def turned(x, tok):
-        return jnp.concatenate([x[:, tok:], x[:, :tok]], axis=1)
-
-    def over_heads(x, tok):
-        got = None
-        for shift in range(1, n_head // 2 + 1):
-            moves = []
-            for s in range(n_seq):
-                for h in range(n_head):
-                    if s % CORES == 0:
-                        moves.append((s * n_head + h, s * n_head + (h + shift) % n_head))
-                    elif 2 * shift != n_head:
-                        moves.append((s * n_head + h, s * n_head + (h - shift) % n_head))
-            came = lax.ppermute(x, ("seq", "head"), moves)
-            got = came if got is None else got + came
-        return x + got + turned(swap(got), tok)
 
     def shards(queries, key_vectors, value_vectors, cotangent, member_ids, in_scale, out_scale):
         tok, both = queries.shape
@@ -301,7 +316,7 @@
         heads = width // DH
         full_width = both * n_head
         rows = 2 * tok
-        core = lax.axis_index("seq") % CORES
+        core = lax.axis_index("core")
 
         other_ids = swap(member_ids)
         v_other = swap(value_vectors)
@@ -315,9 +330,10 @@
         part = pltpu.HBM((MEMBERS, width), F32)
         sent = pltpu.HBM((heads, DH, DH), BF16)
         pairs = [shared(tok), shared(tok)]
+        packed = (chips, 2 * MEMBERS * local.steps, local.block)
         unit = 2 * heads * rows * DH * DH
 
-        meta = jnp.concatenate([place, member_ids, other_ids])
+        meta = (place, member_ids, other_ids)
         scaled, delta = local.call(
             states_kernel,
             meta,
@@ -346,18 +362,18 @@
             mixed_kernel,
             meta,
             [shared(MEMBERS)] + pairs * 2 + [state(), cols(rows)],
-            [cols(rows), local.whole((2, rows))],
+            [cols(rows), local.whole((group, 2, rows))],
             (out_scale, slow(queries), slow(q_other), slow(cotangent), slow(c_other), fast(state_in), slow(inside)),
-            [wide, pltpu.VMEM((2, rows), F32)],
+            [wide, pltpu.HBM((group, 2, rows), F32)],
             "mixed",
             scratch=[pltpu.VMEM((rows, DH), F32)] * 2,
             flops=unit,
         )
-        sums = over_heads(sums + turned(swap(sums), tok), tok)
+        sums = lax.all_to_all(sums, ("core", "head"), 0, 0, tiled=True)
         grad, delta_after = local.call(
             functools.partial(grads_kernel, full_width),
             meta,
-            [shared(MEMBERS)] + pairs * 2 + [cols(rows), local.whole((2, rows))],
+            [shared(MEMBERS)] + pairs * 2 + [cols(rows), local.whole((group, 2, rows))],
             [cols(rows), state()],
             (out_scale, slow(queries), slow(q_other), slow(cotangent), slow(c_other), slow(mixed), sums),
             [low, sent],
@@ -368,7 +384,7 @@
         query_own, query_send, key_in, value_in, out_part = local.call(
             functools.partial(back_kernel, full_width),
             meta,
-            pairs * 3 + [cols(rows), cols(rows), state(), cols(rows), local.whole((2, rows))],
+            pairs * 3 + [cols(rows), cols(rows), state(), cols(rows), local.whole((group, 2, rows))],
             [cols(tok), cols(tok), cols(rows), cols(rows), cols(MEMBERS)],
             (
                 slow(queries), slow(q_other), slow(key_vectors), slow(k_other), slow(cotangent), slow(c_other),
@@ -379,21 +395,21 @@
             flops=11 * unit,
         )
         query_grad = side_by_side(core, query_own, swap(query_send))
-        value_own, value_send, parts = local.call(
+        value_own, value_send, copies = local.call(
             value_kernel,
             meta,
             [shared(MEMBERS)] + pairs * 2 + [state(), cols(rows), cols(MEMBERS)],
-            [cols(tok)] * 2 + [cols(2 * MEMBERS)],
+            [cols(tok)] * 2 + [local.whole(packed)],
             (
                 in_scale, slow(key_vectors), slow(k_other), slow(value_vectors), slow(v_other),
                 fast(state_after), slow(value_in), slow(out_part),
             ),
-            [half] * 2 + [pltpu.HBM((2 * MEMBERS, width), F32)],
+            [half] * 2 + [pltpu.HBM(packed, BF16)],
             "value",
+            scratch=[pltpu.VMEM(packed[1:], F32)],
             flops=unit,
         )
-        copies = jnp.broadcast_to(parts.astype(BF16)[None], (chips,) + parts.shape)
-        copies = lax.all_to_all(copies, "seq", 0, 0, axis_index_groups=same_core, tiled=True)
+        copies = scattered(copies)
         key_own, key_send = local.call(
             key_kernel,
             meta,
@@ -410,6 +426,8 @@
             (copies, key_grad, value_grad, query_grad)
         )
         parts = jnp.sum(copies.astype(F32), axis=0)
+        each = 2 * MEMBERS
+        parts = jnp.concatenate([parts[i * each : (i + 1) * each] for i in range(local.steps)], axis=1)
         parts = side_by_side(core, parts, swap(parts))
         return query_grad, key_grad, value_grad, parts[:MEMBERS], parts[MEMBERS:]
 
@@ -418,26 +436,15 @@
 
 def solution(mesh):
     n_seq, n_head = mesh.shape["seq"], mesh.shape["head"]
-    shards = make_shards(n_seq, n_head)
-    placed = (
-        P("seq", "head"),
-        P("seq", "head"),
-        P("seq", "head"),
-        P("seq", "head"),
-        P("seq"),
-        P(None, "head"),
-        P(None, "head"),
-    )
+    chips = n_seq // CORES
+    finer = Mesh(mesh.devices.reshape(chips, CORES, n_head), ("chip", "core", "head"))
+    tokens = ("chip", "core")
+    wide = P(tokens, "head")
+    scale = P(None, "head")
     return jax.shard_map(
-        shards,
-        mesh=mesh,
-        in_specs=placed,
-        out_specs=(
-            P("seq", "head"),
-            P("seq", "head"),
-            P("seq", "head"),
-            P(None, "head"),
-            P(None, "head"),
-        ),
+        make_shards(n_seq, n_head),
+        mesh=finer,
+        in_specs=(wide, wide, wide, wide, P(tokens), scale, scale),
+        out_specs=(wide, wide, wide, scale, scale),
         check_vma=False,
     )

time: 132 us -> 128 us (0.970)
  starting transfers between devices: 54.9 us -> 41.7 us
  blocking collectives: 14 us -> 26.9 us
  waiting for transfers between devices: 26.7 us -> 24.5 us
  other arithmetic: 4.36 us -> 2.85 us
    ppermute x13 -> x9, starting transfers between devices: 25.8 us -> 12.6 us  [swap(): return lax.ppermute(x, 'core', [(0, 1), (1, 0)])]
    all_to_all x1 -> x2, blocking collectives: 14 us -> 26.9 us  [the longest x1 14 us: scattered(): return lax.all_to_all(pieces, 'chip', 0, 0, tiled=True)]
    ppermute x13 -> x9, waiting for transfers between devices: 5.24 us -> 3.16 us  [swap(): return lax.ppermute(x, 'core', [(0, 1), (1, 0)])]
  transfers between devices with their start and end apart: 17 -> 13, of which waited for: 9 -> 7; matrix products, arithmetic and copies ran while one was open for 3% -> 2% of each run, Pallas kernels for 11% -> 11%
where the time goes in v4:
time: 128 us; the launch traced here: 127 us
  starting transfers between devices  41.7 us (33%)
  Pallas kernels  28.2 us (22%)
  blocking collectives  26.9 us (21%)
  waiting for transfers between devices  24.5 us (19%)
  other arithmetic  2.85 us (2%)
  local copies, waits for them, and re-layouts  2.31 us (2%)
    all_to_all x4, starting transfers between devices, scattered(): return lax.all_to_all(pieces, 'chip', 0, 0, tiled=True)  29.1 us
    pallas_call x7, Pallas kernels, call(): pl.pallas_call(with_meta(body), grid_spec=pltpu.PrefetchScalarGridSpec(nu...  26.7 us
    all_to_all x4, waiting for transfers between devices, scattered(): return lax.all_to_all(pieces, 'chip', 0, 0, tiled=True)  21.4 us
    all_to_all x1, blocking collectives, scattered(): return lax.all_to_all(pieces, 'chip', 0, 0, tiled=True)  14 us
    all_to_all x1, blocking collectives, shards(): sums = lax.all_to_all(sums, ('core', 'head'), 0, 0, tiled=True)  12.9 us
    ppermute x9, starting transfers between devices, swap(): return lax.ppermute(x, 'core', [(0, 1), (1, 0)])  12.6 us
    ppermute x9, waiting for transfers between devices, swap(): return lax.ppermute(x, 'core', [(0, 1), (1, 0)])  3.16 us
    select_n x4, other arithmetic, side_by_side(): jnp.where(core == 0, jnp.concatenate([own, other], axis=1), jnp.concatena...  2.77 us
  transfers between devices with their start and end apart: 13, of which 7 were waited for; matrix products, arithmetic and copies ran while one was open for 2% of the time, Pallas kernels for 11%

profile of v4, /device:TPU:1, one launch (start us, length us, event | category | flops | bytes accessed | tf_op | source)
XLA Modules:
  0.0 127.3 jit_solution(3693155671897297592)
XLA Ops:
  0.6 3.3 %collective-permute-start.1 = (bf16[128,2048]{1,0:T(8,128)(2,1)}, bf16[128,2048]{1,0:T(8,128)(2,1)S(1)}, u32[]{:S(2)}, u32[]{:S(2)}) collective-permute-start(bf16[128,2048]{1,0:T(8,128)(2,1)} %refs_1_.7), channel_id=1, source_target_pairs={{0,4},{4,0},{1,5},{5,1},{2,6},{6,2},{3,7},{7,3},{8,12},{12,8},{9,1... | collective-permute-start | bytes 1572872 | tf_op jit(solution)/shard_map/ppermute | solution.py:295
  4.0 0.1 collective-permute-start.2
  4.1 0.4 collective-permute-start
  4.5 2.0 %collective-permute-done.other_ids = s32[8]{0:T(128)S(1)} collective-permute-done((s32[8]{0:T(128)}, s32[8]{0:T(128)S(1)}, u32[]{:S(2)}, u32[]{:S(2)}) %collective-permute-start) | collective-permute-done | bytes 64 | tf_op jit(solution)/shard_map/ppermute | solution.py:295
  6.5 0.0 collective-permute-done.1.refs_2_.refs_3_
  6.5 0.0 collective-permute-done.2.refs_4_
  6.5 0.0 copy-done.7
  6.5 0.0 copy-start.5
  6.5 0.8 copy-done.5
  7.3 2.9 %states.1 = (bf16[256,1024]{1,0:T(8,128)(2,1)}, bf16[8,128,128]{2,1,0:T(8,128)(2,1)}) custom-call(s32[1]{0:T(128)} %bitcast.place, s32[8]{0:T(128)S(1)} %copy-done.7, s32[8]{0:T(128)S(1)} %collective-permute-done.other_ids, f32[4,2048]{1,0:T(4,128)S(1)} %copy-done.5, bf16[128,2048]{1,0:T(8,128)(2,1)} %refs_1_.7, ...), custom_call_target="tpu_custom_call" | custom-call | flops 67108864 | bytes 4259840 | tf_op jit(solution)/shard_map/states/pallas_call | solution.py:257
  10.2 0.0 copy-done
  10.2 0.0 copy-done.3
  10.2 0.0 copy-start.8
  10.2 9.4 %all-to-all-start = ((bf16[32,32,128]{2,1,0:T(8,128)(2,1)}), bf16[32,32,128]{2,1,0:T(8,128)(2,1)S(1)}, u32[]{:S(2)}, u32[]{:S(2)}) async-start(bf16[32,32,128]{2,1,0:T(8,128)(2,1)} %bitcast.9), calls=%async_computation | async-start | bytes 524288 | tf_op jit(solution)/shard_map/all_to_all | solution.py:298
  19.6 0.0 copy-done.8
  19.7 0.7 collective-permute-start.3
  20.4 0.0 copy-done.10
  20.4 0.1 collective-permute-start.4
  20.5 8.8 %all-to-all-done.pieces = bf16[32,32,128]{2,1,0:T(8,128)(2,1)S(1)} async-done(((bf16[32,32,128]{2,1,0:T(8,128)(2,1)}), bf16[32,32,128]{2,1,0:T(8,128)(2,1)S(1)}, u32[]{:S(2)}, u32[]{:S(2)}) %all-to-all-start) | async-done | bytes 262176 | tf_op jit(solution)/shard_map/all_to_all | solution.py:298
  29.3 0.7 running_sums.2
  30.1 6.7 %all-to-all-start.1 = ((bf16[32,32,128]{2,1,0:T(8,128)(2,1)}), bf16[32,32,128]{2,1,0:T(8,128)(2,1)S(1)}, u32[]{:S(2)}, u32[]{:S(2)}) async-start(bf16[32,32,128]{2,1,0:T(8,128)(2,1)} %running_sums.2), calls=%async_computation.1 | async-start | bytes 524288 | tf_op jit(solution)/shard_map/all_to_all | solution.py:298
  36.8 0.0 collective-permute-done.3.refs_1_.refs_2_
  36.8 0.0 copy-start.9
  36.8 0.8 copy-done.9
  37.6 4.0 %inside.1.refs_6_ = f32[256,1024]{1,0:T(8,128)} custom-call(s32[1]{0:T(128)} %bitcast.place, s32[8]{0:T(128)S(1)} %copy-done.7, s32[8]{0:T(128)S(1)} %collective-permute-done.other_ids, bf16[128,2048]{1,0:T(8,128)(2,1)} %refs_0_.10, bf16[128,2048]{1,0:T(8,128)(2,1)} %copy-done.9, bf16[128,2048]{1,0:T(8,128)(2,1)} %refs_1_.7, bf16[128,2048]{1,0:T(8,128)(2,1)} %copy-done, ...), custom_call_target="tpu_custom_call" | custom-call | flops 268435456 | bytes 5242880 | tf_op jit(solution)/shard_map/inside/pallas_call | solution.py:257
  41.5 0.0 collective-permute-done.4.refs_4_.refs_5_
  41.6 4.9 %all-to-all-done.1 = bf16[32,32,128]{2,1,0:T(8,128)(2,1)S(1)} async-done(((bf16[32,32,128]{2,1,0:T(8,128)(2,1)}), bf16[32,32,128]{2,1,0:T(8,128)(2,1)S(1)}, u32[]{:S(2)}, u32[]{:S(2)}) %all-to-all-start.1) | async-done | bytes 262176 | tf_op jit(solution)/shard_map/all_to_all | solution.py:298
  46.4 0.0 copy-done.11
  46.4 0.0 copy-done.4
  46.4 3.5 %mixed.1 = (f32[256,1024]{1,0:T(8,128)}, f32[8,2,256]{2,1,0:T(2,128)}) custom-call(s32[1]{0:T(128)} %bitcast.place, s32[8]{0:T(128)S(1)} %copy-done.7, s32[8]{0:T(128)S(1)} %collective-permute-done.other_ids, f32[4,2048]{1,0:T(4,128)S(1)} %copy-done.4, bf16[128,2048]{1,0:T(8,128)(2,1)} %refs_0_.10, bf16[128,2048]{1,0:T(8,128)(2,1)} %copy-done.9, ...), custom_call_target="tpu_custom_call" | custom-call | flops 67108864 | bytes 6881280 | tf_op jit(solution)/shard_map/mixed/pallas_call | solution.py:257
  49.9 0.0 copy-done.1
  49.9 12.9 %all_to_all.30.refs_6_.refs_10_ = f32[8,2,256]{2,1,0:T(2,128)S(1)} all-to-all(f32[8,2,256]{2,1,0:T(2,128)} %get-tuple-element.34), channel_id=1, replica_groups=mesh['chip'=32,'core'=2,'head'=4] {'core','head'}, dimensions={0} | all-to-all | bytes 32768 | tf_op jit(solution)/shard_map/all_to_all | solution.py:372
  62.9 3.5 %grads.1 = (bf16[256,1024]{1,0:T(8,128)(2,1)}, bf16[8,128,128]{2,1,0:T(8,128)(2,1)}) custom-call(s32[1]{0:T(128)} %bitcast.place, s32[8]{0:T(128)S(1)} %copy-done.7, s32[8]{0:T(128)S(1)} %collective-permute-done.other_ids, f32[4,2048]{1,0:T(4,128)S(1)} %copy-done.4, bf16[128,2048]{1,0:T(8,128)(2,1)} %refs_0_.10, bf16[128,2048]{1,0:T(8,128)(2,1)} %copy-done.9, ...), custom_call_target="tpu_custom_call" | custom-call | flops 67108864 | bytes 6389760 | tf_op jit(solution)/shard_map/grads/pallas_call | solution.py:257
  66.3 14.0 %all_to_all.31.pieces = bf16[32,32,128]{2,1,0:T(8,128)(2,1)S(1)} all-to-all(bf16[32,32,128]{2,1,0:T(8,128)(2,1)} %bitcast.10), channel_id=1, replica_groups=mesh['chip'=32,'core'=2,'head'=4] {'chip'}, dimensions={0} | all-to-all | bytes 524288 | tf_op jit(solution)/shard_map/all_to_all | solution.py:298
  80.3 0.7 running_sums.3
  81.0 6.5 %all-to-all-start.4 = ((bf16[32,32,128]{2,1,0:T(8,128)(2,1)}), bf16[32,32,128]{2,1,0:T(8,128)(2,1)S(1)}, u32[]{:S(2)}, u32[]{:S(2)}) async-start(bf16[32,32,128]{2,1,0:T(8,128)(2,1)} %running_sums.3), calls=%async_computation.4 | async-start | bytes 524288 | tf_op jit(solution)/shard_map/all_to_all | solution.py:298
  87.5 0.0 copy-start.6
  87.5 6.4 %back.1 = (bf16[128,1024]{1,0:T(8,128)(2,1)}, bf16[128,1024]{1,0:T(8,128)(2,1)}, f32[256,1024]{1,0:T(8,128)}, f32[256,1024]{1,0:T(8,128)}, f32[4,1024]{1,0:T(4,128)}) custom-call(s32[1]{0:T(128)} %bitcast.place, s32[8]{0:T(128)S(1)} %copy-done.7, s32[8]{0:T(128)S(1)} %collective-permute-done.other_ids, bf16[128,2048]{1,0:T(8,128)(2,1)} %refs_0_.10, ...), custom_call_target="tpu_custom_call" | custom-call | flops 738197504 | bytes 11042816 | tf_op jit(solution)/shard_map/back/pallas_call | solution.py:257
  93.9 3.3 %all-to-all-done.4 = bf16[32,32,128]{2,1,0:T(8,128)(2,1)S(1)} async-done(((bf16[32,32,128]{2,1,0:T(8,128)(2,1)}), bf16[32,32,128]{2,1,0:T(8,128)(2,1)S(1)}, u32[]{:S(2)}, u32[]{:S(2)}) %all-to-all-start.4) | async-done | bytes 262176 | tf_op jit(solution)/shard_map/all_to_all | solution.py:298
  97.2 0.0 copy-done.6
  97.2 3.7 %value.1 = (bf16[128,1024]{1,0:T(8,128)(2,1)}, bf16[128,1024]{1,0:T(8,128)(2,1)}, bf16[32,16,512]{2,1,0:T(8,128)(2,1)}) custom-call(s32[1]{0:T(128)} %bitcast.place, s32[8]{0:T(128)S(1)} %copy-done.7, s32[8]{0:T(128)S(1)} %collective-permute-done.other_ids, f32[4,2048]{1,0:T(4,128)S(1)} %copy-done.6, bf16[128,2048]{1,0:T(8,128)(2,1)} %refs_1_.7, ...), custom_call_target="tpu_custom_call" | custom-call | flops 67108864 | bytes 6914048 | tf_op jit(solution)/shard_map/value/pallas_call | solution.py:257
  100.9 0.0 copy-done.2
  100.9 0.0 copy-start.16
  100.9 6.4 %all-to-all-start.5 = ((bf16[32,16,512]{2,1,0:T(8,128)(2,1)}), bf16[32,16,512]{2,1,0:T(8,128)(2,1)S(1)}, u32[]{:S(2)}, u32[]{:S(2)}) async-start(bf16[32,16,512]{2,1,0:T(8,128)(2,1)} %get-tuple-element.39), calls=%async_computation.5 | async-start | bytes 1048576 | tf_op jit(solution)/shard_map/all_to_all | solution.py:298
  107.3 0.0 copy-done.16
  107.3 1.9 %collective-permute-start.7 = (bf16[128,1024]{1,0:T(8,128)(2,1)S(1)}, bf16[128,1024]{1,0:T(8,128)(2,1)S(1)}, u32[]{:S(2)}, u32[]{:S(2)}) collective-permute-start(bf16[128,1024]{1,0:T(8,128)(2,1)S(1)} %copy-done.16), channel_id=1, source_target_pairs={{0,4},{4,0},{1,5},{5,1},{2,6},{6,2},{3,7},{7,3},{8,12},{12,8},{9,1... | collective-permute-start | bytes 786440 | tf_op jit(solution)/shard_map/ppermute | solution.py:295
  109.3 3.0 %key.1 = (bf16[128,1024]{1,0:T(8,128)(2,1)}, bf16[128,1024]{1,0:T(8,128)(2,1)}) custom-call(s32[1]{0:T(128)} %bitcast.place, s32[8]{0:T(128)S(1)} %copy-done.7, s32[8]{0:T(128)S(1)} %collective-permute-done.other_ids, bf16[256,1024]{1,0:T(8,128)(2,1)} %get-tuple-element.32.refs_4_.refs_6_.refs_0_, bf16[8,128,128]{2,1,0:T(8,128)(2,1)} %bitcast.8, ...), custom_call_target="tpu_custom_call" | custom-call | flops 67108864 | bytes 3670016 | tf_op jit(solution)/shard_map/key/pallas_call | solution.py:257
  112.2 0.0 collective-permute-start.5
  112.3 0.0 copy-done.15
  112.3 0.5 collective-permute-start.6
  112.8 0.0 collective-permute-done.7
  112.8 0.0 copy-done.13
  112.8 0.9 maximum_select_fusion.2
  113.7 0.3 collective-permute-done.5
  114.0 0.0 copy-done.14
  114.0 0.9 maximum_select_fusion
  114.9 0.0 collective-permute-done.6
  114.9 0.0 copy-done.12
  114.9 0.9 maximum_select_fusion.1
  115.9 4.4 %all-to-all-done.5 = bf16[32,16,512]{2,1,0:T(8,128)(2,1)S(1)} async-done(((bf16[32,16,512]{2,1,0:T(8,128)(2,1)}), bf16[32,16,512]{2,1,0:T(8,128)(2,1)S(1)}, u32[]{:S(2)}, u32[]{:S(2)}) %all-to-all-start.5) | async-done | bytes 524320 | tf_op jit(solution)/shard_map/all_to_all | solution.py:298
  120.2 0.1 convert_reduce_fusion
  120.3 5.4 %collective-permute-start.8 = (f32[8,1024]{1,0:T(8,128)S(1)}, f32[8,1024]{1,0:T(8,128)S(1)}, u32[]{:S(2)}, u32[]{:S(2)}) collective-permute-start(f32[8,1024]{1,0:T(8,128)S(1)} %pad_maximum_fusion), channel_id=1, source_target_pairs={{0,4},{4,0},{1,5},{5,1},{2,6},{6,2},{3,7},{7,3},{8,12},{12,8},{9,1... | collective-permute-start | bytes 98312 | tf_op jit(solution)/shard_map/ppermute | solution.py:295
  125.8 0.9 collective-permute-done.8
  126.6 0.6 fusion
  (15 shorter events, 0.0 us)
Async XLA Ops:
  0.6 5.8 %collective-permute-start.1 = (bf16[128,2048]{1,0:T(8,128)(2,1)}, bf16[128,2048]{1,0:T(8,128)(2,1)S(1)}, u32[]{:S(2)}, u32[]{:S(2)}) collective-permute-start(bf16[128,2048]{1,0:T(8,128)(2,1)} %refs_1_.7), channel_id=1, source_target_pairs={{0,4},{4,0},{1,5},{5,1},{2,6},{6,2},{3,7},{7,3},{8,12},{12,8},{9,1... | collective-permute-start | bytes 1572872 | tf_op jit(solution)/shard_map/ppermute | solution.py:295
  4.0 2.5 %collective-permute-start.2 = (bf16[128,2048]{1,0:T(8,128)(2,1)}, bf16[128,2048]{1,0:T(8,128)(2,1)S(1)}, u32[]{:S(2)}, u32[]{:S(2)}) collective-permute-start(bf16[128,2048]{1,0:T(8,128)(2,1)} %refs_3_.7), channel_id=1, source_target_pairs={{0,4},{4,0},{1,5},{5,1},{2,6},{6,2},{3,7},{7,3},{8,12},{12,8},{9,1... | collective-permute-start | bytes 1572872 | tf_op jit(solution)/shard_map/ppermute | solution.py:295
  4.1 2.4 %collective-permute-start = (s32[8]{0:T(128)}, s32[8]{0:T(128)S(1)}, u32[]{:S(2)}, u32[]{:S(2)}) collective-permute-start(s32[8]{0:T(128)} %own_ids.13), channel_id=1, source_target_pairs={{0,4},{4,0},{1,5},{5,1},{2,6},{6,2},{3,7},{7,3},{8,12},{12,8},{9,1... | collective-permute-start | bytes 104 | tf_op jit(solution)/shard_map/ppermute | solution.py:295
  4.5 2.0 %copy-start.7 = (s32[8]{0:T(128)S(1)}, s32[8]{0:T(128)}, u32[]{:S(2)}) copy-start(s32[8]{0:T(128)} %own_ids.13) | copy-start | bytes 100
  6.5 3.7 %copy-start = (bf16[128,2048]{1,0:T(8,128)(2,1)}, bf16[128,2048]{1,0:T(8,128)(2,1)S(1)}, u32[]{:S(2)}) copy-start(bf16[128,2048]{1,0:T(8,128)(2,1)S(1)} %collective-permute-done.1.refs_2_.refs_3_) | copy-start | bytes 1572868
  6.5 3.7 %copy-start.3 = (bf16[128,2048]{1,0:T(8,128)(2,1)}, bf16[128,2048]{1,0:T(8,128)(2,1)S(1)}, u32[]{:S(2)}) copy-start(bf16[128,2048]{1,0:T(8,128)(2,1)S(1)} %collective-permute-done.2.refs_4_) | copy-start | bytes 1572868
  6.5 0.8 copy-start.5
  7.3 13.1 %copy-start.10 = (bf16[128,2048]{1,0:T(8,128)(2,1)S(1)}, bf16[128,2048]{1,0:T(8,128)(2,1)}, u32[]{:S(2)}) copy-start(bf16[128,2048]{1,0:T(8,128)(2,1)} %refs_4_.1) | copy-start | bytes 1572868
  10.2 9.5 %copy-start.8 = (bf16[128,2048]{1,0:T(8,128)(2,1)S(1)}, bf16[128,2048]{1,0:T(8,128)(2,1)}, u32[]{:S(2)}) copy-start(bf16[128,2048]{1,0:T(8,128)(2,1)} %refs_0_.10) | copy-start | bytes 1572868
  10.2 19.1 %all-to-all-start = ((bf16[32,32,128]{2,1,0:T(8,128)(2,1)}), bf16[32,32,128]{2,1,0:T(8,128)(2,1)S(1)}, u32[]{:S(2)}, u32[]{:S(2)}) async-start(bf16[32,32,128]{2,1,0:T(8,128)(2,1)} %bitcast.9), calls=%async_computation | async-start | bytes 524288 | tf_op jit(solution)/shard_map/all_to_all | solution.py:298
  19.7 17.1 %collective-permute-start.3 = (bf16[128,2048]{1,0:T(8,128)(2,1)S(1)}, bf16[128,2048]{1,0:T(8,128)(2,1)S(1)}, u32[]{:S(2)}, u32[]{:S(2)}) collective-permute-start(bf16[128,2048]{1,0:T(8,128)(2,1)S(1)} %copy-done.8), channel_id=1, source_target_pairs={{0,4},{4,0},{1,5},{5,1},{2,6},{6,2},{3,7},{7,3},{8,12},{12,8},{9,1... | collective-permute-start | bytes 1572872 | tf_op jit(solution)/shard_map/ppermute | solution.py:295
  20.4 21.2 %collective-permute-start.4 = (bf16[128,2048]{1,0:T(8,128)(2,1)S(1)}, bf16[128,2048]{1,0:T(8,128)(2,1)S(1)}, u32[]{:S(2)}, u32[]{:S(2)}) collective-permute-start(bf16[128,2048]{1,0:T(8,128)(2,1)S(1)} %copy-done.10), channel_id=1, source_target_pairs={{0,4},{4,0},{1,5},{5,1},{2,6},{6,2},{3,7},{7,3},{8,12},{12,8},{9,1... | collective-permute-start | bytes 1572872 | tf_op jit(solution)/shard_map/ppermute | solution.py:295
  30.1 16.4 %all-to-all-start.1 = ((bf16[32,32,128]{2,1,0:T(8,128)(2,1)}), bf16[32,32,128]{2,1,0:T(8,128)(2,1)S(1)}, u32[]{:S(2)}, u32[]{:S(2)}) async-start(bf16[32,32,128]{2,1,0:T(8,128)(2,1)} %running_sums.2), calls=%async_computation.1 | async-start | bytes 524288 | tf_op jit(solution)/shard_map/all_to_all | solution.py:298
  36.8 0.8 copy-start.9
  37.6 8.9 %copy-start.4 = (f32[4,2048]{1,0:T(4,128)S(1)}, f32[4,2048]{1,0:T(4,128)}, u32[]{:S(2)}) copy-start(f32[4,2048]{1,0:T(4,128)} %refs_0_.9) | copy-start | bytes 98308
  41.6 4.9 %copy-start.11 = (bf16[128,2048]{1,0:T(8,128)(2,1)}, bf16[128,2048]{1,0:T(8,128)(2,1)S(1)}, u32[]{:S(2)}) copy-start(bf16[128,2048]{1,0:T(8,128)(2,1)S(1)} %collective-permute-done.4.refs_4_.refs_5_) | copy-start | bytes 1572868
  46.4 3.5 %copy-start.1 = (bf16[32,32,128]{2,1,0:T(8,128)(2,1)}, bf16[32,32,128]{2,1,0:T(8,128)(2,1)S(1)}, u32[]{:S(2)}) copy-start(bf16[32,32,128]{2,1,0:T(8,128)(2,1)S(1)} %all-to-all-done.1) | copy-start | bytes 786436
  81.0 16.2 %all-to-all-start.4 = ((bf16[32,32,128]{2,1,0:T(8,128)(2,1)}), bf16[32,32,128]{2,1,0:T(8,128)(2,1)S(1)}, u32[]{:S(2)}, u32[]{:S(2)}) async-start(bf16[32,32,128]{2,1,0:T(8,128)(2,1)} %running_sums.3), calls=%async_computation.4 | async-start | bytes 524288 | tf_op jit(solution)/shard_map/all_to_all | solution.py:298
  87.5 9.7 %copy-start.6 = (f32[4,2048]{1,0:T(4,128)S(1)}, f32[4,2048]{1,0:T(4,128)}, u32[]{:S(2)}) copy-start(f32[4,2048]{1,0:T(4,128)} %refs_0_.11) | copy-start | bytes 98308
  97.2 3.7 %copy-start.2 = (bf16[32,32,128]{2,1,0:T(8,128)(2,1)}, bf16[32,32,128]{2,1,0:T(8,128)(2,1)S(1)}, u32[]{:S(2)}) copy-start(bf16[32,32,128]{2,1,0:T(8,128)(2,1)S(1)} %all-to-all-done.4) | copy-start | bytes 786436
  100.9 6.5 %copy-start.16 = (bf16[128,1024]{1,0:T(8,128)(2,1)S(1)}, bf16[128,1024]{1,0:T(8,128)(2,1)}, u32[]{:S(2)}) copy-start(bf16[128,1024]{1,0:T(8,128)(2,1)} %get-tuple-element.46) | copy-start | bytes 786436
  100.9 19.4 %all-to-all-start.5 = ((bf16[32,16,512]{2,1,0:T(8,128)(2,1)}), bf16[32,16,512]{2,1,0:T(8,128)(2,1)S(1)}, u32[]{:S(2)}, u32[]{:S(2)}) async-start(bf16[32,16,512]{2,1,0:T(8,128)(2,1)} %get-tuple-element.39), calls=%async_computation.5 | async-start | bytes 1048576 | tf_op jit(solution)/shard_map/all_to_all | solution.py:298
  107.3 5.4 %collective-permute-start.7 = (bf16[128,1024]{1,0:T(8,128)(2,1)S(1)}, bf16[128,1024]{1,0:T(8,128)(2,1)S(1)}, u32[]{:S(2)}, u32[]{:S(2)}) collective-permute-start(bf16[128,1024]{1,0:T(8,128)(2,1)S(1)} %copy-done.16), channel_id=1, source_target_pairs={{0,4},{4,0},{1,5},{5,1},{2,6},{6,2},{3,7},{7,3},{8,12},{12,8},{9,1... | collective-permute-start | bytes 786440 | tf_op jit(solution)/shard_map/ppermute | solution.py:295
  109.3 3.0 %copy-start.15 = (bf16[128,1024]{1,0:T(8,128)(2,1)S(1)}, bf16[128,1024]{1,0:T(8,128)(2,1)}, u32[]{:S(2)}) copy-start(bf16[128,1024]{1,0:T(8,128)(2,1)} %get-tuple-element.44) | copy-start | bytes 786436
  109.3 3.5 %copy-start.13 = (bf16[128,1024]{1,0:T(8,128)(2,1)S(1)}, bf16[128,1024]{1,0:T(8,128)(2,1)}, u32[]{:S(2)}) copy-start(bf16[128,1024]{1,0:T(8,128)(2,1)} %get-tuple-element.45) | copy-start | bytes 786436
  112.2 1.7 %collective-permute-start.5 = (bf16[128,1024]{1,0:T(8,128)(2,1)}, bf16[128,1024]{1,0:T(8,128)(2,1)S(1)}, u32[]{:S(2)}, u32[]{:S(2)}) collective-permute-start(bf16[128,1024]{1,0:T(8,128)(2,1)} %get-tuple-element.42), channel_id=1, source_target_pairs={{0,4},{4,0},{1,5},{5,1},{2,6},{6,2},{3,7},{7,3},{8,12},{12,8},{9,1... | collective-permute-start | bytes 786440 | tf_op jit(solution)/shard_map/ppermute | solution.py:295
  112.3 2.6 %collective-permute-start.6 = (bf16[128,1024]{1,0:T(8,128)(2,1)S(1)}, bf16[128,1024]{1,0:T(8,128)(2,1)S(1)}, u32[]{:S(2)}, u32[]{:S(2)}) collective-permute-start(bf16[128,1024]{1,0:T(8,128)(2,1)S(1)} %copy-done.15), channel_id=1, source_target_pairs={{0,4},{4,0},{1,5},{5,1},{2,6},{6,2},{3,7},{7,3},{8,12},{12,8},{9,1... | collective-permute-start | bytes 786440 | tf_op jit(solution)/shard_map/ppermute | solution.py:295
  112.8 1.2 copy-start.14
  114.0 1.0 copy-start.12
  120.3 6.3 %collective-permute-start.8 = (f32[8,1024]{1,0:T(8,128)S(1)}, f32[8,1024]{1,0:T(8,128)S(1)}, u32[]{:S(2)}, u32[]{:S(2)}) collective-permute-start(f32[8,1024]{1,0:T(8,128)S(1)} %pad_maximum_fusion), channel_id=1, source_target_pairs={{0,4},{4,0},{1,5},{5,1},{2,6},{6,2},{3,7},{7,3},{8,12},{12,8},{9,1... | collective-permute-start | bytes 98312 | tf_op jit(solution)/shard_map/ppermute | solution.py:295

commit v5 on v4

--- a/solution.py
+++ b/solution.py
@@ -146,16 +146,20 @@
 
 
 def grads_kernel(
-    full_width, meta, scale, q_own, q_other, c_own, c_other, mixed, sums, grad, delta
+    full_width, meta, scale, q_own, q_other, c_own, c_other, mixed, sums, grad, delta, turned
 ):
     tok = q_own.shape[0]
     spans = 2 * tok // SPAN
-    totals = head_sums(meta, sums, tok)
-    rms = jnp.sqrt(totals[0:1] / full_width + EPS)
-    inverse = 1.0 / rms
-    factor = totals[1:2] / (full_width * rms * rms * rms)
-    inverse = jnp.transpose(jnp.broadcast_to(inverse, (DH, 2 * tok)))
-    factor = jnp.transpose(jnp.broadcast_to(factor, (DH, 2 * tok)))
+
+    @pl.when(pl.program_id(0) == 0)
+    def _():
+        totals = head_sums(meta, sums, tok)
+        rms = jnp.sqrt(totals[0:1] / full_width + EPS)
+        turned[0] = jnp.transpose(jnp.broadcast_to(1.0 / rms, (DH, 2 * tok)))
+        factor = totals[1:2] / (full_width * rms * rms * rms)
+        turned[1] = jnp.transpose(jnp.broadcast_to(factor, (DH, 2 * tok)))
+
+    inverse, factor = turned[0], turned[1]
     for h in range(delta.shape[0]):
         lanes = lanes_of(h)
         cot = pair(c_own, c_other, lanes).astype(F32) * inverse
@@ -166,8 +170,9 @@
 
 
 def back_kernel(
-    full_width, meta, q_own, q_other, k_own, k_other, c_own, c_other, scaled, grad, state, mixed, sums,
-    query_own, query_other, key_in, value_in, out_part,
+    full_width, meta, q_own, q_other, k_own, k_other, v_own, v_other, c_own, c_other,
+    scaled, grad, state, mixed, sums,
+    query_own, query_other, key_in, value_in, parts,
 ):
     tok = q_own.shape[0]
     spans = 2 * tok // SPAN
@@ -187,40 +192,46 @@
         query_own[:, lanes] = query_grad[:tok]
         query_other[:, lanes] = query_grad[tok:]
         key_in[:, lanes] = dot(grad_weights, query, TN)
-        value_in[:, lanes] = dot(weights, g, TN)
+        inner = dot(weights, g, TN)
+        value_in[:, lanes] = inner
+        in_part = member_sums(meta, pair(v_own, v_other, lanes).astype(F32) * inner, spans)
         normed = pair(c_own, c_other, lanes).astype(F32) * (mixed[:, lanes] * inverse)
-        out_part[:, lanes] = member_sums(meta, normed, spans)
-
-
-def value_kernel(
-    meta, scale, k_own, k_other, v_own, v_other, state, value_in, out_part,
-    value_grad_own, value_grad_other, copies, parts,
+        out_part = member_sums(meta, normed, spans)
+        parts[:, lanes] = jnp.concatenate([in_part, out_part], axis=0)
+
+
+def copies_kernel(meta, k_own, k_other, v_own, v_other, state, known, copies, parts):
+    tok = k_own.shape[0]
+    spans = 2 * tok // SPAN
+    here = pl.ds(pl.multiple_of(pl.program_id(0) * 2 * MEMBERS, 2 * MEMBERS), 2 * MEMBERS)
+    for h in range(state.shape[0]):
+        lanes = lanes_of(h)
+        value = pair(v_own, v_other, lanes).astype(F32)
+        across = dot(pair(k_own, k_other, lanes), state[h], NN)
+        in_part = member_sums(meta, value * across, spans)
+        more = jnp.concatenate([in_part, jnp.zeros_like(in_part)], axis=0)
+        parts[here, lanes] = known[:, lanes] + more
+
+    @pl.when(pl.program_id(0) == pl.num_programs(0) - 1)
+    def _():
+        copies[...] = jnp.broadcast_to(parts[...].astype(BF16)[None], copies.shape)
+
+
+def last_kernel(
+    meta, scale, k_own, k_other, scaled, state, key_in, value_in,
+    key_grad_own, key_grad_other, value_grad_own, value_grad_other,
 ):
     tok = k_own.shape[0]
     spans = 2 * tok // SPAN
     for h in range(state.shape[0]):
         lanes = lanes_of(h)
+        key_grad = (key_in[:, lanes] + dot(scaled[:, lanes], state[h], NT)).astype(BF16)
+        key_grad_own[:, lanes] = key_grad[:tok]
+        key_grad_other[:, lanes] = key_grad[tok:]
         scaled_grad = value_in[:, lanes] + dot(pair(k_own, k_other, lanes), state[h], NN)
         value_grad = (rows_of_members(meta, scale, lanes, spans) * scaled_grad).astype(BF16)
         value_grad_own[:, lanes] = value_grad[:tok]
         value_grad_other[:, lanes] = value_grad[tok:]
-        value = pair(v_own, v_other, lanes).astype(F32)
-        in_part = member_sums(meta, value * scaled_grad, spans)
-        here = pl.ds(pl.multiple_of(pl.program_id(0) * 2 * MEMBERS, 2 * MEMBERS), 2 * MEMBERS)
-        parts[here, lanes] = jnp.concatenate([in_part, out_part[:, lanes]], axis=0)
-
-    @pl.when(pl.program_id(0) == pl.num_programs(0) - 1)
-    def _():
-        copies[...] = jnp.broadcast_to(parts[...].astype(BF16)[None], copies.shape)
-
-
-def key_kernel(meta, scaled, state, key_in, key_grad_own, key_grad_other):
-    tok = key_grad_own.shape[0]
-    for h in range(state.shape[0]):
-        lanes = lanes_of(h)
-        key_grad = (key_in[:, lanes] + dot(scaled[:, lanes], state[h], NT)).astype(BF16)
-        key_grad_own[:, lanes] = key_grad[:tok]
-        key_grad_other[:, lanes] = key_grad[tok:]
 
 
 def running_kernel(backward, pieces, sums):
@@ -327,7 +338,7 @@
         half = pltpu.HBM((tok, width), BF16)
         low = pltpu.HBM((rows, width), BF16)
         wide = pltpu.HBM((rows, width), F32)
-        part = pltpu.HBM((MEMBERS, width), F32)
+        part = pltpu.HBM((2 * MEMBERS, width), F32)
         sent = pltpu.HBM((heads, DH, DH), BF16)
         pairs = [shared(tok), shared(tok)]
         packed = (chips, 2 * MEMBERS * local.steps, local.block)
@@ -339,7 +350,7 @@
             meta,
             [shared(MEMBERS)] + pairs * 2,
             [cols(rows), state()],
-            (in_scale, slow(key_vectors), fast(k_other), slow(value_vectors), fast(v_other)),
+            (slow(in_scale), slow(key_vectors), fast(k_other), slow(value_vectors), fast(v_other)),
             [low, sent],
             "states",
             flops=unit,
@@ -363,7 +374,7 @@
             meta,
             [shared(MEMBERS)] + pairs * 2 + [state(), cols(rows)],
             [cols(rows), local.whole((group, 2, rows))],
-            (out_scale, slow(queries), slow(q_other), slow(cotangent), slow(c_other), fast(state_in), slow(inside)),
+            (slow(out_scale), slow(queries), slow(q_other), slow(cotangent), slow(c_other), fast(state_in), slow(inside)),
             [wide, pltpu.HBM((group, 2, rows), F32)],
             "mixed",
             scratch=[pltpu.VMEM((rows, DH), F32)] * 2,
@@ -375,19 +386,21 @@
             meta,
             [shared(MEMBERS)] + pairs * 2 + [cols(rows), local.whole((group, 2, rows))],
             [cols(rows), state()],
-            (out_scale, slow(queries), slow(q_other), slow(cotangent), slow(c_other), slow(mixed), sums),
+            (slow(out_scale), slow(queries), slow(q_other), slow(cotangent), slow(c_other), slow(mixed), sums),
             [low, sent],
             "grads",
+            scratch=[pltpu.VMEM((2, rows, DH), F32)],
             flops=unit,
         )
         state_after = scanned(delta_after, True)
-        query_own, query_send, key_in, value_in, out_part = local.call(
+        query_own, query_send, key_in, value_in, parts = local.call(
             functools.partial(back_kernel, full_width),
             meta,
-            pairs * 3 + [cols(rows), cols(rows), state(), cols(rows), local.whole((group, 2, rows))],
-            [cols(tok), cols(tok), cols(rows), cols(rows), cols(MEMBERS)],
+            pairs * 4 + [cols(rows), cols(rows), state(), cols(rows), local.whole((group, 2, rows))],
+            [cols(tok), cols(tok), cols(rows), cols(rows), cols(2 * MEMBERS)],
             (
-                slow(queries), slow(q_other), slow(key_vectors), slow(k_other), slow(cotangent), slow(c_other),
+                slow(queries), slow(q_other), slow(key_vectors), slow(k_other),
+                slow(value_vectors), slow(v_other), slow(cotangent), slow(c_other),
                 slow(scaled), slow(grad), slow(state_in), slow(mixed), sums,
             ),
             [half, half, wide, wide, part],
@@ -395,30 +408,33 @@
             flops=11 * unit,
         )
         query_grad = side_by_side(core, query_own, swap(query_send))
-        value_own, value_send, copies = local.call(
-            value_kernel,
-            meta,
-            [shared(MEMBERS)] + pairs * 2 + [state(), cols(rows), cols(MEMBERS)],
-            [cols(tok)] * 2 + [local.whole(packed)],
+        copies = local.call(
+            copies_kernel,
+            meta,
+            pairs * 2 + [state(), cols(2 * MEMBERS)],
+            local.whole(packed),
             (
-                in_scale, slow(key_vectors), slow(k_other), slow(value_vectors), slow(v_other),
-                fast(state_after), slow(value_in), slow(out_part),
+                slow(key_vectors), slow(k_other), slow(value_vectors), slow(v_other),
+                fast(state_after), slow(parts),
             ),
-            [half] * 2 + [pltpu.HBM(packed, BF16)],
-            "value",
+            pltpu.HBM(packed, BF16),
+            "copies",
             scratch=[pltpu.VMEM(packed[1:], F32)],
             flops=unit,
         )
         copies = scattered(copies)
-        key_own, key_send = local.call(
-            key_kernel,
-            meta,
-            [cols(rows), state(), cols(rows)],
-            [cols(tok)] * 2,
-            (slow(scaled), slow(state_after), slow(key_in)),
-            [half] * 2,
-            "key",
-            flops=unit,
+        key_own, key_send, value_own, value_send = local.call(
+            last_kernel,
+            meta,
+            [shared(MEMBERS)] + pairs + [cols(rows), state(), cols(rows), cols(rows)],
+            [cols(tok)] * 4,
+            (
+                slow(in_scale), slow(key_vectors), slow(k_other), slow(scaled),
+                slow(state_after), slow(key_in), slow(value_in),
+            ),
+            [half] * 4,
+            "last",
+            flops=2 * unit,
         )
         key_grad = side_by_side(core, key_own, swap(key_send))
         value_grad = side_by_side(core, value_own, swap(value_send))

time: 128 us -> 127 us (level)
  transfers between devices with their start and end apart: 13 -> 13, of which waited for: 7 -> 7; matrix products, arithmetic and copies ran while one was open for 2% -> 2% of each run, Pallas kernels for 11% -> 12%
where the time goes in v5:
time: 127 us; the launch traced here: 126 us
  starting transfers between devices  41.7 us (33%)
  Pallas kernels  28.7 us (23%)
  blocking collectives  26.9 us (21%)
  waiting for transfers between devices  23.7 us (19%)
  other arithmetic  2.85 us (2%)
  local copies, waits for them, and re-layouts  1.5 us (1%)
    all_to_all x4, starting transfers between devices, scattered(): return lax.all_to_all(pieces, 'chip', 0, 0, tiled=True)  29.1 us
    pallas_call x7, Pallas kernels, call(): pl.pallas_call(with_meta(body), grid_spec=pltpu.PrefetchScalarGridSpec(nu...  27.2 us
    all_to_all x4, waiting for transfers between devices, scattered(): return lax.all_to_all(pieces, 'chip', 0, 0, tiled=True)  20.5 us
    all_to_all x1, blocking collectives, scattered(): return lax.all_to_all(pieces, 'chip', 0, 0, tiled=True)  14 us
    all_to_all x1, blocking collectives, shards(): sums = lax.all_to_all(sums, ('core', 'head'), 0, 0, tiled=True)  13 us
    ppermute x9, starting transfers between devices, swap(): return lax.ppermute(x, 'core', [(0, 1), (1, 0)])  12.6 us
    ppermute x9, waiting for transfers between devices, swap(): return lax.ppermute(x, 'core', [(0, 1), (1, 0)])  3.17 us
    select_n x4, other arithmetic, side_by_side(): jnp.where(core == 0, jnp.concatenate([own, other], axis=1), jnp.concatena...  2.77 us
  transfers between devices with their start and end apart: 13, of which 7 were waited for; matrix products, arithmetic and copies ran while one was open for 2% of the time, Pallas kernels for 12%

profile of v5, /device:TPU:1, one launch (start us, length us, event | category | flops | bytes accessed | tf_op | source)
XLA Modules:
  0.0 126.1 jit_solution(13053371797229458961)
XLA Ops:
  0.6 3.3 %collective-permute-start.1 = (bf16[128,2048]{1,0:T(8,128)(2,1)}, bf16[128,2048]{1,0:T(8,128)(2,1)S(1)}, u32[]{:S(2)}, u32[]{:S(2)}) collective-permute-start(bf16[128,2048]{1,0:T(8,128)(2,1)} %refs_1_.7), channel_id=1, source_target_pairs={{0,4},{4,0},{1,5},{5,1},{2,6},{6,2},{3,7},{7,3},{8,12},{12,8},{9,1... | collective-permute-start | bytes 1572872 | tf_op jit(solution)/shard_map/ppermute | solution.py:306
  4.0 0.1 collective-permute-start.2
  4.1 0.4 collective-permute-start
  4.5 0.0 copy-start.4
  4.5 2.0 %collective-permute-done.other_ids = s32[8]{0:T(128)S(1)} collective-permute-done((s32[8]{0:T(128)}, s32[8]{0:T(128)S(1)}, u32[]{:S(2)}, u32[]{:S(2)}) %collective-permute-start) | collective-permute-done | bytes 64 | tf_op jit(solution)/shard_map/ppermute | solution.py:306
  6.5 0.0 collective-permute-done.1.refs_2_.refs_3_.refs_1_
  6.5 0.0 copy-start
  6.5 0.0 collective-permute-done.2.refs_4_.refs_5_.refs_3_
  6.5 0.0 copy-start.1
  6.5 0.0 copy-done.4
  6.5 0.0 copy-start.7
  6.5 2.9 %states.1 = (bf16[256,1024]{1,0:T(8,128)(2,1)}, bf16[8,128,128]{2,1,0:T(8,128)(2,1)}) custom-call(s32[1]{0:T(128)} %bitcast.place, s32[8]{0:T(128)S(1)} %copy-done.4, s32[8]{0:T(128)S(1)} %collective-permute-done.other_ids, f32[4,2048]{1,0:T(4,128)} %refs_0_.13, bf16[128,2048]{1,0:T(8,128)(2,1)} %refs_1_.7, ...), custom_call_target="tpu_custom_call" | custom-call | flops 67108864 | bytes 4259840 | tf_op jit(solution)/shard_map/states/pallas_call | solution.py:268
  9.4 0.0 copy-done
  9.4 0.0 copy-done.1
  9.4 0.0 copy-start.5
  9.4 9.4 %all-to-all-start = ((bf16[32,32,128]{2,1,0:T(8,128)(2,1)}), bf16[32,32,128]{2,1,0:T(8,128)(2,1)S(1)}, u32[]{:S(2)}, u32[]{:S(2)}) async-start(bf16[32,32,128]{2,1,0:T(8,128)(2,1)} %bitcast.9), calls=%async_computation | async-start | bytes 524288 | tf_op jit(solution)/shard_map/all_to_all | solution.py:309
  18.9 0.0 copy-done.5
  18.9 0.7 collective-permute-start.3
  19.6 0.0 copy-done.7
  19.6 0.1 collective-permute-start.4
  19.8 8.8 %all-to-all-done.pieces = bf16[32,32,128]{2,1,0:T(8,128)(2,1)S(1)} async-done(((bf16[32,32,128]{2,1,0:T(8,128)(2,1)}), bf16[32,32,128]{2,1,0:T(8,128)(2,1)S(1)}, u32[]{:S(2)}, u32[]{:S(2)}) %all-to-all-start) | async-done | bytes 262176 | tf_op jit(solution)/shard_map/all_to_all | solution.py:309
  28.6 0.7 running_sums.2
  29.3 6.7 %all-to-all-start.1 = ((bf16[32,32,128]{2,1,0:T(8,128)(2,1)}), bf16[32,32,128]{2,1,0:T(8,128)(2,1)S(1)}, u32[]{:S(2)}, u32[]{:S(2)}) async-start(bf16[32,32,128]{2,1,0:T(8,128)(2,1)} %running_sums.2), calls=%async_computation.1 | async-start | bytes 524288 | tf_op jit(solution)/shard_map/all_to_all | solution.py:309
  36.0 0.0 collective-permute-done.3.refs_1_.refs_2_
  36.0 0.0 copy-start.6
  36.0 0.8 copy-done.6
  36.8 4.0 %inside.1.refs_6_ = f32[256,1024]{1,0:T(8,128)} custom-call(s32[1]{0:T(128)} %bitcast.place, s32[8]{0:T(128)S(1)} %copy-done.4, s32[8]{0:T(128)S(1)} %collective-permute-done.other_ids, bf16[128,2048]{1,0:T(8,128)(2,1)} %refs_0_.11, bf16[128,2048]{1,0:T(8,128)(2,1)} %copy-done.6, bf16[128,2048]{1,0:T(8,128)(2,1)} %refs_1_.7, bf16[128,2048]{1,0:T(8,128)(2,1)} %copy-done, ...), custom_call_target="tpu_custom_call" | custom-call | flops 268435456 | bytes 5242880 | tf_op jit(solution)/shard_map/inside/pallas_call | solution.py:268
  40.8 0.0 collective-permute-done.4.refs_4_.refs_7_
  40.8 0.0 copy-start.8
  40.8 4.9 %all-to-all-done.1 = bf16[32,32,128]{2,1,0:T(8,128)(2,1)S(1)} async-done(((bf16[32,32,128]{2,1,0:T(8,128)(2,1)}), bf16[32,32,128]{2,1,0:T(8,128)(2,1)S(1)}, u32[]{:S(2)}, u32[]{:S(2)}) %all-to-all-start.1) | async-done | bytes 262176 | tf_op jit(solution)/shard_map/all_to_all | solution.py:309
  45.7 0.0 copy-start.3
  45.7 0.0 copy-done.8
  45.7 3.5 %mixed.1 = (f32[256,1024]{1,0:T(8,128)}, f32[8,2,256]{2,1,0:T(2,128)}) custom-call(s32[1]{0:T(128)} %bitcast.place, s32[8]{0:T(128)S(1)} %copy-done.4, s32[8]{0:T(128)S(1)} %collective-permute-done.other_ids, f32[4,2048]{1,0:T(4,128)} %refs_0_.10, bf16[128,2048]{1,0:T(8,128)(2,1)} %refs_0_.11, bf16[128,2048]{1,0:T(8,128)(2,1)} %copy-done.6, ...), custom_call_target="tpu_custom_call" | custom-call | flops 67108864 | bytes 6881280 | tf_op jit(solution)/shard_map/mixed/pallas_call | solution.py:268
  49.2 0.0 copy-done.3
  49.2 13.0 %all_to_all.30.refs_6_.refs_12_ = f32[8,2,256]{2,1,0:T(2,128)S(1)} all-to-all(f32[8,2,256]{2,1,0:T(2,128)} %get-tuple-element.33), channel_id=1, replica_groups=mesh['chip'=32,'core'=2,'head'=4] {'core','head'}, dimensions={0} | all-to-all | bytes 32768 | tf_op jit(solution)/shard_map/all_to_all | solution.py:383
  62.1 3.5 %grads.1 = (bf16[256,1024]{1,0:T(8,128)(2,1)}, bf16[8,128,128]{2,1,0:T(8,128)(2,1)}) custom-call(s32[1]{0:T(128)} %bitcast.place, s32[8]{0:T(128)S(1)} %copy-done.4, s32[8]{0:T(128)S(1)} %collective-permute-done.other_ids, f32[4,2048]{1,0:T(4,128)} %refs_0_.10, bf16[128,2048]{1,0:T(8,128)(2,1)} %refs_0_.11, bf16[128,2048]{1,0:T(8,128)(2,1)} %copy-done.6, ...), custom_call_target="tpu_custom_call" | custom-call | flops 67108864 | bytes 6389760 | tf_op jit(solution)/shard_map/grads/pallas_call | solution.py:268
  65.7 14.0 %all_to_all.31.pieces = bf16[32,32,128]{2,1,0:T(8,128)(2,1)S(1)} all-to-all(bf16[32,32,128]{2,1,0:T(8,128)(2,1)} %bitcast.10), channel_id=1, replica_groups=mesh['chip'=32,'core'=2,'head'=4] {'chip'}, dimensions={0} | all-to-all | bytes 524288 | tf_op jit(solution)/shard_map/all_to_all | solution.py:309
  79.6 0.8 running_sums.3
  80.4 6.5 %all-to-all-start.4 = ((bf16[32,32,128]{2,1,0:T(8,128)(2,1)}), bf16[32,32,128]{2,1,0:T(8,128)(2,1)S(1)}, u32[]{:S(2)}, u32[]{:S(2)}) async-start(bf16[32,32,128]{2,1,0:T(8,128)(2,1)} %running_sums.3), calls=%async_computation.4 | async-start | bytes 524288 | tf_op jit(solution)/shard_map/all_to_all | solution.py:309
  86.9 6.5 %back.1 = (bf16[128,1024]{1,0:T(8,128)(2,1)}, bf16[128,1024]{1,0:T(8,128)(2,1)}, f32[256,1024]{1,0:T(8,128)}, f32[256,1024]{1,0:T(8,128)}, f32[8,1024]{1,0:T(8,128)}) custom-call(s32[1]{0:T(128)} %bitcast.place, s32[8]{0:T(128)S(1)} %copy-done.4, s32[8]{0:T(128)S(1)} %collective-permute-done.other_ids, bf16[128,2048]{1,0:T(8,128)(2,1)} %refs_0_.11, ...), custom_call_target="tpu_custom_call" | custom-call | flops 738197504 | bytes 13139968 | tf_op jit(solution)/shard_map/back/pallas_call | solution.py:268
  93.4 3.2 %all-to-all-done.4 = bf16[32,32,128]{2,1,0:T(8,128)(2,1)S(1)} async-done(((bf16[32,32,128]{2,1,0:T(8,128)(2,1)}), bf16[32,32,128]{2,1,0:T(8,128)(2,1)S(1)}, u32[]{:S(2)}, u32[]{:S(2)}) %all-to-all-start.4) | async-done | bytes 262176 | tf_op jit(solution)/shard_map/all_to_all | solution.py:309
  96.6 0.0 copy-start.2
  96.6 3.1 %copies.1 = bf16[32,16,512]{2,1,0:T(8,128)(2,1)} custom-call(s32[1]{0:T(128)} %bitcast.place, s32[8]{0:T(128)S(1)} %copy-done.4, s32[8]{0:T(128)S(1)} %collective-permute-done.other_ids, bf16[128,2048]{1,0:T(8,128)(2,1)} %refs_1_.7, bf16[128,2048]{1,0:T(8,128)(2,1)} %copy-done, bf16[128,2048]{1,0:T(8,128)(2,1)} %refs_2_.5, bf16[128,2048]{1,0:T(8,128)(2,1)} %copy-done.1, ...), custom_call_target="tpu_custom_call" | custom-call | flops 67108864 | bytes 4784128 | tf_op jit(solution)/shard_map/copies/pallas_call | solution.py:268
  99.7 0.0 copy-done.2
  99.7 6.4 %all-to-all-start.5 = ((bf16[32,16,512]{2,1,0:T(8,128)(2,1)}), bf16[32,16,512]{2,1,0:T(8,128)(2,1)S(1)}, u32[]{:S(2)}, u32[]{:S(2)}) async-start(bf16[32,16,512]{2,1,0:T(8,128)(2,1)} %copies.1), calls=%async_computation.5 | async-start | bytes 1048576 | tf_op jit(solution)/shard_map/all_to_all | solution.py:309
  106.2 0.0 copy-done.12
  106.2 2.0 %collective-permute-start.7 = (bf16[128,1024]{1,0:T(8,128)(2,1)S(1)}, bf16[128,1024]{1,0:T(8,128)(2,1)S(1)}, u32[]{:S(2)}, u32[]{:S(2)}) collective-permute-start(bf16[128,1024]{1,0:T(8,128)(2,1)S(1)} %copy-done.12), channel_id=1, source_target_pairs={{0,4},{4,0},{1,5},{5,1},{2,6},{6,2},{3,7},{7,3},{8,12},{12,8},{9,1... | collective-permute-start | bytes 786440 | tf_op jit(solution)/shard_map/ppermute | solution.py:306
  108.2 3.7 %last.1 = (bf16[128,1024]{1,0:T(8,128)(2,1)}, bf16[128,1024]{1,0:T(8,128)(2,1)}, bf16[128,1024]{1,0:T(8,128)(2,1)}, bf16[128,1024]{1,0:T(8,128)(2,1)}) custom-call(s32[1]{0:T(128)} %bitcast.place, s32[8]{0:T(128)S(1)} %copy-done.4, s32[8]{0:T(128)S(1)} %collective-permute-done.other_ids, f32[4,2048]{1,0:T(4,128)} %refs_0_.13, bf16[128,2048]{1,0:T(8,128)(2,1)} %refs_1_.7, ...), custom_call_target="tpu_custom_call" | custom-call | flops 134217728 | bytes 7929856 | tf_op jit(solution)/shard_map/last/pallas_call | solution.py:268
  111.8 0.1 collective-permute-start.5
  111.9 0.5 collective-permute-start.6
  112.4 0.0 collective-permute-done.7
  112.4 0.0 copy-done.9
  112.4 0.9 maximum_select_fusion.2
  113.3 0.3 collective-permute-done.5
  113.6 0.0 copy-done.11
  113.6 0.9 maximum_select_fusion
  114.5 0.0 collective-permute-done.6
  114.5 0.0 copy-done.10
  114.6 0.9 maximum_select_fusion.1
  115.5 3.6 %all-to-all-done.5 = bf16[32,16,512]{2,1,0:T(8,128)(2,1)S(1)} async-done(((bf16[32,16,512]{2,1,0:T(8,128)(2,1)}), bf16[32,16,512]{2,1,0:T(8,128)(2,1)S(1)}, u32[]{:S(2)}, u32[]{:S(2)}) %all-to-all-start.5) | async-done | bytes 524320 | tf_op jit(solution)/shard_map/all_to_all | solution.py:309
  119.1 0.1 convert_reduce_fusion
  119.2 5.4 %collective-permute-start.8 = (f32[8,1024]{1,0:T(8,128)S(1)}, f32[8,1024]{1,0:T(8,128)S(1)}, u32[]{:S(2)}, u32[]{:S(2)}) collective-permute-start(f32[8,1024]{1,0:T(8,128)S(1)} %pad_maximum_fusion), channel_id=1, source_target_pairs={{0,4},{4,0},{1,5},{5,1},{2,6},{6,2},{3,7},{7,3},{8,12},{12,8},{9,1... | collective-permute-start | bytes 98312 | tf_op jit(solution)/shard_map/ppermute | solution.py:306
  124.6 0.9 collective-permute-done.8
  125.5 0.6 fusion
  (7 shorter events, 0.0 us)
Async XLA Ops:
  0.6 5.8 %collective-permute-start.1 = (bf16[128,2048]{1,0:T(8,128)(2,1)}, bf16[128,2048]{1,0:T(8,128)(2,1)S(1)}, u32[]{:S(2)}, u32[]{:S(2)}) collective-permute-start(bf16[128,2048]{1,0:T(8,128)(2,1)} %refs_1_.7), channel_id=1, source_target_pairs={{0,4},{4,0},{1,5},{5,1},{2,6},{6,2},{3,7},{7,3},{8,12},{12,8},{9,1... | collective-permute-start | bytes 1572872 | tf_op jit(solution)/shard_map/ppermute | solution.py:306
  4.0 2.5 %collective-permute-start.2 = (bf16[128,2048]{1,0:T(8,128)(2,1)}, bf16[128,2048]{1,0:T(8,128)(2,1)S(1)}, u32[]{:S(2)}, u32[]{:S(2)}) collective-permute-start(bf16[128,2048]{1,0:T(8,128)(2,1)} %refs_2_.5), channel_id=1, source_target_pairs={{0,4},{4,0},{1,5},{5,1},{2,6},{6,2},{3,7},{7,3},{8,12},{12,8},{9,1... | collective-permute-start | bytes 1572872 | tf_op jit(solution)/shard_map/ppermute | solution.py:306
  4.1 2.4 %collective-permute-start = (s32[8]{0:T(128)}, s32[8]{0:T(128)S(1)}, u32[]{:S(2)}, u32[]{:S(2)}) collective-permute-start(s32[8]{0:T(128)} %own_ids.13), channel_id=1, source_target_pairs={{0,4},{4,0},{1,5},{5,1},{2,6},{6,2},{3,7},{7,3},{8,12},{12,8},{9,1... | collective-permute-start | bytes 104 | tf_op jit(solution)/shard_map/ppermute | solution.py:306
  4.5 2.0 %copy-start.4 = (s32[8]{0:T(128)S(1)}, s32[8]{0:T(128)}, u32[]{:S(2)}) copy-start(s32[8]{0:T(128)} %own_ids.13) | copy-start | bytes 100
  6.5 3.0 %copy-start = (bf16[128,2048]{1,0:T(8,128)(2,1)}, bf16[128,2048]{1,0:T(8,128)(2,1)S(1)}, u32[]{:S(2)}) copy-start(bf16[128,2048]{1,0:T(8,128)(2,1)S(1)} %collective-permute-done.1.refs_2_.refs_3_.refs_1_) | copy-start | bytes 1572868
  6.5 3.0 %copy-start.1 = (bf16[128,2048]{1,0:T(8,128)(2,1)}, bf16[128,2048]{1,0:T(8,128)(2,1)S(1)}, u32[]{:S(2)}) copy-start(bf16[128,2048]{1,0:T(8,128)(2,1)S(1)} %collective-permute-done.2.refs_4_.refs_5_.refs_3_) | copy-start | bytes 1572868
  6.5 13.2 %copy-start.7 = (bf16[128,2048]{1,0:T(8,128)(2,1)S(1)}, bf16[128,2048]{1,0:T(8,128)(2,1)}, u32[]{:S(2)}) copy-start(bf16[128,2048]{1,0:T(8,128)(2,1)} %refs_6_.1) | copy-start | bytes 1572868
  9.4 9.5 %copy-start.5 = (bf16[128,2048]{1,0:T(8,128)(2,1)S(1)}, bf16[128,2048]{1,0:T(8,128)(2,1)}, u32[]{:S(2)}) copy-start(bf16[128,2048]{1,0:T(8,128)(2,1)} %refs_0_.11) | copy-start | bytes 1572868
  9.4 19.1 %all-to-all-start = ((bf16[32,32,128]{2,1,0:T(8,128)(2,1)}), bf16[32,32,128]{2,1,0:T(8,128)(2,1)S(1)}, u32[]{:S(2)}, u32[]{:S(2)}) async-start(bf16[32,32,128]{2,1,0:T(8,128)(2,1)} %bitcast.9), calls=%async_computation | async-start | bytes 524288 | tf_op jit(solution)/shard_map/all_to_all | solution.py:309
  18.9 17.1 %collective-permute-start.3 = (bf16[128,2048]{1,0:T(8,128)(2,1)S(1)}, bf16[128,2048]{1,0:T(8,128)(2,1)S(1)}, u32[]{:S(2)}, u32[]{:S(2)}) collective-permute-start(bf16[128,2048]{1,0:T(8,128)(2,1)S(1)} %copy-done.5), channel_id=1, source_target_pairs={{0,4},{4,0},{1,5},{5,1},{2,6},{6,2},{3,7},{7,3},{8,12},{12,8},{9,1... | collective-permute-start | bytes 1572872 | tf_op jit(solution)/shard_map/ppermute | solution.py:306
  19.6 21.2 %collective-permute-start.4 = (bf16[128,2048]{1,0:T(8,128)(2,1)S(1)}, bf16[128,2048]{1,0:T(8,128)(2,1)S(1)}, u32[]{:S(2)}, u32[]{:S(2)}) collective-permute-start(bf16[128,2048]{1,0:T(8,128)(2,1)S(1)} %copy-done.7), channel_id=1, source_target_pairs={{0,4},{4,0},{1,5},{5,1},{2,6},{6,2},{3,7},{7,3},{8,12},{12,8},{9,1... | collective-permute-start | bytes 1572872 | tf_op jit(solution)/shard_map/ppermute | solution.py:306
  29.3 16.4 %all-to-all-start.1 = ((bf16[32,32,128]{2,1,0:T(8,128)(2,1)}), bf16[32,32,128]{2,1,0:T(8,128)(2,1)S(1)}, u32[]{:S(2)}, u32[]{:S(2)}) async-start(bf16[32,32,128]{2,1,0:T(8,128)(2,1)} %running_sums.2), calls=%async_computation.1 | async-start | bytes 524288 | tf_op jit(solution)/shard_map/all_to_all | solution.py:309
  36.0 0.8 copy-start.6
  40.8 4.9 %copy-start.8 = (bf16[128,2048]{1,0:T(8,128)(2,1)}, bf16[128,2048]{1,0:T(8,128)(2,1)S(1)}, u32[]{:S(2)}) copy-start(bf16[128,2048]{1,0:T(8,128)(2,1)S(1)} %collective-permute-done.4.refs_4_.refs_7_) | copy-start | bytes 1572868
  45.7 3.5 %copy-start.3 = (bf16[32,32,128]{2,1,0:T(8,128)(2,1)}, bf16[32,32,128]{2,1,0:T(8,128)(2,1)S(1)}, u32[]{:S(2)}) copy-start(bf16[32,32,128]{2,1,0:T(8,128)(2,1)S(1)} %all-to-all-done.1) | copy-start | bytes 786436
  80.4 16.2 %all-to-all-start.4 = ((bf16[32,32,128]{2,1,0:T(8,128)(2,1)}), bf16[32,32,128]{2,1,0:T(8,128)(2,1)S(1)}, u32[]{:S(2)}, u32[]{:S(2)}) async-start(bf16[32,32,128]{2,1,0:T(8,128)(2,1)} %running_sums.3), calls=%async_computation.4 | async-start | bytes 524288 | tf_op jit(solution)/shard_map/all_to_all | solution.py:309
  96.6 3.1 %copy-start.2 = (bf16[32,32,128]{2,1,0:T(8,128)(2,1)}, bf16[32,32,128]{2,1,0:T(8,128)(2,1)S(1)}, u32[]{:S(2)}) copy-start(bf16[32,32,128]{2,1,0:T(8,128)(2,1)S(1)} %all-to-all-done.4) | copy-start | bytes 786436
  99.7 6.4 %copy-start.12 = (bf16[128,1024]{1,0:T(8,128)(2,1)S(1)}, bf16[128,1024]{1,0:T(8,128)(2,1)}, u32[]{:S(2)}) copy-start(bf16[128,1024]{1,0:T(8,128)(2,1)} %get-tuple-element.44) | copy-start | bytes 786436
  99.7 19.4 %all-to-all-start.5 = ((bf16[32,16,512]{2,1,0:T(8,128)(2,1)}), bf16[32,16,512]{2,1,0:T(8,128)(2,1)S(1)}, u32[]{:S(2)}, u32[]{:S(2)}) async-start(bf16[32,16,512]{2,1,0:T(8,128)(2,1)} %copies.1), calls=%async_computation.5 | async-start | bytes 1048576 | tf_op jit(solution)/shard_map/all_to_all | solution.py:309
  106.2 6.2 %collective-permute-start.7 = (bf16[128,1024]{1,0:T(8,128)(2,1)S(1)}, bf16[128,1024]{1,0:T(8,128)(2,1)S(1)}, u32[]{:S(2)}, u32[]{:S(2)}) collective-permute-start(bf16[128,1024]{1,0:T(8,128)(2,1)S(1)} %copy-done.12), channel_id=1, source_target_pairs={{0,4},{4,0},{1,5},{5,1},{2,6},{6,2},{3,7},{7,3},{8,12},{12,8},{9,1... | collective-permute-start | bytes 786440 | tf_op jit(solution)/shard_map/ppermute | solution.py:306
  108.2 4.2 %copy-start.9 = (bf16[128,1024]{1,0:T(8,128)(2,1)S(1)}, bf16[128,1024]{1,0:T(8,128)(2,1)}, u32[]{:S(2)}) copy-start(bf16[128,1024]{1,0:T(8,128)(2,1)} %get-tuple-element.43) | copy-start | bytes 786436
  111.8 1.8 %collective-permute-start.5 = (bf16[128,1024]{1,0:T(8,128)(2,1)}, bf16[128,1024]{1,0:T(8,128)(2,1)S(1)}, u32[]{:S(2)}, u32[]{:S(2)}) collective-permute-start(bf16[128,1024]{1,0:T(8,128)(2,1)} %get-tuple-element.40), channel_id=1, source_target_pairs={{0,4},{4,0},{1,5},{5,1},{2,6},{6,2},{3,7},{7,3},{8,12},{12,8},{9,1... | collective-permute-start | bytes 786440 | tf_op jit(solution)/shard_map/ppermute | solution.py:306
  111.9 2.6 %collective-permute-start.6 = (bf16[128,1024]{1,0:T(8,128)(2,1)}, bf16[128,1024]{1,0:T(8,128)(2,1)S(1)}, u32[]{:S(2)}, u32[]{:S(2)}) collective-permute-start(bf16[128,1024]{1,0:T(8,128)(2,1)} %get-tuple-element.42), channel_id=1, source_target_pairs={{0,4},{4,0},{1,5},{5,1},{2,6},{6,2},{3,7},{7,3},{8,12},{12,8},{9,1... | collective-permute-start | bytes 786440 | tf_op jit(solution)/shard_map/ppermute | solution.py:306
  112.4 1.2 copy-start.11
  113.6 1.0 copy-start.10
  119.2 6.2 %collective-permute-start.8 = (f32[8,1024]{1,0:T(8,128)S(1)}, f32[8,1024]{1,0:T(8,128)S(1)}, u32[]{:S(2)}, u32[]{:S(2)}) collective-permute-start(f32[8,1024]{1,0:T(8,128)S(1)} %pad_maximum_fusion), channel_id=1, source_target_pairs={{0,4},{4,0},{1,5},{5,1},{2,6},{6,2},{3,7},{7,3},{8,12},{12,8},{9,1... | collective-permute-start | bytes 98312 | tf_op jit(solution)/shard_map/ppermute | solution.py:306

commit v6 on v5

--- a/solution.py
+++ b/solution.py
@@ -105,21 +105,28 @@
         delta[h] = dot(pair(k_own, k_other, lanes), low, TN).astype(BF16)
 
 
-def inside_kernel(meta, q_own, q_other, k_own, k_other, scaled, inside):
+def inside_kernel(
+    meta, q_own, q_other, k_own, k_other, v_own, v_other, c_own, c_other, scaled,
+    inside, q, k, v, c,
+):
     tok = q_own.shape[0]
     causal = causal_mask(meta, tok)
+    for both, own, other in ((q, q_own, q_other), (k, k_own, k_other), (v, v_own, v_other), (c, c_own, c_other)):
+        both[:tok] = own[...]
+        both[tok:] = other[...]
     for h in range(scaled.shape[1] // DH):
         lanes = lanes_of(h)
-        scores = dot(pair(q_own, q_other, lanes), pair(k_own, k_other, lanes), NT)
+        scores = dot(q[:, lanes], k[:, lanes], NT)
         weights = jnp.where(causal, scores, 0.0).astype(BF16)
         inside[:, lanes] = dot(weights, scaled[:, lanes], NN)
 
 
 def mixed_kernel(
-    meta, scale, q_own, q_other, c_own, c_other, state, inside, mixed, sums, squares, crosses
+    meta, scale, q, c, state, inside, mixed, sums, squares, crosses
 ):
-    tok = q_own.shape[0]
-    spans = 2 * tok // SPAN
+    rows = q.shape[0]
+    tok = rows // 2
+    spans = rows // SPAN
     step = pl.program_id(0)
 
     @pl.when(step == 0)
@@ -130,9 +137,9 @@
     square, cross = squares[...], crosses[...]
     for h in range(state.shape[0]):
         lanes = lanes_of(h)
-        mix = inside[:, lanes] + dot(pair(q_own, q_other, lanes), state[h], NN)
+        mix = inside[:, lanes] + dot(q[:, lanes], state[h], NN)
         mixed[:, lanes] = mix
-        cot = pair(c_own, c_other, lanes).astype(F32)
+        cot = c[:, lanes].astype(F32)
         square = square + mix * mix
         cross = cross + rows_of_members(meta, scale, lanes, spans) * cot * mix
     squares[...] = square
@@ -146,10 +153,11 @@
 
 
 def grads_kernel(
-    full_width, meta, scale, q_own, q_other, c_own, c_other, mixed, sums, grad, delta, turned
+    full_width, meta, scale, q, c, mixed, sums, grad, delta, turned
 ):
-    tok = q_own.shape[0]
-    spans = 2 * tok // SPAN
+    rows = q.shape[0]
+    tok = rows // 2
+    spans = rows // SPAN
 
     @pl.when(pl.program_id(0) == 0)
     def _():
@@ -162,52 +170,56 @@
     inverse, factor = turned[0], turned[1]
     for h in range(delta.shape[0]):
         lanes = lanes_of(h)
-        cot = pair(c_own, c_other, lanes).astype(F32) * inverse
+        cot = c[:, lanes].astype(F32) * inverse
         mix = mixed[:, lanes]
         low = (rows_of_members(meta, scale, lanes, spans) * cot - mix * factor).astype(BF16)
         grad[:, lanes] = low
-        delta[h] = dot(pair(q_own, q_other, lanes), low, TN).astype(BF16)
-
-
-def back_kernel(
-    full_width, meta, q_own, q_other, k_own, k_other, v_own, v_other, c_own, c_other,
-    scaled, grad, state, mixed, sums,
-    query_own, query_other, key_in, value_in, parts,
-):
-    tok = q_own.shape[0]
-    spans = 2 * tok // SPAN
+        delta[h] = dot(q[:, lanes], low, TN).astype(BF16)
+
+
+def query_kernel(meta, k, scaled, grad, state, query_own, query_other):
+    tok = k.shape[0] // 2
+    causal = causal_mask(meta, tok)
+    for h in range(state.shape[0]):
+        lanes = lanes_of(h)
+        g = grad[:, lanes]
+        grad_weights = jnp.where(causal, dot(g, scaled[:, lanes], NT), 0.0).astype(BF16)
+        query_grad = (dot(grad_weights, k[:, lanes], NN) + dot(g, state[h], NT)).astype(BF16)
+        query_own[:, lanes] = query_grad[:tok]
+        query_other[:, lanes] = query_grad[tok:]
+
+
+def back_kernel(full_width, meta, q, k, v, c, scaled, grad, mixed, sums, key_in, value_in, parts):
+    rows = k.shape[0]
+    tok = rows // 2
+    spans = rows // SPAN
     causal = causal_mask(meta, tok)
     totals = head_sums(meta, sums, tok)
     inverse = 1.0 / jnp.sqrt(totals[0:1] / full_width + EPS)
-    inverse = jnp.transpose(jnp.broadcast_to(inverse, (DH, 2 * tok)))
-    for h in range(state.shape[0]):
-        lanes = lanes_of(h)
-        query = pair(q_own, q_other, lanes)
-        key = pair(k_own, k_other, lanes)
-        low = scaled[:, lanes]
-        g = grad[:, lanes]
-        weights = jnp.where(causal, dot(query, key, NT), 0.0).astype(BF16)
-        grad_weights = jnp.where(causal, dot(g, low, NT), 0.0).astype(BF16)
-        query_grad = (dot(grad_weights, key, NN) + dot(g, state[h], NT)).astype(BF16)
-        query_own[:, lanes] = query_grad[:tok]
-        query_other[:, lanes] = query_grad[tok:]
+    inverse = jnp.transpose(jnp.broadcast_to(inverse, (DH, rows)))
+    for h in range(scaled.shape[1] // DH):
+        lanes = lanes_of(h)
+        query, g = q[:, lanes], grad[:, lanes]
+        weights = jnp.where(causal, dot(query, k[:, lanes], NT), 0.0).astype(BF16)
+        grad_weights = jnp.where(causal, dot(g, scaled[:, lanes], NT), 0.0).astype(BF16)
         key_in[:, lanes] = dot(grad_weights, query, TN)
         inner = dot(weights, g, TN)
         value_in[:, lanes] = inner
-        in_part = member_sums(meta, pair(v_own, v_other, lanes).astype(F32) * inner, spans)
-        normed = pair(c_own, c_other, lanes).astype(F32) * (mixed[:, lanes] * inverse)
+        in_part = member_sums(meta, v[:, lanes].astype(F32) * inner, spans)
+        normed = c[:, lanes].astype(F32) * (mixed[:, lanes] * inverse)
         out_part = member_sums(meta, normed, spans)
         parts[:, lanes] = jnp.concatenate([in_part, out_part], axis=0)
 
 
-def copies_kernel(meta, k_own, k_other, v_own, v_other, state, known, copies, parts):
-    tok = k_own.shape[0]
-    spans = 2 * tok // SPAN
+def copies_kernel(meta, k, v, state, known, copies, parts):
+    rows = k.shape[0]
+    tok = rows // 2
+    spans = rows // SPAN
     here = pl.ds(pl.multiple_of(pl.program_id(0) * 2 * MEMBERS, 2 * MEMBERS), 2 * MEMBERS)
     for h in range(state.shape[0]):
         lanes = lanes_of(h)
-        value = pair(v_own, v_other, lanes).astype(F32)
-        across = dot(pair(k_own, k_other, lanes), state[h], NN)
+        value = v[:, lanes].astype(F32)
+        across = dot(k[:, lanes], state[h], NN)
         in_part = member_sums(meta, value * across, spans)
         more = jnp.concatenate([in_part, jnp.zeros_like(in_part)], axis=0)
         parts[here, lanes] = known[:, lanes] + more
@@ -218,17 +230,18 @@
 
 
 def last_kernel(
-    meta, scale, k_own, k_other, scaled, state, key_in, value_in,
+    meta, scale, k, scaled, state, key_in, value_in,
     key_grad_own, key_grad_other, value_grad_own, value_grad_other,
 ):
-    tok = k_own.shape[0]
-    spans = 2 * tok // SPAN
+    rows = k.shape[0]
+    tok = rows // 2
+    spans = rows // SPAN
     for h in range(state.shape[0]):
         lanes = lanes_of(h)
         key_grad = (key_in[:, lanes] + dot(scaled[:, lanes], state[h], NT)).astype(BF16)
         key_grad_own[:, lanes] = key_grad[:tok]
         key_grad_other[:, lanes] = key_grad[tok:]
-        scaled_grad = value_in[:, lanes] + dot(pair(k_own, k_other, lanes), state[h], NN)
+        scaled_grad = value_in[:, lanes] + dot(k[:, lanes], state[h], NN)
         value_grad = (rows_of_members(meta, scale, lanes, spans) * scaled_grad).astype(BF16)
         value_grad_own[:, lanes] = value_grad[:tok]
         value_grad_other[:, lanes] = value_grad[tok:]
@@ -308,11 +321,13 @@
     def scattered(pieces):
         return lax.all_to_all(pieces, "chip", 0, 0, tiled=True)
 
-    def scanned(delta, backward):
+    def scanned(delta, backward, beside=None):
         heads = delta.shape[0]
-        pieces = delta.reshape(chips, heads * DH // chips, DH)
-        sums = scattered(running_sums(scattered(pieces), backward))
-        return sums.reshape(heads, DH, DH)
+        pieces = scattered(delta.reshape(chips, heads * DH // chips, DH))
+        if beside is not None:
+            pieces, beside = lax.optimization_barrier((pieces, beside))
+        state = scattered(running_sums(pieces, backward)).reshape(heads, DH, DH)
+        return state if beside is None else (state, beside)
 
     def side_by_side(core, own, other):
         return jnp.where(
@@ -359,22 +374,26 @@
         q_other = swap(queries_late)
         c_other = swap(cotangent_late)
         state_in = scanned(delta, False)
-        inside = local.call(
+        inside, q, k, v, c = local.call(
             inside_kernel,
             meta,
-            pairs * 2 + [cols(rows)],
-            cols(rows),
-            (slow(queries), slow(q_other), slow(key_vectors), slow(k_other), slow(scaled)),
-            wide,
+            pairs * 4 + [cols(rows)],
+            [cols(rows)] * 5,
+            (
+                slow(queries), slow(q_other), slow(key_vectors), slow(k_other),
+                slow(value_vectors), slow(v_other), slow(cotangent), slow(c_other), slow(scaled),
+            ),
+            [wide] + [low] * 4,
             "inside",
             flops=4 * unit,
         )
+        q, k, v, c = slow(q), slow(k), slow(v), slow(c)
         mixed, sums = local.call(
             mixed_kernel,
             meta,
-            [shared(MEMBERS)] + pairs * 2 + [state(), cols(rows)],
+            [shared(MEMBERS), cols(rows), cols(rows), state(), cols(rows)],
             [cols(rows), local.whole((group, 2, rows))],
-            (slow(out_scale), slow(queries), slow(q_other), slow(cotangent), slow(c_other), fast(state_in), slow(inside)),
+            (slow(out_scale), q, c, fast(state_in), slow(inside)),
             [wide, pltpu.HBM((group, 2, rows), F32)],
             "mixed",
             scratch=[pltpu.VMEM((rows, DH), F32)] * 2,
@@ -384,39 +403,42 @@
         grad, delta_after = local.call(
             functools.partial(grads_kernel, full_width),
             meta,
-            [shared(MEMBERS)] + pairs * 2 + [cols(rows), local.whole((group, 2, rows))],
+            [shared(MEMBERS)] + [cols(rows)] * 3 + [local.whole((group, 2, rows))],
             [cols(rows), state()],
-            (slow(out_scale), slow(queries), slow(q_other), slow(cotangent), slow(c_other), slow(mixed), sums),
+            (slow(out_scale), q, c, slow(mixed), sums),
             [low, sent],
             "grads",
             scratch=[pltpu.VMEM((2, rows, DH), F32)],
             flops=unit,
         )
-        state_after = scanned(delta_after, True)
-        query_own, query_send, key_in, value_in, parts = local.call(
+        query_own, query_send = local.call(
+            query_kernel,
+            meta,
+            [cols(rows)] * 3 + [state()],
+            [cols(tok)] * 2,
+            (k, slow(scaled), slow(grad), slow(state_in)),
+            [half] * 2,
+            "query",
+            flops=5 * unit,
+        )
+        state_after, query_own = scanned(delta_after, True, query_own)
+        key_in, value_in, parts = local.call(
             functools.partial(back_kernel, full_width),
             meta,
-            pairs * 4 + [cols(rows), cols(rows), state(), cols(rows), local.whole((group, 2, rows))],
-            [cols(tok), cols(tok), cols(rows), cols(rows), cols(2 * MEMBERS)],
-            (
-                slow(queries), slow(q_other), slow(key_vectors), slow(k_other),
-                slow(value_vectors), slow(v_other), slow(cotangent), slow(c_other),
-                slow(scaled), slow(grad), slow(state_in), slow(mixed), sums,
-            ),
-            [half, half, wide, wide, part],
+            [cols(rows)] * 7 + [local.whole((group, 2, rows))],
+            [cols(rows), cols(rows), cols(2 * MEMBERS)],
+            (q, k, v, c, slow(scaled), slow(grad), slow(mixed), sums),
+            [wide, wide, part],
             "back",
-            flops=11 * unit,
+            flops=8 * unit,
         )
         query_grad = side_by_side(core, query_own, swap(query_send))
         copies = local.call(
             copies_kernel,
             meta,
-            pairs * 2 + [state(), cols(2 * MEMBERS)],
+            [cols(rows), cols(rows), state(), cols(2 * MEMBERS)],
             local.whole(packed),
-            (
-                slow(key_vectors), slow(k_other), slow(value_vectors), slow(v_other),
-                fast(state_after), slow(parts),
-            ),
+            (k, v, fast(state_after), slow(parts)),
             pltpu.HBM(packed, BF16),
             "copies",
             scratch=[pltpu.VMEM(packed[1:], F32)],
@@ -426,12 +448,9 @@
         key_own, key_send, value_own, value_send = local.call(
             last_kernel,
             meta,
-            [shared(MEMBERS)] + pairs + [cols(rows), state(), cols(rows), cols(rows)],
+            [shared(MEMBERS), cols(rows), cols(rows), state(), cols(rows), cols(rows)],
             [cols(tok)] * 4,
-            (
-                slow(in_scale), slow(key_vectors), slow(k_other), slow(scaled),
-                slow(state_after), slow(key_in), slow(value_in),
-            ),
+            (slow(in_scale), k, slow(scaled), slow(state_after), slow(key_in), slow(value_in)),
             [half] * 4,
             "last",
             flops=2 * unit,

time: 127 us -> 126 us (level)
  blocking collectives: 26.9 us -> 13 us
  waiting for transfers between devices: 23.7 us -> 29.5 us
  starting transfers between devices: 41.7 us -> 46 us
  Pallas kernels: 28.7 us -> 31.9 us
    all_to_all x1 -> x0, blocking collectives: 14 us -> none  [scattered(): return lax.all_to_all(pieces, 'chip', 0, 0, tiled=True)]
    all_to_all x4 -> x5, waiting for transfers between devices: 20.5 us -> 26.3 us  [scattered(): return lax.all_to_all(pieces, 'chip', 0, 0, tiled=True)]
    all_to_all x4 -> x5, starting transfers between devices: 29.1 us -> 33.4 us  [scattered(): return lax.all_to_all(pieces, 'chip', 0, 0, tiled=True)]
    pallas_call x7 -> x8, Pallas kernels: 27.2 us -> 30.4 us  [call(): pl.pallas_call(with_meta(body), grid_spec=pltpu.PrefetchScalarGridSpec(nu...]
  transfers between devices with their start and end apart: 13 -> 14, of which waited for: 7 -> 8; matrix products, arithmetic and copies ran while one was open for 2% -> 2% of each run, Pallas kernels for 12% -> 15%
where the time goes in v6:
time: 126 us
  starting transfers between devices  46 us (37%)
  Pallas kernels  31.9 us (25%)
  waiting for transfers between devices  29.5 us (23%)
  blocking collectives  13 us (10%)
  other arithmetic  2.85 us (2%)
  local copies, waits for them, and re-layouts  1.66 us (1%)
    all_to_all x5, starting transfers between devices, scattered(): return lax.all_to_all(pieces, 'chip', 0, 0, tiled=True)  33.4 us
    pallas_call x8, Pallas kernels, call(): pl.pallas_call(with_meta(body), grid_spec=pltpu.PrefetchScalarGridSpec(nu...  30.4 us
    all_to_all x5, waiting for transfers between devices, scattered(): return lax.all_to_all(pieces, 'chip', 0, 0, tiled=True)  26.3 us
    all_to_all x1, blocking collectives, shards(): sums = lax.all_to_all(sums, ('core', 'head'), 0, 0, tiled=True)  13 us
    ppermute x9, starting transfers between devices, swap(): return lax.ppermute(x, 'core', [(0, 1), (1, 0)])  12.6 us
    ppermute x9, waiting for transfers between devices, swap(): return lax.ppermute(x, 'core', [(0, 1), (1, 0)])  3.17 us
    select_n x4, other arithmetic, side_by_side(): jnp.where(core == 0, jnp.concatenate([own, other], axis=1), jnp.concatena...  2.77 us
  transfers between devices with their start and end apart: 14, of which 8 were waited for; matrix products, arithmetic and copies ran while one was open for 2% of the time, Pallas kernels for 15%

profile of v6, /device:TPU:1, one launch (start us, length us, event | category | flops | bytes accessed | tf_op | source)
XLA Modules:
  0.0 125.7 jit_solution(7792627443452036711)
XLA Ops:
  0.6 3.3 %collective-permute-start.1 = (bf16[128,2048]{1,0:T(8,128)(2,1)}, bf16[128,2048]{1,0:T(8,128)(2,1)S(1)}, u32[]{:S(2)}, u32[]{:S(2)}) collective-permute-start(bf16[128,2048]{1,0:T(8,128)(2,1)} %refs_2_.1), channel_id=1, source_target_pairs={{0,4},{4,0},{1,5},{5,1},{2,6},{6,2},{3,7},{7,3},{8,12},{12,8},{9,1... | collective-permute-start | bytes 1572872 | tf_op jit(solution)/shard_map/ppermute | solution.py:319
  4.0 0.1 collective-permute-start.2
  4.1 0.4 collective-permute-start
  4.5 0.0 copy-start.4
  4.5 2.0 %collective-permute-done.other_ids = s32[8]{0:T(128)S(1)} collective-permute-done((s32[8]{0:T(128)}, s32[8]{0:T(128)S(1)}, u32[]{:S(2)}, u32[]{:S(2)}) %collective-permute-start) | collective-permute-done | bytes 64 | tf_op jit(solution)/shard_map/ppermute | solution.py:319
  6.5 0.0 collective-permute-done.1.refs_2_.refs_3_
  6.5 0.0 copy-start.2
  6.5 0.0 collective-permute-done.2.refs_4_.refs_5_
  6.5 0.0 copy-start.3
  6.5 0.0 copy-done.4
  6.5 0.0 copy-start.6
  6.5 2.9 %states.1 = (bf16[256,1024]{1,0:T(8,128)(2,1)}, bf16[8,128,128]{2,1,0:T(8,128)(2,1)}) custom-call(s32[1]{0:T(128)} %bitcast.place, s32[8]{0:T(128)S(1)} %copy-done.4, s32[8]{0:T(128)S(1)} %collective-permute-done.other_ids, f32[4,2048]{1,0:T(4,128)} %refs_0_.9, bf16[128,2048]{1,0:T(8,128)(2,1)} %refs_2_.1, ...), custom_call_target="tpu_custom_call" | custom-call | flops 67108864 | bytes 4259840 | tf_op jit(solution)/shard_map/states/pallas_call | solution.py:281
  9.4 0.0 copy-done.2
  9.4 0.0 copy-done.3
  9.4 0.0 copy-start.5
  9.4 9.4 %all-to-all-start = ((bf16[32,32,128]{2,1,0:T(8,128)(2,1)}), bf16[32,32,128]{2,1,0:T(8,128)(2,1)S(1)}, u32[]{:S(2)}, u32[]{:S(2)}) async-start(bf16[32,32,128]{2,1,0:T(8,128)(2,1)} %bitcast.9), calls=%async_computation | async-start | bytes 524288 | tf_op jit(solution)/shard_map/all_to_all | solution.py:322
  18.9 0.0 copy-done.5
  18.9 0.7 collective-permute-start.3
  19.6 0.0 copy-done.6
  19.6 0.1 collective-permute-start.4
  19.8 8.8 %all-to-all-done.pieces = bf16[32,32,128]{2,1,0:T(8,128)(2,1)S(1)} async-done(((bf16[32,32,128]{2,1,0:T(8,128)(2,1)}), bf16[32,32,128]{2,1,0:T(8,128)(2,1)S(1)}, u32[]{:S(2)}, u32[]{:S(2)}) %all-to-all-start) | async-done | bytes 262176 | tf_op jit(solution)/shard_map/all_to_all | solution.py:322
  28.6 0.7 running_sums.2
  29.3 6.7 %all-to-all-start.1 = ((bf16[32,32,128]{2,1,0:T(8,128)(2,1)}), bf16[32,32,128]{2,1,0:T(8,128)(2,1)S(1)}, u32[]{:S(2)}, u32[]{:S(2)}) async-start(bf16[32,32,128]{2,1,0:T(8,128)(2,1)} %running_sums.2), calls=%async_computation.1 | async-start | bytes 524288 | tf_op jit(solution)/shard_map/all_to_all | solution.py:322
  36.0 0.0 collective-permute-done.3.refs_1_
  36.0 0.0 copy-start.7
  36.0 0.0 collective-permute-done.4.refs_7_
  36.1 0.0 copy-start.8
  36.1 0.8 copy-done.7
  36.8 0.2 copy-done.8
  37.0 4.5 %inside.1 = (f32[256,1024]{1,0:T(8,128)}, bf16[256,1024]{1,0:T(8,128)(2,1)}, bf16[256,1024]{1,0:T(8,128)(2,1)}, bf16[256,1024]{1,0:T(8,128)(2,1)}, bf16[256,1024]{1,0:T(8,128)(2,1)}) custom-call(s32[1]{0:T(128)} %bitcast.place, s32[8]{0:T(128)S(1)} %copy-done.4, s32[8]{0:T(128)S(1)} %collective-permute-done.other_ids, bf16[128,2048]{1,0:T(8,128)(2,1)} %refs_0_.6, ...), custom_call_target="tpu_custom_call" | custom-call | flops 268435456 | bytes 9437184 | tf_op jit(solution)/shard_map/inside/pallas_call | solution.py:281
  41.5 4.2 %all-to-all-done.1 = bf16[32,32,128]{2,1,0:T(8,128)(2,1)S(1)} async-done(((bf16[32,32,128]{2,1,0:T(8,128)(2,1)}), bf16[32,32,128]{2,1,0:T(8,128)(2,1)S(1)}, u32[]{:S(2)}, u32[]{:S(2)}) %all-to-all-start.1) | async-done | bytes 262176 | tf_op jit(solution)/shard_map/all_to_all | solution.py:322
  45.7 3.3 %mixed.1 = (f32[256,1024]{1,0:T(8,128)}, f32[8,2,256]{2,1,0:T(2,128)}) custom-call(s32[1]{0:T(128)} %bitcast.place, s32[8]{0:T(128)S(1)} %copy-done.4, s32[8]{0:T(128)S(1)} %collective-permute-done.other_ids, f32[4,2048]{1,0:T(4,128)} %refs_0_.8, bf16[256,1024]{1,0:T(8,128)(2,1)} %get-tuple-element.40.refs_1_.refs_0_, ...), custom_call_target="tpu_custom_call" | custom-call | flops 67108864 | bytes 4784128 | tf_op jit(solution)/shard_map/mixed/pallas_call | solution.py:281
  49.0 0.0 copy-done
  49.0 13.0 %all_to_all.30.refs_4_.refs_7_ = f32[8,2,256]{2,1,0:T(2,128)S(1)} all-to-all(f32[8,2,256]{2,1,0:T(2,128)} %get-tuple-element.45), channel_id=1, replica_groups=mesh['chip'=32,'core'=2,'head'=4] {'core','head'}, dimensions={0} | all-to-all | bytes 32768 | tf_op jit(solution)/shard_map/all_to_all | solution.py:402
  62.0 3.4 %grads.1 = (bf16[256,1024]{1,0:T(8,128)(2,1)}, bf16[8,128,128]{2,1,0:T(8,128)(2,1)}) custom-call(s32[1]{0:T(128)} %bitcast.place, s32[8]{0:T(128)S(1)} %copy-done.4, s32[8]{0:T(128)S(1)} %collective-permute-done.other_ids, f32[4,2048]{1,0:T(4,128)} %refs_0_.8, bf16[256,1024]{1,0:T(8,128)(2,1)} %get-tuple-element.40.refs_1_.refs_0_, ...), custom_call_target="tpu_custom_call" | custom-call | flops 67108864 | bytes 4292608 | tf_op jit(solution)/shard_map/grads/pallas_call | solution.py:281
  65.4 4.3 %all-to-all-start.3 = ((bf16[32,32,128]{2,1,0:T(8,128)(2,1)}), bf16[32,32,128]{2,1,0:T(8,128)(2,1)S(1)}, u32[]{:S(2)}, u32[]{:S(2)}) async-start(bf16[32,32,128]{2,1,0:T(8,128)(2,1)} %bitcast.10), calls=%async_computation.3 | async-start | bytes 524288 | tf_op jit(solution)/shard_map/all_to_all | solution.py:322
  69.6 3.7 %query.1 = (bf16[128,1024]{1,0:T(8,128)(2,1)}, bf16[128,1024]{1,0:T(8,128)(2,1)}) custom-call(s32[1]{0:T(128)} %bitcast.place, s32[8]{0:T(128)S(1)} %copy-done.4, s32[8]{0:T(128)S(1)} %collective-permute-done.other_ids, bf16[256,1024]{1,0:T(8,128)(2,1)} %get-tuple-element.38.refs_0_.refs_1_, ...), custom_call_target="tpu_custom_call" | custom-call | flops 335544320 | bytes 3670016 | tf_op jit(solution)/shard_map/query/pallas_call | solution.py:281
  73.4 6.0 %all-to-all-done.3.pieces = bf16[32,32,128]{2,1,0:T(8,128)(2,1)S(1)} async-done(((bf16[32,32,128]{2,1,0:T(8,128)(2,1)}), bf16[32,32,128]{2,1,0:T(8,128)(2,1)S(1)}, u32[]{:S(2)}, u32[]{:S(2)}) %all-to-all-start.3) | async-done | bytes 262176 | tf_op jit(solution)/shard_map/all_to_all | solution.py:322
  79.3 0.7 running_sums.3
  80.1 6.5 %all-to-all-start.4 = ((bf16[32,32,128]{2,1,0:T(8,128)(2,1)}), bf16[32,32,128]{2,1,0:T(8,128)(2,1)S(1)}, u32[]{:S(2)}, u32[]{:S(2)}) async-start(bf16[32,32,128]{2,1,0:T(8,128)(2,1)} %running_sums.3), calls=%async_computation.4 | async-start | bytes 524288 | tf_op jit(solution)/shard_map/all_to_all | solution.py:322
  86.6 6.0 %back.1 = (f32[256,1024]{1,0:T(8,128)}, f32[256,1024]{1,0:T(8,128)}, f32[8,1024]{1,0:T(8,128)}) custom-call(s32[1]{0:T(128)} %bitcast.place, s32[8]{0:T(128)S(1)} %copy-done.4, s32[8]{0:T(128)S(1)} %collective-permute-done.other_ids, bf16[256,1024]{1,0:T(8,128)(2,1)} %get-tuple-element.40.refs_1_.refs_0_, ...), custom_call_target="tpu_custom_call" | custom-call | flops 536870912 | bytes 8421376 | tf_op jit(solution)/shard_map/back/pallas_call | solution.py:281
  92.6 3.7 %all-to-all-done.4 = bf16[32,32,128]{2,1,0:T(8,128)(2,1)S(1)} async-done(((bf16[32,32,128]{2,1,0:T(8,128)(2,1)}), bf16[32,32,128]{2,1,0:T(8,128)(2,1)S(1)}, u32[]{:S(2)}, u32[]{:S(2)}) %all-to-all-start.4) | async-done | bytes 262176 | tf_op jit(solution)/shard_map/all_to_all | solution.py:322
  96.3 3.0 %copies.1 = bf16[32,16,512]{2,1,0:T(8,128)(2,1)} custom-call(s32[1]{0:T(128)} %bitcast.place, s32[8]{0:T(128)S(1)} %copy-done.4, s32[8]{0:T(128)S(1)} %collective-permute-done.other_ids, bf16[256,1024]{1,0:T(8,128)(2,1)} %get-tuple-element.38.refs_0_.refs_1_, bf16[256,1024]{1,0:T(8,128)(2,1)} %get-tuple-element.39.refs_2_.refs_1_, ...), custom_call_target="tpu_custom_call" | custom-call | flops 67108864 | bytes 2686976 | tf_op jit(solution)/shard_map/copies/pallas_call | solution.py:281
  99.3 0.0 copy-done.1
  99.3 6.4 %all-to-all-start.5 = ((bf16[32,16,512]{2,1,0:T(8,128)(2,1)}), bf16[32,16,512]{2,1,0:T(8,128)(2,1)S(1)}, u32[]{:S(2)}, u32[]{:S(2)}) async-start(bf16[32,16,512]{2,1,0:T(8,128)(2,1)} %copies.1), calls=%async_computation.5 | async-start | bytes 1048576 | tf_op jit(solution)/shard_map/all_to_all | solution.py:322
  105.7 0.0 copy-done.12
  105.7 1.9 %collective-permute-start.7 = (bf16[128,1024]{1,0:T(8,128)(2,1)S(1)}, bf16[128,1024]{1,0:T(8,128)(2,1)S(1)}, u32[]{:S(2)}, u32[]{:S(2)}) collective-permute-start(bf16[128,1024]{1,0:T(8,128)(2,1)S(1)} %copy-done.12), channel_id=1, source_target_pairs={{0,4},{4,0},{1,5},{5,1},{2,6},{6,2},{3,7},{7,3},{8,12},{12,8},{9,1... | collective-permute-start | bytes 786440 | tf_op jit(solution)/shard_map/ppermute | solution.py:319
  107.7 3.6 %last.1 = (bf16[128,1024]{1,0:T(8,128)(2,1)}, bf16[128,1024]{1,0:T(8,128)(2,1)}, bf16[128,1024]{1,0:T(8,128)(2,1)}, bf16[128,1024]{1,0:T(8,128)(2,1)}) custom-call(s32[1]{0:T(128)} %bitcast.place, s32[8]{0:T(128)S(1)} %copy-done.4, s32[8]{0:T(128)S(1)} %collective-permute-done.other_ids, f32[4,2048]{1,0:T(4,128)} %refs_0_.9, ...), custom_call_target="tpu_custom_call" | custom-call | flops 134217728 | bytes 6881280 | tf_op jit(solution)/shard_map/last/pallas_call | solution.py:281
  111.3 0.1 collective-permute-start.5
  111.4 0.5 collective-permute-start.6
  111.9 0.0 collective-permute-done.7
  111.9 0.0 copy-done.9
  111.9 0.9 maximum_select_fusion.2
  112.8 0.3 collective-permute-done.5
  113.1 0.0 copy-done.11
  113.1 0.9 maximum_select_fusion
  114.0 0.0 collective-permute-done.6
  114.0 0.0 copy-done.10
  114.1 0.9 maximum_select_fusion.1
  115.0 3.7 %all-to-all-done.5 = bf16[32,16,512]{2,1,0:T(8,128)(2,1)S(1)} async-done(((bf16[32,16,512]{2,1,0:T(8,128)(2,1)}), bf16[32,16,512]{2,1,0:T(8,128)(2,1)S(1)}, u32[]{:S(2)}, u32[]{:S(2)}) %all-to-all-start.5) | async-done | bytes 524320 | tf_op jit(solution)/shard_map/all_to_all | solution.py:322
  118.6 0.1 convert_reduce_fusion
  118.8 5.4 %collective-permute-start.8 = (f32[8,1024]{1,0:T(8,128)S(1)}, f32[8,1024]{1,0:T(8,128)S(1)}, u32[]{:S(2)}, u32[]{:S(2)}) collective-permute-start(f32[8,1024]{1,0:T(8,128)S(1)} %pad_maximum_fusion), channel_id=1, source_target_pairs={{0,4},{4,0},{1,5},{5,1},{2,6},{6,2},{3,7},{7,3},{8,12},{12,8},{9,1... | collective-permute-start | bytes 98312 | tf_op jit(solution)/shard_map/ppermute | solution.py:319
  124.2 0.9 collective-permute-done.8
  125.1 0.6 fusion
  (9 shorter events, 0.0 us)
Async XLA Ops:
  0.6 5.8 %collective-permute-start.1 = (bf16[128,2048]{1,0:T(8,128)(2,1)}, bf16[128,2048]{1,0:T(8,128)(2,1)S(1)}, u32[]{:S(2)}, u32[]{:S(2)}) collective-permute-start(bf16[128,2048]{1,0:T(8,128)(2,1)} %refs_2_.1), channel_id=1, source_target_pairs={{0,4},{4,0},{1,5},{5,1},{2,6},{6,2},{3,7},{7,3},{8,12},{12,8},{9,1... | collective-permute-start | bytes 1572872 | tf_op jit(solution)/shard_map/ppermute | solution.py:319
  4.0 2.5 %collective-permute-start.2 = (bf16[128,2048]{1,0:T(8,128)(2,1)}, bf16[128,2048]{1,0:T(8,128)(2,1)S(1)}, u32[]{:S(2)}, u32[]{:S(2)}) collective-permute-start(bf16[128,2048]{1,0:T(8,128)(2,1)} %refs_4_.1), channel_id=1, source_target_pairs={{0,4},{4,0},{1,5},{5,1},{2,6},{6,2},{3,7},{7,3},{8,12},{12,8},{9,1... | collective-permute-start | bytes 1572872 | tf_op jit(solution)/shard_map/ppermute | solution.py:319
  4.1 2.4 %collective-permute-start = (s32[8]{0:T(128)}, s32[8]{0:T(128)S(1)}, u32[]{:S(2)}, u32[]{:S(2)}) collective-permute-start(s32[8]{0:T(128)} %own_ids.15), channel_id=1, source_target_pairs={{0,4},{4,0},{1,5},{5,1},{2,6},{6,2},{3,7},{7,3},{8,12},{12,8},{9,1... | collective-permute-start | bytes 104 | tf_op jit(solution)/shard_map/ppermute | solution.py:319
  4.5 2.0 %copy-start.4 = (s32[8]{0:T(128)S(1)}, s32[8]{0:T(128)}, u32[]{:S(2)}) copy-start(s32[8]{0:T(128)} %own_ids.15) | copy-start | bytes 100
  6.5 3.0 %copy-start.2 = (bf16[128,2048]{1,0:T(8,128)(2,1)}, bf16[128,2048]{1,0:T(8,128)(2,1)S(1)}, u32[]{:S(2)}) copy-start(bf16[128,2048]{1,0:T(8,128)(2,1)S(1)} %collective-permute-done.1.refs_2_.refs_3_) | copy-start | bytes 1572868
  6.5 3.0 %copy-start.3 = (bf16[128,2048]{1,0:T(8,128)(2,1)}, bf16[128,2048]{1,0:T(8,128)(2,1)S(1)}, u32[]{:S(2)}) copy-start(bf16[128,2048]{1,0:T(8,128)(2,1)S(1)} %collective-permute-done.2.refs_4_.refs_5_) | copy-start | bytes 1572868
  6.5 13.2 %copy-start.6 = (bf16[128,2048]{1,0:T(8,128)(2,1)S(1)}, bf16[128,2048]{1,0:T(8,128)(2,1)}, u32[]{:S(2)}) copy-start(bf16[128,2048]{1,0:T(8,128)(2,1)} %refs_6_.1) | copy-start | bytes 1572868
  9.4 9.5 %copy-start.5 = (bf16[128,2048]{1,0:T(8,128)(2,1)S(1)}, bf16[128,2048]{1,0:T(8,128)(2,1)}, u32[]{:S(2)}) copy-start(bf16[128,2048]{1,0:T(8,128)(2,1)} %refs_0_.6) | copy-start | bytes 1572868
  9.4 19.1 %all-to-all-start = ((bf16[32,32,128]{2,1,0:T(8,128)(2,1)}), bf16[32,32,128]{2,1,0:T(8,128)(2,1)S(1)}, u32[]{:S(2)}, u32[]{:S(2)}) async-start(bf16[32,32,128]{2,1,0:T(8,128)(2,1)} %bitcast.9), calls=%async_computation | async-start | bytes 524288 | tf_op jit(solution)/shard_map/all_to_all | solution.py:322
  18.9 17.1 %collective-permute-start.3 = (bf16[128,2048]{1,0:T(8,128)(2,1)S(1)}, bf16[128,2048]{1,0:T(8,128)(2,1)S(1)}, u32[]{:S(2)}, u32[]{:S(2)}) collective-permute-start(bf16[128,2048]{1,0:T(8,128)(2,1)S(1)} %copy-done.5), channel_id=1, source_target_pairs={{0,4},{4,0},{1,5},{5,1},{2,6},{6,2},{3,7},{7,3},{8,12},{12,8},{9,1... | collective-permute-start | bytes 1572872 | tf_op jit(solution)/shard_map/ppermute | solution.py:319
  19.6 16.4 %collective-permute-start.4 = (bf16[128,2048]{1,0:T(8,128)(2,1)S(1)}, bf16[128,2048]{1,0:T(8,128)(2,1)S(1)}, u32[]{:S(2)}, u32[]{:S(2)}) collective-permute-start(bf16[128,2048]{1,0:T(8,128)(2,1)S(1)} %copy-done.6), channel_id=1, source_target_pairs={{0,4},{4,0},{1,5},{5,1},{2,6},{6,2},{3,7},{7,3},{8,12},{12,8},{9,1... | collective-permute-start | bytes 1572872 | tf_op jit(solution)/shard_map/ppermute | solution.py:319
  29.3 16.4 %all-to-all-start.1 = ((bf16[32,32,128]{2,1,0:T(8,128)(2,1)}), bf16[32,32,128]{2,1,0:T(8,128)(2,1)S(1)}, u32[]{:S(2)}, u32[]{:S(2)}) async-start(bf16[32,32,128]{2,1,0:T(8,128)(2,1)} %running_sums.2), calls=%async_computation.1 | async-start | bytes 524288 | tf_op jit(solution)/shard_map/all_to_all | solution.py:322
  36.0 0.8 copy-start.7
  36.1 1.0 copy-start.8
  45.7 3.3 %copy-start = (bf16[32,32,128]{2,1,0:T(8,128)(2,1)}, bf16[32,32,128]{2,1,0:T(8,128)(2,1)S(1)}, u32[]{:S(2)}) copy-start(bf16[32,32,128]{2,1,0:T(8,128)(2,1)S(1)} %all-to-all-done.1) | copy-start | bytes 786436
  65.4 14.0 %all-to-all-start.3 = ((bf16[32,32,128]{2,1,0:T(8,128)(2,1)}), bf16[32,32,128]{2,1,0:T(8,128)(2,1)S(1)}, u32[]{:S(2)}, u32[]{:S(2)}) async-start(bf16[32,32,128]{2,1,0:T(8,128)(2,1)} %bitcast.10), calls=%async_computation.3 | async-start | bytes 524288 | tf_op jit(solution)/shard_map/all_to_all | solution.py:322
  80.1 16.2 %all-to-all-start.4 = ((bf16[32,32,128]{2,1,0:T(8,128)(2,1)}), bf16[32,32,128]{2,1,0:T(8,128)(2,1)S(1)}, u32[]{:S(2)}, u32[]{:S(2)}) async-start(bf16[32,32,128]{2,1,0:T(8,128)(2,1)} %running_sums.3), calls=%async_computation.4 | async-start | bytes 524288 | tf_op jit(solution)/shard_map/all_to_all | solution.py:322
  96.3 3.0 %copy-start.1 = (bf16[32,32,128]{2,1,0:T(8,128)(2,1)}, bf16[32,32,128]{2,1,0:T(8,128)(2,1)S(1)}, u32[]{:S(2)}) copy-start(bf16[32,32,128]{2,1,0:T(8,128)(2,1)S(1)} %all-to-all-done.4) | copy-start | bytes 786436
  99.3 6.4 %copy-start.12 = (bf16[128,1024]{1,0:T(8,128)(2,1)S(1)}, bf16[128,1024]{1,0:T(8,128)(2,1)}, u32[]{:S(2)}) copy-start(bf16[128,1024]{1,0:T(8,128)(2,1)} %get-tuple-element.58) | copy-start | bytes 786436
  99.3 19.3 %all-to-all-start.5 = ((bf16[32,16,512]{2,1,0:T(8,128)(2,1)}), bf16[32,16,512]{2,1,0:T(8,128)(2,1)S(1)}, u32[]{:S(2)}, u32[]{:S(2)}) async-start(bf16[32,16,512]{2,1,0:T(8,128)(2,1)} %copies.1), calls=%async_computation.5 | async-start | bytes 1048576 | tf_op jit(solution)/shard_map/all_to_all | solution.py:322
  105.7 6.1 %collective-permute-start.7 = (bf16[128,1024]{1,0:T(8,128)(2,1)S(1)}, bf16[128,1024]{1,0:T(8,128)(2,1)S(1)}, u32[]{:S(2)}, u32[]{:S(2)}) collective-permute-start(bf16[128,1024]{1,0:T(8,128)(2,1)S(1)} %copy-done.12), channel_id=1, source_target_pairs={{0,4},{4,0},{1,5},{5,1},{2,6},{6,2},{3,7},{7,3},{8,12},{12,8},{9,1... | collective-permute-start | bytes 786440 | tf_op jit(solution)/shard_map/ppermute | solution.py:319
  107.7 4.2 %copy-start.9 = (bf16[128,1024]{1,0:T(8,128)(2,1)S(1)}, bf16[128,1024]{1,0:T(8,128)(2,1)}, u32[]{:S(2)}) copy-start(bf16[128,1024]{1,0:T(8,128)(2,1)} %get-tuple-element.57) | copy-start | bytes 786436
  111.3 1.8 %collective-permute-start.5 = (bf16[128,1024]{1,0:T(8,128)(2,1)}, bf16[128,1024]{1,0:T(8,128)(2,1)S(1)}, u32[]{:S(2)}, u32[]{:S(2)}) collective-permute-start(bf16[128,1024]{1,0:T(8,128)(2,1)} %get-tuple-element.54), channel_id=1, source_target_pairs={{0,4},{4,0},{1,5},{5,1},{2,6},{6,2},{3,7},{7,3},{8,12},{12,8},{9,1... | collective-permute-start | bytes 786440 | tf_op jit(solution)/shard_map/ppermute | solution.py:319
  111.4 1.7 %copy-start.11 = (bf16[128,1024]{1,0:T(8,128)(2,1)S(1)}, bf16[128,1024]{1,0:T(8,128)(2,1)}, u32[]{:S(2)}) copy-start(bf16[128,1024]{1,0:T(8,128)(2,1)} %get-tuple-element.53) | copy-start | bytes 786436
  111.4 2.6 %collective-permute-start.6 = (bf16[128,1024]{1,0:T(8,128)(2,1)}, bf16[128,1024]{1,0:T(8,128)(2,1)S(1)}, u32[]{:S(2)}, u32[]{:S(2)}) collective-permute-start(bf16[128,1024]{1,0:T(8,128)(2,1)} %get-tuple-element.56), channel_id=1, source_target_pairs={{0,4},{4,0},{1,5},{5,1},{2,6},{6,2},{3,7},{7,3},{8,12},{12,8},{9,1... | collective-permute-start | bytes 786440 | tf_op jit(solution)/shard_map/ppermute | solution.py:319
  113.1 1.0 copy-start.10
  118.8 6.3 %collective-permute-start.8 = (f32[8,1024]{1,0:T(8,128)S(1)}, f32[8,1024]{1,0:T(8,128)S(1)}, u32[]{:S(2)}, u32[]{:S(2)}) collective-permute-start(f32[8,1024]{1,0:T(8,128)S(1)} %pad_maximum_fusion), channel_id=1, source_target_pairs={{0,4},{4,0},{1,5},{5,1},{2,6},{6,2},{3,7},{7,3},{8,12},{12,8},{9,1... | collective-permute-start | bytes 98312 | tf_op jit(solution)/shard_map/ppermute | solution.py:319

commit v7 on v6

--- a/solution.py
+++ b/solution.py
@@ -13,6 +13,7 @@
 EPS = 1e-06
 CORES = 2
 STEP_HEADS = 4
+LANE_GROUPS = 4
 VMEM_BYTES = 24 * 2**20
 F32 = jnp.float32
 BF16 = jnp.bfloat16
@@ -189,14 +190,23 @@
         query_other[:, lanes] = query_grad[tok:]
 
 
-def back_kernel(full_width, meta, q, k, v, c, scaled, grad, mixed, sums, key_in, value_in, parts):
+def outs_kernel(full_width, meta, c, mixed, sums, out_part):
+    rows = c.shape[0]
+    spans = rows // SPAN
+    totals = head_sums(meta, sums, rows // 2)
+    inverse = 1.0 / jnp.sqrt(totals[0:1] / full_width + EPS)
+    inverse = jnp.transpose(jnp.broadcast_to(inverse, (DH, rows)))
+    for h in range(mixed.shape[1] // DH):
+        lanes = lanes_of(h)
+        normed = c[:, lanes].astype(F32) * (mixed[:, lanes] * inverse)
+        out_part[:, lanes] = member_sums(meta, normed, spans)
+
+
+def back_kernel(meta, q, k, v, scaled, grad, key_in, value_in, in_part):
     rows = k.shape[0]
     tok = rows // 2
     spans = rows // SPAN
     causal = causal_mask(meta, tok)
-    totals = head_sums(meta, sums, tok)
-    inverse = 1.0 / jnp.sqrt(totals[0:1] / full_width + EPS)
-    inverse = jnp.transpose(jnp.broadcast_to(inverse, (DH, rows)))
     for h in range(scaled.shape[1] // DH):
         lanes = lanes_of(h)
         query, g = q[:, lanes], grad[:, lanes]
@@ -205,28 +215,30 @@
         key_in[:, lanes] = dot(grad_weights, query, TN)
         inner = dot(weights, g, TN)
         value_in[:, lanes] = inner
-        in_part = member_sums(meta, v[:, lanes].astype(F32) * inner, spans)
-        normed = c[:, lanes].astype(F32) * (mixed[:, lanes] * inverse)
-        out_part = member_sums(meta, normed, spans)
-        parts[:, lanes] = jnp.concatenate([in_part, out_part], axis=0)
-
-
-def copies_kernel(meta, k, v, state, known, copies, parts):
-    rows = k.shape[0]
-    tok = rows // 2
-    spans = rows // SPAN
-    here = pl.ds(pl.multiple_of(pl.program_id(0) * 2 * MEMBERS, 2 * MEMBERS), 2 * MEMBERS)
+        in_part[:, lanes] = member_sums(meta, v[:, lanes].astype(F32) * inner, spans)
+
+
+def copies_kernel(meta, k, v, state, known, extra, copies, parts):
+    spans = k.shape[0] // SPAN
+    step = pl.program_id(0)
+    found = []
     for h in range(state.shape[0]):
         lanes = lanes_of(h)
         value = v[:, lanes].astype(F32)
         across = dot(k[:, lanes], state[h], NN)
-        in_part = member_sums(meta, value * across, spans)
-        more = jnp.concatenate([in_part, jnp.zeros_like(in_part)], axis=0)
-        parts[here, lanes] = known[:, lanes] + more
-
-    @pl.when(pl.program_id(0) == pl.num_programs(0) - 1)
+        found.append(known[:, lanes] + member_sums(meta, value * across, spans))
+    per_row = parts.shape[1] // DH
+    rows = [
+        jnp.concatenate(found[at : at + per_row], axis=1) for at in range(0, len(found), per_row)
+    ]
+    rows = jnp.concatenate(rows, axis=0)
+    count = rows.shape[0]
+    parts[pl.ds(pl.multiple_of(step * count, count), count)] = rows
+
+    @pl.when(step == pl.num_programs(0) - 1)
     def _():
-        copies[...] = jnp.broadcast_to(parts[...].astype(BF16)[None], copies.shape)
+        whole = jnp.concatenate([parts[...], extra[...]], axis=1).astype(BF16)
+        copies[...] = jnp.broadcast_to(whole[None], copies.shape)
 
 
 def last_kernel(
@@ -245,6 +257,27 @@
         value_grad = (rows_of_members(meta, scale, lanes, spans) * scaled_grad).astype(BF16)
         value_grad_own[:, lanes] = value_grad[:tok]
         value_grad_other[:, lanes] = value_grad[tok:]
+
+
+def total_kernel(copies, parts):
+    count, _, lanes = copies.shape
+    halves = []
+    for first in range(2):
+        total = copies[first].astype(F32)
+        for at in range(first + 2, count, 2):
+            total = total + copies[at].astype(F32)
+        halves.append(total)
+    wide_line = lanes - DH
+    both = halves[0][:, :wide_line] + halves[1][:, :wide_line]
+    groups = [both[i : i + MEMBERS] for i in range(0, both.shape[0], MEMBERS)]
+    found = [jnp.concatenate(groups, axis=1)]
+    for total in halves:
+        lines = total[:, wide_line:]
+        width = parts.shape[1] // DH
+        for m in range(lines.shape[0] // width):
+            row = [lines[m * width + i : m * width + i + 1] for i in range(width)]
+            found.append(jnp.concatenate(row, axis=1))
+    parts[...] = jnp.concatenate(found, axis=0)
 
 
 def running_kernel(backward, pieces, sums):
@@ -327,7 +360,7 @@
         if beside is not None:
             pieces, beside = lax.optimization_barrier((pieces, beside))
         state = scattered(running_sums(pieces, backward)).reshape(heads, DH, DH)
-        return state if beside is None else (state, beside)
+        return state if beside is None else (state,) + beside
 
     def side_by_side(core, own, other):
         return jnp.where(
@@ -353,10 +386,11 @@
         half = pltpu.HBM((tok, width), BF16)
         low = pltpu.HBM((rows, width), BF16)
         wide = pltpu.HBM((rows, width), F32)
-        part = pltpu.HBM((2 * MEMBERS, width), F32)
+        part = pltpu.HBM((MEMBERS, width), F32)
         sent = pltpu.HBM((heads, DH, DH), BF16)
         pairs = [shared(tok), shared(tok)]
-        packed = (chips, 2 * MEMBERS * local.steps, local.block)
+        lines, wide_line = LANE_GROUPS * MEMBERS, width // LANE_GROUPS
+        packed = (chips, lines, wide_line + DH)
         unit = 2 * heads * rows * DH * DH
 
         meta = (place, member_ids, other_ids)
@@ -411,6 +445,15 @@
             scratch=[pltpu.VMEM((2, rows, DH), F32)],
             flops=unit,
         )
+        out_part = local.call(
+            functools.partial(outs_kernel, full_width),
+            meta,
+            [cols(rows)] * 2 + [local.whole((group, 2, rows))],
+            cols(MEMBERS),
+            (c, slow(mixed), sums),
+            part,
+            "outs",
+        )
         query_own, query_send = local.call(
             query_kernel,
             meta,
@@ -421,13 +464,17 @@
             "query",
             flops=5 * unit,
         )
-        state_after, query_own = scanned(delta_after, True, query_own)
-        key_in, value_in, parts = local.call(
-            functools.partial(back_kernel, full_width),
-            meta,
-            [cols(rows)] * 7 + [local.whole((group, 2, rows))],
-            [cols(rows), cols(rows), cols(2 * MEMBERS)],
-            (q, k, v, c, slow(scaled), slow(grad), slow(mixed), sums),
+        out_part = out_part + lax.ppermute(out_part, "chip", [(i, i ^ 1) for i in range(chips)])
+        mine = MEMBERS // 2
+        first = lax.axis_index("chip") % 2 * mine
+        extra = lax.dynamic_slice_in_dim(out_part, first, mine, 0).reshape(lines, DH)
+        state_after, query_own, extra = scanned(delta_after, True, (query_own, extra))
+        key_in, value_in, in_part = local.call(
+            back_kernel,
+            meta,
+            [cols(rows)] * 5,
+            [cols(rows), cols(rows), cols(MEMBERS)],
+            (q, k, v, slow(scaled), slow(grad)),
             [wide, wide, part],
             "back",
             flops=8 * unit,
@@ -436,12 +483,12 @@
         copies = local.call(
             copies_kernel,
             meta,
-            [cols(rows), cols(rows), state(), cols(2 * MEMBERS)],
+            [cols(rows), cols(rows), state(), cols(MEMBERS), local.whole((lines, DH))],
             local.whole(packed),
-            (k, v, fast(state_after), slow(parts)),
+            (k, v, fast(state_after), slow(in_part), extra),
             pltpu.HBM(packed, BF16),
             "copies",
-            scratch=[pltpu.VMEM(packed[1:], F32)],
+            scratch=[pltpu.VMEM((lines, wide_line), F32)],
             flops=unit,
         )
         copies = scattered(copies)
@@ -460,9 +507,12 @@
         copies, key_grad, value_grad, query_grad = lax.optimization_barrier(
             (copies, key_grad, value_grad, query_grad)
         )
-        parts = jnp.sum(copies.astype(F32), axis=0)
-        each = 2 * MEMBERS
-        parts = jnp.concatenate([parts[i * each : (i + 1) * each] for i in range(local.steps)], axis=1)
+        parts = pl.pallas_call(
+            total_kernel,
+            out_shape=jax.ShapeDtypeStruct((2 * MEMBERS, width), F32),
+            name="total",
+            compiler_params=pltpu.CompilerParams(vmem_limit_bytes=VMEM_BYTES),
+        )(copies)
         parts = side_by_side(core, parts, swap(parts))
         return query_grad, key_grad, value_grad, parts[:MEMBERS], parts[MEMBERS:]
 

time: 126 us -> 125 us (level)
  waiting for transfers between devices: 29.5 us -> 24.3 us
  Pallas kernels: 31.9 us -> 34.3 us
    all_to_all x5, waiting for transfers between devices: 26.3 us -> 21.1 us  [scattered(): return lax.all_to_all(pieces, 'chip', 0, 0, tiled=True)]
    pallas_call x8 -> x9, Pallas kernels: 30.4 us -> 32.7 us  [call(): pl.pallas_call(with_meta(body), grid_spec=pltpu.PrefetchScalarGridSpec(nu...]
    ppermute x9, starting transfers between devices: 12.6 us -> 11.3 us  [swap(): return lax.ppermute(x, 'core', [(0, 1), (1, 0)])]
  transfers between devices with their start and end apart: 14 -> 15, of which waited for: 8 -> 8; matrix products, arithmetic and copies ran while one was open for 2% -> 2% of each run, Pallas kernels for 15% -> 19%
where the time goes in v7:
time: 125 us; the launch traced here: 124 us
  starting transfers between devices  47 us (38%)
  Pallas kernels  34.3 us (27%)
  waiting for transfers between devices  24.3 us (19%)
  blocking collectives  13 us (10%)
  other arithmetic  2.78 us (2%)
  local copies, waits for them, and re-layouts  1.66 us (1%)
    all_to_all x5, starting transfers between devices, scattered(): return lax.all_to_all(pieces, 'chip', 0, 0, tiled=True)  34.4 us
    pallas_call x9, Pallas kernels, call(): pl.pallas_call(with_meta(body), grid_spec=pltpu.PrefetchScalarGridSpec(nu...  32.7 us
    all_to_all x5, waiting for transfers between devices, scattered(): return lax.all_to_all(pieces, 'chip', 0, 0, tiled=True)  21.1 us
    all_to_all x1, blocking collectives, shards(): sums = lax.all_to_all(sums, ('core', 'head'), 0, 0, tiled=True)  13 us
    ppermute x9, starting transfers between devices, swap(): return lax.ppermute(x, 'core', [(0, 1), (1, 0)])  11.3 us
    ppermute x9, waiting for transfers between devices, swap(): return lax.ppermute(x, 'core', [(0, 1), (1, 0)])  3.19 us
    select_n x4, other arithmetic, side_by_side(): jnp.where(core == 0, jnp.concatenate([own, other], axis=1), jnp.concatena...  2.76 us
  transfers between devices with their start and end apart: 15, of which 8 were waited for; matrix products, arithmetic and copies ran while one was open for 2% of the time, Pallas kernels for 19%

profile of v7, /device:TPU:1, one launch (start us, length us, event | category | flops | bytes accessed | tf_op | source)
XLA Modules:
  0.0 123.7 jit_solution(4197963141684301116)
XLA Ops:
  0.6 3.3 %collective-permute-start.1 = (bf16[128,2048]{1,0:T(8,128)(2,1)}, bf16[128,2048]{1,0:T(8,128)(2,1)S(1)}, u32[]{:S(2)}, u32[]{:S(2)}) collective-permute-start(bf16[128,2048]{1,0:T(8,128)(2,1)} %refs_2_.1), channel_id=1, source_target_pairs={{0,4},{4,0},{1,5},{5,1},{2,6},{6,2},{3,7},{7,3},{8,12},{12,8},{9,1... | collective-permute-start | bytes 1572872 | tf_op jit(solution)/shard_map/ppermute | solution.py:352
  4.0 0.1 collective-permute-start.2
  4.1 0.4 collective-permute-start
  4.5 2.0 %collective-permute-done.other_ids = s32[8]{0:T(128)S(1)} collective-permute-done((s32[8]{0:T(128)}, s32[8]{0:T(128)S(1)}, u32[]{:S(2)}, u32[]{:S(2)}) %collective-permute-start) | collective-permute-done | bytes 64 | tf_op jit(solution)/shard_map/ppermute | solution.py:352
  6.5 0.0 collective-permute-done.1.refs_2_.refs_3_
  6.5 0.0 collective-permute-done.2.refs_4_.refs_5_
  6.5 0.0 copy-done.4
  6.5 0.0 copy-start.6
  6.5 2.9 %states.1 = (bf16[256,1024]{1,0:T(8,128)(2,1)}, bf16[8,128,128]{2,1,0:T(8,128)(2,1)}) custom-call(s32[1]{0:T(128)} %bitcast.place, s32[8]{0:T(128)S(1)} %copy-done.4, s32[8]{0:T(128)S(1)} %collective-permute-done.other_ids, f32[4,2048]{1,0:T(4,128)} %refs_0_.9, bf16[128,2048]{1,0:T(8,128)(2,1)} %refs_2_.1, ...), custom_call_target="tpu_custom_call" | custom-call | flops 67108864 | bytes 4259840 | tf_op jit(solution)/shard_map/states/pallas_call | solution.py:314
  9.4 0.0 copy-done.2
  9.4 0.0 copy-done.3
  9.4 0.0 copy-start.5
  9.4 9.4 %all-to-all-start = ((bf16[32,32,128]{2,1,0:T(8,128)(2,1)}), bf16[32,32,128]{2,1,0:T(8,128)(2,1)S(1)}, u32[]{:S(2)}, u32[]{:S(2)}) async-start(bf16[32,32,128]{2,1,0:T(8,128)(2,1)} %bitcast.10), calls=%async_computation | async-start | bytes 524288 | tf_op jit(solution)/shard_map/all_to_all | solution.py:355
  18.9 0.0 copy-done.5
  18.9 0.7 collective-permute-start.3
  19.6 0.0 copy-done.6
  19.6 0.1 collective-permute-start.4
  19.8 8.8 %all-to-all-done.pieces = bf16[32,32,128]{2,1,0:T(8,128)(2,1)S(1)} async-done(((bf16[32,32,128]{2,1,0:T(8,128)(2,1)}), bf16[32,32,128]{2,1,0:T(8,128)(2,1)S(1)}, u32[]{:S(2)}, u32[]{:S(2)}) %all-to-all-start) | async-done | bytes 262176 | tf_op jit(solution)/shard_map/all_to_all | solution.py:355
  28.6 0.7 running_sums.2
  29.3 6.7 %all-to-all-start.1 = ((bf16[32,32,128]{2,1,0:T(8,128)(2,1)}), bf16[32,32,128]{2,1,0:T(8,128)(2,1)S(1)}, u32[]{:S(2)}, u32[]{:S(2)}) async-start(bf16[32,32,128]{2,1,0:T(8,128)(2,1)} %running_sums.2), calls=%async_computation.1 | async-start | bytes 524288 | tf_op jit(solution)/shard_map/all_to_all | solution.py:355
  36.0 0.0 collective-permute-done.3.refs_1_
  36.0 0.0 copy-start.7
  36.0 0.0 collective-permute-done.4.refs_7_
  36.1 0.0 copy-start.8
  36.1 0.8 copy-done.7
  36.8 0.2 copy-done.8
  37.0 4.4 %inside.1 = (f32[256,1024]{1,0:T(8,128)}, bf16[256,1024]{1,0:T(8,128)(2,1)}, bf16[256,1024]{1,0:T(8,128)(2,1)}, bf16[256,1024]{1,0:T(8,128)(2,1)}, bf16[256,1024]{1,0:T(8,128)(2,1)}) custom-call(s32[1]{0:T(128)} %bitcast.place, s32[8]{0:T(128)S(1)} %copy-done.4, s32[8]{0:T(128)S(1)} %collective-permute-done.other_ids, bf16[128,2048]{1,0:T(8,128)(2,1)} %refs_0_.6, ...), custom_call_target="tpu_custom_call" | custom-call | flops 268435456 | bytes 9437184 | tf_op jit(solution)/shard_map/inside/pallas_call | solution.py:314
  41.4 4.3 %all-to-all-done.1 = bf16[32,32,128]{2,1,0:T(8,128)(2,1)S(1)} async-done(((bf16[32,32,128]{2,1,0:T(8,128)(2,1)}), bf16[32,32,128]{2,1,0:T(8,128)(2,1)S(1)}, u32[]{:S(2)}, u32[]{:S(2)}) %all-to-all-start.1) | async-done | bytes 262176 | tf_op jit(solution)/shard_map/all_to_all | solution.py:355
  45.7 3.3 %mixed.1 = (f32[256,1024]{1,0:T(8,128)}, f32[8,2,256]{2,1,0:T(2,128)}) custom-call(s32[1]{0:T(128)} %bitcast.place, s32[8]{0:T(128)S(1)} %copy-done.4, s32[8]{0:T(128)S(1)} %collective-permute-done.other_ids, f32[4,2048]{1,0:T(4,128)} %refs_0_.8, bf16[256,1024]{1,0:T(8,128)(2,1)} %get-tuple-element.41.refs_1_.refs_0_, ...), custom_call_target="tpu_custom_call" | custom-call | flops 67108864 | bytes 4784128 | tf_op jit(solution)/shard_map/mixed/pallas_call | solution.py:314
  49.0 0.0 copy-done
  49.0 13.0 %all_to_all.30.refs_4_.refs_2_ = f32[8,2,256]{2,1,0:T(2,128)S(1)} all-to-all(f32[8,2,256]{2,1,0:T(2,128)} %get-tuple-element.46), channel_id=1, replica_groups=mesh['chip'=32,'core'=2,'head'=4] {'core','head'}, dimensions={0} | all-to-all | bytes 32768 | tf_op jit(solution)/shard_map/all_to_all | solution.py:436
  62.0 3.4 %grads.1 = (bf16[256,1024]{1,0:T(8,128)(2,1)}, bf16[8,128,128]{2,1,0:T(8,128)(2,1)}) custom-call(s32[1]{0:T(128)} %bitcast.place, s32[8]{0:T(128)S(1)} %copy-done.4, s32[8]{0:T(128)S(1)} %collective-permute-done.other_ids, f32[4,2048]{1,0:T(4,128)} %refs_0_.8, bf16[256,1024]{1,0:T(8,128)(2,1)} %get-tuple-element.41.refs_1_.refs_0_, ...), custom_call_target="tpu_custom_call" | custom-call | flops 67108864 | bytes 4292608 | tf_op jit(solution)/shard_map/grads/pallas_call | solution.py:314
  65.4 4.3 %all-to-all-start.3 = ((bf16[32,32,128]{2,1,0:T(8,128)(2,1)}), bf16[32,32,128]{2,1,0:T(8,128)(2,1)S(1)}, u32[]{:S(2)}, u32[]{:S(2)}) async-start(bf16[32,32,128]{2,1,0:T(8,128)(2,1)} %bitcast.9), calls=%async_computation.3 | async-start | bytes 524288 | tf_op jit(solution)/shard_map/all_to_all | solution.py:355
  69.7 2.8 %outs.1 = f32[4,1024]{1,0:T(4,128)} custom-call(s32[1]{0:T(128)} %bitcast.place, s32[8]{0:T(128)S(1)} %copy-done.4, s32[8]{0:T(128)S(1)} %collective-permute-done.other_ids, bf16[256,1024]{1,0:T(8,128)(2,1)} %get-tuple-element.42.refs_2_.refs_0_, f32[256,1024]{1,0:T(8,128)} %get-tuple-element.45.refs_3_.refs_1_, f32[8,2,256]{2,1,0:T(2,128)S(1)} %all_to_all.30.refs_4_.refs_2_), custom_call_target="tpu_custom_call" | custom-call | bytes 3178496 | tf_op jit(solution)/shard_map/outs/pallas_call | solution.py:314
  72.5 1.2 collective-permute-start.5
  73.7 3.7 %query.1 = (bf16[128,1024]{1,0:T(8,128)(2,1)}, bf16[128,1024]{1,0:T(8,128)(2,1)}) custom-call(s32[1]{0:T(128)} %bitcast.place, s32[8]{0:T(128)S(1)} %copy-done.4, s32[8]{0:T(128)S(1)} %collective-permute-done.other_ids, bf16[256,1024]{1,0:T(8,128)(2,1)} %get-tuple-element.39.refs_0_.refs_1_, ...), custom_call_target="tpu_custom_call" | custom-call | flops 335544320 | bytes 3670016 | tf_op jit(solution)/shard_map/query/pallas_call | solution.py:314
  77.4 0.0 collective-permute-done.5
  77.4 0.0 copy-done.12
  77.4 1.9 %all-to-all-done.3.pieces = bf16[32,32,128]{2,1,0:T(8,128)(2,1)S(1)} async-done(((bf16[32,32,128]{2,1,0:T(8,128)(2,1)}), bf16[32,32,128]{2,1,0:T(8,128)(2,1)S(1)}, u32[]{:S(2)}, u32[]{:S(2)}) %all-to-all-start.3) | async-done | bytes 262176 | tf_op jit(solution)/shard_map/all_to_all | solution.py:355
  79.3 0.7 running_sums.3
  80.1 6.7 %all-to-all-start.4 = ((bf16[32,32,128]{2,1,0:T(8,128)(2,1)}), bf16[32,32,128]{2,1,0:T(8,128)(2,1)S(1)}, u32[]{:S(2)}, u32[]{:S(2)}) async-start(bf16[32,32,128]{2,1,0:T(8,128)(2,1)} %running_sums.3), calls=%async_computation.4 | async-start | bytes 524288 | tf_op jit(solution)/shard_map/all_to_all | solution.py:355
  86.8 0.0 copy-done.13
  86.8 1.8 %collective-permute-start.8 = (bf16[128,1024]{1,0:T(8,128)(2,1)S(1)}, bf16[128,1024]{1,0:T(8,128)(2,1)S(1)}, u32[]{:S(2)}, u32[]{:S(2)}) collective-permute-start(bf16[128,1024]{1,0:T(8,128)(2,1)S(1)} %copy-done.13), channel_id=1, source_target_pairs={{0,4},{4,0},{1,5},{5,1},{2,6},{6,2},{3,7},{7,3},{8,12},{12,8},{9,1... | collective-permute-start | bytes 786440 | tf_op jit(solution)/shard_map/ppermute | solution.py:352
  88.6 5.6 %back.1 = (f32[256,1024]{1,0:T(8,128)}, f32[256,1024]{1,0:T(8,128)}, f32[4,1024]{1,0:T(4,128)}) custom-call(s32[1]{0:T(128)} %bitcast.place, s32[8]{0:T(128)S(1)} %copy-done.4, s32[8]{0:T(128)S(1)} %collective-permute-done.other_ids, bf16[256,1024]{1,0:T(8,128)(2,1)} %get-tuple-element.41.refs_1_.refs_0_, ...), custom_call_target="tpu_custom_call" | custom-call | flops 536870912 | bytes 5242880 | tf_op jit(solution)/shard_map/back/pallas_call | solution.py:314
  94.2 2.2 %all-to-all-done.4 = bf16[32,32,128]{2,1,0:T(8,128)(2,1)S(1)} async-done(((bf16[32,32,128]{2,1,0:T(8,128)(2,1)}), bf16[32,32,128]{2,1,0:T(8,128)(2,1)S(1)}, u32[]{:S(2)}, u32[]{:S(2)}) %all-to-all-start.4) | async-done | bytes 262176 | tf_op jit(solution)/shard_map/all_to_all | solution.py:355
  96.4 2.9 %copies.1 = bf16[32,16,384]{2,1,0:T(8,128)(2,1)} custom-call(s32[1]{0:T(128)} %bitcast.place, s32[8]{0:T(128)S(1)} %copy-done.4, s32[8]{0:T(128)S(1)} %collective-permute-done.other_ids, bf16[256,1024]{1,0:T(8,128)(2,1)} %get-tuple-element.39.refs_0_.refs_1_, bf16[256,1024]{1,0:T(8,128)(2,1)} %get-tuple-element.40.refs_2_.refs_1_, ...), custom_call_target="tpu_custom_call" | custom-call | flops 67108864 | bytes 2670592 | tf_op jit(solution)/shard_map/copies/pallas_call | solution.py:314
  99.4 0.0 copy-done.1
  99.4 7.3 %all-to-all-start.5 = ((bf16[32,16,384]{2,1,0:T(8,128)(2,1)}), bf16[32,16,384]{2,1,0:T(8,128)(2,1)S(1)}, u32[]{:S(2)}, u32[]{:S(2)}) async-start(bf16[32,16,384]{2,1,0:T(8,128)(2,1)} %copies.1), calls=%async_computation.5 | async-start | bytes 786432 | tf_op jit(solution)/shard_map/all_to_all | solution.py:355
  106.7 0.0 copy-start.9
  106.7 3.6 %last.1 = (bf16[128,1024]{1,0:T(8,128)(2,1)}, bf16[128,1024]{1,0:T(8,128)(2,1)}, bf16[128,1024]{1,0:T(8,128)(2,1)}, bf16[128,1024]{1,0:T(8,128)(2,1)}) custom-call(s32[1]{0:T(128)} %bitcast.place, s32[8]{0:T(128)S(1)} %copy-done.4, s32[8]{0:T(128)S(1)} %collective-permute-done.other_ids, f32[4,2048]{1,0:T(4,128)} %refs_0_.9, ...), custom_call_target="tpu_custom_call" | custom-call | flops 134217728 | bytes 6881280 | tf_op jit(solution)/shard_map/last/pallas_call | solution.py:314
  110.3 0.9 collective-permute-start.7
  111.2 0.1 collective-permute-start.6
  111.3 0.0 collective-permute-done.8
  111.3 0.9 maximum_select_fusion.2
  112.2 0.3 collective-permute-done.7
  112.6 0.9 maximum_select_fusion.1
  113.5 0.0 collective-permute-done.6
  113.5 0.0 copy-done.10
  113.5 0.9 maximum_select_fusion
  114.5 3.9 %all-to-all-done.5.copies = bf16[32,16,384]{2,1,0:T(8,128)(2,1)S(1)} async-done(((bf16[32,16,384]{2,1,0:T(8,128)(2,1)}), bf16[32,16,384]{2,1,0:T(8,128)(2,1)S(1)}, u32[]{:S(2)}, u32[]{:S(2)}) %all-to-all-start.5) | async-done | bytes 393248 | tf_op jit(solution)/shard_map/all_to_all | solution.py:355
  118.4 0.1 total.1
  118.4 3.8 %collective-permute-start.9 = (f32[8,1024]{1,0:T(8,128)S(1)}, f32[8,1024]{1,0:T(8,128)S(1)}, u32[]{:S(2)}, u32[]{:S(2)}) collective-permute-start(f32[8,1024]{1,0:T(8,128)S(1)} %total.1), channel_id=1, source_target_pairs={{0,4},{4,0},{1,5},{5,1},{2,6},{6,2},{3,7},{7,3},{8,12},{12,8},{9,1... | collective-permute-start | bytes 98312 | tf_op jit(solution)/shard_map/ppermute | solution.py:352
  122.2 0.9 collective-permute-done.9
  123.1 0.6 fusion
  (14 shorter events, 0.1 us)
Async XLA Ops:
  0.6 5.8 %collective-permute-start.1 = (bf16[128,2048]{1,0:T(8,128)(2,1)}, bf16[128,2048]{1,0:T(8,128)(2,1)S(1)}, u32[]{:S(2)}, u32[]{:S(2)}) collective-permute-start(bf16[128,2048]{1,0:T(8,128)(2,1)} %refs_2_.1), channel_id=1, source_target_pairs={{0,4},{4,0},{1,5},{5,1},{2,6},{6,2},{3,7},{7,3},{8,12},{12,8},{9,1... | collective-permute-start | bytes 1572872 | tf_op jit(solution)/shard_map/ppermute | solution.py:352
  4.0 2.5 %collective-permute-start.2 = (bf16[128,2048]{1,0:T(8,128)(2,1)}, bf16[128,2048]{1,0:T(8,128)(2,1)S(1)}, u32[]{:S(2)}, u32[]{:S(2)}) collective-permute-start(bf16[128,2048]{1,0:T(8,128)(2,1)} %refs_4_.1), channel_id=1, source_target_pairs={{0,4},{4,0},{1,5},{5,1},{2,6},{6,2},{3,7},{7,3},{8,12},{12,8},{9,1... | collective-permute-start | bytes 1572872 | tf_op jit(solution)/shard_map/ppermute | solution.py:352
  4.1 2.4 %collective-permute-start = (s32[8]{0:T(128)}, s32[8]{0:T(128)S(1)}, u32[]{:S(2)}, u32[]{:S(2)}) collective-permute-start(s32[8]{0:T(128)} %own_ids.17), channel_id=1, source_target_pairs={{0,4},{4,0},{1,5},{5,1},{2,6},{6,2},{3,7},{7,3},{8,12},{12,8},{9,1... | collective-permute-start | bytes 104 | tf_op jit(solution)/shard_map/ppermute | solution.py:352
  4.5 2.0 %copy-start.4 = (s32[8]{0:T(128)S(1)}, s32[8]{0:T(128)}, u32[]{:S(2)}) copy-start(s32[8]{0:T(128)} %own_ids.17) | copy-start | bytes 100
  6.5 3.0 %copy-start.2 = (bf16[128,2048]{1,0:T(8,128)(2,1)}, bf16[128,2048]{1,0:T(8,128)(2,1)S(1)}, u32[]{:S(2)}) copy-start(bf16[128,2048]{1,0:T(8,128)(2,1)S(1)} %collective-permute-done.1.refs_2_.refs_3_) | copy-start | bytes 1572868
  6.5 3.0 %copy-start.3 = (bf16[128,2048]{1,0:T(8,128)(2,1)}, bf16[128,2048]{1,0:T(8,128)(2,1)S(1)}, u32[]{:S(2)}) copy-start(bf16[128,2048]{1,0:T(8,128)(2,1)S(1)} %collective-permute-done.2.refs_4_.refs_5_) | copy-start | bytes 1572868
  6.5 13.2 %copy-start.6 = (bf16[128,2048]{1,0:T(8,128)(2,1)S(1)}, bf16[128,2048]{1,0:T(8,128)(2,1)}, u32[]{:S(2)}) copy-start(bf16[128,2048]{1,0:T(8,128)(2,1)} %refs_6_.1) | copy-start | bytes 1572868
  9.4 9.5 %copy-start.5 = (bf16[128,2048]{1,0:T(8,128)(2,1)S(1)}, bf16[128,2048]{1,0:T(8,128)(2,1)}, u32[]{:S(2)}) copy-start(bf16[128,2048]{1,0:T(8,128)(2,1)} %refs_0_.6) | copy-start | bytes 1572868
  9.4 19.1 %all-to-all-start = ((bf16[32,32,128]{2,1,0:T(8,128)(2,1)}), bf16[32,32,128]{2,1,0:T(8,128)(2,1)S(1)}, u32[]{:S(2)}, u32[]{:S(2)}) async-start(bf16[32,32,128]{2,1,0:T(8,128)(2,1)} %bitcast.10), calls=%async_computation | async-start | bytes 524288 | tf_op jit(solution)/shard_map/all_to_all | solution.py:355
  18.9 17.1 %collective-permute-start.3 = (bf16[128,2048]{1,0:T(8,128)(2,1)S(1)}, bf16[128,2048]{1,0:T(8,128)(2,1)S(1)}, u32[]{:S(2)}, u32[]{:S(2)}) collective-permute-start(bf16[128,2048]{1,0:T(8,128)(2,1)S(1)} %copy-done.5), channel_id=1, source_target_pairs={{0,4},{4,0},{1,5},{5,1},{2,6},{6,2},{3,7},{7,3},{8,12},{12,8},{9,1... | collective-permute-start | bytes 1572872 | tf_op jit(solution)/shard_map/ppermute | solution.py:352
  19.6 16.4 %collective-permute-start.4 = (bf16[128,2048]{1,0:T(8,128)(2,1)S(1)}, bf16[128,2048]{1,0:T(8,128)(2,1)S(1)}, u32[]{:S(2)}, u32[]{:S(2)}) collective-permute-start(bf16[128,2048]{1,0:T(8,128)(2,1)S(1)} %copy-done.6), channel_id=1, source_target_pairs={{0,4},{4,0},{1,5},{5,1},{2,6},{6,2},{3,7},{7,3},{8,12},{12,8},{9,1... | collective-permute-start | bytes 1572872 | tf_op jit(solution)/shard_map/ppermute | solution.py:352
  29.3 16.4 %all-to-all-start.1 = ((bf16[32,32,128]{2,1,0:T(8,128)(2,1)}), bf16[32,32,128]{2,1,0:T(8,128)(2,1)S(1)}, u32[]{:S(2)}, u32[]{:S(2)}) async-start(bf16[32,32,128]{2,1,0:T(8,128)(2,1)} %running_sums.2), calls=%async_computation.1 | async-start | bytes 524288 | tf_op jit(solution)/shard_map/all_to_all | solution.py:355
  36.0 0.8 copy-start.7
  36.1 0.9 copy-start.8
  45.7 3.3 %copy-start = (bf16[32,32,128]{2,1,0:T(8,128)(2,1)}, bf16[32,32,128]{2,1,0:T(8,128)(2,1)S(1)}, u32[]{:S(2)}) copy-start(bf16[32,32,128]{2,1,0:T(8,128)(2,1)S(1)} %all-to-all-done.1) | copy-start | bytes 786436
  65.4 14.0 %all-to-all-start.3 = ((bf16[32,32,128]{2,1,0:T(8,128)(2,1)}), bf16[32,32,128]{2,1,0:T(8,128)(2,1)S(1)}, u32[]{:S(2)}, u32[]{:S(2)}) async-start(bf16[32,32,128]{2,1,0:T(8,128)(2,1)} %bitcast.9), calls=%async_computation.3 | async-start | bytes 524288 | tf_op jit(solution)/shard_map/all_to_all | solution.py:355
  72.5 4.9 %collective-permute-start.5 = (f32[4,1024]{1,0:T(4,128)}, f32[4,1024]{1,0:T(4,128)S(1)}, u32[]{:S(2)}, u32[]{:S(2)}) collective-permute-start(f32[4,1024]{1,0:T(4,128)} %outs.1), channel_id=1, source_target_pairs={{0,8},{8,0},{16,24},{24,16},{32,40},{40,32},{48,56},{56,48},{64,72... | collective-permute-start | bytes 49160 | tf_op jit(solution)/shard_map/ppermute | solution.py:467
  73.7 3.7 %copy-start.12 = (f32[4,1024]{1,0:T(4,128)S(1)}, f32[4,1024]{1,0:T(4,128)}, u32[]{:S(2)}) copy-start(f32[4,1024]{1,0:T(4,128)} %outs.1) | copy-start | bytes 49156
  80.1 6.7 %copy-start.13 = (bf16[128,1024]{1,0:T(8,128)(2,1)S(1)}, bf16[128,1024]{1,0:T(8,128)(2,1)}, u32[]{:S(2)}) copy-start(bf16[128,1024]{1,0:T(8,128)(2,1)} %get-tuple-element.60) | copy-start | bytes 786436
  80.1 16.3 %all-to-all-start.4 = ((bf16[32,32,128]{2,1,0:T(8,128)(2,1)}), bf16[32,32,128]{2,1,0:T(8,128)(2,1)S(1)}, u32[]{:S(2)}, u32[]{:S(2)}) async-start(bf16[32,32,128]{2,1,0:T(8,128)(2,1)} %running_sums.3), calls=%async_computation.4 | async-start | bytes 524288 | tf_op jit(solution)/shard_map/all_to_all | solution.py:355
  86.8 24.6 %collective-permute-start.8 = (bf16[128,1024]{1,0:T(8,128)(2,1)S(1)}, bf16[128,1024]{1,0:T(8,128)(2,1)S(1)}, u32[]{:S(2)}, u32[]{:S(2)}) collective-permute-start(bf16[128,1024]{1,0:T(8,128)(2,1)S(1)} %copy-done.13), channel_id=1, source_target_pairs={{0,4},{4,0},{1,5},{5,1},{2,6},{6,2},{3,7},{7,3},{8,12},{12,8},{9,1... | collective-permute-start | bytes 786440 | tf_op jit(solution)/shard_map/ppermute | solution.py:352
  96.4 3.0 %copy-start.1 = (bf16[32,32,128]{2,1,0:T(8,128)(2,1)}, bf16[32,32,128]{2,1,0:T(8,128)(2,1)S(1)}, u32[]{:S(2)}) copy-start(bf16[32,32,128]{2,1,0:T(8,128)(2,1)S(1)} %all-to-all-done.4) | copy-start | bytes 786436
  99.4 19.0 %all-to-all-start.5 = ((bf16[32,16,384]{2,1,0:T(8,128)(2,1)}), bf16[32,16,384]{2,1,0:T(8,128)(2,1)S(1)}, u32[]{:S(2)}, u32[]{:S(2)}) async-start(bf16[32,16,384]{2,1,0:T(8,128)(2,1)} %copies.1), calls=%async_computation.5 | async-start | bytes 786432 | tf_op jit(solution)/shard_map/all_to_all | solution.py:355
  106.7 4.6 %copy-start.9 = (bf16[128,1024]{1,0:T(8,128)(2,1)S(1)}, bf16[128,1024]{1,0:T(8,128)(2,1)}, u32[]{:S(2)}) copy-start(bf16[128,1024]{1,0:T(8,128)(2,1)} %get-tuple-element.59) | copy-start | bytes 786436
  110.3 2.3 %collective-permute-start.7 = (bf16[128,1024]{1,0:T(8,128)(2,1)}, bf16[128,1024]{1,0:T(8,128)(2,1)S(1)}, u32[]{:S(2)}, u32[]{:S(2)}) collective-permute-start(bf16[128,1024]{1,0:T(8,128)(2,1)} %get-tuple-element.58), channel_id=1, source_target_pairs={{0,4},{4,0},{1,5},{5,1},{2,6},{6,2},{3,7},{7,3},{8,12},{12,8},{9,1... | collective-permute-start | bytes 786440 | tf_op jit(solution)/shard_map/ppermute | solution.py:352
  111.2 1.4 %copy-start.11 = (bf16[128,1024]{1,0:T(8,128)(2,1)S(1)}, bf16[128,1024]{1,0:T(8,128)(2,1)}, u32[]{:S(2)}) copy-start(bf16[128,1024]{1,0:T(8,128)(2,1)} %get-tuple-element.57) | copy-start | bytes 786436
  111.2 2.3 %collective-permute-start.6 = (bf16[128,1024]{1,0:T(8,128)(2,1)}, bf16[128,1024]{1,0:T(8,128)(2,1)S(1)}, u32[]{:S(2)}, u32[]{:S(2)}) collective-permute-start(bf16[128,1024]{1,0:T(8,128)(2,1)} %get-tuple-element.56), channel_id=1, source_target_pairs={{0,4},{4,0},{1,5},{5,1},{2,6},{6,2},{3,7},{7,3},{8,12},{12,8},{9,1... | collective-permute-start | bytes 786440 | tf_op jit(solution)/shard_map/ppermute | solution.py:352
  112.6 1.0 copy-start.10
  118.4 4.7 %collective-permute-start.9 = (f32[8,1024]{1,0:T(8,128)S(1)}, f32[8,1024]{1,0:T(8,128)S(1)}, u32[]{:S(2)}, u32[]{:S(2)}) collective-permute-start(f32[8,1024]{1,0:T(8,128)S(1)} %total.1), channel_id=1, source_target_pairs={{0,4},{4,0},{1,5},{5,1},{2,6},{6,2},{3,7},{7,3},{8,12},{12,8},{9,1... | collective-permute-start | bytes 98312 | tf_op jit(solution)/shard_map/ppermute | solution.py:352

commit v8 on v7

--- a/solution.py
+++ b/solution.py
@@ -13,6 +13,7 @@
 EPS = 1e-06
 CORES = 2
 STEP_HEADS = 4
+FLOW_HEADS = 2
 LANE_GROUPS = 4
 VMEM_BYTES = 24 * 2**20
 F32 = jnp.float32
@@ -122,20 +123,12 @@
         inside[:, lanes] = dot(weights, scaled[:, lanes], NN)
 
 
-def mixed_kernel(
-    meta, scale, q, c, state, inside, mixed, sums, squares, crosses
-):
+def mixed_kernel(meta, step, steps, scale, q, c, state, inside, mixed, sums, squares, crosses):
     rows = q.shape[0]
     tok = rows // 2
     spans = rows // SPAN
-    step = pl.program_id(0)
-
-    @pl.when(step == 0)
-    def _():
-        squares[...] = jnp.zeros_like(squares)
-        crosses[...] = jnp.zeros_like(crosses)
-
-    square, cross = squares[...], crosses[...]
+    empty = jnp.zeros(squares.shape, F32)
+    square, cross = (empty, empty) if step == 0 else (squares[...], crosses[...])
     for h in range(state.shape[0]):
         lanes = lanes_of(h)
         mix = inside[:, lanes] + dot(q[:, lanes], state[h], NN)
@@ -143,25 +136,23 @@
         cot = c[:, lanes].astype(F32)
         square = square + mix * mix
         cross = cross + rows_of_members(meta, scale, lanes, spans) * cot * mix
-    squares[...] = square
-    crosses[...] = cross
-
-    @pl.when(step == pl.num_programs(0) - 1)
-    def _():
+    if step < steps - 1:
+        squares[...] = square
+        crosses[...] = cross
+    else:
         totals = [jnp.sum(jnp.transpose(t), axis=0, keepdims=True) for t in (square, cross)]
         totals = in_order(meta, jnp.concatenate(totals, axis=0), tok)
         sums[...] = jnp.broadcast_to(totals[None], sums.shape)
 
 
 def grads_kernel(
-    full_width, meta, scale, q, c, mixed, sums, grad, delta, turned
+    full_width, meta, step, steps, scale, q, c, mixed, sums, grad, delta, turned
 ):
     rows = q.shape[0]
     tok = rows // 2
     spans = rows // SPAN
 
-    @pl.when(pl.program_id(0) == 0)
-    def _():
+    if step == 0:
         totals = head_sums(meta, sums, tok)
         rms = jnp.sqrt(totals[0:1] / full_width + EPS)
         turned[0] = jnp.transpose(jnp.broadcast_to(1.0 / rms, (DH, 2 * tok)))
@@ -218,9 +209,8 @@
         in_part[:, lanes] = member_sums(meta, v[:, lanes].astype(F32) * inner, spans)
 
 
-def copies_kernel(meta, k, v, state, known, extra, copies, parts):
+def copies_kernel(meta, step, steps, k, v, state, known, extra, copies, parts):
     spans = k.shape[0] // SPAN
-    step = pl.program_id(0)
     found = []
     for h in range(state.shape[0]):
         lanes = lanes_of(h)
@@ -233,10 +223,8 @@
     ]
     rows = jnp.concatenate(rows, axis=0)
     count = rows.shape[0]
-    parts[pl.ds(pl.multiple_of(step * count, count), count)] = rows
-
-    @pl.when(step == pl.num_programs(0) - 1)
-    def _():
+    parts[step * count : (step + 1) * count] = rows
+    if step == steps - 1:
         whole = jnp.concatenate([parts[...], extra[...]], axis=1).astype(BF16)
         copies[...] = jnp.broadcast_to(whole[None], copies.shape)
 
@@ -289,6 +277,63 @@
         total = total + pieces[at].astype(F32)
 
 
+def streamed_kernel(body, kinds, scratch_count, width, place, own_ids, other_ids, *refs):
+    meta = Meta(place, own_ids, other_ids)
+    ins, outs = kinds
+    steps = width // (FLOW_HEADS * DH)
+    taken = [refs[: len(ins)], refs[len(ins) : len(ins) + len(outs)]]
+    rest = refs[len(ins) + len(outs) :]
+    in_bufs, out_bufs = rest[: len(ins)], rest[len(ins) : len(ins) + len(outs)]
+    sent, got = rest[len(ins) + len(outs) : len(ins) + len(outs) + 2]
+    extra = rest[len(ins) + len(outs) + 2 :]
+
+    def part(kind, ref, step):
+        if kind == "cols":
+            return ref.at[:, pl.ds(step * FLOW_HEADS * DH, FLOW_HEADS * DH)]
+        if kind == "state":
+            return ref.at[pl.ds(step * FLOW_HEADS, FLOW_HEADS)]
+        return ref
+
+    arrivals = []
+    for step in range(steps):
+        here = []
+        for at, kind in enumerate(ins):
+            source, target = taken[0][at], in_bufs[at]
+            if kind == "held" or (kind != "cols" and step > 0):
+                continue
+            if kind == "scale":
+                start = pl.multiple_of(meta.core * width, width)
+                source = source.at[:, pl.ds(start, width)]
+            copy = pltpu.make_async_copy(
+                part(kind, source, step), part(kind, target, step), got.at[at, step]
+            )
+            copy.start()
+            here.append(copy)
+        arrivals.append(here)
+    leaving = []
+    for step in range(steps):
+        for copy in arrivals[step]:
+            copy.wait()
+        views = []
+        for at, kind in enumerate(ins):
+            if kind == "held":
+                views.append(part("state", taken[0][at], step))
+            else:
+                views.append(part("cols" if kind == "scale" else kind, in_bufs[at], step))
+        views += [part(kind, out_bufs[at], step) for at, kind in enumerate(outs)]
+        body(meta, step, steps, *views, *extra)
+        for at, kind in enumerate(outs):
+            if kind == "whole" and step < steps - 1:
+                continue
+            copy = pltpu.make_async_copy(
+                part(kind, out_bufs[at], step), part(kind, taken[1][at], step), sent.at[at, step]
+            )
+            copy.start()
+            leaving.append(copy)
+    for copy in leaving:
+        copy.wait()
+
+
 class Local:
     def __init__(self, tok, width):
         self.tok = tok
@@ -308,6 +353,32 @@
 
     def whole(self, shape):
         return pl.BlockSpec(shape, lambda i, *_: (0,) * len(shape))
+
+    def flow(self, body, meta, kinds, args, shapes, name, scratch=(), flops=0):
+        ins, outs = kinds
+        steps = self.width // (FLOW_HEADS * DH)
+        buffers = []
+        for kind, arg in zip(ins, args):
+            shape = (arg.shape[0], self.width) if kind == "scale" else arg.shape
+            buffers.append(pltpu.VMEM((8, DH) if kind == "held" else shape, arg.dtype))
+        buffers += [pltpu.VMEM(x.shape, x.dtype) for x in shapes]
+        sems = [
+            pltpu.SemaphoreType.DMA((len(outs), steps)),
+            pltpu.SemaphoreType.DMA((len(ins), steps)),
+        ]
+        spaces = [pltpu.VMEM if kind == "held" else pltpu.HBM for kind in ins]
+        moved = sum(a.size * a.dtype.itemsize for a in args)
+        return pl.pallas_call(
+            functools.partial(streamed_kernel, body, kinds, len(scratch), self.width),
+            in_specs=[pl.BlockSpec(memory_space=pltpu.SMEM)] * len(meta)
+            + [pl.BlockSpec(memory_space=space) for space in spaces],
+            out_specs=[pl.BlockSpec(memory_space=pltpu.HBM) for _ in outs],
+            out_shape=shapes,
+            scratch_shapes=buffers + sems + list(scratch),
+            name=name,
+            compiler_params=pltpu.CompilerParams(vmem_limit_bytes=VMEM_BYTES),
+            cost_estimate=pl.CostEstimate(flops=flops, bytes_accessed=2 * moved, transcendentals=0),
+        )(*meta, *args)
 
     def call(self, body, meta, ins, outs, args, shapes, name, scratch=(), flops=0):
         moved = sum(a.size * a.dtype.itemsize for a in args)
@@ -422,11 +493,10 @@
             flops=4 * unit,
         )
         q, k, v, c = slow(q), slow(k), slow(v), slow(c)
-        mixed, sums = local.call(
+        mixed, sums = local.flow(
             mixed_kernel,
             meta,
-            [shared(MEMBERS), cols(rows), cols(rows), state(), cols(rows)],
-            [cols(rows), local.whole((group, 2, rows))],
+            (("scale", "cols", "cols", "held", "cols"), ("cols", "whole")),
             (slow(out_scale), q, c, fast(state_in), slow(inside)),
             [wide, pltpu.HBM((group, 2, rows), F32)],
             "mixed",
@@ -434,11 +504,10 @@
             flops=unit,
         )
         sums = lax.all_to_all(sums, ("core", "head"), 0, 0, tiled=True)
-        grad, delta_after = local.call(
+        grad, delta_after = local.flow(
             functools.partial(grads_kernel, full_width),
             meta,
-            [shared(MEMBERS)] + [cols(rows)] * 3 + [local.whole((group, 2, rows))],
-            [cols(rows), state()],
+            (("scale", "cols", "cols", "cols", "whole"), ("cols", "state")),
             (slow(out_scale), q, c, slow(mixed), sums),
             [low, sent],
             "grads",
@@ -480,13 +549,12 @@
             flops=8 * unit,
         )
         query_grad = side_by_side(core, query_own, swap(query_send))
-        copies = local.call(
+        copies, = local.flow(
             copies_kernel,
             meta,
-            [cols(rows), cols(rows), state(), cols(MEMBERS), local.whole((lines, DH))],
-            local.whole(packed),
-            (k, v, fast(state_after), slow(in_part), extra),
-            pltpu.HBM(packed, BF16),
+            (("cols", "cols", "held", "cols", "whole"), ("whole",)),
+            (k, v, fast(state_after), slow(in_part), slow(extra)),
+            [pltpu.HBM(packed, BF16)],
             "copies",
             scratch=[pltpu.VMEM((lines, wide_line), F32)],
             flops=unit,

time: 125 us -> 126 us (level)
  waiting for transfers between devices: 24.3 us -> 22.7 us
  starting transfers between devices: 47 us -> 48.3 us
    pallas_call x0 -> x3, Pallas kernels: none -> 10.4 us  [flow(): pl.pallas_call(functools.partial(streamed_kernel, body, kinds, len(scratc...]
    pallas_call x9 -> x6, Pallas kernels: 32.7 us -> 23 us  [call(): pl.pallas_call(with_meta(body), grid_spec=pltpu.PrefetchScalarGridSpec(nu...]
    all_to_all x5, waiting for transfers between devices: 21.1 us -> 19.6 us  [scattered(): return lax.all_to_all(pieces, 'chip', 0, 0, tiled=True)]
  transfers between devices with their start and end apart: 15 -> 15, of which waited for: 8 -> 8; matrix products, arithmetic and copies ran while one was open for 2% -> 3% of each run, Pallas kernels for 19% -> 19%
where the time goes in v8:
time: 126 us; the launch traced here: 125 us
  starting transfers between devices  48.3 us (38%)
  Pallas kernels  35 us (28%)
  waiting for transfers between devices  22.7 us (18%)
  blocking collectives  13 us (10%)
  other arithmetic  2.78 us (2%)
  local copies, waits for them, and re-layouts  2.25 us (2%)
    all_to_all x5, starting transfers between devices, scattered(): return lax.all_to_all(pieces, 'chip', 0, 0, tiled=True)  34.8 us
    pallas_call x6, Pallas kernels, call(): pl.pallas_call(with_meta(body), grid_spec=pltpu.PrefetchScalarGridSpec(nu...  23 us
    all_to_all x5, waiting for transfers between devices, scattered(): return lax.all_to_all(pieces, 'chip', 0, 0, tiled=True)  19.6 us
    all_to_all x1, blocking collectives, shards(): sums = lax.all_to_all(sums, ('core', 'head'), 0, 0, tiled=True)  13 us
    ppermute x9, starting transfers between devices, swap(): return lax.ppermute(x, 'core', [(0, 1), (1, 0)])  12.2 us
    pallas_call x3, Pallas kernels, flow(): pl.pallas_call(functools.partial(streamed_kernel, body, kinds, len(scratc...  10.4 us
    ppermute x9, waiting for transfers between devices, swap(): return lax.ppermute(x, 'core', [(0, 1), (1, 0)])  3.19 us
    select_n x4, other arithmetic, side_by_side(): jnp.where(core == 0, jnp.concatenate([own, other], axis=1), jnp.concatena...  2.76 us
  transfers between devices with their start and end apart: 15, of which 8 were waited for; matrix products, arithmetic and copies ran while one was open for 3% of the time, Pallas kernels for 19%

profile of v8, /device:TPU:1, one launch (start us, length us, event | category | flops | bytes accessed | tf_op | source)
XLA Modules:
  0.0 124.9 jit_solution(5893523840828044958)
XLA Ops:
  0.6 3.3 %collective-permute-start.1 = (bf16[128,2048]{1,0:T(8,128)(2,1)}, bf16[128,2048]{1,0:T(8,128)(2,1)S(1)}, u32[]{:S(2)}, u32[]{:S(2)}) collective-permute-start(bf16[128,2048]{1,0:T(8,128)(2,1)} %refs_2_.1), channel_id=1, source_target_pairs={{0,4},{4,0},{1,5},{5,1},{2,6},{6,2},{3,7},{7,3},{8,12},{12,8},{9,1... | collective-permute-start | bytes 1572872 | tf_op jit(solution)/shard_map/ppermute | solution.py:423
  4.0 0.1 collective-permute-start.2
  4.1 0.4 collective-permute-start
  4.5 2.0 %collective-permute-done.other_ids = s32[8]{0:T(128)S(1)} collective-permute-done((s32[8]{0:T(128)}, s32[8]{0:T(128)S(1)}, u32[]{:S(2)}, u32[]{:S(2)}) %collective-permute-start) | collective-permute-done | bytes 64 | tf_op jit(solution)/shard_map/ppermute | solution.py:423
  6.5 0.0 collective-permute-done.1.refs_2_.refs_3_
  6.5 0.0 collective-permute-done.2.refs_4_.refs_5_
  6.5 0.0 copy-done.4
  6.5 0.0 copy-start.6
  6.5 2.9 %states.1 = (bf16[256,1024]{1,0:T(8,128)(2,1)}, bf16[8,128,128]{2,1,0:T(8,128)(2,1)}) custom-call(s32[1]{0:T(128)} %bitcast.place, s32[8]{0:T(128)S(1)} %copy-done.4, s32[8]{0:T(128)S(1)} %collective-permute-done.other_ids, f32[4,2048]{1,0:T(4,128)} %refs_0_.9, bf16[128,2048]{1,0:T(8,128)(2,1)} %refs_2_.1, ...), custom_call_target="tpu_custom_call" | custom-call | flops 67108864 | bytes 4259840 | tf_op jit(solution)/shard_map/states/pallas_call | solution.py:385
  9.4 0.0 copy-done.2
  9.4 0.0 copy-done.3
  9.4 0.0 copy-start.5
  9.4 9.4 %all-to-all-start = ((bf16[32,32,128]{2,1,0:T(8,128)(2,1)}), bf16[32,32,128]{2,1,0:T(8,128)(2,1)S(1)}, u32[]{:S(2)}, u32[]{:S(2)}) async-start(bf16[32,32,128]{2,1,0:T(8,128)(2,1)} %bitcast.10), calls=%async_computation | async-start | bytes 524288 | tf_op jit(solution)/shard_map/all_to_all | solution.py:426
  18.9 0.0 copy-done.5
  18.9 0.7 collective-permute-start.3
  19.6 0.0 copy-done.6
  19.6 0.1 collective-permute-start.4
  19.8 8.8 %all-to-all-done.pieces = bf16[32,32,128]{2,1,0:T(8,128)(2,1)S(1)} async-done(((bf16[32,32,128]{2,1,0:T(8,128)(2,1)}), bf16[32,32,128]{2,1,0:T(8,128)(2,1)S(1)}, u32[]{:S(2)}, u32[]{:S(2)}) %all-to-all-start) | async-done | bytes 262176 | tf_op jit(solution)/shard_map/all_to_all | solution.py:426
  28.6 0.7 running_sums.2
  29.3 6.7 %all-to-all-start.1 = ((bf16[32,32,128]{2,1,0:T(8,128)(2,1)}), bf16[32,32,128]{2,1,0:T(8,128)(2,1)S(1)}, u32[]{:S(2)}, u32[]{:S(2)}) async-start(bf16[32,32,128]{2,1,0:T(8,128)(2,1)} %running_sums.2), calls=%async_computation.1 | async-start | bytes 524288 | tf_op jit(solution)/shard_map/all_to_all | solution.py:426
  36.0 0.0 collective-permute-done.3.refs_1_
  36.0 0.0 copy-start.7
  36.0 0.0 collective-permute-done.4.refs_7_
  36.1 0.0 copy-start.8
  36.1 0.8 copy-done.7
  36.8 0.2 copy-done.8
  37.0 4.4 %inside.1 = (f32[256,1024]{1,0:T(8,128)}, bf16[256,1024]{1,0:T(8,128)(2,1)}, bf16[256,1024]{1,0:T(8,128)(2,1)}, bf16[256,1024]{1,0:T(8,128)(2,1)}, bf16[256,1024]{1,0:T(8,128)(2,1)}) custom-call(s32[1]{0:T(128)} %bitcast.place, s32[8]{0:T(128)S(1)} %copy-done.4, s32[8]{0:T(128)S(1)} %collective-permute-done.other_ids, bf16[128,2048]{1,0:T(8,128)(2,1)} %refs_0_.6, ...), custom_call_target="tpu_custom_call" | custom-call | flops 268435456 | bytes 9437184 | tf_op jit(solution)/shard_map/inside/pallas_call | solution.py:385
  41.4 4.3 %all-to-all-done.1 = bf16[32,32,128]{2,1,0:T(8,128)(2,1)S(1)} async-done(((bf16[32,32,128]{2,1,0:T(8,128)(2,1)}), bf16[32,32,128]{2,1,0:T(8,128)(2,1)S(1)}, u32[]{:S(2)}, u32[]{:S(2)}) %all-to-all-start.1) | async-done | bytes 262176 | tf_op jit(solution)/shard_map/all_to_all | solution.py:426
  45.7 3.4 %mixed.1 = (f32[256,1024]{1,0:T(8,128)}, f32[8,2,256]{2,1,0:T(2,128)}) custom-call(s32[1]{0:T(128)} %bitcast.place, s32[8]{0:T(128)S(1)} %copy-done.4, s32[8]{0:T(128)S(1)} %collective-permute-done.other_ids, f32[4,2048]{1,0:T(4,128)} %refs_0_.8, bf16[256,1024]{1,0:T(8,128)(2,1)} %get-tuple-element.41.refs_1_.refs_0_, ...), custom_call_target="tpu_custom_call" | custom-call | flops 67108864 | bytes 4784128 | tf_op jit(solution)/shard_map/mixed/pallas_call | solution.py:371
  49.1 0.0 copy-done
  49.1 13.0 %all_to_all.30.refs_4_.refs_2_ = f32[8,2,256]{2,1,0:T(2,128)S(1)} all-to-all(f32[8,2,256]{2,1,0:T(2,128)} %get-tuple-element.46), channel_id=1, replica_groups=mesh['chip'=32,'core'=2,'head'=4] {'core','head'}, dimensions={0} | all-to-all | bytes 32768 | tf_op jit(solution)/shard_map/all_to_all | solution.py:506
  62.1 3.7 %grads.1 = (bf16[256,1024]{1,0:T(8,128)(2,1)}, bf16[8,128,128]{2,1,0:T(8,128)(2,1)}) custom-call(s32[1]{0:T(128)} %bitcast.place, s32[8]{0:T(128)S(1)} %copy-done.4, s32[8]{0:T(128)S(1)} %collective-permute-done.other_ids, f32[4,2048]{1,0:T(4,128)} %refs_0_.8, bf16[256,1024]{1,0:T(8,128)(2,1)} %get-tuple-element.41.refs_1_.refs_0_, ...), custom_call_target="tpu_custom_call" | custom-call | flops 67108864 | bytes 4292608 | tf_op jit(solution)/shard_map/grads/pallas_call | solution.py:371
  65.8 4.3 %all-to-all-start.3 = ((bf16[32,32,128]{2,1,0:T(8,128)(2,1)}), bf16[32,32,128]{2,1,0:T(8,128)(2,1)S(1)}, u32[]{:S(2)}, u32[]{:S(2)}) async-start(bf16[32,32,128]{2,1,0:T(8,128)(2,1)} %bitcast.9), calls=%async_computation.3 | async-start | bytes 524288 | tf_op jit(solution)/shard_map/all_to_all | solution.py:426
  70.1 2.8 %outs.1 = f32[4,1024]{1,0:T(4,128)} custom-call(s32[1]{0:T(128)} %bitcast.place, s32[8]{0:T(128)S(1)} %copy-done.4, s32[8]{0:T(128)S(1)} %collective-permute-done.other_ids, bf16[256,1024]{1,0:T(8,128)(2,1)} %get-tuple-element.42.refs_2_.refs_0_, f32[256,1024]{1,0:T(8,128)} %get-tuple-element.45.refs_3_.refs_1_, f32[8,2,256]{2,1,0:T(2,128)S(1)} %all_to_all.30.refs_4_.refs_2_), custom_call_target="tpu_custom_call" | custom-call | bytes 3178496 | tf_op jit(solution)/shard_map/outs/pallas_call | solution.py:385
  72.9 1.2 collective-permute-start.5
  74.1 3.7 %query.1 = (bf16[128,1024]{1,0:T(8,128)(2,1)}, bf16[128,1024]{1,0:T(8,128)(2,1)}) custom-call(s32[1]{0:T(128)} %bitcast.place, s32[8]{0:T(128)S(1)} %copy-done.4, s32[8]{0:T(128)S(1)} %collective-permute-done.other_ids, bf16[256,1024]{1,0:T(8,128)(2,1)} %get-tuple-element.39.refs_0_.refs_1_, ...), custom_call_target="tpu_custom_call" | custom-call | flops 335544320 | bytes 3670016 | tf_op jit(solution)/shard_map/query/pallas_call | solution.py:385
  77.8 0.0 collective-permute-done.5
  77.8 0.0 copy-done.12
  77.8 0.6 reshape.28.refs_4_
  78.4 1.3 %all-to-all-done.3.pieces = bf16[32,32,128]{2,1,0:T(8,128)(2,1)S(1)} async-done(((bf16[32,32,128]{2,1,0:T(8,128)(2,1)}), bf16[32,32,128]{2,1,0:T(8,128)(2,1)S(1)}, u32[]{:S(2)}, u32[]{:S(2)}) %all-to-all-start.3) | async-done | bytes 262176 | tf_op jit(solution)/shard_map/all_to_all | solution.py:426
  79.8 0.7 running_sums.3
  80.5 7.2 %all-to-all-start.4 = ((bf16[32,32,128]{2,1,0:T(8,128)(2,1)}), bf16[32,32,128]{2,1,0:T(8,128)(2,1)S(1)}, u32[]{:S(2)}, u32[]{:S(2)}) async-start(bf16[32,32,128]{2,1,0:T(8,128)(2,1)} %running_sums.3), calls=%async_computation.4 | async-start | bytes 524288 | tf_op jit(solution)/shard_map/all_to_all | solution.py:426
  87.8 0.0 copy-done.13
  87.8 1.5 %collective-permute-start.8 = (bf16[128,1024]{1,0:T(8,128)(2,1)S(1)}, bf16[128,1024]{1,0:T(8,128)(2,1)S(1)}, u32[]{:S(2)}, u32[]{:S(2)}) collective-permute-start(bf16[128,1024]{1,0:T(8,128)(2,1)S(1)} %copy-done.13), channel_id=1, source_target_pairs={{0,4},{4,0},{1,5},{5,1},{2,6},{6,2},{3,7},{7,3},{8,12},{12,8},{9,1... | collective-permute-start | bytes 786440 | tf_op jit(solution)/shard_map/ppermute | solution.py:423
  89.2 5.6 %back.1 = (f32[256,1024]{1,0:T(8,128)}, f32[256,1024]{1,0:T(8,128)}, f32[4,1024]{1,0:T(4,128)}) custom-call(s32[1]{0:T(128)} %bitcast.place, s32[8]{0:T(128)S(1)} %copy-done.4, s32[8]{0:T(128)S(1)} %collective-permute-done.other_ids, bf16[256,1024]{1,0:T(8,128)(2,1)} %get-tuple-element.41.refs_1_.refs_0_, ...), custom_call_target="tpu_custom_call" | custom-call | flops 536870912 | bytes 5242880 | tf_op jit(solution)/shard_map/back/pallas_call | solution.py:385
  94.8 2.6 %all-to-all-done.4 = bf16[32,32,128]{2,1,0:T(8,128)(2,1)S(1)} async-done(((bf16[32,32,128]{2,1,0:T(8,128)(2,1)}), bf16[32,32,128]{2,1,0:T(8,128)(2,1)S(1)}, u32[]{:S(2)}, u32[]{:S(2)}) %all-to-all-start.4) | async-done | bytes 262176 | tf_op jit(solution)/shard_map/all_to_all | solution.py:426
  97.4 3.3 %copies.1 = bf16[32,16,384]{2,1,0:T(8,128)(2,1)} custom-call(s32[1]{0:T(128)} %bitcast.place, s32[8]{0:T(128)S(1)} %copy-done.4, s32[8]{0:T(128)S(1)} %collective-permute-done.other_ids, bf16[256,1024]{1,0:T(8,128)(2,1)} %get-tuple-element.39.refs_0_.refs_1_, bf16[256,1024]{1,0:T(8,128)(2,1)} %get-tuple-element.40.refs_2_.refs_1_, ...), custom_call_target="tpu_custom_call" | custom-call | flops 67108864 | bytes 2670592 | tf_op jit(solution)/shard_map/copies/pallas_call | solution.py:371
  100.8 0.0 copy-done.1
  100.8 7.1 %all-to-all-start.5 = ((bf16[32,16,384]{2,1,0:T(8,128)(2,1)}), bf16[32,16,384]{2,1,0:T(8,128)(2,1)S(1)}, u32[]{:S(2)}, u32[]{:S(2)}) async-start(bf16[32,16,384]{2,1,0:T(8,128)(2,1)} %copies.1), calls=%async_computation.5 | async-start | bytes 786432 | tf_op jit(solution)/shard_map/all_to_all | solution.py:426
  107.9 3.6 %last.1 = (bf16[128,1024]{1,0:T(8,128)(2,1)}, bf16[128,1024]{1,0:T(8,128)(2,1)}, bf16[128,1024]{1,0:T(8,128)(2,1)}, bf16[128,1024]{1,0:T(8,128)(2,1)}) custom-call(s32[1]{0:T(128)} %bitcast.place, s32[8]{0:T(128)S(1)} %copy-done.4, s32[8]{0:T(128)S(1)} %collective-permute-done.other_ids, f32[4,2048]{1,0:T(4,128)} %refs_0_.9, ...), custom_call_target="tpu_custom_call" | custom-call | flops 134217728 | bytes 6881280 | tf_op jit(solution)/shard_map/last/pallas_call | solution.py:385
  111.5 1.3 %collective-permute-start.7 = (bf16[128,1024]{1,0:T(8,128)(2,1)}, bf16[128,1024]{1,0:T(8,128)(2,1)S(1)}, u32[]{:S(2)}, u32[]{:S(2)}) collective-permute-start(bf16[128,1024]{1,0:T(8,128)(2,1)} %get-tuple-element.58), channel_id=1, source_target_pairs={{0,4},{4,0},{1,5},{5,1},{2,6},{6,2},{3,7},{7,3},{8,12},{12,8},{9,1... | collective-permute-start | bytes 786440 | tf_op jit(solution)/shard_map/ppermute | solution.py:423
  112.8 0.1 collective-permute-start.6
  112.9 0.0 collective-permute-done.8
  112.9 0.9 maximum_select_fusion.2
  113.8 0.3 collective-permute-done.7
  114.2 0.9 maximum_select_fusion.1
  115.1 0.0 collective-permute-done.6
  115.1 0.0 copy-done.10
  115.1 0.9 maximum_select_fusion
  116.0 2.6 %all-to-all-done.5.copies = bf16[32,16,384]{2,1,0:T(8,128)(2,1)S(1)} async-done(((bf16[32,16,384]{2,1,0:T(8,128)(2,1)}), bf16[32,16,384]{2,1,0:T(8,128)(2,1)S(1)}, u32[]{:S(2)}, u32[]{:S(2)}) %all-to-all-start.5) | async-done | bytes 393248 | tf_op jit(solution)/shard_map/all_to_all | solution.py:426
  118.6 0.1 total.1
  118.7 4.7 %collective-permute-start.9 = (f32[8,1024]{1,0:T(8,128)S(1)}, f32[8,1024]{1,0:T(8,128)S(1)}, u32[]{:S(2)}, u32[]{:S(2)}) collective-permute-start(f32[8,1024]{1,0:T(8,128)S(1)} %total.1), channel_id=1, source_target_pairs={{0,4},{4,0},{1,5},{5,1},{2,6},{6,2},{3,7},{7,3},{8,12},{12,8},{9,1... | collective-permute-start | bytes 98312 | tf_op jit(solution)/shard_map/ppermute | solution.py:423
  123.4 0.9 collective-permute-done.9
  124.2 0.6 fusion
  (14 shorter events, 0.0 us)
Async XLA Ops:
  0.6 5.8 %collective-permute-start.1 = (bf16[128,2048]{1,0:T(8,128)(2,1)}, bf16[128,2048]{1,0:T(8,128)(2,1)S(1)}, u32[]{:S(2)}, u32[]{:S(2)}) collective-permute-start(bf16[128,2048]{1,0:T(8,128)(2,1)} %refs_2_.1), channel_id=1, source_target_pairs={{0,4},{4,0},{1,5},{5,1},{2,6},{6,2},{3,7},{7,3},{8,12},{12,8},{9,1... | collective-permute-start | bytes 1572872 | tf_op jit(solution)/shard_map/ppermute | solution.py:423
  4.0 2.5 %collective-permute-start.2 = (bf16[128,2048]{1,0:T(8,128)(2,1)}, bf16[128,2048]{1,0:T(8,128)(2,1)S(1)}, u32[]{:S(2)}, u32[]{:S(2)}) collective-permute-start(bf16[128,2048]{1,0:T(8,128)(2,1)} %refs_4_.1), channel_id=1, source_target_pairs={{0,4},{4,0},{1,5},{5,1},{2,6},{6,2},{3,7},{7,3},{8,12},{12,8},{9,1... | collective-permute-start | bytes 1572872 | tf_op jit(solution)/shard_map/ppermute | solution.py:423
  4.1 2.4 %collective-permute-start = (s32[8]{0:T(128)}, s32[8]{0:T(128)S(1)}, u32[]{:S(2)}, u32[]{:S(2)}) collective-permute-start(s32[8]{0:T(128)} %own_ids.17), channel_id=1, source_target_pairs={{0,4},{4,0},{1,5},{5,1},{2,6},{6,2},{3,7},{7,3},{8,12},{12,8},{9,1... | collective-permute-start | bytes 104 | tf_op jit(solution)/shard_map/ppermute | solution.py:423
  4.5 2.0 %copy-start.4 = (s32[8]{0:T(128)S(1)}, s32[8]{0:T(128)}, u32[]{:S(2)}) copy-start(s32[8]{0:T(128)} %own_ids.17) | copy-start | bytes 100
  6.5 3.0 %copy-start.2 = (bf16[128,2048]{1,0:T(8,128)(2,1)}, bf16[128,2048]{1,0:T(8,128)(2,1)S(1)}, u32[]{:S(2)}) copy-start(bf16[128,2048]{1,0:T(8,128)(2,1)S(1)} %collective-permute-done.1.refs_2_.refs_3_) | copy-start | bytes 1572868
  6.5 3.0 %copy-start.3 = (bf16[128,2048]{1,0:T(8,128)(2,1)}, bf16[128,2048]{1,0:T(8,128)(2,1)S(1)}, u32[]{:S(2)}) copy-start(bf16[128,2048]{1,0:T(8,128)(2,1)S(1)} %collective-permute-done.2.refs_4_.refs_5_) | copy-start | bytes 1572868
  6.5 13.2 %copy-start.6 = (bf16[128,2048]{1,0:T(8,128)(2,1)S(1)}, bf16[128,2048]{1,0:T(8,128)(2,1)}, u32[]{:S(2)}) copy-start(bf16[128,2048]{1,0:T(8,128)(2,1)} %refs_6_.1) | copy-start | bytes 1572868
  9.4 9.5 %copy-start.5 = (bf16[128,2048]{1,0:T(8,128)(2,1)S(1)}, bf16[128,2048]{1,0:T(8,128)(2,1)}, u32[]{:S(2)}) copy-start(bf16[128,2048]{1,0:T(8,128)(2,1)} %refs_0_.6) | copy-start | bytes 1572868
  9.4 19.1 %all-to-all-start = ((bf16[32,32,128]{2,1,0:T(8,128)(2,1)}), bf16[32,32,128]{2,1,0:T(8,128)(2,1)S(1)}, u32[]{:S(2)}, u32[]{:S(2)}) async-start(bf16[32,32,128]{2,1,0:T(8,128)(2,1)} %bitcast.10), calls=%async_computation | async-start | bytes 524288 | tf_op jit(solution)/shard_map/all_to_all | solution.py:426
  18.9 17.1 %collective-permute-start.3 = (bf16[128,2048]{1,0:T(8,128)(2,1)S(1)}, bf16[128,2048]{1,0:T(8,128)(2,1)S(1)}, u32[]{:S(2)}, u32[]{:S(2)}) collective-permute-start(bf16[128,2048]{1,0:T(8,128)(2,1)S(1)} %copy-done.5), channel_id=1, source_target_pairs={{0,4},{4,0},{1,5},{5,1},{2,6},{6,2},{3,7},{7,3},{8,12},{12,8},{9,1... | collective-permute-start | bytes 1572872 | tf_op jit(solution)/shard_map/ppermute | solution.py:423
  19.6 16.4 %collective-permute-start.4 = (bf16[128,2048]{1,0:T(8,128)(2,1)S(1)}, bf16[128,2048]{1,0:T(8,128)(2,1)S(1)}, u32[]{:S(2)}, u32[]{:S(2)}) collective-permute-start(bf16[128,2048]{1,0:T(8,128)(2,1)S(1)} %copy-done.6), channel_id=1, source_target_pairs={{0,4},{4,0},{1,5},{5,1},{2,6},{6,2},{3,7},{7,3},{8,12},{12,8},{9,1... | collective-permute-start | bytes 1572872 | tf_op jit(solution)/shard_map/ppermute | solution.py:423
  29.3 16.4 %all-to-all-start.1 = ((bf16[32,32,128]{2,1,0:T(8,128)(2,1)}), bf16[32,32,128]{2,1,0:T(8,128)(2,1)S(1)}, u32[]{:S(2)}, u32[]{:S(2)}) async-start(bf16[32,32,128]{2,1,0:T(8,128)(2,1)} %running_sums.2), calls=%async_computation.1 | async-start | bytes 524288 | tf_op jit(solution)/shard_map/all_to_all | solution.py:426
  36.0 0.8 copy-start.7
  36.1 0.9 copy-start.8
  45.7 3.4 %copy-start = (bf16[32,32,128]{2,1,0:T(8,128)(2,1)}, bf16[32,32,128]{2,1,0:T(8,128)(2,1)S(1)}, u32[]{:S(2)}) copy-start(bf16[32,32,128]{2,1,0:T(8,128)(2,1)S(1)} %all-to-all-done.1) | copy-start | bytes 786436
  65.8 14.0 %all-to-all-start.3 = ((bf16[32,32,128]{2,1,0:T(8,128)(2,1)}), bf16[32,32,128]{2,1,0:T(8,128)(2,1)S(1)}, u32[]{:S(2)}, u32[]{:S(2)}) async-start(bf16[32,32,128]{2,1,0:T(8,128)(2,1)} %bitcast.9), calls=%async_computation.3 | async-start | bytes 524288 | tf_op jit(solution)/shard_map/all_to_all | solution.py:426
  72.9 4.9 %collective-permute-start.5 = (f32[4,1024]{1,0:T(4,128)}, f32[4,1024]{1,0:T(4,128)S(1)}, u32[]{:S(2)}, u32[]{:S(2)}) collective-permute-start(f32[4,1024]{1,0:T(4,128)} %outs.1), channel_id=1, source_target_pairs={{0,8},{8,0},{16,24},{24,16},{32,40},{40,32},{48,56},{56,48},{64,72... | collective-permute-start | bytes 49160 | tf_op jit(solution)/shard_map/ppermute | solution.py:536
  74.1 3.7 %copy-start.12 = (f32[4,1024]{1,0:T(4,128)S(1)}, f32[4,1024]{1,0:T(4,128)}, u32[]{:S(2)}) copy-start(f32[4,1024]{1,0:T(4,128)} %outs.1) | copy-start | bytes 49156
  80.5 7.3 %copy-start.13 = (bf16[128,1024]{1,0:T(8,128)(2,1)S(1)}, bf16[128,1024]{1,0:T(8,128)(2,1)}, u32[]{:S(2)}) copy-start(bf16[128,1024]{1,0:T(8,128)(2,1)} %get-tuple-element.60) | copy-start | bytes 786436
  80.5 16.9 %all-to-all-start.4 = ((bf16[32,32,128]{2,1,0:T(8,128)(2,1)}), bf16[32,32,128]{2,1,0:T(8,128)(2,1)S(1)}, u32[]{:S(2)}, u32[]{:S(2)}) async-start(bf16[32,32,128]{2,1,0:T(8,128)(2,1)} %running_sums.3), calls=%async_computation.4 | async-start | bytes 524288 | tf_op jit(solution)/shard_map/all_to_all | solution.py:426
  87.8 25.1 %collective-permute-start.8 = (bf16[128,1024]{1,0:T(8,128)(2,1)S(1)}, bf16[128,1024]{1,0:T(8,128)(2,1)S(1)}, u32[]{:S(2)}, u32[]{:S(2)}) collective-permute-start(bf16[128,1024]{1,0:T(8,128)(2,1)S(1)} %copy-done.13), channel_id=1, source_target_pairs={{0,4},{4,0},{1,5},{5,1},{2,6},{6,2},{3,7},{7,3},{8,12},{12,8},{9,1... | collective-permute-start | bytes 786440 | tf_op jit(solution)/shard_map/ppermute | solution.py:423
  97.4 3.3 %copy-start.1 = (bf16[32,32,128]{2,1,0:T(8,128)(2,1)}, bf16[32,32,128]{2,1,0:T(8,128)(2,1)S(1)}, u32[]{:S(2)}) copy-start(bf16[32,32,128]{2,1,0:T(8,128)(2,1)S(1)} %all-to-all-done.4) | copy-start | bytes 786436
  100.8 17.9 %all-to-all-start.5 = ((bf16[32,16,384]{2,1,0:T(8,128)(2,1)}), bf16[32,16,384]{2,1,0:T(8,128)(2,1)S(1)}, u32[]{:S(2)}, u32[]{:S(2)}) async-start(bf16[32,16,384]{2,1,0:T(8,128)(2,1)} %copies.1), calls=%async_computation.5 | async-start | bytes 786432 | tf_op jit(solution)/shard_map/all_to_all | solution.py:426
  107.9 5.0 %copy-start.9 = (bf16[128,1024]{1,0:T(8,128)(2,1)S(1)}, bf16[128,1024]{1,0:T(8,128)(2,1)}, u32[]{:S(2)}) copy-start(bf16[128,1024]{1,0:T(8,128)(2,1)} %get-tuple-element.59) | copy-start | bytes 786436
  111.5 2.6 %collective-permute-start.7 = (bf16[128,1024]{1,0:T(8,128)(2,1)}, bf16[128,1024]{1,0:T(8,128)(2,1)S(1)}, u32[]{:S(2)}, u32[]{:S(2)}) collective-permute-start(bf16[128,1024]{1,0:T(8,128)(2,1)} %get-tuple-element.58), channel_id=1, source_target_pairs={{0,4},{4,0},{1,5},{5,1},{2,6},{6,2},{3,7},{7,3},{8,12},{12,8},{9,1... | collective-permute-start | bytes 786440 | tf_op jit(solution)/shard_map/ppermute | solution.py:423
  112.8 1.4 %copy-start.11 = (bf16[128,1024]{1,0:T(8,128)(2,1)S(1)}, bf16[128,1024]{1,0:T(8,128)(2,1)}, u32[]{:S(2)}) copy-start(bf16[128,1024]{1,0:T(8,128)(2,1)} %get-tuple-element.57) | copy-start | bytes 786436
  112.8 2.3 %collective-permute-start.6 = (bf16[128,1024]{1,0:T(8,128)(2,1)}, bf16[128,1024]{1,0:T(8,128)(2,1)S(1)}, u32[]{:S(2)}, u32[]{:S(2)}) collective-permute-start(bf16[128,1024]{1,0:T(8,128)(2,1)} %get-tuple-element.56), channel_id=1, source_target_pairs={{0,4},{4,0},{1,5},{5,1},{2,6},{6,2},{3,7},{7,3},{8,12},{12,8},{9,1... | collective-permute-start | bytes 786440 | tf_op jit(solution)/shard_map/ppermute | solution.py:423
  114.2 1.0 copy-start.10
  118.7 5.5 %collective-permute-start.9 = (f32[8,1024]{1,0:T(8,128)S(1)}, f32[8,1024]{1,0:T(8,128)S(1)}, u32[]{:S(2)}, u32[]{:S(2)}) collective-permute-start(f32[8,1024]{1,0:T(8,128)S(1)} %total.1), channel_id=1, source_target_pairs={{0,4},{4,0},{1,5},{5,1},{2,6},{6,2},{3,7},{7,3},{8,12},{12,8},{9,1... | collective-permute-start | bytes 98312 | tf_op jit(solution)/shard_map/ppermute | solution.py:423

commit v9 on v7

--- a/solution.py
+++ b/solution.py
@@ -119,7 +119,7 @@
         lanes = lanes_of(h)
         scores = dot(q[:, lanes], k[:, lanes], NT)
         weights = jnp.where(causal, scores, 0.0).astype(BF16)
-        inside[:, lanes] = dot(weights, scaled[:, lanes], NN)
+        inside[:, lanes] = dot(weights, scaled[:, lanes], NN).astype(BF16)
 
 
 def mixed_kernel(
@@ -138,8 +138,8 @@
     square, cross = squares[...], crosses[...]
     for h in range(state.shape[0]):
         lanes = lanes_of(h)
-        mix = inside[:, lanes] + dot(q[:, lanes], state[h], NN)
-        mixed[:, lanes] = mix
+        mix = inside[:, lanes].astype(F32) + dot(q[:, lanes], state[h], NN)
+        mixed[:, lanes] = mix.astype(BF16)
         cot = c[:, lanes].astype(F32)
         square = square + mix * mix
         cross = cross + rows_of_members(meta, scale, lanes, spans) * cot * mix
@@ -172,7 +172,7 @@
     for h in range(delta.shape[0]):
         lanes = lanes_of(h)
         cot = c[:, lanes].astype(F32) * inverse
-        mix = mixed[:, lanes]
+        mix = mixed[:, lanes].astype(F32)
         low = (rows_of_members(meta, scale, lanes, spans) * cot - mix * factor).astype(BF16)
         grad[:, lanes] = low
         delta[h] = dot(q[:, lanes], low, TN).astype(BF16)
@@ -198,7 +198,7 @@
     inverse = jnp.transpose(jnp.broadcast_to(inverse, (DH, rows)))
     for h in range(mixed.shape[1] // DH):
         lanes = lanes_of(h)
-        normed = c[:, lanes].astype(F32) * (mixed[:, lanes] * inverse)
+        normed = c[:, lanes].astype(F32) * (mixed[:, lanes].astype(F32) * inverse)
         out_part[:, lanes] = member_sums(meta, normed, spans)
 
 
@@ -417,7 +417,7 @@
                 slow(queries), slow(q_other), slow(key_vectors), slow(k_other),
                 slow(value_vectors), slow(v_other), slow(cotangent), slow(c_other), slow(scaled),
             ),
-            [wide] + [low] * 4,
+            [low] * 5,
             "inside",
             flops=4 * unit,
         )
@@ -428,7 +428,7 @@
             [shared(MEMBERS), cols(rows), cols(rows), state(), cols(rows)],
             [cols(rows), local.whole((group, 2, rows))],
             (slow(out_scale), q, c, fast(state_in), slow(inside)),
-            [wide, pltpu.HBM((group, 2, rows), F32)],
+            [low, pltpu.HBM((group, 2, rows), F32)],
             "mixed",
             scratch=[pltpu.VMEM((rows, DH), F32)] * 2,
             flops=unit,

time: 125 us -> 124 us (level)
  no operation moved by 1% of the time
where the time goes in v9:
time: 124 us
  starting transfers between devices  47 us (38%)
  Pallas kernels  34 us (27%)
  waiting for transfers between devices  24.3 us (20%)
  blocking collectives  13 us (10%)
  other arithmetic  2.78 us (2%)
  local copies, waits for them, and re-layouts  1.66 us (1%)
    all_to_all x5, starting transfers between devices, scattered(): return lax.all_to_all(pieces, 'chip', 0, 0, tiled=True)  34.4 us
    pallas_call x9, Pallas kernels, call(): pl.pallas_call(with_meta(body), grid_spec=pltpu.PrefetchScalarGridSpec(nu...  32.4 us
    all_to_all x5, waiting for transfers between devices, scattered(): return lax.all_to_all(pieces, 'chip', 0, 0, tiled=True)  21.1 us
    all_to_all x1, blocking collectives, shards(): sums = lax.all_to_all(sums, ('core', 'head'), 0, 0, tiled=True)  13 us
    ppermute x9, starting transfers between devices, swap(): return lax.ppermute(x, 'core', [(0, 1), (1, 0)])  11.4 us
    ppermute x9, waiting for transfers between devices, swap(): return lax.ppermute(x, 'core', [(0, 1), (1, 0)])  3.19 us
    select_n x4, other arithmetic, side_by_side(): jnp.where(core == 0, jnp.concatenate([own, other], axis=1), jnp.concatena...  2.76 us
  transfers between devices with their start and end apart: 15, of which 8 were waited for; matrix products, arithmetic and copies ran while one was open for 2% of the time, Pallas kernels for 19%

profile of v9, /device:TPU:1, one launch (start us, length us, event | category | flops | bytes accessed | tf_op | source)
XLA Modules:
  0.0 123.6 jit_solution(17887032939436857908)
XLA Ops:
  0.6 3.3 %collective-permute-start.1 = (bf16[128,2048]{1,0:T(8,128)(2,1)}, bf16[128,2048]{1,0:T(8,128)(2,1)S(1)}, u32[]{:S(2)}, u32[]{:S(2)}) collective-permute-start(bf16[128,2048]{1,0:T(8,128)(2,1)} %refs_2_.1), channel_id=1, source_target_pairs={{0,4},{4,0},{1,5},{5,1},{2,6},{6,2},{3,7},{7,3},{8,12},{12,8},{9,1... | collective-permute-start | bytes 1572872 | tf_op jit(solution)/shard_map/ppermute | solution.py:352
  4.0 0.1 collective-permute-start.2
  4.1 0.4 collective-permute-start
  4.5 2.0 %collective-permute-done.other_ids = s32[8]{0:T(128)S(1)} collective-permute-done((s32[8]{0:T(128)}, s32[8]{0:T(128)S(1)}, u32[]{:S(2)}, u32[]{:S(2)}) %collective-permute-start) | collective-permute-done | bytes 64 | tf_op jit(solution)/shard_map/ppermute | solution.py:352
  6.5 0.0 collective-permute-done.1.refs_2_.refs_3_
  6.5 0.0 collective-permute-done.2.refs_4_.refs_5_
  6.5 0.0 copy-done.4
  6.5 0.0 copy-start.6
  6.5 2.9 %states.1 = (bf16[256,1024]{1,0:T(8,128)(2,1)}, bf16[8,128,128]{2,1,0:T(8,128)(2,1)}) custom-call(s32[1]{0:T(128)} %bitcast.place, s32[8]{0:T(128)S(1)} %copy-done.4, s32[8]{0:T(128)S(1)} %collective-permute-done.other_ids, f32[4,2048]{1,0:T(4,128)} %refs_0_.9, bf16[128,2048]{1,0:T(8,128)(2,1)} %refs_2_.1, ...), custom_call_target="tpu_custom_call" | custom-call | flops 67108864 | bytes 4259840 | tf_op jit(solution)/shard_map/states/pallas_call | solution.py:314
  9.4 0.0 copy-done.2
  9.4 0.0 copy-done.3
  9.4 0.0 copy-start.5
  9.4 9.4 %all-to-all-start = ((bf16[32,32,128]{2,1,0:T(8,128)(2,1)}), bf16[32,32,128]{2,1,0:T(8,128)(2,1)S(1)}, u32[]{:S(2)}, u32[]{:S(2)}) async-start(bf16[32,32,128]{2,1,0:T(8,128)(2,1)} %bitcast.10), calls=%async_computation | async-start | bytes 524288 | tf_op jit(solution)/shard_map/all_to_all | solution.py:355
  18.9 0.0 copy-done.5
  18.9 0.7 collective-permute-start.3
  19.6 0.0 copy-done.6
  19.6 0.1 collective-permute-start.4
  19.8 8.8 %all-to-all-done.pieces = bf16[32,32,128]{2,1,0:T(8,128)(2,1)S(1)} async-done(((bf16[32,32,128]{2,1,0:T(8,128)(2,1)}), bf16[32,32,128]{2,1,0:T(8,128)(2,1)S(1)}, u32[]{:S(2)}, u32[]{:S(2)}) %all-to-all-start) | async-done | bytes 262176 | tf_op jit(solution)/shard_map/all_to_all | solution.py:355
  28.6 0.7 running_sums.2
  29.3 6.7 %all-to-all-start.1 = ((bf16[32,32,128]{2,1,0:T(8,128)(2,1)}), bf16[32,32,128]{2,1,0:T(8,128)(2,1)S(1)}, u32[]{:S(2)}, u32[]{:S(2)}) async-start(bf16[32,32,128]{2,1,0:T(8,128)(2,1)} %running_sums.2), calls=%async_computation.1 | async-start | bytes 524288 | tf_op jit(solution)/shard_map/all_to_all | solution.py:355
  36.0 0.0 collective-permute-done.3.refs_1_
  36.0 0.0 copy-start.7
  36.0 0.0 collective-permute-done.4.refs_7_
  36.1 0.0 copy-start.8
  36.1 0.8 copy-done.7
  36.8 0.2 copy-done.8
  37.0 4.4 %inside.1 = (bf16[256,1024]{1,0:T(8,128)(2,1)}, bf16[256,1024]{1,0:T(8,128)(2,1)}, bf16[256,1024]{1,0:T(8,128)(2,1)}, bf16[256,1024]{1,0:T(8,128)(2,1)}, bf16[256,1024]{1,0:T(8,128)(2,1)}) custom-call(s32[1]{0:T(128)} %bitcast.place, s32[8]{0:T(128)S(1)} %copy-done.4, s32[8]{0:T(128)S(1)} %collective-permute-done.other_ids, bf16[128,2048]{1,0:T(8,128)(2,1)} %refs_0_.6, ...), custom_call_target="tpu_custom_call" | custom-call | flops 268435456 | bytes 9437184 | tf_op jit(solution)/shard_map/inside/pallas_call | solution.py:314
  41.4 4.3 %all-to-all-done.1 = bf16[32,32,128]{2,1,0:T(8,128)(2,1)S(1)} async-done(((bf16[32,32,128]{2,1,0:T(8,128)(2,1)}), bf16[32,32,128]{2,1,0:T(8,128)(2,1)S(1)}, u32[]{:S(2)}, u32[]{:S(2)}) %all-to-all-start.1) | async-done | bytes 262176 | tf_op jit(solution)/shard_map/all_to_all | solution.py:355
  45.7 3.2 %mixed.1 = (bf16[256,1024]{1,0:T(8,128)(2,1)}, f32[8,2,256]{2,1,0:T(2,128)}) custom-call(s32[1]{0:T(128)} %bitcast.place, s32[8]{0:T(128)S(1)} %copy-done.4, s32[8]{0:T(128)S(1)} %collective-permute-done.other_ids, f32[4,2048]{1,0:T(4,128)} %refs_0_.8, bf16[256,1024]{1,0:T(8,128)(2,1)} %get-tuple-element.41.refs_1_.refs_0_, ...), custom_call_target="tpu_custom_call" | custom-call | flops 67108864 | bytes 3735552 | tf_op jit(solution)/shard_map/mixed/pallas_call | solution.py:314
  48.9 0.0 copy-done.1
  48.9 13.0 %all_to_all.30.refs_4_.refs_2_ = f32[8,2,256]{2,1,0:T(2,128)S(1)} all-to-all(f32[8,2,256]{2,1,0:T(2,128)} %get-tuple-element.46), channel_id=1, replica_groups=mesh['chip'=32,'core'=2,'head'=4] {'core','head'}, dimensions={0} | all-to-all | bytes 32768 | tf_op jit(solution)/shard_map/all_to_all | solution.py:436
  61.9 3.3 %grads.1 = (bf16[256,1024]{1,0:T(8,128)(2,1)}, bf16[8,128,128]{2,1,0:T(8,128)(2,1)}) custom-call(s32[1]{0:T(128)} %bitcast.place, s32[8]{0:T(128)S(1)} %copy-done.4, s32[8]{0:T(128)S(1)} %collective-permute-done.other_ids, f32[4,2048]{1,0:T(4,128)} %refs_0_.8, bf16[256,1024]{1,0:T(8,128)(2,1)} %get-tuple-element.41.refs_1_.refs_0_, ...), custom_call_target="tpu_custom_call" | custom-call | flops 67108864 | bytes 3244032 | tf_op jit(solution)/shard_map/grads/pallas_call | solution.py:314
  65.2 4.3 %all-to-all-start.3 = ((bf16[32,32,128]{2,1,0:T(8,128)(2,1)}), bf16[32,32,128]{2,1,0:T(8,128)(2,1)S(1)}, u32[]{:S(2)}, u32[]{:S(2)}) async-start(bf16[32,32,128]{2,1,0:T(8,128)(2,1)} %bitcast.9), calls=%async_computation.3 | async-start | bytes 524288 | tf_op jit(solution)/shard_map/all_to_all | solution.py:355
  69.5 2.7 %outs.1 = f32[4,1024]{1,0:T(4,128)} custom-call(s32[1]{0:T(128)} %bitcast.place, s32[8]{0:T(128)S(1)} %copy-done.4, s32[8]{0:T(128)S(1)} %collective-permute-done.other_ids, bf16[256,1024]{1,0:T(8,128)(2,1)} %get-tuple-element.42.refs_2_.refs_0_, bf16[256,1024]{1,0:T(8,128)(2,1)} %get-tuple-element.45.refs_3_.refs_1_, ...), custom_call_target="tpu_custom_call" | custom-call | bytes 2129920 | tf_op jit(solution)/shard_map/outs/pallas_call | solution.py:314
  72.2 1.2 collective-permute-start.5
  73.5 3.7 %query.1 = (bf16[128,1024]{1,0:T(8,128)(2,1)}, bf16[128,1024]{1,0:T(8,128)(2,1)}) custom-call(s32[1]{0:T(128)} %bitcast.place, s32[8]{0:T(128)S(1)} %copy-done.4, s32[8]{0:T(128)S(1)} %collective-permute-done.other_ids, bf16[256,1024]{1,0:T(8,128)(2,1)} %get-tuple-element.39.refs_0_.refs_1_, ...), custom_call_target="tpu_custom_call" | custom-call | flops 335544320 | bytes 3670016 | tf_op jit(solution)/shard_map/query/pallas_call | solution.py:314
  77.1 0.0 collective-permute-done.5
  77.1 0.0 copy-done.12
  77.2 2.0 %all-to-all-done.3.pieces = bf16[32,32,128]{2,1,0:T(8,128)(2,1)S(1)} async-done(((bf16[32,32,128]{2,1,0:T(8,128)(2,1)}), bf16[32,32,128]{2,1,0:T(8,128)(2,1)S(1)}, u32[]{:S(2)}, u32[]{:S(2)}) %all-to-all-start.3) | async-done | bytes 262176 | tf_op jit(solution)/shard_map/all_to_all | solution.py:355
  79.2 0.7 running_sums.3
  79.9 6.7 %all-to-all-start.4 = ((bf16[32,32,128]{2,1,0:T(8,128)(2,1)}), bf16[32,32,128]{2,1,0:T(8,128)(2,1)S(1)}, u32[]{:S(2)}, u32[]{:S(2)}) async-start(bf16[32,32,128]{2,1,0:T(8,128)(2,1)} %running_sums.3), calls=%async_computation.4 | async-start | bytes 524288 | tf_op jit(solution)/shard_map/all_to_all | solution.py:355
  86.6 0.0 copy-done.13
  86.6 1.8 %collective-permute-start.8 = (bf16[128,1024]{1,0:T(8,128)(2,1)S(1)}, bf16[128,1024]{1,0:T(8,128)(2,1)S(1)}, u32[]{:S(2)}, u32[]{:S(2)}) collective-permute-start(bf16[128,1024]{1,0:T(8,128)(2,1)S(1)} %copy-done.13), channel_id=1, source_target_pairs={{0,4},{4,0},{1,5},{5,1},{2,6},{6,2},{3,7},{7,3},{8,12},{12,8},{9,1... | collective-permute-start | bytes 786440 | tf_op jit(solution)/shard_map/ppermute | solution.py:352
  88.4 5.6 %back.1 = (f32[256,1024]{1,0:T(8,128)}, f32[256,1024]{1,0:T(8,128)}, f32[4,1024]{1,0:T(4,128)}) custom-call(s32[1]{0:T(128)} %bitcast.place, s32[8]{0:T(128)S(1)} %copy-done.4, s32[8]{0:T(128)S(1)} %collective-permute-done.other_ids, bf16[256,1024]{1,0:T(8,128)(2,1)} %get-tuple-element.41.refs_1_.refs_0_, ...), custom_call_target="tpu_custom_call" | custom-call | flops 536870912 | bytes 5242880 | tf_op jit(solution)/shard_map/back/pallas_call | solution.py:314
  94.0 2.2 %all-to-all-done.4 = bf16[32,32,128]{2,1,0:T(8,128)(2,1)S(1)} async-done(((bf16[32,32,128]{2,1,0:T(8,128)(2,1)}), bf16[32,32,128]{2,1,0:T(8,128)(2,1)S(1)}, u32[]{:S(2)}, u32[]{:S(2)}) %all-to-all-start.4) | async-done | bytes 262176 | tf_op jit(solution)/shard_map/all_to_all | solution.py:355
  96.2 2.9 %copies.1 = bf16[32,16,384]{2,1,0:T(8,128)(2,1)} custom-call(s32[1]{0:T(128)} %bitcast.place, s32[8]{0:T(128)S(1)} %copy-done.4, s32[8]{0:T(128)S(1)} %collective-permute-done.other_ids, bf16[256,1024]{1,0:T(8,128)(2,1)} %get-tuple-element.39.refs_0_.refs_1_, bf16[256,1024]{1,0:T(8,128)(2,1)} %get-tuple-element.40.refs_2_.refs_1_, ...), custom_call_target="tpu_custom_call" | custom-call | flops 67108864 | bytes 2670592 | tf_op jit(solution)/shard_map/copies/pallas_call | solution.py:314
  99.2 0.0 copy-done
  99.2 7.3 %all-to-all-start.5 = ((bf16[32,16,384]{2,1,0:T(8,128)(2,1)}), bf16[32,16,384]{2,1,0:T(8,128)(2,1)S(1)}, u32[]{:S(2)}, u32[]{:S(2)}) async-start(bf16[32,16,384]{2,1,0:T(8,128)(2,1)} %copies.1), calls=%async_computation.5 | async-start | bytes 786432 | tf_op jit(solution)/shard_map/all_to_all | solution.py:355
  106.5 0.0 copy-start.9
  106.5 3.6 %last.1 = (bf16[128,1024]{1,0:T(8,128)(2,1)}, bf16[128,1024]{1,0:T(8,128)(2,1)}, bf16[128,1024]{1,0:T(8,128)(2,1)}, bf16[128,1024]{1,0:T(8,128)(2,1)}) custom-call(s32[1]{0:T(128)} %bitcast.place, s32[8]{0:T(128)S(1)} %copy-done.4, s32[8]{0:T(128)S(1)} %collective-permute-done.other_ids, f32[4,2048]{1,0:T(4,128)} %refs_0_.9, ...), custom_call_target="tpu_custom_call" | custom-call | flops 134217728 | bytes 6881280 | tf_op jit(solution)/shard_map/last/pallas_call | solution.py:314
  110.2 0.9 collective-permute-start.6
  111.1 0.1 collective-permute-start.7
  111.2 0.0 collective-permute-done.8
  111.2 0.9 maximum_select_fusion.2
  112.1 0.3 collective-permute-done.6
  112.4 0.9 maximum_select_fusion
  113.4 0.0 collective-permute-done.7
  113.4 0.0 copy-done.10
  113.4 0.9 maximum_select_fusion.1
  114.3 3.9 %all-to-all-done.5.copies = bf16[32,16,384]{2,1,0:T(8,128)(2,1)S(1)} async-done(((bf16[32,16,384]{2,1,0:T(8,128)(2,1)}), bf16[32,16,384]{2,1,0:T(8,128)(2,1)S(1)}, u32[]{:S(2)}, u32[]{:S(2)}) %all-to-all-start.5) | async-done | bytes 393248 | tf_op jit(solution)/shard_map/all_to_all | solution.py:355
  118.2 0.1 total.1
  118.2 3.8 %collective-permute-start.9 = (f32[8,1024]{1,0:T(8,128)S(1)}, f32[8,1024]{1,0:T(8,128)S(1)}, u32[]{:S(2)}, u32[]{:S(2)}) collective-permute-start(f32[8,1024]{1,0:T(8,128)S(1)} %total.1), channel_id=1, source_target_pairs={{0,4},{4,0},{1,5},{5,1},{2,6},{6,2},{3,7},{7,3},{8,12},{12,8},{9,1... | collective-permute-start | bytes 98312 | tf_op jit(solution)/shard_map/ppermute | solution.py:352
  122.1 0.9 collective-permute-done.9
  122.9 0.6 fusion
  (14 shorter events, 0.1 us)
Async XLA Ops:
  0.6 5.8 %collective-permute-start.1 = (bf16[128,2048]{1,0:T(8,128)(2,1)}, bf16[128,2048]{1,0:T(8,128)(2,1)S(1)}, u32[]{:S(2)}, u32[]{:S(2)}) collective-permute-start(bf16[128,2048]{1,0:T(8,128)(2,1)} %refs_2_.1), channel_id=1, source_target_pairs={{0,4},{4,0},{1,5},{5,1},{2,6},{6,2},{3,7},{7,3},{8,12},{12,8},{9,1... | collective-permute-start | bytes 1572872 | tf_op jit(solution)/shard_map/ppermute | solution.py:352
  4.0 2.5 %collective-permute-start.2 = (bf16[128,2048]{1,0:T(8,128)(2,1)}, bf16[128,2048]{1,0:T(8,128)(2,1)S(1)}, u32[]{:S(2)}, u32[]{:S(2)}) collective-permute-start(bf16[128,2048]{1,0:T(8,128)(2,1)} %refs_4_.1), channel_id=1, source_target_pairs={{0,4},{4,0},{1,5},{5,1},{2,6},{6,2},{3,7},{7,3},{8,12},{12,8},{9,1... | collective-permute-start | bytes 1572872 | tf_op jit(solution)/shard_map/ppermute | solution.py:352
  4.1 2.4 %collective-permute-start = (s32[8]{0:T(128)}, s32[8]{0:T(128)S(1)}, u32[]{:S(2)}, u32[]{:S(2)}) collective-permute-start(s32[8]{0:T(128)} %own_ids.17), channel_id=1, source_target_pairs={{0,4},{4,0},{1,5},{5,1},{2,6},{6,2},{3,7},{7,3},{8,12},{12,8},{9,1... | collective-permute-start | bytes 104 | tf_op jit(solution)/shard_map/ppermute | solution.py:352
  4.5 2.0 %copy-start.4 = (s32[8]{0:T(128)S(1)}, s32[8]{0:T(128)}, u32[]{:S(2)}) copy-start(s32[8]{0:T(128)} %own_ids.17) | copy-start | bytes 100
  6.5 3.0 %copy-start.2 = (bf16[128,2048]{1,0:T(8,128)(2,1)}, bf16[128,2048]{1,0:T(8,128)(2,1)S(1)}, u32[]{:S(2)}) copy-start(bf16[128,2048]{1,0:T(8,128)(2,1)S(1)} %collective-permute-done.1.refs_2_.refs_3_) | copy-start | bytes 1572868
  6.5 3.0 %copy-start.3 = (bf16[128,2048]{1,0:T(8,128)(2,1)}, bf16[128,2048]{1,0:T(8,128)(2,1)S(1)}, u32[]{:S(2)}) copy-start(bf16[128,2048]{1,0:T(8,128)(2,1)S(1)} %collective-permute-done.2.refs_4_.refs_5_) | copy-start | bytes 1572868
  6.5 13.2 %copy-start.6 = (bf16[128,2048]{1,0:T(8,128)(2,1)S(1)}, bf16[128,2048]{1,0:T(8,128)(2,1)}, u32[]{:S(2)}) copy-start(bf16[128,2048]{1,0:T(8,128)(2,1)} %refs_6_.1) | copy-start | bytes 1572868
  9.4 9.5 %copy-start.5 = (bf16[128,2048]{1,0:T(8,128)(2,1)S(1)}, bf16[128,2048]{1,0:T(8,128)(2,1)}, u32[]{:S(2)}) copy-start(bf16[128,2048]{1,0:T(8,128)(2,1)} %refs_0_.6) | copy-start | bytes 1572868
  9.4 19.1 %all-to-all-start = ((bf16[32,32,128]{2,1,0:T(8,128)(2,1)}), bf16[32,32,128]{2,1,0:T(8,128)(2,1)S(1)}, u32[]{:S(2)}, u32[]{:S(2)}) async-start(bf16[32,32,128]{2,1,0:T(8,128)(2,1)} %bitcast.10), calls=%async_computation | async-start | bytes 524288 | tf_op jit(solution)/shard_map/all_to_all | solution.py:355
  18.9 17.1 %collective-permute-start.3 = (bf16[128,2048]{1,0:T(8,128)(2,1)S(1)}, bf16[128,2048]{1,0:T(8,128)(2,1)S(1)}, u32[]{:S(2)}, u32[]{:S(2)}) collective-permute-start(bf16[128,2048]{1,0:T(8,128)(2,1)S(1)} %copy-done.5), channel_id=1, source_target_pairs={{0,4},{4,0},{1,5},{5,1},{2,6},{6,2},{3,7},{7,3},{8,12},{12,8},{9,1... | collective-permute-start | bytes 1572872 | tf_op jit(solution)/shard_map/ppermute | solution.py:352
  19.6 16.4 %collective-permute-start.4 = (bf16[128,2048]{1,0:T(8,128)(2,1)S(1)}, bf16[128,2048]{1,0:T(8,128)(2,1)S(1)}, u32[]{:S(2)}, u32[]{:S(2)}) collective-permute-start(bf16[128,2048]{1,0:T(8,128)(2,1)S(1)} %copy-done.6), channel_id=1, source_target_pairs={{0,4},{4,0},{1,5},{5,1},{2,6},{6,2},{3,7},{7,3},{8,12},{12,8},{9,1... | collective-permute-start | bytes 1572872 | tf_op jit(solution)/shard_map/ppermute | solution.py:352
  29.3 16.4 %all-to-all-start.1 = ((bf16[32,32,128]{2,1,0:T(8,128)(2,1)}), bf16[32,32,128]{2,1,0:T(8,128)(2,1)S(1)}, u32[]{:S(2)}, u32[]{:S(2)}) async-start(bf16[32,32,128]{2,1,0:T(8,128)(2,1)} %running_sums.2), calls=%async_computation.1 | async-start | bytes 524288 | tf_op jit(solution)/shard_map/all_to_all | solution.py:355
  36.0 0.8 copy-start.7
  36.1 0.9 copy-start.8
  45.7 3.2 %copy-start.1 = (bf16[32,32,128]{2,1,0:T(8,128)(2,1)}, bf16[32,32,128]{2,1,0:T(8,128)(2,1)S(1)}, u32[]{:S(2)}) copy-start(bf16[32,32,128]{2,1,0:T(8,128)(2,1)S(1)} %all-to-all-done.1) | copy-start | bytes 786436
  65.2 14.0 %all-to-all-start.3 = ((bf16[32,32,128]{2,1,0:T(8,128)(2,1)}), bf16[32,32,128]{2,1,0:T(8,128)(2,1)S(1)}, u32[]{:S(2)}, u32[]{:S(2)}) async-start(bf16[32,32,128]{2,1,0:T(8,128)(2,1)} %bitcast.9), calls=%async_computation.3 | async-start | bytes 524288 | tf_op jit(solution)/shard_map/all_to_all | solution.py:355
  72.2 4.9 %collective-permute-start.5 = (f32[4,1024]{1,0:T(4,128)}, f32[4,1024]{1,0:T(4,128)S(1)}, u32[]{:S(2)}, u32[]{:S(2)}) collective-permute-start(f32[4,1024]{1,0:T(4,128)} %outs.1), channel_id=1, source_target_pairs={{0,8},{8,0},{16,24},{24,16},{32,40},{40,32},{48,56},{56,48},{64,72... | collective-permute-start | bytes 49160 | tf_op jit(solution)/shard_map/ppermute | solution.py:467
  73.5 3.7 %copy-start.12 = (f32[4,1024]{1,0:T(4,128)S(1)}, f32[4,1024]{1,0:T(4,128)}, u32[]{:S(2)}) copy-start(f32[4,1024]{1,0:T(4,128)} %outs.1) | copy-start | bytes 49156
  79.9 6.7 %copy-start.13 = (bf16[128,1024]{1,0:T(8,128)(2,1)S(1)}, bf16[128,1024]{1,0:T(8,128)(2,1)}, u32[]{:S(2)}) copy-start(bf16[128,1024]{1,0:T(8,128)(2,1)} %get-tuple-element.60) | copy-start | bytes 786436
  79.9 16.3 %all-to-all-start.4 = ((bf16[32,32,128]{2,1,0:T(8,128)(2,1)}), bf16[32,32,128]{2,1,0:T(8,128)(2,1)S(1)}, u32[]{:S(2)}, u32[]{:S(2)}) async-start(bf16[32,32,128]{2,1,0:T(8,128)(2,1)} %running_sums.3), calls=%async_computation.4 | async-start | bytes 524288 | tf_op jit(solution)/shard_map/all_to_all | solution.py:355
  86.6 24.6 %collective-permute-start.8 = (bf16[128,1024]{1,0:T(8,128)(2,1)S(1)}, bf16[128,1024]{1,0:T(8,128)(2,1)S(1)}, u32[]{:S(2)}, u32[]{:S(2)}) collective-permute-start(bf16[128,1024]{1,0:T(8,128)(2,1)S(1)} %copy-done.13), channel_id=1, source_target_pairs={{0,4},{4,0},{1,5},{5,1},{2,6},{6,2},{3,7},{7,3},{8,12},{12,8},{9,1... | collective-permute-start | bytes 786440 | tf_op jit(solution)/shard_map/ppermute | solution.py:352
  96.2 3.0 %copy-start = (bf16[32,32,128]{2,1,0:T(8,128)(2,1)}, bf16[32,32,128]{2,1,0:T(8,128)(2,1)S(1)}, u32[]{:S(2)}) copy-start(bf16[32,32,128]{2,1,0:T(8,128)(2,1)S(1)} %all-to-all-done.4) | copy-start | bytes 786436
  99.2 19.0 %all-to-all-start.5 = ((bf16[32,16,384]{2,1,0:T(8,128)(2,1)}), bf16[32,16,384]{2,1,0:T(8,128)(2,1)S(1)}, u32[]{:S(2)}, u32[]{:S(2)}) async-start(bf16[32,16,384]{2,1,0:T(8,128)(2,1)} %copies.1), calls=%async_computation.5 | async-start | bytes 786432 | tf_op jit(solution)/shard_map/all_to_all | solution.py:355
  106.5 4.7 %copy-start.9 = (bf16[128,1024]{1,0:T(8,128)(2,1)S(1)}, bf16[128,1024]{1,0:T(8,128)(2,1)}, u32[]{:S(2)}) copy-start(bf16[128,1024]{1,0:T(8,128)(2,1)} %get-tuple-element.59) | copy-start | bytes 786436
  110.2 2.3 %collective-permute-start.6 = (bf16[128,1024]{1,0:T(8,128)(2,1)}, bf16[128,1024]{1,0:T(8,128)(2,1)S(1)}, u32[]{:S(2)}, u32[]{:S(2)}) collective-permute-start(bf16[128,1024]{1,0:T(8,128)(2,1)} %get-tuple-element.56), channel_id=1, source_target_pairs={{0,4},{4,0},{1,5},{5,1},{2,6},{6,2},{3,7},{7,3},{8,12},{12,8},{9,1... | collective-permute-start | bytes 786440 | tf_op jit(solution)/shard_map/ppermute | solution.py:352
  111.1 1.4 %copy-start.11 = (bf16[128,1024]{1,0:T(8,128)(2,1)S(1)}, bf16[128,1024]{1,0:T(8,128)(2,1)}, u32[]{:S(2)}) copy-start(bf16[128,1024]{1,0:T(8,128)(2,1)} %get-tuple-element.55) | copy-start | bytes 786436
  111.1 2.3 %collective-permute-start.7 = (bf16[128,1024]{1,0:T(8,128)(2,1)}, bf16[128,1024]{1,0:T(8,128)(2,1)S(1)}, u32[]{:S(2)}, u32[]{:S(2)}) collective-permute-start(bf16[128,1024]{1,0:T(8,128)(2,1)} %get-tuple-element.58), channel_id=1, source_target_pairs={{0,4},{4,0},{1,5},{5,1},{2,6},{6,2},{3,7},{7,3},{8,12},{12,8},{9,1... | collective-permute-start | bytes 786440 | tf_op jit(solution)/shard_map/ppermute | solution.py:352
  112.4 1.0 copy-start.10
  118.2 4.7 %collective-permute-start.9 = (f32[8,1024]{1,0:T(8,128)S(1)}, f32[8,1024]{1,0:T(8,128)S(1)}, u32[]{:S(2)}, u32[]{:S(2)}) collective-permute-start(f32[8,1024]{1,0:T(8,128)S(1)} %total.1), channel_id=1, source_target_pairs={{0,4},{4,0},{1,5},{5,1},{2,6},{6,2},{3,7},{7,3},{8,12},{12,8},{9,1... | collective-permute-start | bytes 98312 | tf_op jit(solution)/shard_map/ppermute | solution.py:352

commit v10 on v7

--- a/solution.py
+++ b/solution.py
@@ -135,20 +135,25 @@
         squares[...] = jnp.zeros_like(squares)
         crosses[...] = jnp.zeros_like(crosses)
 
-    square, cross = squares[...], crosses[...]
-    for h in range(state.shape[0]):
-        lanes = lanes_of(h)
-        mix = inside[:, lanes] + dot(q[:, lanes], state[h], NN)
-        mixed[:, lanes] = mix
-        cot = c[:, lanes].astype(F32)
-        square = square + mix * mix
-        cross = cross + rows_of_members(meta, scale, lanes, spans) * cot * mix
-    squares[...] = square
-    crosses[...] = cross
+    heads = [lanes_of(h) for h in range(state.shape[0])]
+    for h, lanes in enumerate(heads):
+        mixed[:, lanes] = inside[:, lanes] + dot(q[:, lanes], state[h], NN)
+    for s in range(spans):
+        span = pl.ds(s * SPAN, SPAN)
+        square, cross = squares[span], crosses[span]
+        for lanes in heads:
+            row = scale[0:1, lanes]
+            for m in range(1, MEMBERS):
+                row = jnp.where(meta.ids[s] == m, scale[m : m + 1, lanes], row)
+            mix = mixed[span, lanes]
+            square = square + mix * mix
+            cross = cross + row * c[span, lanes].astype(F32) * mix
+        squares[span] = square
+        crosses[span] = cross
 
     @pl.when(step == pl.num_programs(0) - 1)
     def _():
-        totals = [jnp.sum(jnp.transpose(t), axis=0, keepdims=True) for t in (square, cross)]
+        totals = [jnp.sum(jnp.transpose(t[...]), axis=0, keepdims=True) for t in (squares, crosses)]
         totals = in_order(meta, jnp.concatenate(totals, axis=0), tok)
         sums[...] = jnp.broadcast_to(totals[None], sums.shape)
 

time: 125 us -> 125 us (level)
  no operation moved by 1% of the time
where the time goes in v10:
time: 125 us; the launch traced here: 124 us
  starting transfers between devices  47 us (38%)
  Pallas kernels  34.3 us (27%)
  waiting for transfers between devices  24.3 us (19%)
  blocking collectives  13 us (10%)
  other arithmetic  2.78 us (2%)
  local copies, waits for them, and re-layouts  1.66 us (1%)
    all_to_all x5, starting transfers between devices, scattered(): return lax.all_to_all(pieces, 'chip', 0, 0, tiled=True)  34.4 us
    pallas_call x9, Pallas kernels, call(): pl.pallas_call(with_meta(body), grid_spec=pltpu.PrefetchScalarGridSpec(nu...  32.7 us
    all_to_all x5, waiting for transfers between devices, scattered(): return lax.all_to_all(pieces, 'chip', 0, 0, tiled=True)  21.1 us
    all_to_all x1, blocking collectives, shards(): sums = lax.all_to_all(sums, ('core', 'head'), 0, 0, tiled=True)  13 us
    ppermute x9, starting transfers between devices, swap(): return lax.ppermute(x, 'core', [(0, 1), (1, 0)])  11.3 us
    ppermute x9, waiting for transfers between devices, swap(): return lax.ppermute(x, 'core', [(0, 1), (1, 0)])  3.19 us
    select_n x4, other arithmetic, side_by_side(): jnp.where(core == 0, jnp.concatenate([own, other], axis=1), jnp.concatena...  2.76 us
  transfers between devices with their start and end apart: 15, of which 8 were waited for; matrix products, arithmetic and copies ran while one was open for 2% of the time, Pallas kernels for 19%

profile of v10, /device:TPU:1, one launch (start us, length us, event | category | flops | bytes accessed | tf_op | source)
XLA Modules:
  0.0 123.7 jit_solution(1261135926461798050)
XLA Ops:
  0.6 3.3 %collective-permute-start.1 = (bf16[128,2048]{1,0:T(8,128)(2,1)}, bf16[128,2048]{1,0:T(8,128)(2,1)S(1)}, u32[]{:S(2)}, u32[]{:S(2)}) collective-permute-start(bf16[128,2048]{1,0:T(8,128)(2,1)} %refs_2_.1), channel_id=1, source_target_pairs={{0,4},{4,0},{1,5},{5,1},{2,6},{6,2},{3,7},{7,3},{8,12},{12,8},{9,1... | collective-permute-start | bytes 1572872 | tf_op jit(solution)/shard_map/ppermute | solution.py:357
  4.0 0.1 collective-permute-start.2
  4.1 0.4 collective-permute-start
  4.5 2.0 %collective-permute-done.other_ids = s32[8]{0:T(128)S(1)} collective-permute-done((s32[8]{0:T(128)}, s32[8]{0:T(128)S(1)}, u32[]{:S(2)}, u32[]{:S(2)}) %collective-permute-start) | collective-permute-done | bytes 64 | tf_op jit(solution)/shard_map/ppermute | solution.py:357
  6.5 0.0 collective-permute-done.1.refs_2_.refs_3_
  6.5 0.0 collective-permute-done.2.refs_4_.refs_5_
  6.5 0.0 copy-done.4
  6.5 0.0 copy-start.6
  6.5 2.9 %states.1 = (bf16[256,1024]{1,0:T(8,128)(2,1)}, bf16[8,128,128]{2,1,0:T(8,128)(2,1)}) custom-call(s32[1]{0:T(128)} %bitcast.place, s32[8]{0:T(128)S(1)} %copy-done.4, s32[8]{0:T(128)S(1)} %collective-permute-done.other_ids, f32[4,2048]{1,0:T(4,128)} %refs_0_.9, bf16[128,2048]{1,0:T(8,128)(2,1)} %refs_2_.1, ...), custom_call_target="tpu_custom_call" | custom-call | flops 67108864 | bytes 4259840 | tf_op jit(solution)/shard_map/states/pallas_call | solution.py:319
  9.4 0.0 copy-done.2
  9.4 0.0 copy-done.3
  9.4 0.0 copy-start.5
  9.4 9.4 %all-to-all-start = ((bf16[32,32,128]{2,1,0:T(8,128)(2,1)}), bf16[32,32,128]{2,1,0:T(8,128)(2,1)S(1)}, u32[]{:S(2)}, u32[]{:S(2)}) async-start(bf16[32,32,128]{2,1,0:T(8,128)(2,1)} %bitcast.10), calls=%async_computation | async-start | bytes 524288 | tf_op jit(solution)/shard_map/all_to_all | solution.py:360
  18.9 0.0 copy-done.5
  18.9 0.7 collective-permute-start.3
  19.6 0.0 copy-done.6
  19.6 0.1 collective-permute-start.4
  19.8 8.8 %all-to-all-done.pieces = bf16[32,32,128]{2,1,0:T(8,128)(2,1)S(1)} async-done(((bf16[32,32,128]{2,1,0:T(8,128)(2,1)}), bf16[32,32,128]{2,1,0:T(8,128)(2,1)S(1)}, u32[]{:S(2)}, u32[]{:S(2)}) %all-to-all-start) | async-done | bytes 262176 | tf_op jit(solution)/shard_map/all_to_all | solution.py:360
  28.6 0.7 running_sums.2
  29.3 6.7 %all-to-all-start.1 = ((bf16[32,32,128]{2,1,0:T(8,128)(2,1)}), bf16[32,32,128]{2,1,0:T(8,128)(2,1)S(1)}, u32[]{:S(2)}, u32[]{:S(2)}) async-start(bf16[32,32,128]{2,1,0:T(8,128)(2,1)} %running_sums.2), calls=%async_computation.1 | async-start | bytes 524288 | tf_op jit(solution)/shard_map/all_to_all | solution.py:360
  36.0 0.0 collective-permute-done.3.refs_1_
  36.0 0.0 copy-start.7
  36.0 0.0 collective-permute-done.4.refs_7_
  36.1 0.0 copy-start.8
  36.1 0.8 copy-done.7
  36.8 0.2 copy-done.8
  37.0 4.4 %inside.1 = (f32[256,1024]{1,0:T(8,128)}, bf16[256,1024]{1,0:T(8,128)(2,1)}, bf16[256,1024]{1,0:T(8,128)(2,1)}, bf16[256,1024]{1,0:T(8,128)(2,1)}, bf16[256,1024]{1,0:T(8,128)(2,1)}) custom-call(s32[1]{0:T(128)} %bitcast.place, s32[8]{0:T(128)S(1)} %copy-done.4, s32[8]{0:T(128)S(1)} %collective-permute-done.other_ids, bf16[128,2048]{1,0:T(8,128)(2,1)} %refs_0_.6, ...), custom_call_target="tpu_custom_call" | custom-call | flops 268435456 | bytes 9437184 | tf_op jit(solution)/shard_map/inside/pallas_call | solution.py:319
  41.4 4.3 %all-to-all-done.1 = bf16[32,32,128]{2,1,0:T(8,128)(2,1)S(1)} async-done(((bf16[32,32,128]{2,1,0:T(8,128)(2,1)}), bf16[32,32,128]{2,1,0:T(8,128)(2,1)S(1)}, u32[]{:S(2)}, u32[]{:S(2)}) %all-to-all-start.1) | async-done | bytes 262176 | tf_op jit(solution)/shard_map/all_to_all | solution.py:360
  45.7 3.3 %mixed.1 = (f32[256,1024]{1,0:T(8,128)}, f32[8,2,256]{2,1,0:T(2,128)}) custom-call(s32[1]{0:T(128)} %bitcast.place, s32[8]{0:T(128)S(1)} %copy-done.4, s32[8]{0:T(128)S(1)} %collective-permute-done.other_ids, f32[4,2048]{1,0:T(4,128)} %refs_0_.8, bf16[256,1024]{1,0:T(8,128)(2,1)} %get-tuple-element.41.refs_1_.refs_0_, ...), custom_call_target="tpu_custom_call" | custom-call | flops 67108864 | bytes 4784128 | tf_op jit(solution)/shard_map/mixed/pallas_call | solution.py:319
  49.0 0.0 copy-done
  49.0 13.0 %all_to_all.30.refs_4_.refs_2_ = f32[8,2,256]{2,1,0:T(2,128)S(1)} all-to-all(f32[8,2,256]{2,1,0:T(2,128)} %get-tuple-element.46), channel_id=1, replica_groups=mesh['chip'=32,'core'=2,'head'=4] {'core','head'}, dimensions={0} | all-to-all | bytes 32768 | tf_op jit(solution)/shard_map/all_to_all | solution.py:441
  62.0 3.4 %grads.1 = (bf16[256,1024]{1,0:T(8,128)(2,1)}, bf16[8,128,128]{2,1,0:T(8,128)(2,1)}) custom-call(s32[1]{0:T(128)} %bitcast.place, s32[8]{0:T(128)S(1)} %copy-done.4, s32[8]{0:T(128)S(1)} %collective-permute-done.other_ids, f32[4,2048]{1,0:T(4,128)} %refs_0_.8, bf16[256,1024]{1,0:T(8,128)(2,1)} %get-tuple-element.41.refs_1_.refs_0_, ...), custom_call_target="tpu_custom_call" | custom-call | flops 67108864 | bytes 4292608 | tf_op jit(solution)/shard_map/grads/pallas_call | solution.py:319
  65.4 4.3 %all-to-all-start.3 = ((bf16[32,32,128]{2,1,0:T(8,128)(2,1)}), bf16[32,32,128]{2,1,0:T(8,128)(2,1)S(1)}, u32[]{:S(2)}, u32[]{:S(2)}) async-start(bf16[32,32,128]{2,1,0:T(8,128)(2,1)} %bitcast.9), calls=%async_computation.3 | async-start | bytes 524288 | tf_op jit(solution)/shard_map/all_to_all | solution.py:360
  69.7 2.8 %outs.1 = f32[4,1024]{1,0:T(4,128)} custom-call(s32[1]{0:T(128)} %bitcast.place, s32[8]{0:T(128)S(1)} %copy-done.4, s32[8]{0:T(128)S(1)} %collective-permute-done.other_ids, bf16[256,1024]{1,0:T(8,128)(2,1)} %get-tuple-element.42.refs_2_.refs_0_, f32[256,1024]{1,0:T(8,128)} %get-tuple-element.45.refs_3_.refs_1_, f32[8,2,256]{2,1,0:T(2,128)S(1)} %all_to_all.30.refs_4_.refs_2_), custom_call_target="tpu_custom_call" | custom-call | bytes 3178496 | tf_op jit(solution)/shard_map/outs/pallas_call | solution.py:319
  72.5 1.2 collective-permute-start.5
  73.7 3.7 %query.1 = (bf16[128,1024]{1,0:T(8,128)(2,1)}, bf16[128,1024]{1,0:T(8,128)(2,1)}) custom-call(s32[1]{0:T(128)} %bitcast.place, s32[8]{0:T(128)S(1)} %copy-done.4, s32[8]{0:T(128)S(1)} %collective-permute-done.other_ids, bf16[256,1024]{1,0:T(8,128)(2,1)} %get-tuple-element.39.refs_0_.refs_1_, ...), custom_call_target="tpu_custom_call" | custom-call | flops 335544320 | bytes 3670016 | tf_op jit(solution)/shard_map/query/pallas_call | solution.py:319
  77.4 0.0 collective-permute-done.5
  77.4 0.0 copy-done.12
  77.4 1.9 %all-to-all-done.3.pieces = bf16[32,32,128]{2,1,0:T(8,128)(2,1)S(1)} async-done(((bf16[32,32,128]{2,1,0:T(8,128)(2,1)}), bf16[32,32,128]{2,1,0:T(8,128)(2,1)S(1)}, u32[]{:S(2)}, u32[]{:S(2)}) %all-to-all-start.3) | async-done | bytes 262176 | tf_op jit(solution)/shard_map/all_to_all | solution.py:360
  79.3 0.7 running_sums.3
  80.1 6.7 %all-to-all-start.4 = ((bf16[32,32,128]{2,1,0:T(8,128)(2,1)}), bf16[32,32,128]{2,1,0:T(8,128)(2,1)S(1)}, u32[]{:S(2)}, u32[]{:S(2)}) async-start(bf16[32,32,128]{2,1,0:T(8,128)(2,1)} %running_sums.3), calls=%async_computation.4 | async-start | bytes 524288 | tf_op jit(solution)/shard_map/all_to_all | solution.py:360
  86.7 0.0 copy-done.13
  86.8 1.8 %collective-permute-start.8 = (bf16[128,1024]{1,0:T(8,128)(2,1)S(1)}, bf16[128,1024]{1,0:T(8,128)(2,1)S(1)}, u32[]{:S(2)}, u32[]{:S(2)}) collective-permute-start(bf16[128,1024]{1,0:T(8,128)(2,1)S(1)} %copy-done.13), channel_id=1, source_target_pairs={{0,4},{4,0},{1,5},{5,1},{2,6},{6,2},{3,7},{7,3},{8,12},{12,8},{9,1... | collective-permute-start | bytes 786440 | tf_op jit(solution)/shard_map/ppermute | solution.py:357
  88.6 5.6 %back.1 = (f32[256,1024]{1,0:T(8,128)}, f32[256,1024]{1,0:T(8,128)}, f32[4,1024]{1,0:T(4,128)}) custom-call(s32[1]{0:T(128)} %bitcast.place, s32[8]{0:T(128)S(1)} %copy-done.4, s32[8]{0:T(128)S(1)} %collective-permute-done.other_ids, bf16[256,1024]{1,0:T(8,128)(2,1)} %get-tuple-element.41.refs_1_.refs_0_, ...), custom_call_target="tpu_custom_call" | custom-call | flops 536870912 | bytes 5242880 | tf_op jit(solution)/shard_map/back/pallas_call | solution.py:319
  94.2 2.2 %all-to-all-done.4 = bf16[32,32,128]{2,1,0:T(8,128)(2,1)S(1)} async-done(((bf16[32,32,128]{2,1,0:T(8,128)(2,1)}), bf16[32,32,128]{2,1,0:T(8,128)(2,1)S(1)}, u32[]{:S(2)}, u32[]{:S(2)}) %all-to-all-start.4) | async-done | bytes 262176 | tf_op jit(solution)/shard_map/all_to_all | solution.py:360
  96.4 2.9 %copies.1 = bf16[32,16,384]{2,1,0:T(8,128)(2,1)} custom-call(s32[1]{0:T(128)} %bitcast.place, s32[8]{0:T(128)S(1)} %copy-done.4, s32[8]{0:T(128)S(1)} %collective-permute-done.other_ids, bf16[256,1024]{1,0:T(8,128)(2,1)} %get-tuple-element.39.refs_0_.refs_1_, bf16[256,1024]{1,0:T(8,128)(2,1)} %get-tuple-element.40.refs_2_.refs_1_, ...), custom_call_target="tpu_custom_call" | custom-call | flops 67108864 | bytes 2670592 | tf_op jit(solution)/shard_map/copies/pallas_call | solution.py:319
  99.4 0.0 copy-done.1
  99.4 7.3 %all-to-all-start.5 = ((bf16[32,16,384]{2,1,0:T(8,128)(2,1)}), bf16[32,16,384]{2,1,0:T(8,128)(2,1)S(1)}, u32[]{:S(2)}, u32[]{:S(2)}) async-start(bf16[32,16,384]{2,1,0:T(8,128)(2,1)} %copies.1), calls=%async_computation.5 | async-start | bytes 786432 | tf_op jit(solution)/shard_map/all_to_all | solution.py:360
  106.7 0.0 copy-start.9
  106.7 3.6 %last.1 = (bf16[128,1024]{1,0:T(8,128)(2,1)}, bf16[128,1024]{1,0:T(8,128)(2,1)}, bf16[128,1024]{1,0:T(8,128)(2,1)}, bf16[128,1024]{1,0:T(8,128)(2,1)}) custom-call(s32[1]{0:T(128)} %bitcast.place, s32[8]{0:T(128)S(1)} %copy-done.4, s32[8]{0:T(128)S(1)} %collective-permute-done.other_ids, f32[4,2048]{1,0:T(4,128)} %refs_0_.9, ...), custom_call_target="tpu_custom_call" | custom-call | flops 134217728 | bytes 6881280 | tf_op jit(solution)/shard_map/last/pallas_call | solution.py:319
  110.3 0.9 collective-permute-start.7
  111.2 0.1 collective-permute-start.6
  111.3 0.0 collective-permute-done.8
  111.3 0.9 maximum_select_fusion.2
  112.2 0.3 collective-permute-done.7
  112.6 0.9 maximum_select_fusion.1
  113.5 0.0 collective-permute-done.6
  113.5 0.0 copy-done.10
  113.5 0.9 maximum_select_fusion
  114.4 3.9 %all-to-all-done.5.copies = bf16[32,16,384]{2,1,0:T(8,128)(2,1)S(1)} async-done(((bf16[32,16,384]{2,1,0:T(8,128)(2,1)}), bf16[32,16,384]{2,1,0:T(8,128)(2,1)S(1)}, u32[]{:S(2)}, u32[]{:S(2)}) %all-to-all-start.5) | async-done | bytes 393248 | tf_op jit(solution)/shard_map/all_to_all | solution.py:360
  118.4 0.1 total.1
  118.4 3.8 %collective-permute-start.9 = (f32[8,1024]{1,0:T(8,128)S(1)}, f32[8,1024]{1,0:T(8,128)S(1)}, u32[]{:S(2)}, u32[]{:S(2)}) collective-permute-start(f32[8,1024]{1,0:T(8,128)S(1)} %total.1), channel_id=1, source_target_pairs={{0,4},{4,0},{1,5},{5,1},{2,6},{6,2},{3,7},{7,3},{8,12},{12,8},{9,1... | collective-permute-start | bytes 98312 | tf_op jit(solution)/shard_map/ppermute | solution.py:357
  122.2 0.9 collective-permute-done.9
  123.1 0.6 fusion
  (14 shorter events, 0.1 us)
Async XLA Ops:
  0.6 5.8 %collective-permute-start.1 = (bf16[128,2048]{1,0:T(8,128)(2,1)}, bf16[128,2048]{1,0:T(8,128)(2,1)S(1)}, u32[]{:S(2)}, u32[]{:S(2)}) collective-permute-start(bf16[128,2048]{1,0:T(8,128)(2,1)} %refs_2_.1), channel_id=1, source_target_pairs={{0,4},{4,0},{1,5},{5,1},{2,6},{6,2},{3,7},{7,3},{8,12},{12,8},{9,1... | collective-permute-start | bytes 1572872 | tf_op jit(solution)/shard_map/ppermute | solution.py:357
  4.0 2.5 %collective-permute-start.2 = (bf16[128,2048]{1,0:T(8,128)(2,1)}, bf16[128,2048]{1,0:T(8,128)(2,1)S(1)}, u32[]{:S(2)}, u32[]{:S(2)}) collective-permute-start(bf16[128,2048]{1,0:T(8,128)(2,1)} %refs_4_.1), channel_id=1, source_target_pairs={{0,4},{4,0},{1,5},{5,1},{2,6},{6,2},{3,7},{7,3},{8,12},{12,8},{9,1... | collective-permute-start | bytes 1572872 | tf_op jit(solution)/shard_map/ppermute | solution.py:357
  4.1 2.4 %collective-permute-start = (s32[8]{0:T(128)}, s32[8]{0:T(128)S(1)}, u32[]{:S(2)}, u32[]{:S(2)}) collective-permute-start(s32[8]{0:T(128)} %own_ids.17), channel_id=1, source_target_pairs={{0,4},{4,0},{1,5},{5,1},{2,6},{6,2},{3,7},{7,3},{8,12},{12,8},{9,1... | collective-permute-start | bytes 104 | tf_op jit(solution)/shard_map/ppermute | solution.py:357
  4.5 2.0 %copy-start.4 = (s32[8]{0:T(128)S(1)}, s32[8]{0:T(128)}, u32[]{:S(2)}) copy-start(s32[8]{0:T(128)} %own_ids.17) | copy-start | bytes 100
  6.5 3.0 %copy-start.2 = (bf16[128,2048]{1,0:T(8,128)(2,1)}, bf16[128,2048]{1,0:T(8,128)(2,1)S(1)}, u32[]{:S(2)}) copy-start(bf16[128,2048]{1,0:T(8,128)(2,1)S(1)} %collective-permute-done.1.refs_2_.refs_3_) | copy-start | bytes 1572868
  6.5 3.0 %copy-start.3 = (bf16[128,2048]{1,0:T(8,128)(2,1)}, bf16[128,2048]{1,0:T(8,128)(2,1)S(1)}, u32[]{:S(2)}) copy-start(bf16[128,2048]{1,0:T(8,128)(2,1)S(1)} %collective-permute-done.2.refs_4_.refs_5_) | copy-start | bytes 1572868
  6.5 13.2 %copy-start.6 = (bf16[128,2048]{1,0:T(8,128)(2,1)S(1)}, bf16[128,2048]{1,0:T(8,128)(2,1)}, u32[]{:S(2)}) copy-start(bf16[128,2048]{1,0:T(8,128)(2,1)} %refs_6_.1) | copy-start | bytes 1572868
  9.4 9.5 %copy-start.5 = (bf16[128,2048]{1,0:T(8,128)(2,1)S(1)}, bf16[128,2048]{1,0:T(8,128)(2,1)}, u32[]{:S(2)}) copy-start(bf16[128,2048]{1,0:T(8,128)(2,1)} %refs_0_.6) | copy-start | bytes 1572868
  9.4 19.1 %all-to-all-start = ((bf16[32,32,128]{2,1,0:T(8,128)(2,1)}), bf16[32,32,128]{2,1,0:T(8,128)(2,1)S(1)}, u32[]{:S(2)}, u32[]{:S(2)}) async-start(bf16[32,32,128]{2,1,0:T(8,128)(2,1)} %bitcast.10), calls=%async_computation | async-start | bytes 524288 | tf_op jit(solution)/shard_map/all_to_all | solution.py:360
  18.9 17.1 %collective-permute-start.3 = (bf16[128,2048]{1,0:T(8,128)(2,1)S(1)}, bf16[128,2048]{1,0:T(8,128)(2,1)S(1)}, u32[]{:S(2)}, u32[]{:S(2)}) collective-permute-start(bf16[128,2048]{1,0:T(8,128)(2,1)S(1)} %copy-done.5), channel_id=1, source_target_pairs={{0,4},{4,0},{1,5},{5,1},{2,6},{6,2},{3,7},{7,3},{8,12},{12,8},{9,1... | collective-permute-start | bytes 1572872 | tf_op jit(solution)/shard_map/ppermute | solution.py:357
  19.6 16.4 %collective-permute-start.4 = (bf16[128,2048]{1,0:T(8,128)(2,1)S(1)}, bf16[128,2048]{1,0:T(8,128)(2,1)S(1)}, u32[]{:S(2)}, u32[]{:S(2)}) collective-permute-start(bf16[128,2048]{1,0:T(8,128)(2,1)S(1)} %copy-done.6), channel_id=1, source_target_pairs={{0,4},{4,0},{1,5},{5,1},{2,6},{6,2},{3,7},{7,3},{8,12},{12,8},{9,1... | collective-permute-start | bytes 1572872 | tf_op jit(solution)/shard_map/ppermute | solution.py:357
  29.3 16.4 %all-to-all-start.1 = ((bf16[32,32,128]{2,1,0:T(8,128)(2,1)}), bf16[32,32,128]{2,1,0:T(8,128)(2,1)S(1)}, u32[]{:S(2)}, u32[]{:S(2)}) async-start(bf16[32,32,128]{2,1,0:T(8,128)(2,1)} %running_sums.2), calls=%async_computation.1 | async-start | bytes 524288 | tf_op jit(solution)/shard_map/all_to_all | solution.py:360
  36.0 0.8 copy-start.7
  36.1 0.9 copy-start.8
  45.7 3.3 %copy-start = (bf16[32,32,128]{2,1,0:T(8,128)(2,1)}, bf16[32,32,128]{2,1,0:T(8,128)(2,1)S(1)}, u32[]{:S(2)}) copy-start(bf16[32,32,128]{2,1,0:T(8,128)(2,1)S(1)} %all-to-all-done.1) | copy-start | bytes 786436
  65.4 14.0 %all-to-all-start.3 = ((bf16[32,32,128]{2,1,0:T(8,128)(2,1)}), bf16[32,32,128]{2,1,0:T(8,128)(2,1)S(1)}, u32[]{:S(2)}, u32[]{:S(2)}) async-start(bf16[32,32,128]{2,1,0:T(8,128)(2,1)} %bitcast.9), calls=%async_computation.3 | async-start | bytes 524288 | tf_op jit(solution)/shard_map/all_to_all | solution.py:360
  72.5 4.9 %collective-permute-start.5 = (f32[4,1024]{1,0:T(4,128)}, f32[4,1024]{1,0:T(4,128)S(1)}, u32[]{:S(2)}, u32[]{:S(2)}) collective-permute-start(f32[4,1024]{1,0:T(4,128)} %outs.1), channel_id=1, source_target_pairs={{0,8},{8,0},{16,24},{24,16},{32,40},{40,32},{48,56},{56,48},{64,72... | collective-permute-start | bytes 49160 | tf_op jit(solution)/shard_map/ppermute | solution.py:472
  73.7 3.7 %copy-start.12 = (f32[4,1024]{1,0:T(4,128)S(1)}, f32[4,1024]{1,0:T(4,128)}, u32[]{:S(2)}) copy-start(f32[4,1024]{1,0:T(4,128)} %outs.1) | copy-start | bytes 49156
  80.1 6.7 %copy-start.13 = (bf16[128,1024]{1,0:T(8,128)(2,1)S(1)}, bf16[128,1024]{1,0:T(8,128)(2,1)}, u32[]{:S(2)}) copy-start(bf16[128,1024]{1,0:T(8,128)(2,1)} %get-tuple-element.60) | copy-start | bytes 786436
  80.1 16.3 %all-to-all-start.4 = ((bf16[32,32,128]{2,1,0:T(8,128)(2,1)}), bf16[32,32,128]{2,1,0:T(8,128)(2,1)S(1)}, u32[]{:S(2)}, u32[]{:S(2)}) async-start(bf16[32,32,128]{2,1,0:T(8,128)(2,1)} %running_sums.3), calls=%async_computation.4 | async-start | bytes 524288 | tf_op jit(solution)/shard_map/all_to_all | solution.py:360
  86.8 24.6 %collective-permute-start.8 = (bf16[128,1024]{1,0:T(8,128)(2,1)S(1)}, bf16[128,1024]{1,0:T(8,128)(2,1)S(1)}, u32[]{:S(2)}, u32[]{:S(2)}) collective-permute-start(bf16[128,1024]{1,0:T(8,128)(2,1)S(1)} %copy-done.13), channel_id=1, source_target_pairs={{0,4},{4,0},{1,5},{5,1},{2,6},{6,2},{3,7},{7,3},{8,12},{12,8},{9,1... | collective-permute-start | bytes 786440 | tf_op jit(solution)/shard_map/ppermute | solution.py:357
  96.4 3.0 %copy-start.1 = (bf16[32,32,128]{2,1,0:T(8,128)(2,1)}, bf16[32,32,128]{2,1,0:T(8,128)(2,1)S(1)}, u32[]{:S(2)}) copy-start(bf16[32,32,128]{2,1,0:T(8,128)(2,1)S(1)} %all-to-all-done.4) | copy-start | bytes 786436
  99.4 19.0 %all-to-all-start.5 = ((bf16[32,16,384]{2,1,0:T(8,128)(2,1)}), bf16[32,16,384]{2,1,0:T(8,128)(2,1)S(1)}, u32[]{:S(2)}, u32[]{:S(2)}) async-start(bf16[32,16,384]{2,1,0:T(8,128)(2,1)} %copies.1), calls=%async_computation.5 | async-start | bytes 786432 | tf_op jit(solution)/shard_map/all_to_all | solution.py:360
  106.7 4.6 %copy-start.9 = (bf16[128,1024]{1,0:T(8,128)(2,1)S(1)}, bf16[128,1024]{1,0:T(8,128)(2,1)}, u32[]{:S(2)}) copy-start(bf16[128,1024]{1,0:T(8,128)(2,1)} %get-tuple-element.59) | copy-start | bytes 786436
  110.3 2.2 %collective-permute-start.7 = (bf16[128,1024]{1,0:T(8,128)(2,1)}, bf16[128,1024]{1,0:T(8,128)(2,1)S(1)}, u32[]{:S(2)}, u32[]{:S(2)}) collective-permute-start(bf16[128,1024]{1,0:T(8,128)(2,1)} %get-tuple-element.58), channel_id=1, source_target_pairs={{0,4},{4,0},{1,5},{5,1},{2,6},{6,2},{3,7},{7,3},{8,12},{12,8},{9,1... | collective-permute-start | bytes 786440 | tf_op jit(solution)/shard_map/ppermute | solution.py:357
  111.2 1.4 %copy-start.11 = (bf16[128,1024]{1,0:T(8,128)(2,1)S(1)}, bf16[128,1024]{1,0:T(8,128)(2,1)}, u32[]{:S(2)}) copy-start(bf16[128,1024]{1,0:T(8,128)(2,1)} %get-tuple-element.57) | copy-start | bytes 786436
  111.2 2.3 %collective-permute-start.6 = (bf16[128,1024]{1,0:T(8,128)(2,1)}, bf16[128,1024]{1,0:T(8,128)(2,1)S(1)}, u32[]{:S(2)}, u32[]{:S(2)}) collective-permute-start(bf16[128,1024]{1,0:T(8,128)(2,1)} %get-tuple-element.56), channel_id=1, source_target_pairs={{0,4},{4,0},{1,5},{5,1},{2,6},{6,2},{3,7},{7,3},{8,12},{12,8},{9,1... | collective-permute-start | bytes 786440 | tf_op jit(solution)/shard_map/ppermute | solution.py:357
  112.6 1.0 copy-start.10
  118.4 4.7 %collective-permute-start.9 = (f32[8,1024]{1,0:T(8,128)S(1)}, f32[8,1024]{1,0:T(8,128)S(1)}, u32[]{:S(2)}, u32[]{:S(2)}) collective-permute-start(f32[8,1024]{1,0:T(8,128)S(1)} %total.1), channel_id=1, source_target_pairs={{0,4},{4,0},{1,5},{5,1},{2,6},{6,2},{3,7},{7,3},{8,12},{12,8},{9,1... | collective-permute-start | bytes 98312 | tf_op jit(solution)/shard_map/ppermute | solution.py:357

commit v11 on v10

--- a/solution.py
+++ b/solution.py
@@ -119,7 +119,7 @@
         lanes = lanes_of(h)
         scores = dot(q[:, lanes], k[:, lanes], NT)
         weights = jnp.where(causal, scores, 0.0).astype(BF16)
-        inside[:, lanes] = dot(weights, scaled[:, lanes], NN)
+        inside[:, lanes] = dot(weights, scaled[:, lanes], NN).astype(BF16)
 
 
 def mixed_kernel(
@@ -137,7 +137,8 @@
 
     heads = [lanes_of(h) for h in range(state.shape[0])]
     for h, lanes in enumerate(heads):
-        mixed[:, lanes] = inside[:, lanes] + dot(q[:, lanes], state[h], NN)
+        mix = inside[:, lanes].astype(F32) + dot(q[:, lanes], state[h], NN)
+        mixed[:, lanes] = mix.astype(BF16)
     for s in range(spans):
         span = pl.ds(s * SPAN, SPAN)
         square, cross = squares[span], crosses[span]
@@ -145,7 +146,7 @@
             row = scale[0:1, lanes]
             for m in range(1, MEMBERS):
                 row = jnp.where(meta.ids[s] == m, scale[m : m + 1, lanes], row)
-            mix = mixed[span, lanes]
+            mix = mixed[span, lanes].astype(F32)
             square = square + mix * mix
             cross = cross + row * c[span, lanes].astype(F32) * mix
         squares[span] = square
@@ -177,7 +178,7 @@
     for h in range(delta.shape[0]):
         lanes = lanes_of(h)
         cot = c[:, lanes].astype(F32) * inverse
-        mix = mixed[:, lanes]
+        mix = mixed[:, lanes].astype(F32)
         low = (rows_of_members(meta, scale, lanes, spans) * cot - mix * factor).astype(BF16)
         grad[:, lanes] = low
         delta[h] = dot(q[:, lanes], low, TN).astype(BF16)
@@ -203,7 +204,7 @@
     inverse = jnp.transpose(jnp.broadcast_to(inverse, (DH, rows)))
     for h in range(mixed.shape[1] // DH):
         lanes = lanes_of(h)
-        normed = c[:, lanes].astype(F32) * (mixed[:, lanes] * inverse)
+        normed = c[:, lanes].astype(F32) * (mixed[:, lanes].astype(F32) * inverse)
         out_part[:, lanes] = member_sums(meta, normed, spans)
 
 
@@ -422,7 +423,7 @@
                 slow(queries), slow(q_other), slow(key_vectors), slow(k_other),
                 slow(value_vectors), slow(v_other), slow(cotangent), slow(c_other), slow(scaled),
             ),
-            [wide] + [low] * 4,
+            [low] * 5,
             "inside",
             flops=4 * unit,
         )
@@ -433,7 +434,7 @@
             [shared(MEMBERS), cols(rows), cols(rows), state(), cols(rows)],
             [cols(rows), local.whole((group, 2, rows))],
             (slow(out_scale), q, c, fast(state_in), slow(inside)),
-            [wide, pltpu.HBM((group, 2, rows), F32)],
+            [low, pltpu.HBM((group, 2, rows), F32)],
             "mixed",
             scratch=[pltpu.VMEM((rows, DH), F32)] * 2,
             flops=unit,

time: 125 us -> 124 us (level)
  no operation moved by 1% of the time
where the time goes in v11:
time: 124 us
  starting transfers between devices  47 us (38%)
  Pallas kernels  34.1 us (28%)
  waiting for transfers between devices  24.4 us (20%)
  blocking collectives  13 us (10%)
  other arithmetic  2.78 us (2%)
  local copies, waits for them, and re-layouts  1.66 us (1%)
    all_to_all x5, starting transfers between devices, scattered(): return lax.all_to_all(pieces, 'chip', 0, 0, tiled=True)  34.4 us
    pallas_call x9, Pallas kernels, call(): pl.pallas_call(with_meta(body), grid_spec=pltpu.PrefetchScalarGridSpec(nu...  32.5 us
    all_to_all x5, waiting for transfers between devices, scattered(): return lax.all_to_all(pieces, 'chip', 0, 0, tiled=True)  21.2 us
    all_to_all x1, blocking collectives, shards(): sums = lax.all_to_all(sums, ('core', 'head'), 0, 0, tiled=True)  13 us
    ppermute x9, starting transfers between devices, swap(): return lax.ppermute(x, 'core', [(0, 1), (1, 0)])  11.3 us
    ppermute x9, waiting for transfers between devices, swap(): return lax.ppermute(x, 'core', [(0, 1), (1, 0)])  3.19 us
    select_n x4, other arithmetic, side_by_side(): jnp.where(core == 0, jnp.concatenate([own, other], axis=1), jnp.concatena...  2.76 us
  transfers between devices with their start and end apart: 15, of which 8 were waited for; matrix products, arithmetic and copies ran while one was open for 2% of the time, Pallas kernels for 19%

profile of v11, /device:TPU:1, one launch (start us, length us, event | category | flops | bytes accessed | tf_op | source)
XLA Modules:
  0.0 123.7 jit_solution(14693529762007745552)
XLA Ops:
  0.6 3.3 %collective-permute-start.1 = (bf16[128,2048]{1,0:T(8,128)(2,1)}, bf16[128,2048]{1,0:T(8,128)(2,1)S(1)}, u32[]{:S(2)}, u32[]{:S(2)}) collective-permute-start(bf16[128,2048]{1,0:T(8,128)(2,1)} %refs_2_.1), channel_id=1, source_target_pairs={{0,4},{4,0},{1,5},{5,1},{2,6},{6,2},{3,7},{7,3},{8,12},{12,8},{9,1... | collective-permute-start | bytes 1572872 | tf_op jit(solution)/shard_map/ppermute | solution.py:358
  4.0 0.1 collective-permute-start.2
  4.1 0.4 collective-permute-start
  4.5 2.0 %collective-permute-done.other_ids = s32[8]{0:T(128)S(1)} collective-permute-done((s32[8]{0:T(128)}, s32[8]{0:T(128)S(1)}, u32[]{:S(2)}, u32[]{:S(2)}) %collective-permute-start) | collective-permute-done | bytes 64 | tf_op jit(solution)/shard_map/ppermute | solution.py:358
  6.5 0.0 collective-permute-done.1.refs_2_.refs_3_
  6.5 0.0 collective-permute-done.2.refs_4_.refs_5_
  6.5 0.0 copy-done.4
  6.5 0.0 copy-start.6
  6.5 2.9 %states.1 = (bf16[256,1024]{1,0:T(8,128)(2,1)}, bf16[8,128,128]{2,1,0:T(8,128)(2,1)}) custom-call(s32[1]{0:T(128)} %bitcast.place, s32[8]{0:T(128)S(1)} %copy-done.4, s32[8]{0:T(128)S(1)} %collective-permute-done.other_ids, f32[4,2048]{1,0:T(4,128)} %refs_0_.9, bf16[128,2048]{1,0:T(8,128)(2,1)} %refs_2_.1, ...), custom_call_target="tpu_custom_call" | custom-call | flops 67108864 | bytes 4259840 | tf_op jit(solution)/shard_map/states/pallas_call | solution.py:320
  9.4 0.0 copy-done.2
  9.4 0.0 copy-done.3
  9.4 0.0 copy-start.5
  9.4 9.4 %all-to-all-start = ((bf16[32,32,128]{2,1,0:T(8,128)(2,1)}), bf16[32,32,128]{2,1,0:T(8,128)(2,1)S(1)}, u32[]{:S(2)}, u32[]{:S(2)}) async-start(bf16[32,32,128]{2,1,0:T(8,128)(2,1)} %bitcast.10), calls=%async_computation | async-start | bytes 524288 | tf_op jit(solution)/shard_map/all_to_all | solution.py:361
  18.9 0.0 copy-done.5
  18.9 0.7 collective-permute-start.3
  19.6 0.0 copy-done.6
  19.6 0.1 collective-permute-start.4
  19.8 8.8 %all-to-all-done.pieces = bf16[32,32,128]{2,1,0:T(8,128)(2,1)S(1)} async-done(((bf16[32,32,128]{2,1,0:T(8,128)(2,1)}), bf16[32,32,128]{2,1,0:T(8,128)(2,1)S(1)}, u32[]{:S(2)}, u32[]{:S(2)}) %all-to-all-start) | async-done | bytes 262176 | tf_op jit(solution)/shard_map/all_to_all | solution.py:361
  28.6 0.7 running_sums.2
  29.3 6.7 %all-to-all-start.1 = ((bf16[32,32,128]{2,1,0:T(8,128)(2,1)}), bf16[32,32,128]{2,1,0:T(8,128)(2,1)S(1)}, u32[]{:S(2)}, u32[]{:S(2)}) async-start(bf16[32,32,128]{2,1,0:T(8,128)(2,1)} %running_sums.2), calls=%async_computation.1 | async-start | bytes 524288 | tf_op jit(solution)/shard_map/all_to_all | solution.py:361
  36.0 0.0 collective-permute-done.3.refs_1_
  36.0 0.0 copy-start.7
  36.0 0.0 collective-permute-done.4.refs_7_
  36.1 0.0 copy-start.8
  36.1 0.8 copy-done.7
  36.8 0.2 copy-done.8
  37.0 4.4 %inside.1 = (bf16[256,1024]{1,0:T(8,128)(2,1)}, bf16[256,1024]{1,0:T(8,128)(2,1)}, bf16[256,1024]{1,0:T(8,128)(2,1)}, bf16[256,1024]{1,0:T(8,128)(2,1)}, bf16[256,1024]{1,0:T(8,128)(2,1)}) custom-call(s32[1]{0:T(128)} %bitcast.place, s32[8]{0:T(128)S(1)} %copy-done.4, s32[8]{0:T(128)S(1)} %collective-permute-done.other_ids, bf16[128,2048]{1,0:T(8,128)(2,1)} %refs_0_.6, ...), custom_call_target="tpu_custom_call" | custom-call | flops 268435456 | bytes 9437184 | tf_op jit(solution)/shard_map/inside/pallas_call | solution.py:320
  41.4 4.3 %all-to-all-done.1 = bf16[32,32,128]{2,1,0:T(8,128)(2,1)S(1)} async-done(((bf16[32,32,128]{2,1,0:T(8,128)(2,1)}), bf16[32,32,128]{2,1,0:T(8,128)(2,1)S(1)}, u32[]{:S(2)}, u32[]{:S(2)}) %all-to-all-start.1) | async-done | bytes 262176 | tf_op jit(solution)/shard_map/all_to_all | solution.py:361
  45.7 3.3 %mixed.1 = (bf16[256,1024]{1,0:T(8,128)(2,1)}, f32[8,2,256]{2,1,0:T(2,128)}) custom-call(s32[1]{0:T(128)} %bitcast.place, s32[8]{0:T(128)S(1)} %copy-done.4, s32[8]{0:T(128)S(1)} %collective-permute-done.other_ids, f32[4,2048]{1,0:T(4,128)} %refs_0_.8, bf16[256,1024]{1,0:T(8,128)(2,1)} %get-tuple-element.41.refs_1_.refs_0_, ...), custom_call_target="tpu_custom_call" | custom-call | flops 67108864 | bytes 3735552 | tf_op jit(solution)/shard_map/mixed/pallas_call | solution.py:320
  49.0 0.0 copy-done.1
  49.0 13.0 %all_to_all.30.refs_4_.refs_2_ = f32[8,2,256]{2,1,0:T(2,128)S(1)} all-to-all(f32[8,2,256]{2,1,0:T(2,128)} %get-tuple-element.46), channel_id=1, replica_groups=mesh['chip'=32,'core'=2,'head'=4] {'core','head'}, dimensions={0} | all-to-all | bytes 32768 | tf_op jit(solution)/shard_map/all_to_all | solution.py:442
  62.0 3.3 %grads.1 = (bf16[256,1024]{1,0:T(8,128)(2,1)}, bf16[8,128,128]{2,1,0:T(8,128)(2,1)}) custom-call(s32[1]{0:T(128)} %bitcast.place, s32[8]{0:T(128)S(1)} %copy-done.4, s32[8]{0:T(128)S(1)} %collective-permute-done.other_ids, f32[4,2048]{1,0:T(4,128)} %refs_0_.8, bf16[256,1024]{1,0:T(8,128)(2,1)} %get-tuple-element.41.refs_1_.refs_0_, ...), custom_call_target="tpu_custom_call" | custom-call | flops 67108864 | bytes 3244032 | tf_op jit(solution)/shard_map/grads/pallas_call | solution.py:320
  65.3 4.3 %all-to-all-start.3 = ((bf16[32,32,128]{2,1,0:T(8,128)(2,1)}), bf16[32,32,128]{2,1,0:T(8,128)(2,1)S(1)}, u32[]{:S(2)}, u32[]{:S(2)}) async-start(bf16[32,32,128]{2,1,0:T(8,128)(2,1)} %bitcast.9), calls=%async_computation.3 | async-start | bytes 524288 | tf_op jit(solution)/shard_map/all_to_all | solution.py:361
  69.6 2.7 %outs.1 = f32[4,1024]{1,0:T(4,128)} custom-call(s32[1]{0:T(128)} %bitcast.place, s32[8]{0:T(128)S(1)} %copy-done.4, s32[8]{0:T(128)S(1)} %collective-permute-done.other_ids, bf16[256,1024]{1,0:T(8,128)(2,1)} %get-tuple-element.42.refs_2_.refs_0_, bf16[256,1024]{1,0:T(8,128)(2,1)} %get-tuple-element.45.refs_3_.refs_1_, ...), custom_call_target="tpu_custom_call" | custom-call | bytes 2129920 | tf_op jit(solution)/shard_map/outs/pallas_call | solution.py:320
  72.3 1.2 collective-permute-start.5
  73.6 3.7 %query.1 = (bf16[128,1024]{1,0:T(8,128)(2,1)}, bf16[128,1024]{1,0:T(8,128)(2,1)}) custom-call(s32[1]{0:T(128)} %bitcast.place, s32[8]{0:T(128)S(1)} %copy-done.4, s32[8]{0:T(128)S(1)} %collective-permute-done.other_ids, bf16[256,1024]{1,0:T(8,128)(2,1)} %get-tuple-element.39.refs_0_.refs_1_, ...), custom_call_target="tpu_custom_call" | custom-call | flops 335544320 | bytes 3670016 | tf_op jit(solution)/shard_map/query/pallas_call | solution.py:320
  77.2 0.0 collective-permute-done.5
  77.2 0.0 copy-done.12
  77.3 2.0 %all-to-all-done.3.pieces = bf16[32,32,128]{2,1,0:T(8,128)(2,1)S(1)} async-done(((bf16[32,32,128]{2,1,0:T(8,128)(2,1)}), bf16[32,32,128]{2,1,0:T(8,128)(2,1)S(1)}, u32[]{:S(2)}, u32[]{:S(2)}) %all-to-all-start.3) | async-done | bytes 262176 | tf_op jit(solution)/shard_map/all_to_all | solution.py:361
  79.3 0.7 running_sums.3
  80.0 6.7 %all-to-all-start.4 = ((bf16[32,32,128]{2,1,0:T(8,128)(2,1)}), bf16[32,32,128]{2,1,0:T(8,128)(2,1)S(1)}, u32[]{:S(2)}, u32[]{:S(2)}) async-start(bf16[32,32,128]{2,1,0:T(8,128)(2,1)} %running_sums.3), calls=%async_computation.4 | async-start | bytes 524288 | tf_op jit(solution)/shard_map/all_to_all | solution.py:361
  86.7 0.0 copy-done.13
  86.7 1.8 %collective-permute-start.8 = (bf16[128,1024]{1,0:T(8,128)(2,1)S(1)}, bf16[128,1024]{1,0:T(8,128)(2,1)S(1)}, u32[]{:S(2)}, u32[]{:S(2)}) collective-permute-start(bf16[128,1024]{1,0:T(8,128)(2,1)S(1)} %copy-done.13), channel_id=1, source_target_pairs={{0,4},{4,0},{1,5},{5,1},{2,6},{6,2},{3,7},{7,3},{8,12},{12,8},{9,1... | collective-permute-start | bytes 786440 | tf_op jit(solution)/shard_map/ppermute | solution.py:358
  88.5 5.6 %back.1 = (f32[256,1024]{1,0:T(8,128)}, f32[256,1024]{1,0:T(8,128)}, f32[4,1024]{1,0:T(4,128)}) custom-call(s32[1]{0:T(128)} %bitcast.place, s32[8]{0:T(128)S(1)} %copy-done.4, s32[8]{0:T(128)S(1)} %collective-permute-done.other_ids, bf16[256,1024]{1,0:T(8,128)(2,1)} %get-tuple-element.41.refs_1_.refs_0_, ...), custom_call_target="tpu_custom_call" | custom-call | flops 536870912 | bytes 5242880 | tf_op jit(solution)/shard_map/back/pallas_call | solution.py:320
  94.1 2.2 %all-to-all-done.4 = bf16[32,32,128]{2,1,0:T(8,128)(2,1)S(1)} async-done(((bf16[32,32,128]{2,1,0:T(8,128)(2,1)}), bf16[32,32,128]{2,1,0:T(8,128)(2,1)S(1)}, u32[]{:S(2)}, u32[]{:S(2)}) %all-to-all-start.4) | async-done | bytes 262176 | tf_op jit(solution)/shard_map/all_to_all | solution.py:361
  96.3 2.9 %copies.1 = bf16[32,16,384]{2,1,0:T(8,128)(2,1)} custom-call(s32[1]{0:T(128)} %bitcast.place, s32[8]{0:T(128)S(1)} %copy-done.4, s32[8]{0:T(128)S(1)} %collective-permute-done.other_ids, bf16[256,1024]{1,0:T(8,128)(2,1)} %get-tuple-element.39.refs_0_.refs_1_, bf16[256,1024]{1,0:T(8,128)(2,1)} %get-tuple-element.40.refs_2_.refs_1_, ...), custom_call_target="tpu_custom_call" | custom-call | flops 67108864 | bytes 2670592 | tf_op jit(solution)/shard_map/copies/pallas_call | solution.py:320
  99.3 0.0 copy-done
  99.3 7.3 %all-to-all-start.5 = ((bf16[32,16,384]{2,1,0:T(8,128)(2,1)}), bf16[32,16,384]{2,1,0:T(8,128)(2,1)S(1)}, u32[]{:S(2)}, u32[]{:S(2)}) async-start(bf16[32,16,384]{2,1,0:T(8,128)(2,1)} %copies.1), calls=%async_computation.5 | async-start | bytes 786432 | tf_op jit(solution)/shard_map/all_to_all | solution.py:361
  106.6 0.0 copy-start.9
  106.6 3.6 %last.1 = (bf16[128,1024]{1,0:T(8,128)(2,1)}, bf16[128,1024]{1,0:T(8,128)(2,1)}, bf16[128,1024]{1,0:T(8,128)(2,1)}, bf16[128,1024]{1,0:T(8,128)(2,1)}) custom-call(s32[1]{0:T(128)} %bitcast.place, s32[8]{0:T(128)S(1)} %copy-done.4, s32[8]{0:T(128)S(1)} %collective-permute-done.other_ids, f32[4,2048]{1,0:T(4,128)} %refs_0_.9, ...), custom_call_target="tpu_custom_call" | custom-call | flops 134217728 | bytes 6881280 | tf_op jit(solution)/shard_map/last/pallas_call | solution.py:320
  110.3 0.9 collective-permute-start.6
  111.2 0.1 collective-permute-start.7
  111.3 0.0 collective-permute-done.8
  111.3 0.9 maximum_select_fusion.2
  112.2 0.3 collective-permute-done.6
  112.5 0.9 maximum_select_fusion
  113.5 0.0 collective-permute-done.7
  113.5 0.0 copy-done.10
  113.5 0.9 maximum_select_fusion.1
  114.4 3.9 %all-to-all-done.5.copies = bf16[32,16,384]{2,1,0:T(8,128)(2,1)S(1)} async-done(((bf16[32,16,384]{2,1,0:T(8,128)(2,1)}), bf16[32,16,384]{2,1,0:T(8,128)(2,1)S(1)}, u32[]{:S(2)}, u32[]{:S(2)}) %all-to-all-start.5) | async-done | bytes 393248 | tf_op jit(solution)/shard_map/all_to_all | solution.py:361
  118.3 0.1 total.1
  118.4 3.8 %collective-permute-start.9 = (f32[8,1024]{1,0:T(8,128)S(1)}, f32[8,1024]{1,0:T(8,128)S(1)}, u32[]{:S(2)}, u32[]{:S(2)}) collective-permute-start(f32[8,1024]{1,0:T(8,128)S(1)} %total.1), channel_id=1, source_target_pairs={{0,4},{4,0},{1,5},{5,1},{2,6},{6,2},{3,7},{7,3},{8,12},{12,8},{9,1... | collective-permute-start | bytes 98312 | tf_op jit(solution)/shard_map/ppermute | solution.py:358
  122.2 0.9 collective-permute-done.9
  123.0 0.6 fusion
  (14 shorter events, 0.1 us)
Async XLA Ops:
  0.6 5.8 %collective-permute-start.1 = (bf16[128,2048]{1,0:T(8,128)(2,1)}, bf16[128,2048]{1,0:T(8,128)(2,1)S(1)}, u32[]{:S(2)}, u32[]{:S(2)}) collective-permute-start(bf16[128,2048]{1,0:T(8,128)(2,1)} %refs_2_.1), channel_id=1, source_target_pairs={{0,4},{4,0},{1,5},{5,1},{2,6},{6,2},{3,7},{7,3},{8,12},{12,8},{9,1... | collective-permute-start | bytes 1572872 | tf_op jit(solution)/shard_map/ppermute | solution.py:358
  4.0 2.5 %collective-permute-start.2 = (bf16[128,2048]{1,0:T(8,128)(2,1)}, bf16[128,2048]{1,0:T(8,128)(2,1)S(1)}, u32[]{:S(2)}, u32[]{:S(2)}) collective-permute-start(bf16[128,2048]{1,0:T(8,128)(2,1)} %refs_4_.1), channel_id=1, source_target_pairs={{0,4},{4,0},{1,5},{5,1},{2,6},{6,2},{3,7},{7,3},{8,12},{12,8},{9,1... | collective-permute-start | bytes 1572872 | tf_op jit(solution)/shard_map/ppermute | solution.py:358
  4.1 2.4 %collective-permute-start = (s32[8]{0:T(128)}, s32[8]{0:T(128)S(1)}, u32[]{:S(2)}, u32[]{:S(2)}) collective-permute-start(s32[8]{0:T(128)} %own_ids.17), channel_id=1, source_target_pairs={{0,4},{4,0},{1,5},{5,1},{2,6},{6,2},{3,7},{7,3},{8,12},{12,8},{9,1... | collective-permute-start | bytes 104 | tf_op jit(solution)/shard_map/ppermute | solution.py:358
  4.5 2.0 %copy-start.4 = (s32[8]{0:T(128)S(1)}, s32[8]{0:T(128)}, u32[]{:S(2)}) copy-start(s32[8]{0:T(128)} %own_ids.17) | copy-start | bytes 100
  6.5 3.0 %copy-start.2 = (bf16[128,2048]{1,0:T(8,128)(2,1)}, bf16[128,2048]{1,0:T(8,128)(2,1)S(1)}, u32[]{:S(2)}) copy-start(bf16[128,2048]{1,0:T(8,128)(2,1)S(1)} %collective-permute-done.1.refs_2_.refs_3_) | copy-start | bytes 1572868
  6.5 3.0 %copy-start.3 = (bf16[128,2048]{1,0:T(8,128)(2,1)}, bf16[128,2048]{1,0:T(8,128)(2,1)S(1)}, u32[]{:S(2)}) copy-start(bf16[128,2048]{1,0:T(8,128)(2,1)S(1)} %collective-permute-done.2.refs_4_.refs_5_) | copy-start | bytes 1572868
  6.5 13.2 %copy-start.6 = (bf16[128,2048]{1,0:T(8,128)(2,1)S(1)}, bf16[128,2048]{1,0:T(8,128)(2,1)}, u32[]{:S(2)}) copy-start(bf16[128,2048]{1,0:T(8,128)(2,1)} %refs_6_.1) | copy-start | bytes 1572868
  9.4 9.5 %copy-start.5 = (bf16[128,2048]{1,0:T(8,128)(2,1)S(1)}, bf16[128,2048]{1,0:T(8,128)(2,1)}, u32[]{:S(2)}) copy-start(bf16[128,2048]{1,0:T(8,128)(2,1)} %refs_0_.6) | copy-start | bytes 1572868
  9.4 19.1 %all-to-all-start = ((bf16[32,32,128]{2,1,0:T(8,128)(2,1)}), bf16[32,32,128]{2,1,0:T(8,128)(2,1)S(1)}, u32[]{:S(2)}, u32[]{:S(2)}) async-start(bf16[32,32,128]{2,1,0:T(8,128)(2,1)} %bitcast.10), calls=%async_computation | async-start | bytes 524288 | tf_op jit(solution)/shard_map/all_to_all | solution.py:361
  18.9 17.1 %collective-permute-start.3 = (bf16[128,2048]{1,0:T(8,128)(2,1)S(1)}, bf16[128,2048]{1,0:T(8,128)(2,1)S(1)}, u32[]{:S(2)}, u32[]{:S(2)}) collective-permute-start(bf16[128,2048]{1,0:T(8,128)(2,1)S(1)} %copy-done.5), channel_id=1, source_target_pairs={{0,4},{4,0},{1,5},{5,1},{2,6},{6,2},{3,7},{7,3},{8,12},{12,8},{9,1... | collective-permute-start | bytes 1572872 | tf_op jit(solution)/shard_map/ppermute | solution.py:358
  19.6 16.4 %collective-permute-start.4 = (bf16[128,2048]{1,0:T(8,128)(2,1)S(1)}, bf16[128,2048]{1,0:T(8,128)(2,1)S(1)}, u32[]{:S(2)}, u32[]{:S(2)}) collective-permute-start(bf16[128,2048]{1,0:T(8,128)(2,1)S(1)} %copy-done.6), channel_id=1, source_target_pairs={{0,4},{4,0},{1,5},{5,1},{2,6},{6,2},{3,7},{7,3},{8,12},{12,8},{9,1... | collective-permute-start | bytes 1572872 | tf_op jit(solution)/shard_map/ppermute | solution.py:358
  29.3 16.4 %all-to-all-start.1 = ((bf16[32,32,128]{2,1,0:T(8,128)(2,1)}), bf16[32,32,128]{2,1,0:T(8,128)(2,1)S(1)}, u32[]{:S(2)}, u32[]{:S(2)}) async-start(bf16[32,32,128]{2,1,0:T(8,128)(2,1)} %running_sums.2), calls=%async_computation.1 | async-start | bytes 524288 | tf_op jit(solution)/shard_map/all_to_all | solution.py:361
  36.0 0.8 copy-start.7
  36.1 0.9 copy-start.8
  45.7 3.3 %copy-start.1 = (bf16[32,32,128]{2,1,0:T(8,128)(2,1)}, bf16[32,32,128]{2,1,0:T(8,128)(2,1)S(1)}, u32[]{:S(2)}) copy-start(bf16[32,32,128]{2,1,0:T(8,128)(2,1)S(1)} %all-to-all-done.1) | copy-start | bytes 786436
  65.3 14.0 %all-to-all-start.3 = ((bf16[32,32,128]{2,1,0:T(8,128)(2,1)}), bf16[32,32,128]{2,1,0:T(8,128)(2,1)S(1)}, u32[]{:S(2)}, u32[]{:S(2)}) async-start(bf16[32,32,128]{2,1,0:T(8,128)(2,1)} %bitcast.9), calls=%async_computation.3 | async-start | bytes 524288 | tf_op jit(solution)/shard_map/all_to_all | solution.py:361
  72.3 4.9 %collective-permute-start.5 = (f32[4,1024]{1,0:T(4,128)}, f32[4,1024]{1,0:T(4,128)S(1)}, u32[]{:S(2)}, u32[]{:S(2)}) collective-permute-start(f32[4,1024]{1,0:T(4,128)} %outs.1), channel_id=1, source_target_pairs={{0,8},{8,0},{16,24},{24,16},{32,40},{40,32},{48,56},{56,48},{64,72... | collective-permute-start | bytes 49160 | tf_op jit(solution)/shard_map/ppermute | solution.py:473
  73.6 3.7 %copy-start.12 = (f32[4,1024]{1,0:T(4,128)S(1)}, f32[4,1024]{1,0:T(4,128)}, u32[]{:S(2)}) copy-start(f32[4,1024]{1,0:T(4,128)} %outs.1) | copy-start | bytes 49156
  80.0 6.7 %copy-start.13 = (bf16[128,1024]{1,0:T(8,128)(2,1)S(1)}, bf16[128,1024]{1,0:T(8,128)(2,1)}, u32[]{:S(2)}) copy-start(bf16[128,1024]{1,0:T(8,128)(2,1)} %get-tuple-element.60) | copy-start | bytes 786436
  80.0 16.3 %all-to-all-start.4 = ((bf16[32,32,128]{2,1,0:T(8,128)(2,1)}), bf16[32,32,128]{2,1,0:T(8,128)(2,1)S(1)}, u32[]{:S(2)}, u32[]{:S(2)}) async-start(bf16[32,32,128]{2,1,0:T(8,128)(2,1)} %running_sums.3), calls=%async_computation.4 | async-start | bytes 524288 | tf_op jit(solution)/shard_map/all_to_all | solution.py:361
  86.7 24.6 %collective-permute-start.8 = (bf16[128,1024]{1,0:T(8,128)(2,1)S(1)}, bf16[128,1024]{1,0:T(8,128)(2,1)S(1)}, u32[]{:S(2)}, u32[]{:S(2)}) collective-permute-start(bf16[128,1024]{1,0:T(8,128)(2,1)S(1)} %copy-done.13), channel_id=1, source_target_pairs={{0,4},{4,0},{1,5},{5,1},{2,6},{6,2},{3,7},{7,3},{8,12},{12,8},{9,1... | collective-permute-start | bytes 786440 | tf_op jit(solution)/shard_map/ppermute | solution.py:358
  96.3 3.0 %copy-start = (bf16[32,32,128]{2,1,0:T(8,128)(2,1)}, bf16[32,32,128]{2,1,0:T(8,128)(2,1)S(1)}, u32[]{:S(2)}) copy-start(bf16[32,32,128]{2,1,0:T(8,128)(2,1)S(1)} %all-to-all-done.4) | copy-start | bytes 786436
  99.3 19.0 %all-to-all-start.5 = ((bf16[32,16,384]{2,1,0:T(8,128)(2,1)}), bf16[32,16,384]{2,1,0:T(8,128)(2,1)S(1)}, u32[]{:S(2)}, u32[]{:S(2)}) async-start(bf16[32,16,384]{2,1,0:T(8,128)(2,1)} %copies.1), calls=%async_computation.5 | async-start | bytes 786432 | tf_op jit(solution)/shard_map/all_to_all | solution.py:361
  106.6 4.7 %copy-start.9 = (bf16[128,1024]{1,0:T(8,128)(2,1)S(1)}, bf16[128,1024]{1,0:T(8,128)(2,1)}, u32[]{:S(2)}) copy-start(bf16[128,1024]{1,0:T(8,128)(2,1)} %get-tuple-element.59) | copy-start | bytes 786436
  110.3 2.3 %collective-permute-start.6 = (bf16[128,1024]{1,0:T(8,128)(2,1)}, bf16[128,1024]{1,0:T(8,128)(2,1)S(1)}, u32[]{:S(2)}, u32[]{:S(2)}) collective-permute-start(bf16[128,1024]{1,0:T(8,128)(2,1)} %get-tuple-element.56), channel_id=1, source_target_pairs={{0,4},{4,0},{1,5},{5,1},{2,6},{6,2},{3,7},{7,3},{8,12},{12,8},{9,1... | collective-permute-start | bytes 786440 | tf_op jit(solution)/shard_map/ppermute | solution.py:358
  111.2 1.4 %copy-start.11 = (bf16[128,1024]{1,0:T(8,128)(2,1)S(1)}, bf16[128,1024]{1,0:T(8,128)(2,1)}, u32[]{:S(2)}) copy-start(bf16[128,1024]{1,0:T(8,128)(2,1)} %get-tuple-element.55) | copy-start | bytes 786436
  111.2 2.3 %collective-permute-start.7 = (bf16[128,1024]{1,0:T(8,128)(2,1)}, bf16[128,1024]{1,0:T(8,128)(2,1)S(1)}, u32[]{:S(2)}, u32[]{:S(2)}) collective-permute-start(bf16[128,1024]{1,0:T(8,128)(2,1)} %get-tuple-element.58), channel_id=1, source_target_pairs={{0,4},{4,0},{1,5},{5,1},{2,6},{6,2},{3,7},{7,3},{8,12},{12,8},{9,1... | collective-permute-start | bytes 786440 | tf_op jit(solution)/shard_map/ppermute | solution.py:358
  112.5 1.0 copy-start.10
  118.4 4.7 %collective-permute-start.9 = (f32[8,1024]{1,0:T(8,128)S(1)}, f32[8,1024]{1,0:T(8,128)S(1)}, u32[]{:S(2)}, u32[]{:S(2)}) collective-permute-start(f32[8,1024]{1,0:T(8,128)S(1)} %total.1), channel_id=1, source_target_pairs={{0,4},{4,0},{1,5},{5,1},{2,6},{6,2},{3,7},{7,3},{8,12},{12,8},{9,1... | collective-permute-start | bytes 98312 | tf_op jit(solution)/shard_map/ppermute | solution.py:358
